TPU v7x, 32 devices: a whole 2x2x4 slice. The times are simulated.
32 devices in a mesh: row: 4 (over y, core), col: 8 (over z, x).
Axes of the slice: x: 2, y: 2, z: 4, core: 2. Of those that a mesh axis runs over, the one named last changes fastest.
Arguments:
- tokens: bfloat16 [8192, 2048], P('row', 'col'), may hold values from -7 to 7
- lengths: int32 [8, 4], P('row'), may hold values from 1 to 800, 1024 in all within a row
- w_query: bfloat16 [2048, 2048], P('row', 'col'), may hold values from -0.1875 to 0.1875
- b_query: float32 [2048], P('col'), may hold values from -3 to 3
- w_key: bfloat16 [2048, 2048], P('row', 'col'), may hold values from -0.125 to 0.125
- w_value: bfloat16 [2048, 2048], P('row', 'col'), may hold values from -0.125 to 0.125
- b_value: float32 [2048], P('col'), may hold values from -3 to 3
- w_proj: bfloat16 [2048, 2048], P('col', 'row'), may hold values from -0.5 to 0.5
- b_proj: float32 [2048], P('col'), may hold values from -2 to 2
- norm_gain: float32 [2048], P('col'), may hold values from 0.5 to 1.5
- norm_shift: float32 [2048], P('col'), may hold values from -2 to 2
- w_up: bfloat16 [2048, 8192], P('row', 'col'), may hold values from -0.125 to 0.125
- b_up: float32 [8192], P('col'), may hold values from -3 to 3
- w_down: bfloat16 [8192, 2048], P('col', 'row'), may hold values from -0.0625 to 0.0625
- b_down: float32 [2048], P('col'), may hold values from -2 to 2
- final_gain: float32 [2048], P('col'), may hold values from 0.5 to 1.5
- final_shift: float32 [2048], P('col'), may hold values from -2 to 2
- cotangent: bfloat16 [8192, 2048], P('row', 'col'), may hold values from -6 to 6
Outputs:
- layer_out: bfloat16 [8192, 2048], P('row', 'col')
- grad_tokens: float32 [8192, 2048], P('row', 'col')
- grad_query: float32 [2048, 2048], P('row', 'col')
- grad_qbias: float32 [2048], P('col')
- grad_key: float32 [2048, 2048], P('row', 'col')
- grad_value: float32 [2048, 2048], P('row', 'col')
- grad_vbias: float32 [2048], P('col')
- grad_proj: float32 [2048, 2048], P('col', 'row')
- grad_pbias: float32 [2048], P('col')
- grad_ngain: float32 [2048], P('col')
- grad_nshift: float32 [2048], P('col')
- grad_up: float32 [2048, 8192], P('row', 'col')
- grad_ubias: float32 [8192], P('col')
- grad_down: float32 [8192, 2048], P('col', 'row')
- grad_dbias: float32 [2048], P('col')
- grad_fgain: float32 [2048], P('col')
- grad_fshift: float32 [2048], P('col')
- norms: float32 [3], replicated
Inputs may be any that keep to these rules, and one draw needn't show every extreme that they name: Each row of 4 entries sums to 1024; its first 3 entries are the lengths of its documents in order, the last counts the padding tokens at the sequence's end.
All inputs are finite; a program needn't handle non-finite values.
Results may differ from a plain program's by a relative error of at most 0.017.
Values may be sent and summed in bfloat16 or wider, within the bound.
No kernel may reach another device: no remote copies, remote signals or barrier semaphores. Data moves between devices by JAX's collectives and lax.ppermute only.
A program may use at most 192 MiB of HBM per device.

v0:
```python
import jax
import jax.numpy as jnp
from jax import lax
from jax.sharding import PartitionSpec as P

HD = 128
LEN = 1024


EPS = 1e-06
NEGATIVE = -1000000000.0


def segment_ids(lengths):
    slots = lengths.shape[1]
    ends = jnp.cumsum(lengths, axis=1)
    places = jnp.arange(LEN, dtype=jnp.int32)
    hits = (places[None, :, None] >= ends[:, None, : slots - 1]).astype(jnp.int32)
    return jnp.sum(hits, axis=2)


def gather_features(piece):
    return lax.all_gather(piece, "col", axis=1, tiled=True)


def scatter_features(partial_sum):
    return lax.psum_scatter(partial_sum, "col", scatter_dimension=1, tiled=True)


def row_totals(first, second):
    return lax.psum((first, second), "col")


def gather_weights(w_query, w_key, w_value, w_up, w_proj, w_down):
    inner = (
        lax.all_gather(w_query, "row", axis=0, tiled=True),
        lax.all_gather(w_key, "row", axis=0, tiled=True),
        lax.all_gather(w_value, "row", axis=0, tiled=True),
        lax.all_gather(w_up, "row", axis=0, tiled=True),
    )
    outer = (
        lax.all_gather(w_proj, "row", axis=1, tiled=True),
        lax.all_gather(w_down, "row", axis=1, tiled=True),
    )
    return (inner, outer)


def norm_shares(resid, gain, shift):
    width = resid.shape[1] * lax.axis_size("col")
    total, squares = row_totals(jnp.sum(resid, axis=1), jnp.sum(resid * resid, axis=1))
    mean = total / width
    rstd = lax.rsqrt(squares / width - mean * mean + EPS)
    normed = (resid - mean[:, None]) * rstd[:, None]
    return (normed * gain + shift, normed, rstd)


def norm_back(upstream, normed, rstd, gain):
    width = upstream.shape[1] * lax.axis_size("col")
    scaled = upstream * gain
    total, along = row_totals(jnp.sum(scaled, axis=1), jnp.sum(scaled * normed, axis=1))
    back = rstd[:, None] * (scaled - total[:, None] / width - normed * (along[:, None] / width))
    return (back, jnp.sum(upstream * normed, axis=0), jnp.sum(upstream, axis=0))


def attend_forward(pack):
    queries, keys, values, ids = pack
    scale = queries.shape[2] ** (-0.5)
    block = min(512, queries.shape[0])
    same = ids[:, None] == ids[None, :]
    outputs = []
    logsums = []
    for begin in range(0, queries.shape[0], block):
        scores = (
            jnp.einsum(
                "qhd,khd->hqk",
                queries[begin : begin + block],
                keys,
                preferred_element_type=jnp.float32,
            )
            * scale
        )
        scores = jnp.where(same[None, begin : begin + block], scores, NEGATIVE)
        peak = jnp.max(scores, axis=2, keepdims=True)
        expo = jnp.exp(scores - peak)
        total = jnp.sum(expo, axis=2, keepdims=True)
        probs = (expo / total).astype(jnp.bfloat16)
        outputs.append(
            jnp.einsum("hqk,khd->qhd", probs, values, preferred_element_type=jnp.float32)
        )
        logsums.append((peak + jnp.log(total))[:, :, 0])
    return (jnp.concatenate(outputs, axis=0), jnp.concatenate(logsums, axis=1))


def attend_back(pack):
    queries, keys, values, ids, logsum, grad_out = pack
    scale = queries.shape[2] ** (-0.5)
    block = min(512, queries.shape[0])
    same = ids[:, None] == ids[None, :]
    grad_keys = jnp.zeros(keys.shape, jnp.float32)
    grad_values = jnp.zeros(values.shape, jnp.float32)
    grad_queries = []
    for begin in range(0, queries.shape[0], block):
        query_rows = queries[begin : begin + block]
        grad_rows = grad_out[begin : begin + block]
        scores = (
            jnp.einsum("qhd,khd->hqk", query_rows, keys, preferred_element_type=jnp.float32) * scale
        )
        scores = jnp.where(same[None, begin : begin + block], scores, NEGATIVE)
        probs = jnp.exp(scores - logsum[:, begin : begin + block, None])
        grad_probs = jnp.einsum(
            "qhd,khd->hqk", grad_rows, values, preferred_element_type=jnp.float32
        )
        inner = jnp.sum(probs * grad_probs, axis=2, keepdims=True)
        grad_scores = (probs * (grad_probs - inner)).astype(jnp.bfloat16)
        grad_queries.append(
            jnp.einsum("hqk,khd->qhd", grad_scores, keys, preferred_element_type=jnp.float32)
            * scale
        )
        grad_keys = (
            grad_keys
            + jnp.einsum(
                "hqk,qhd->khd", grad_scores, query_rows, preferred_element_type=jnp.float32
            )
            * scale
        )
        grad_values = grad_values + jnp.einsum(
            "hqk,qhd->khd",
            probs.astype(jnp.bfloat16),
            grad_rows,
            preferred_element_type=jnp.float32,
        )
    return (jnp.concatenate(grad_queries, axis=0), grad_keys, grad_values)


def per_device(
    tokens,
    lengths,
    w_query,
    b_query,
    w_key,
    w_value,
    b_value,
    w_proj,
    b_proj,
    norm_gain,
    norm_shift,
    w_up,
    b_up,
    w_down,
    b_down,
    final_gain,
    final_shift,
    cotangent,
):
    rows, share = tokens.shape
    heads = w_query.shape[1] // HD
    ids = segment_ids(lengths)
    seq_count = ids.shape[0]
    valid = (ids.reshape(rows) != lengths.shape[1] - 1).astype(jnp.float32)[:, None]
    inner, outer = gather_weights(w_query, w_key, w_value, w_up, w_proj, w_down)
    full_query, full_key, full_value, full_up = inner
    full_proj, full_down = outer
    stream = tokens.astype(jnp.float32)
    gathered = gather_features(tokens)
    queries = (jnp.dot(gathered, full_query, preferred_element_type=jnp.float32) + b_query).astype(
        jnp.bfloat16
    )
    keys = jnp.dot(gathered, full_key, preferred_element_type=jnp.float32).astype(jnp.bfloat16)
    values = (jnp.dot(gathered, full_value, preferred_element_type=jnp.float32) + b_value).astype(
        jnp.bfloat16
    )
    shape = (seq_count, LEN, heads, HD)
    query_seq = queries.reshape(shape)
    key_seq = keys.reshape(shape)
    value_seq = values.reshape(shape)
    mixed, logsum = lax.map(attend_forward, (query_seq, key_seq, value_seq, ids))
    heads_out = mixed.reshape(rows, heads * HD).astype(jnp.bfloat16)
    attn = (
        scatter_features(jnp.dot(heads_out, full_proj, preferred_element_type=jnp.float32)) + b_proj
    )
    hidden, normed_one, rstd_one = norm_shares(stream + attn, norm_gain, norm_shift)
    hidden_low = gather_features(hidden.astype(jnp.bfloat16))
    pre = jnp.dot(hidden_low, full_up, preferred_element_type=jnp.float32) + b_up
    act, gelu_back = jax.vjp(lambda inputs: jax.nn.gelu(inputs, approximate=True), pre)
    act_low = act.astype(jnp.bfloat16)
    ffn = scatter_features(jnp.dot(act_low, full_down, preferred_element_type=jnp.float32)) + b_down
    result, normed_two, rstd_two = norm_shares(hidden + ffn, final_gain, final_shift)
    totals = lax.psum(
        (
            jnp.sum(valid * stream * stream),
            jnp.sum(valid * attn * attn),
            jnp.sum(valid * ffn * ffn),
            jnp.sum(valid) * share,
        ),
        ("row", "col"),
    )
    norms = jnp.sqrt(jnp.stack([totals[0], totals[1], totals[2]]) / totals[3])
    back_inner, back_outer = gather_weights(w_query, w_key, w_value, w_up, w_proj, w_down)
    full_query, full_key, full_value, full_up = back_inner
    full_proj, full_down = back_outer
    grad_two, grad_fgain, grad_fshift = norm_back(
        cotangent.astype(jnp.float32), normed_two, rstd_two, final_gain
    )
    grad_ffn = grad_two.astype(jnp.bfloat16)
    grad_dbias = jnp.sum(grad_ffn.astype(jnp.float32), axis=0)
    ffn_wide = gather_features(grad_ffn)
    grad_down = jnp.einsum("tf,td->fd", act_low, ffn_wide, preferred_element_type=jnp.float32)
    grad_act = jnp.einsum("td,fd->tf", ffn_wide, full_down, preferred_element_type=jnp.float32)
    grad_pre = gelu_back(grad_act)[0].astype(jnp.bfloat16)
    grad_ubias = jnp.sum(grad_pre.astype(jnp.float32), axis=0)
    grad_up = jnp.einsum("td,tf->df", hidden_low, grad_pre, preferred_element_type=jnp.float32)
    grad_hidden = (
        scatter_features(
            jnp.einsum("tf,df->td", grad_pre, full_up, preferred_element_type=jnp.float32)
        )
        + grad_two
    )
    grad_one, grad_ngain, grad_nshift = norm_back(grad_hidden, normed_one, rstd_one, norm_gain)
    grad_attn = grad_one.astype(jnp.bfloat16)
    grad_pbias = jnp.sum(grad_attn.astype(jnp.float32), axis=0)
    attn_wide = gather_features(grad_attn)
    grad_proj = jnp.einsum("th,td->hd", heads_out, attn_wide, preferred_element_type=jnp.float32)
    grad_heads = jnp.einsum(
        "td,hd->th", attn_wide, full_proj, preferred_element_type=jnp.float32
    ).astype(jnp.bfloat16)
    back_query, back_key, back_value = lax.map(
        attend_back, (query_seq, key_seq, value_seq, ids, logsum, grad_heads.reshape(shape))
    )
    grad_queries = back_query.reshape(rows, heads * HD).astype(jnp.bfloat16)
    grad_keys = back_key.reshape(rows, heads * HD).astype(jnp.bfloat16)
    grad_values = back_value.reshape(rows, heads * HD).astype(jnp.bfloat16)
    grad_qbias = jnp.sum(grad_queries.astype(jnp.float32), axis=0)
    grad_vbias = jnp.sum(grad_values.astype(jnp.float32), axis=0)
    grad_query = jnp.einsum("td,th->dh", gathered, grad_queries, preferred_element_type=jnp.float32)
    grad_key = jnp.einsum("td,th->dh", gathered, grad_keys, preferred_element_type=jnp.float32)
    grad_value = jnp.einsum("td,th->dh", gathered, grad_values, preferred_element_type=jnp.float32)
    partial_back = (
        jnp.einsum("th,dh->td", grad_queries, full_query, preferred_element_type=jnp.float32)
        + jnp.einsum("th,dh->td", grad_keys, full_key, preferred_element_type=jnp.float32)
        + jnp.einsum("th,dh->td", grad_values, full_value, preferred_element_type=jnp.float32)
    )
    grad_tokens = scatter_features(partial_back) + grad_one
    grad_query, grad_key, grad_value, grad_up = (
        lax.psum_scatter(
            grad_query.astype(jnp.bfloat16), "row", scatter_dimension=0, tiled=True
        ).astype(jnp.float32),
        lax.psum_scatter(
            grad_key.astype(jnp.bfloat16), "row", scatter_dimension=0, tiled=True
        ).astype(jnp.float32),
        lax.psum_scatter(
            grad_value.astype(jnp.bfloat16), "row", scatter_dimension=0, tiled=True
        ).astype(jnp.float32),
        lax.psum_scatter(
            grad_up.astype(jnp.bfloat16), "row", scatter_dimension=0, tiled=True
        ).astype(jnp.float32),
    )
    grad_proj, grad_down = (
        lax.psum_scatter(
            grad_proj.astype(jnp.bfloat16), "row", scatter_dimension=1, tiled=True
        ).astype(jnp.float32),
        lax.psum_scatter(
            grad_down.astype(jnp.bfloat16), "row", scatter_dimension=1, tiled=True
        ).astype(jnp.float32),
    )
    vectors = lax.psum(
        (
            grad_qbias,
            grad_vbias,
            grad_pbias,
            grad_ngain,
            grad_nshift,
            grad_ubias,
            grad_dbias,
            grad_fgain,
            grad_fshift,
        ),
        "row",
    )
    return (
        result.astype(jnp.bfloat16),
        grad_tokens,
        grad_query,
        vectors[0],
        grad_key,
        grad_value,
        vectors[1],
        grad_proj,
        vectors[2],
        vectors[3],
        vectors[4],
        grad_up,
        vectors[5],
        grad_down,
        vectors[6],
        vectors[7],
        vectors[8],
        norms,
    )


def solution(mesh):
    placed = (
        P("row", "col"),
        P("row", None),
        P("row", "col"),
        P("col"),
        P("row", "col"),
        P("row", "col"),
        P("col"),
        P("col", "row"),
        P("col"),
        P("col"),
        P("col"),
        P("row", "col"),
        P("col"),
        P("col", "row"),
        P("col"),
        P("col"),
        P("col"),
        P("row", "col"),
    )
    return jax.shard_map(
        per_device,
        mesh=mesh,
        in_specs=placed,
        out_specs=(
            P("row", "col"),
            P("row", "col"),
            P("row", "col"),
            P("col"),
            P("row", "col"),
            P("row", "col"),
            P("col"),
            P("col", "row"),
            P("col"),
            P("col"),
            P("col"),
            P("row", "col"),
            P("col"),
            P("col", "row"),
            P("col"),
            P("col"),
            P("col"),
            P(),
        ),
        check_vma=False,
    )
```

profile of v0, /device:TPU:0, one launch (start us, length us, event | category | flops | bytes accessed | tf_op | source)
XLA Modules:
  0.0 2204.3 jit_solution(9946414243634641131)
XLA Ops:
  11.7 17.4 all-gather.17.cloned.1.call-done
  29.0 127.5 %all-gather.11.cloned.1.call-done = bf16[2048,2048]{1,0:T(8,128)(2,1)} async-done(((bf16[2048,256]{1,0:T(8,128)(2,1)}), bf16[2048,2048]{1,0:T(8,128)(2,1)}) %all-gather.11.cloned.1.call-update) | async-done | bytes 8388624 | tf_op jit(solution)/shard_map/all_gather | solution.py:23
  156.5 6.0 convolution_convert_fusion.7
  163.4 9.6 all-gather.15.cloned.1.call-done
  173.0 6.0 fusion.87
  179.4 11.8 all-gather.13.cloned.1.call-done
  191.2 6.0 fusion.86
  199.4 23.2 %while.26 = (s32[]{:T(128)}, bf16[2,1024,2,128]{1,3,2,0:T(8,128)(2,1)}, f32[2,2,1024]{2,1,0:T(2,128)S(1)}, bf16[2,1024,2,128]{3,2,1,0:T(2,128)(2,1)}, s32[2,1024...) while((s32[]{:T(128)}, ...), condition=%wide.region_7.8_spmd, body=%wide.region_2.7_spmd.sunk | while | flops 1101004800 | bytes 46234304 | solution.py:176
  204.1 2.5 fusion.201
  215.7 2.5 fusion.201
  222.5 2.9 copy.82
  225.5 9.6 fusion.108
  236.0 282.1 %reduce-scatter.11.cloned.1.call-done = f32[2048,256]{1,0:T(8,128)} async-done(((f32[2048,2048]{1,0:T(8,128)}), f32[2048,256]{1,0:T(8,128)}) %reduce-scatter.11.cloned.1.call-update) | async-done | bytes 2097168 | tf_op jit(solution)/shard_map/reduce_scatter | solution.py:27
  518.1 2.2 fusion.126
  520.3 35.2 %all-reduce.4 = (f32[2048]{0:T(1024)S(1)}, f32[2048]{0:T(1024)S(1)}) all-reduce(f32[2048]{0:T(1024)S(1)} %get-tuple-element.229, f32[2048]{0:T(1024)S(1)} %get-tuple-element.228), channel_id=1, replica_groups=mesh['row'=4,'col'=8] {'col'}, use_global_device_ids=true, to_apply=%region_12.13 | all-reduce | flops 4096 | bytes 32768 | tf_op jit(solution)/shard_map/psum | solution.py:31
  557.9 123.6 %all-gather.21.cloned.1.call-done = bf16[2048,2048]{1,0:T(8,128)(2,1)} async-done(((bf16[2048,256]{1,0:T(8,128)(2,1)}), bf16[2048,2048]{1,0:T(8,128)(2,1)}) %all-gather.21.cloned.1.call-update) | async-done | bytes 8388624 | tf_op jit(solution)/shard_map/all_gather | solution.py:23
  681.5 14.4 fusion.133
  695.9 20.0 all-gather.25.cloned.1.call-done
  715.9 16.6 fusion.124
  732.6 282.7 %reduce-scatter.13.cloned.1.call-done = f32[2048,256]{1,0:T(8,128)} async-done(((f32[2048,2048]{1,0:T(8,128)}), f32[2048,256]{1,0:T(8,128)}) %reduce-scatter.13.cloned.1.call-update) | async-done | bytes 2097168 | tf_op jit(solution)/shard_map/reduce_scatter | solution.py:27
  1015.2 5.3 fusion.95
  1020.6 35.8 %all-reduce.3 = (f32[2048]{0:T(1024)S(1)}, f32[2048]{0:T(1024)S(1)}) all-reduce(f32[2048]{0:T(1024)S(1)} %get-tuple-element.321, f32[2048]{0:T(1024)S(1)} %get-tuple-element.322), channel_id=1, replica_groups=mesh['row'=4,'col'=8] {'col'}, use_global_device_ids=true, to_apply=%region_17.18 | all-reduce | flops 4096 | bytes 32768 | tf_op jit(solution)/shard_map/psum | solution.py:31
  1056.4 3.1 fusion.94
  1059.5 33.0 %all-reduce.2 = (f32[2048]{0:T(1024)S(1)}, f32[2048]{0:T(1024)S(1)}) all-reduce(f32[2048]{0:T(1024)S(1)} %get-tuple-element.223, f32[2048]{0:T(1024)S(1)} %get-tuple-element.230), channel_id=1, replica_groups=mesh['row'=4,'col'=8] {'col'}, use_global_device_ids=true, to_apply=%region_21.22 | all-reduce | flops 4096 | bytes 32768 | tf_op jit(solution)/shard_map/psum | solution.py:31
  1092.5 4.6 convert_reduce_fusion.2
  1097.2 122.7 %all-gather.27.cloned.1.call-done = bf16[2048,2048]{1,0:T(8,128)(2,1)} async-done(((bf16[2048,256]{1,0:T(8,128)(2,1)}), bf16[2048,2048]{1,0:T(8,128)(2,1)}) %all-gather.27.cloned.1.call-update) | async-done | bytes 8388624 | tf_op jit(solution)/shard_map/all_gather | solution.py:23
  1219.9 20.8 convert_reduce_fusion
  1240.7 1.9 copy-done.43
  1242.7 11.7 fusion.134
  1254.5 281.0 %reduce-scatter.15.cloned.1.call-done = f32[2048,256]{1,0:T(8,128)} async-done(((f32[2048,2048]{1,0:T(8,128)}), f32[2048,256]{1,0:T(8,128)}) %reduce-scatter.15.cloned.1.call-update) | async-done | bytes 2097168 | tf_op jit(solution)/shard_map/reduce_scatter | solution.py:27
  1535.5 6.3 multiply_reduce_fusion.2
  1541.8 35.2 %all-reduce.1 = (f32[2048]{0:T(1024)S(1)}, f32[2048]{0:T(1024)S(1)}) all-reduce(f32[2048]{0:T(1024)S(1)} %get-tuple-element.221, f32[2048]{0:T(1024)S(1)} %get-tuple-element.224), channel_id=1, replica_groups=mesh['row'=4,'col'=8] {'col'}, use_global_device_ids=true, to_apply=%region_26.27 | all-reduce | flops 4096 | bytes 32768 | tf_op jit(solution)/shard_map/psum | solution.py:31
  1577.0 5.3 convert_reduce_fusion.3
  1582.3 16.7 convolution_convert_fusion
  1599.1 14.0 convolution_convert_fusion.1
  1613.2 91.8 %all-gather.29.cloned.1.call-done = bf16[2048,2048]{1,0:T(8,128)(2,1)} async-done(((bf16[2048,256]{1,0:T(8,128)(2,1)}), bf16[2048,2048]{1,0:T(8,128)(2,1)}) %all-gather.29.cloned.1.call-update) | async-done | bytes 8388624 | tf_op jit(solution)/shard_map/all_gather | solution.py:23
  1705.1 5.8 convolution_convert_fusion.6
  1712.0 7.9 convolution_convert_fusion.2
  1723.7 35.5 %while.27 = (s32[]{:T(128)}, bf16[2,1024,2,128]{1,3,2,0:T(8,128)(2,1)}, bf16[2,1024,2,128]{1,3,2,0:T(8,128)(2,1)}, bf16[2,1024,2,128]{1,3,2,0:T(8,128)(2,1)}, bf...) while((s32[]{:T(128)}, ...), condition=%wide.region_30.31_spmd, body=%wide.region_27.30_spmd.sunk | while | flops 2719217664 | bytes 109666664 | solution.py:226
  1730.7 1.6 multiply_reduce_fusion.10
  1732.3 1.6 multiply_reduce_fusion.9
  1734.0 2.7 multiply_convert_fusion.6
  1748.4 1.6 multiply_reduce_fusion.10
  1751.7 2.7 multiply_convert_fusion.6
  1759.3 2.7 copy.87
  1762.0 7.1 fusion.88
  1770.1 7.4 fusion.90
  1777.6 2.5 copy.88
  1780.0 6.8 fusion.89
  1786.9 9.4 fusion.102
  1796.3 8.1 fusion.105
  1804.4 18.6 add_add_fusion
  1824.3 39.4 %all-reduce = (f32[1]{0:T(128)}, f32[1]{0:T(128)}, f32[1]{0:T(128)}, f32[]{:T(128)}) all-reduce(f32[1]{0:T(128)} %bitcast.31, f32[1]{0:T(128)} %bitcast.30, f32[1]{0:T(128)} %bitcast.29, f32[]{:T(128)S(6)} %mul.262), channel_id=1, replica_groups=mesh['row'=4,'col'=8] {'row','col'}, use_global_device_ids=true, to_apply=%region_61.62 | all-reduce | flops 4 | bytes 32 | tf_op jit(solution)/shard_map/psum | solution.py:188
  1863.8 3.2 fusion.121
  1867.0 2.9 convert_element_type.197
  1869.9 2.9 convert_element_type.194
  1873.3 11.7 all-reduce.5
  1885.0 1.8 convert_element_type.191
  1886.8 1.9 copy.90
  1888.7 1.9 copy.92
  1890.6 16.5 reduce-scatter.21.cloned.1.call-done
  1907.1 1.9 copy.91
  1909.0 285.0 %reduce-scatter.17.cloned.1.call-done = f32[2048,256]{1,0:T(8,128)} async-done(((f32[2048,2048]{1,0:T(8,128)}), f32[2048,256]{1,0:T(8,128)}) %reduce-scatter.17.cloned.1.call-update) | async-done | bytes 2097168 | tf_op jit(solution)/shard_map/reduce_scatter | solution.py:27
  2194.1 3.2 add.202
  (235 shorter events, 61.6 us)
Async XLA Ops:
  7.2 21.9 all-gather.17.cloned.1.call-start
  7.9 148.6 %all-gather.11.cloned.1.call-start = ((), (), s32[]{:S(2)}) async-start(), calls=%async_computation.10 | async-start | bytes 9437184 | tf_op jit(solution)/shard_map/all_gather | solution.py:23
  8.7 164.3 %all-gather.15.cloned.1.call-start = ((), (), s32[]{:S(2)}) async-start(), calls=%async_computation.12 | async-start | bytes 1310720 | tf_op jit(solution)/shard_map/all_gather | solution.py:36
  9.4 181.8 %all-gather.13.cloned.1.call-start = ((), (), s32[]{:S(2)}) async-start(), calls=%async_computation.11 | async-start | bytes 1310720 | tf_op jit(solution)/shard_map/all_gather | solution.py:38
  10.0 215.5 %all-gather.19.cloned.1.call-start = ((), (), s32[]{:S(2)}) async-start(), calls=%async_computation.14 | async-start | bytes 1310720 | tf_op jit(solution)/shard_map/all_gather | solution.py:42
  10.6 507.6 %reduce-scatter.11.cloned.1.call-start = ((), (), s32[]{:S(2)}) async-start(), calls=%async_computation.15 | async-start | bytes 18874368 | tf_op jit(solution)/shard_map/reduce_scatter | solution.py:27
  162.5 10.6 copy-start.41
  179.0 12.2 copy-start.42
  208.2 1.7 copy-start.19
  219.8 1.7 copy-start.19
  222.5 12.6 copy-start
  222.5 12.6 copy-start.2
  222.5 12.6 copy-start.24
  225.5 9.7 copy-start.5
  235.2 283.0 %copy-start.15 = (bf16[2048,256]{1,0:T(8,128)(2,1)S(1)}, bf16[2048,256]{1,0:T(8,128)(2,1)}, u32[]{:S(2)}) copy-start(bf16[2048,256]{1,0:T(8,128)(2,1)} %param.22) | copy-start | bytes 3145732
  235.2 283.0 %copy-start.36 = (f32[256]{0:T(256)S(1)}, f32[256]{0:T(256)}, u32[]{:S(2)}) copy-start(f32[256]{0:T(256)} %param.30) | copy-start | bytes 3076
  235.2 320.3 %copy-start.26 = (f32[256]{0:T(256)S(1)}, f32[256]{0:T(256)}, u32[]{:S(2)}) copy-start(f32[256]{0:T(256)} %param.31) | copy-start | bytes 3076
  235.2 320.3 %copy-start.35 = (f32[256]{0:T(256)S(1)}, f32[256]{0:T(256)}, u32[]{:S(2)}) copy-start(f32[256]{0:T(256)} %param.32) | copy-start | bytes 3076
  235.2 322.7 %all-gather.23.cloned.1.call-start = ((), (), s32[]{:S(2)}) async-start(), calls=%async_computation.17 | async-start | bytes 5242880 | tf_op jit(solution)/shard_map/all_gather | solution.py:39
  236.0 445.5 %all-gather.21.cloned.1.call-start = ((), (), s32[]{:S(2)}) async-start(), calls=%async_computation.16 | async-start | bytes 9437184 | tf_op jit(solution)/shard_map/all_gather | solution.py:23
  557.1 158.8 %all-gather.25.cloned.1.call-start = ((), (), s32[]{:S(2)}) async-start(), calls=%async_computation.18 | async-start | bytes 5242880 | tf_op jit(solution)/shard_map/all_gather | solution.py:43
  557.8 158.1 %copy-start.40 = (f32[1024]{0:T(1024)S(1)}, f32[1024]{0:T(1024)}, u32[]{:S(2)}) copy-start(f32[1024]{0:T(1024)} %param.34) | copy-start | bytes 12292
  557.8 457.4 %reduce-scatter.13.cloned.1.call-start = ((), (), s32[]{:S(2)}) async-start(), calls=%async_computation.19 | async-start | bytes 18874368 | tf_op jit(solution)/shard_map/reduce_scatter | solution.py:27
  732.5 282.8 %copy-start.38 = (f32[256]{0:T(256)S(1)}, f32[256]{0:T(256)}, u32[]{:S(2)}) copy-start(f32[256]{0:T(256)} %param.36) | copy-start | bytes 3076
  732.5 487.4 %all-gather.27.cloned.1.call-start = ((), (), s32[]{:S(2)}) async-start(), calls=%async_computation.20 | async-start | bytes 9437184 | tf_op jit(solution)/shard_map/all_gather | solution.py:23
  1015.2 41.1 %copy-start.7 = (bf16[2048,256]{1,0:T(8,128)(2,1)S(1)}, bf16[2048,256]{1,0:T(8,128)(2,1)}, u32[]{:S(2)}) copy-start(bf16[2048,256]{1,0:T(8,128)(2,1)} %param.39) | copy-start | bytes 3145732
  1015.2 41.1 %copy-start.27 = (f32[256]{0:T(256)S(1)}, f32[256]{0:T(256)}, u32[]{:S(2)}) copy-start(f32[256]{0:T(256)} %param.37) | copy-start | bytes 3076
  1097.2 438.4 %reduce-scatter.15.cloned.1.call-start = ((), (), s32[]{:S(2)}) async-start(), calls=%async_computation.21 | async-start | bytes 18874368 | tf_op jit(solution)/shard_map/reduce_scatter | solution.py:27
  1219.9 22.7 %copy-start.39 = (bf16[2048,1024]{1,0:T(8,128)(2,1)S(1)}, bf16[2048,1024]{1,0:T(8,128)(2,1)}, u32[]{:S(2)}) copy-start(bf16[2048,1024]{1,0:T(8,128)(2,1)} %all-gather.23.cloned.1.call-done) | copy-start | bytes 12582916
  1240.7 2.0 copy-start.43
  1254.4 281.1 %copy-start.37 = (f32[256]{0:T(256)S(1)}, f32[256]{0:T(256)}, u32[]{:S(2)}) copy-start(f32[256]{0:T(256)} %param.38) | copy-start | bytes 3076
  1254.4 450.6 %all-gather.29.cloned.1.call-start = ((), (), s32[]{:S(2)}) async-start(), calls=%async_computation.22 | async-start | bytes 9437184 | tf_op jit(solution)/shard_map/all_gather | solution.py:23
  1582.3 284.7 %reduce-scatter.29.cloned.1.call-start = ((), (), s32[]{:S(2)}) async-start(), calls=%async_computation.29 | async-start | bytes 5242880 | tf_op jit(solution)/shard_map/reduce_scatter | solution.py:261
  1599.1 270.8 %reduce-scatter.27.cloned.1.call-start = ((), (), s32[]{:S(2)}) async-start(), calls=%async_computation.28 | async-start | bytes 5242880 | tf_op jit(solution)/shard_map/reduce_scatter | solution.py:253
  1613.1 91.9 %copy-start.23 = (bf16[256,2048]{1,0:T(8,128)(2,1)S(1)}, bf16[256,2048]{1,0:T(8,128)(2,1)}, u32[]{:S(2)}) copy-start(bf16[256,2048]{1,0:T(8,128)(2,1)} %all-gather.19.cloned.1.call-done) | copy-start | bytes 3145732
  1613.2 271.8 %reduce-scatter.25.cloned.1.call-start = ((), (), s32[]{:S(2)}) async-start(), calls=%async_computation.27 | async-start | bytes 1310720 | tf_op jit(solution)/shard_map/reduce_scatter | solution.py:258
  1613.2 98.8 %copy-start.6 = (bf16[2,1024,2,128]{3,2,1,0:T(2,128)(2,1)S(1)}, bf16[2,1024,2,128]{3,2,1,0:T(2,128)(2,1)}, u32[]{:S(2)}) copy-start(bf16[2,1024,2,128]{3,2,1,0:T(2,128)(2,1)} %copy-done.5) | copy-start | bytes 3145732
  1719.9 3.9 copy-start.1
  1719.9 3.9 copy-start.3
  1719.9 3.9 copy-start.4
  1719.9 3.9 copy-start.25
  1719.9 166.9 %reduce-scatter.19.cloned.1.call-start = ((), (), s32[]{:S(2)}) async-start(), calls=%async_computation.24 | async-start | bytes 1310720 | tf_op jit(solution)/shard_map/reduce_scatter | solution.py:244
  1727.9 1.4 copy-start.8
  1730.7 1.6 copy-start.9
  1736.7 2.2 copy-start.17
  1745.6 1.4 copy-start.8
  1748.4 1.6 copy-start.9
  1754.4 2.2 copy-start.17
  1762.0 7.2 copy-start.10
  1769.2 119.5 %reduce-scatter.23.cloned.1.call-start = ((), (), s32[]{:S(2)}) async-start(), calls=%async_computation.26 | async-start | bytes 1310720 | tf_op jit(solution)/shard_map/reduce_scatter | solution.py:250
  1777.5 129.6 %reduce-scatter.21.cloned.1.call-start = ((), (), s32[]{:S(2)}) async-start(), calls=%async_computation.25 | async-start | bytes 1310720 | tf_op jit(solution)/shard_map/reduce_scatter | solution.py:247
  1786.8 407.3 %reduce-scatter.17.cloned.1.call-start = ((), (), s32[]{:S(2)}) async-start(), calls=%async_computation.23 | async-start | bytes 18874368 | tf_op jit(solution)/shard_map/reduce_scatter | solution.py:27
  1786.9 9.4 copy-start.21
  1796.3 8.1 copy-start.22
  1823.0 49.7 %copy-start.11 = (bf16[2,1024,2,128]{1,3,2,0:T(8,128)(2,1)S(1)}, bf16[2,1024,2,128]{1,3,2,0:T(8,128)(2,1)}, u32[]{:S(2)}) copy-start(bf16[2,1024,2,128]{1,3,2,0:T(8,128)(2,1)} %get-tuple-element.114) | copy-start | bytes 3145732
  1823.0 50.0 %copy-start.14 = (bf16[2,1024,2,128]{1,3,2,0:T(8,128)(2,1)S(1)}, bf16[2,1024,2,128]{1,3,2,0:T(8,128)(2,1)}, u32[]{:S(2)}) copy-start(bf16[2,1024,2,128]{1,3,2,0:T(8,128)(2,1)} %get-tuple-element.112) | copy-start | bytes 3145732
  1867.0 6.3 copy-start.28
  1867.0 6.3 copy-start.29
  1867.0 6.3 copy-start.30
  1867.0 6.3 copy-start.31
  1867.0 6.3 copy-start.32
  1867.0 6.3 copy-start.33
  1867.0 6.3 copy-start.34
  1873.2 320.8 %copy-start.16 = (f32[2048,256]{1,0:T(8,128)S(1)}, f32[2048,256]{1,0:T(8,128)}, u32[]{:S(2)}) copy-start(f32[2048,256]{1,0:T(8,128)} %get-tuple-element.296) | copy-start | bytes 6291460
  (8 other events, 8.3 us)
Sparse Core Ops, SparseCore 0:
  9.6 19.4 all-gather.16
  31.1 125.3 all-gather.10
  158.1 14.9 all-gather.14
  174.4 16.7 all-gather.12
  192.6 16.7 all-gather.18
  235.3 282.7 reduce-scatter.10
  519.8 33.4 all-gather.22
  557.2 124.2 all-gather.20
  683.2 32.6 all-gather.24
  732.6 282.5 reduce-scatter.12
  1097.3 122.5 all-gather.26
  1254.6 280.9 reduce-scatter.14
  1582.4 122.6 all-gather.28
  1707.6 42.6 reduce-scatter.28
  1752.7 44.5 reduce-scatter.26
  1799.8 24.8 reduce-scatter.24
  1827.1 24.8 reduce-scatter.18
  1854.6 24.9 reduce-scatter.22
  1882.1 24.9 reduce-scatter.20
  1911.3 282.7 reduce-scatter.16
where the time goes:
time: 2210 us; the launch traced here: 2200 us
  waiting for transfers between devices  1680 us (76%)
  matrix products  224 us (10%)
  blocking collectives  190 us (9%)
  other arithmetic  57.6 us (3%)
  local copies, waits for them, and re-layouts  38.7 us (2%)
    reduce_scatter x4, waiting for transfers between devices, scatter_features(): return lax.psum_scatter(partial_sum, 'col', scatter_dimension=1, tiled=True)  1130 us
    all_gather x4, waiting for transfers between devices, gather_features(): return lax.all_gather(piece, 'col', axis=1, tiled=True)  466 us
    psum x4, blocking collectives, row_totals(): return lax.psum((first, second), 'col')  139 us
  transfers between devices with their start and end apart: 20, of which 13 were waited for; matrix products, arithmetic and copies ran while one was open for 10% of the time, Pallas kernels for 0%

commit v1 on v0

--- a/solution.py
+++ b/solution.py
@@ -1,14 +1,15 @@
 import jax
 import jax.numpy as jnp
 from jax import lax
+from jax.sharding import Mesh
 from jax.sharding import PartitionSpec as P
 
 HD = 128
 LEN = 1024
-
-
 EPS = 1e-06
 NEGATIVE = -1000000000.0
+BF = jnp.bfloat16
+F32 = jnp.float32
 
 
 def segment_ids(lengths):
@@ -19,12 +20,289 @@
     return jnp.sum(hits, axis=2)
 
 
+def dot(left, right, dims):
+    return lax.dot_general(left, right, (dims, ((), ())), preferred_element_type=F32)
+
+
+AXES = ("y", "c", "z", "x")
+X_BIT, Z_LOW, Z_HIGH, C_BIT, Y_BIT = 1, 2, 4, 8, 16
+XY_BIT = X_BIT | Y_BIT
+
+
+def swap(piece, mask):
+    return lax.ppermute(piece, AXES, [(i, i ^ mask) for i in range(32)])
+
+
+def to_share(piece):
+    rows, width = piece.shape
+    half = lax.all_to_all(piece, "y", 1, 0, tiled=True).reshape(4, rows // 2, width // 2)
+    return lax.all_to_all(half, "z", 0, 2, tiled=True)[0]
+
+
+def from_share(share):
+    rows, width = share.shape
+    parts = lax.all_to_all(share[None], "z", 2, 0, tiled=True)
+    return lax.all_to_all(parts.reshape(2, 2 * rows, width // 4), "y", 0, 2, tiled=True)[0]
+
+
+def square_gather(share):
+    half = share.shape[0] // 2
+    width = share.shape[1]
+    from_x = swap(share, X_BIT)
+    from_y = swap(share, Y_BIT)
+    low = swap(from_x[:half], Y_BIT)
+    high = swap(from_y[half:], X_BIT)
+    from_xy = jnp.concatenate([low, high], axis=0)
+    place = lax.axis_index("x") * 2 + lax.axis_index("y")
+    whole = jnp.zeros((share.shape[0], 4 * width), share.dtype)
+    for mask, block in ((0, share), (2, from_x), (1, from_y), (3, from_xy)):
+        whole = lax.dynamic_update_slice_in_dim(whole, block, (place ^ mask) * width, 1)
+    return whole
+
+
+def square_scatter(produce):
+    place = lax.axis_index("x") * 2 + lax.axis_index("y")
+    far = produce(place ^ 3)
+    half = far.shape[0] // 2
+    low = slice(0, half)
+    high = slice(half, None)
+    far = far.astype(BF)
+    far_low = swap(far[low], X_BIT)
+    far_high = swap(far[high], Y_BIT)
+    side_x = produce(place ^ 2)
+    side_y = produce(place ^ 1)
+    near_low = swap(side_x[low].astype(BF), X_BIT)
+    near_high = swap(side_y[high].astype(BF), Y_BIT)
+    pass_low = (side_y[low] + far_low.astype(F32)).astype(BF)
+    pass_high = (side_x[high] + far_high.astype(F32)).astype(BF)
+    last_low = swap(pass_low, Y_BIT)
+    last_high = swap(pass_high, X_BIT)
+    own = produce(place)
+    return jnp.concatenate(
+        [
+            own[low] + near_low.astype(F32) + last_low.astype(F32),
+            own[high] + near_high.astype(F32) + last_high.astype(F32),
+        ],
+        axis=0,
+    )
+
+
+def square_total(stats):
+    return stats + swap(stats, X_BIT) + swap(stats, Y_BIT) + swap(stats, XY_BIT)
+
+
+def gather_columns(pieces):
+    halves = [lax.all_to_all(p, "y", 1, 0, tiled=True) for p in pieces]
+    piece = jnp.concatenate(halves, axis=1) if len(halves) > 1 else halves[0]
+    full = lax.all_gather(piece, ("z", "c"), axis=0)
+    width = piece.shape[1]
+    full = full.reshape(4, 2, 2, 4, 128, width)
+    return full.transpose(3, 2, 1, 4, 0, 5).reshape(2048, 4 * width)
+
+
+def gather_rows(piece):
+    half = lax.all_to_all(piece, "y", 0, 1, tiled=True)
+    full = lax.all_gather(half, ("z", "c"), axis=0)
+    depth = half.shape[0]
+    full = full.reshape(4, 2, depth, 2, 4, 128)
+    return full.transpose(0, 2, 4, 3, 1, 5).reshape(4 * depth, 2048)
+
+
+def scatter_columns(grad, count):
+    width = grad.shape[1] // 4
+    full = grad.reshape(4, 2, 2, 128, 4, width)
+    full = full.transpose(4, 2, 1, 0, 3, 5).reshape(8, 1024, width)
+    piece = lax.psum_scatter(full, ("z", "c"), scatter_dimension=0)
+    n = width // count
+    return [
+        lax.all_to_all(piece[:, i * n : (i + 1) * n], "y", 0, 1, tiled=True).astype(F32)
+        for i in range(count)
+    ]
+
+
+def scatter_rows(grad):
+    depth = grad.shape[0] // 4
+    full = grad.reshape(4, depth, 4, 2, 2, 128)
+    full = full.transpose(0, 4, 1, 3, 2, 5).reshape(8, depth, 1024)
+    piece = lax.psum_scatter(full, ("z", "c"), scatter_dimension=0)
+    return lax.all_to_all(piece, "y", 1, 0, tiled=True).astype(F32)
+
+
+def heads_of(block, part):
+    return block.reshape(block.shape[0], 4, 3, HD)[:, :, part]
+
+
+def square_device(
+    tokens, lengths, w_query, b_query, w_key, w_value, b_value, w_proj, b_proj, norm_gain, norm_shift,
+    w_up, b_up, w_down, b_down, final_gain, final_shift, cotangent,
+):
+    yi = lax.axis_index("y")
+    zi = lax.axis_index("z")
+    place = lax.axis_index("x") * 2 + yi
+    width = 4 * 512
+
+    other = swap(lengths, Y_BIT)
+    both = jnp.where(yi == 0, jnp.concatenate([lengths, other]), jnp.concatenate([other, lengths]))
+    ids = segment_ids(lax.dynamic_slice_in_dim(both, zi, 1, 0))[0]
+    valid = (ids != lengths.shape[1] - 1).astype(F32)[:, None]
+
+    vectors = jnp.concatenate(
+        [v.reshape(2, -1) for v in (b_query, b_value, b_proj, norm_gain, norm_shift, b_down, final_gain, final_shift, b_up)],
+        axis=1,
+    )
+    vectors = lax.dynamic_slice_in_dim(vectors, yi, 1, 0)
+    vectors = lax.all_to_all(jnp.broadcast_to(vectors, (4, vectors.shape[1])), "z", 0, 0, tiled=True)
+    small = [vectors[:, i * 128 : (i + 1) * 128] for i in range(8)]
+    q_bias, v_bias, p_bias, n_gain, n_shift, d_bias, f_gain, f_shift = small
+    p_bias, n_gain, n_shift, d_bias, f_gain, f_shift = (
+        v.reshape(512) for v in (p_bias, n_gain, n_shift, d_bias, f_gain, f_shift)
+    )
+    u_bias = vectors[:, 1024:].reshape(-1)
+    qkv_bias = jnp.stack([q_bias, jnp.zeros_like(q_bias), v_bias], axis=1).reshape(-1)
+
+    token_share = to_share(tokens)
+    full_qkv = gather_columns([w_query, w_key, w_value])
+    full_proj = gather_rows(w_proj)
+    full_up = gather_columns([w_up])
+    full_down = gather_rows(w_down)
+    dy = to_share(cotangent).astype(F32)
+    stream = token_share.astype(F32)
+
+    gathered = square_gather(token_share)
+    qkv = (dot(gathered, full_qkv, ((1,), (0,))) + qkv_bias).astype(BF)
+    queries, keys, values = (heads_of(qkv, i) for i in range(3))
+    scale = HD ** (-0.5)
+    same = (ids[:, None] == ids[None, :])[None]
+    scores = jnp.einsum("qhd,khd->hqk", queries, keys, preferred_element_type=F32) * scale
+    scores = jnp.where(same, scores, NEGATIVE)
+    peak = jnp.max(scores, axis=2, keepdims=True)
+    expo = jnp.exp(scores - peak)
+    total = jnp.sum(expo, axis=2, keepdims=True)
+    probs = (expo / total).astype(BF)
+    logsum = peak + jnp.log(total)
+    heads_out = jnp.einsum("hqk,khd->qhd", probs, values, preferred_element_type=F32)
+    heads_out = heads_out.astype(BF).reshape(LEN, 512)
+
+    def quarter(weights, where, axis):
+        return lax.dynamic_slice_in_dim(weights, where * 512, 512, axis)
+
+    attn = square_scatter(lambda w: dot(heads_out, quarter(full_proj, w, 1), ((1,), (0,)))) + p_bias
+    resid = stream + attn
+    stats = square_total(jnp.stack([jnp.sum(resid, axis=1), jnp.sum(resid * resid, axis=1)]))
+    mean = stats[0] / width
+    rstd_one = lax.rsqrt(stats[1] / width - mean * mean + EPS)[:, None]
+    normed_one = (resid - mean[:, None]) * rstd_one
+    hidden = normed_one * n_gain + n_shift
+    hidden_low = square_gather(hidden.astype(BF))
+    pre = dot(hidden_low, full_up, ((1,), (0,))) + u_bias
+    act, gelu_back = jax.vjp(lambda inputs: jax.nn.gelu(inputs, approximate=True), pre)
+    act_low = act.astype(BF)
+    ffn = square_scatter(lambda w: dot(act_low, quarter(full_down, w, 1), ((1,), (0,)))) + d_bias
+
+    resid_two = hidden + ffn
+    scaled = dy * f_gain
+    stats = square_total(
+        jnp.stack(
+            [
+                jnp.sum(resid_two, axis=1),
+                jnp.sum(resid_two * resid_two, axis=1),
+                jnp.sum(scaled, axis=1),
+                jnp.sum(scaled * resid_two, axis=1),
+            ]
+        )
+    )
+    mean = stats[0] / width
+    rstd = lax.rsqrt(stats[1] / width - mean * mean + EPS)
+    mean_e = stats[2] / width
+    along = rstd * (stats[3] / width - mean * mean_e)
+    normed_two = (resid_two - mean[:, None]) * rstd[:, None]
+    layer_out = from_share((normed_two * f_gain + f_shift).astype(BF))
+    grad_two = rstd[:, None] * (scaled - mean_e[:, None] - normed_two * along[:, None])
+    grad_fgain = jnp.sum(dy * normed_two, axis=0)
+    grad_fshift = jnp.sum(dy, axis=0)
+    grad_ffn = grad_two.astype(BF)
+    grad_dbias = jnp.sum(grad_ffn.astype(F32), axis=0)
+
+    ffn_wide = square_gather(grad_ffn)
+    grad_act = dot(ffn_wide, full_down, ((1,), (1,)))
+    grad_pre = gelu_back(grad_act)[0].astype(BF)
+    grad_down = dot(act_low, ffn_wide, ((0,), (0,))).astype(BF)
+    grad_ubias = jnp.sum(grad_pre.astype(F32), axis=0)
+    grad_hidden = square_scatter(lambda w: dot(grad_pre, quarter(full_up, w, 0), ((1,), (1,)))) + grad_two
+    grad_up = dot(hidden_low, grad_pre, ((0,), (0,))).astype(BF)
+    scaled = grad_hidden * n_gain
+    stats = square_total(jnp.stack([jnp.sum(scaled, axis=1), jnp.sum(scaled * normed_one, axis=1)])) / width
+    grad_one = rstd_one * (scaled - stats[0][:, None] - normed_one * stats[1][:, None])
+    grad_ngain = jnp.sum(grad_hidden * normed_one, axis=0)
+    grad_nshift = jnp.sum(grad_hidden, axis=0)
+    grad_attn = grad_one.astype(BF)
+    grad_pbias = jnp.sum(grad_attn.astype(F32), axis=0)
+
+    attn_wide = square_gather(grad_attn)
+    grad_heads = dot(attn_wide, full_proj, ((1,), (1,))).astype(BF)
+    grad_proj = dot(heads_out, attn_wide, ((0,), (0,))).astype(BF)
+    grad_out = grad_heads.reshape(LEN, 4, HD)
+    probs_full = jnp.exp(
+        jnp.where(same, jnp.einsum("qhd,khd->hqk", queries, keys, preferred_element_type=F32) * scale, NEGATIVE)
+        - logsum
+    )
+    grad_probs = jnp.einsum("qhd,khd->hqk", grad_out, values, preferred_element_type=F32)
+    inner = jnp.sum(probs_full * grad_probs, axis=2, keepdims=True)
+    grad_scores = (probs_full * (grad_probs - inner)).astype(BF)
+    back_query = jnp.einsum("hqk,khd->qhd", grad_scores, keys, preferred_element_type=F32) * scale
+    back_key = jnp.einsum("hqk,qhd->khd", grad_scores, queries, preferred_element_type=F32) * scale
+    back_value = jnp.einsum("hqk,qhd->khd", probs_full.astype(BF), grad_out, preferred_element_type=F32)
+    grad_qkv = jnp.stack([b.astype(BF) for b in (back_query, back_key, back_value)], axis=2)
+    sums_qkv = jnp.sum(grad_qkv.astype(F32), axis=0)
+    grad_qkv = grad_qkv.reshape(LEN, 1536)
+    back = square_scatter(lambda w: dot(grad_qkv, quarter(full_qkv, w, 0), ((1,), (1,))))
+    grad_tokens = from_share((back + grad_one).astype(BF)).astype(F32)
+    grad_wqkv = dot(gathered, grad_qkv, ((0,), (0,))).astype(BF)
+
+    grad_down = scatter_rows(grad_down)
+    (grad_up,) = scatter_columns(grad_up, 1)
+    grad_proj = scatter_rows(grad_proj)
+    grad_query, grad_key, grad_value = scatter_columns(grad_wqkv, 3)
+
+    sums = jnp.concatenate(
+        [
+            v.reshape(4, -1)
+            for v in (
+                sums_qkv[:, 0], sums_qkv[:, 2], grad_pbias, grad_ngain, grad_nshift, grad_dbias, grad_fgain, grad_fshift, grad_ubias,
+            )
+        ],
+        axis=1,
+    )
+    sums = jnp.sum(lax.all_to_all(sums, "z", 0, 0, tiled=True), axis=0)
+    sums = sums + swap(sums, C_BIT)
+    other = swap(sums, Y_BIT)
+    sums = jnp.where(yi == 0, jnp.stack([sums, other]), jnp.stack([other, sums]))
+    vecs = [sums[:, i * 128 : (i + 1) * 128].reshape(-1) for i in range(8)] + [sums[:, 1024:].reshape(-1)]
+
+    totals = jnp.stack(
+        [
+            jnp.sum(valid * stream * stream),
+            jnp.sum(valid * attn * attn),
+            jnp.sum(valid * ffn * ffn),
+            jnp.sum(valid) * 512,
+        ]
+    )
+    for mask in (X_BIT, Z_LOW, Z_HIGH, C_BIT, Y_BIT):
+        totals = totals + swap(totals, mask)
+    norms = jnp.sqrt(totals[:3] / totals[3])
+    return (
+        layer_out, grad_tokens, grad_query, vecs[0], grad_key, grad_value, vecs[1], grad_proj, vecs[2], vecs[3], vecs[4],
+        grad_up, vecs[8], grad_down, vecs[5], vecs[6], vecs[7], norms,
+    )
+
+
 def gather_features(piece):
     return lax.all_gather(piece, "col", axis=1, tiled=True)
 
 
 def scatter_features(partial_sum):
-    return lax.psum_scatter(partial_sum, "col", scatter_dimension=1, tiled=True)
+    low = partial_sum.astype(jnp.bfloat16)
+    return lax.psum_scatter(low, "col", scatter_dimension=1, tiled=True).astype(F32)
 
 
 def row_totals(first, second):
@@ -298,50 +576,23 @@
     )
 
 
+def placements(row, col):
+    grid, turned, share = P(row, col), P(col, row), P(col)
+    args = (
+        grid, P(row, None), grid, share, grid, grid, share, turned, share, share, share, grid, share, turned, share, share, share, grid,
+    )
+    outs = (
+        grid, grid, grid, share, grid, grid, share, turned, share, share, share, grid, share, turned, share, share, share, P(),
+    )
+    return (args, outs)
+
+
 def solution(mesh):
-    placed = (
-        P("row", "col"),
-        P("row", None),
-        P("row", "col"),
-        P("col"),
-        P("row", "col"),
-        P("row", "col"),
-        P("col"),
-        P("col", "row"),
-        P("col"),
-        P("col"),
-        P("col"),
-        P("row", "col"),
-        P("col"),
-        P("col", "row"),
-        P("col"),
-        P("col"),
-        P("col"),
-        P("row", "col"),
-    )
-    return jax.shard_map(
-        per_device,
-        mesh=mesh,
-        in_specs=placed,
-        out_specs=(
-            P("row", "col"),
-            P("row", "col"),
-            P("row", "col"),
-            P("col"),
-            P("row", "col"),
-            P("row", "col"),
-            P("col"),
-            P("col", "row"),
-            P("col"),
-            P("col"),
-            P("col"),
-            P("row", "col"),
-            P("col"),
-            P("col", "row"),
-            P("col"),
-            P("col"),
-            P("col"),
-            P(),
-        ),
-        check_vma=False,
-    )
+    if mesh.shape["row"] == 4 and mesh.shape["col"] == 8:
+        mesh = Mesh(mesh.devices.reshape(2, 2, 4, 2), AXES)
+        args, outs = placements(("y", "c"), ("z", "x"))
+        body = square_device
+    else:
+        args, outs = placements("row", "col")
+        body = per_device
+    return jax.shard_map(body, mesh=mesh, in_specs=args, out_specs=outs, check_vma=False)

time: 2210 us -> 1080 us (0.49)
  waiting for transfers between devices: 1680 us -> 287 us
  local copies, waits for them, and re-layouts: 38.7 us -> 305 us
  blocking collectives: 190 us -> 35.8 us
  starting transfers between devices: 1.21 us -> 136 us
  other arithmetic: 57.6 us -> 104 us
  matrix products: 224 us -> 179 us
    reduce_scatter x10 -> x4, waiting for transfers between devices: 1150 us -> 0.04 us  [the longest x2 0.02 us: scatter_columns(): piece = lax.psum_scatter(full, ('z', 'c'), scatter_dimension=0)]
    all_gather x10 -> x4, waiting for transfers between devices: 524 us -> 0.03 us  [the longest x2 0.02 us: gather_columns(): full = lax.all_gather(piece, ('z', 'c'), axis=0)]
    psum x6 -> x0, blocking collectives: 190 us -> none  [the longest x4 139 us: row_totals(): return lax.psum((first, second), 'col')]
    reshape x4 -> x19, local copies, waits for them, and re-layouts: 3.38 us -> 170 us  [the longest x4 45.7 us: gather_rows(): full = full.reshape(4, 2, depth, 2, 4, 128)]
    ppermute x0 -> x57, waiting for transfers between devices: none -> 154 us  [swap(): return lax.ppermute(piece, AXES, [(i, i ^ mask) for i in range(32)])]
    all_to_all x0 -> x19, waiting for transfers between devices: none -> 133 us  [the longest x2 42.1 us: from_share(): parts = lax.all_to_all(share[None], 'z', 2, 0, tiled=True)]
    all_to_all x0 -> x19, starting transfers between devices: none -> 73.3 us  [the longest x4 15.6 us: scatter_columns(): lax.all_to_all(piece[:, i * n:(i + 1) * n], 'y', 0, 1, tiled=True)]
    ppermute x0 -> x57, starting transfers between devices: none -> 62.7 us  [swap(): return lax.ppermute(piece, AXES, [(i, i ^ mask) for i in range(32)])]
  transfers between devices with their start and end apart: 20 -> 84, of which waited for: 13 -> 48; matrix products, arithmetic and copies ran while one was open for 10% -> 46% of each run, Pallas kernels for 0% -> 0%
where the time goes in v1:
time: 1080 us; the launch traced here: 1060 us
  local copies, waits for them, and re-layouts  305 us (28%)
  waiting for transfers between devices  287 us (27%)
  matrix products  179 us (17%)
  starting transfers between devices  136 us (13%)
  other arithmetic  104 us (10%)
  blocking collectives  35.8 us (3%)
  between operations  17.4 us (2%)
    ppermute x57, waiting for transfers between devices, swap(): return lax.ppermute(piece, AXES, [(i, i ^ mask) for i in range(32)])  154 us
    dot_general x24, matrix products, dot(): lax.dot_general(left, right, (dims, ((), ())), preferred_element_type=F32)  133 us
    ppermute x57, starting transfers between devices, swap(): return lax.ppermute(piece, AXES, [(i, i ^ mask) for i in range(32)])  62.7 us
    unnamed x242, local copies, waits for them, and re-layouts  62.2 us
    reshape x4, local copies, waits for them, and re-layouts, gather_rows(): full = full.reshape(4, 2, depth, 2, 4, 128)  45.7 us
    reshape x4, local copies, waits for them, and re-layouts, scatter_rows(): full = grad.reshape(4, depth, 4, 2, 2, 128)  43.3 us
    all_to_all x2, waiting for transfers between devices, from_share(): parts = lax.all_to_all(share[None], 'z', 2, 0, tiled=True)  42.1 us
    reshape x4, local copies, waits for them, and re-layouts, scatter_columns(): full = grad.reshape(4, 2, 2, 128, 4, width)  41.9 us
  transfers between devices with their start and end apart: 84, of which 48 were waited for; matrix products, arithmetic and copies ran while one was open for 46% of the time, Pallas kernels for 0%

profile of v1, /device:TPU:0, one launch (start us, length us, event | category | flops | bytes accessed | tf_op | source)
XLA Modules:
  0.0 1063.9 jit_solution(384894929517310089)
XLA Ops:
  7.3 10.2 all_to_all.311
  41.5 4.7 all-to-all-done.4
  48.0 13.1 %all_to_all.312 = bf16[512,2,512]{0,2,1:T(8,128)(2,1)S(1)} all-to-all(bf16[512,2,512]{0,2,1:T(8,128)(2,1)S(1)} %bitcast.415), channel_id=1, replica_groups=mesh['y'=2,'c'=2,'z'=4,'x'=2] {'y'}, dimensions={1} | all-to-all | bytes 2097152 | tf_op jit(solution)/shard_map/all_to_all | solution.py:95
  63.1 12.4 %all_to_all.313 = bf16[2048,2,128]{0,2,1:T(8,128)(2,1)S(1)} all-to-all(bf16[2048,2,128]{0,2,1:T(8,128)(2,1)S(1)} %bitcast.416), channel_id=1, replica_groups=mesh['y'=2,'c'=2,'z'=4,'x'=2] {'y'}, dimensions={1} | all-to-all | bytes 2097152 | tf_op jit(solution)/shard_map/all_to_all | solution.py:38
  82.5 6.0 all-to-all-done.8
  95.2 40.3 %all-to-all-done.1 = bf16[4,1024,128]{2,1,0:T(8,128)(2,1)S(1)} async-done(((bf16[4,1024,128]{2,1,0:T(8,128)(2,1)}), bf16[4,1024,128]{2,1,0:T(8,128)(2,1)S(1)}, u32[]{:S(2)}, u32[]{:S(2)}) %all-to-all-start.1) | async-done | bytes 1048608 | tf_op jit(solution)/shard_map/all_to_all | solution.py:39
  145.6 17.8 %collective-permute-done = bf16[1024,512]{0,1:T(8,128)(2,1)S(1)} collective-permute-done((bf16[1024,512]{0,1:T(8,128)(2,1)S(1)}, bf16[1024,512]{0,1:T(8,128)(2,1)S(1)}, u32[]{:S(2)}, u32[]{:S(2)}) %collective-permute-start) | collective-permute-done | bytes 1048608 | tf_op jit(solution)/shard_map/ppermute | solution.py:33
  184.0 4.6 copy.508
  188.6 4.7 reshape.2059
  193.3 8.1 copy.393
  205.2 9.7 add_convert_fusion
  218.0 9.7 fusion.142
  227.8 8.3 fusion
  236.1 9.5 fusion.72
  252.5 9.0 collective-permute-done.9
  263.4 11.1 %collective-permute-done.6 = bf16[512,512]{0,1:T(8,128)(2,1)S(1)} collective-permute-done((bf16[512,512]{0,1:T(8,128)(2,1)S(1)}, bf16[512,512]{0,1:T(8,128)(2,1)S(1)}, u32[]{:S(2)}, u32[]{:S(2)}) %collective-permute-start.6) | collective-permute-done | bytes 524320 | tf_op jit(solution)/shard_map/ppermute | solution.py:33
  276.7 4.8 collective-permute-done.10
  287.3 4.4 fusion.131
  312.1 11.6 %collective-permute-done.14 = bf16[1024,512]{0,1:T(8,128)(2,1)} collective-permute-done((bf16[1024,512]{0,1:T(8,128)(2,1)}, bf16[1024,512]{0,1:T(8,128)(2,1)}, u32[]{:S(2)}, u32[]{:S(2)}) %collective-permute-start.14) | collective-permute-done | bytes 1048608 | tf_op jit(solution)/shard_map/ppermute | solution.py:33
  325.6 5.3 collective-permute-done.15
  334.4 5.4 all-to-all-done.9
  353.2 11.1 %copy.412 = bf16[4,2,2,4,128,512]{5,0,4,1,2,3:T(4,128)(2,1)} copy(bf16[4,2,2,4,128,512]{5,4,3,2,1,0:T(8,128)(2,1)} %bitcast.384) | data formatting | bytes 16777216 | tf_op jit(solution)/shard_map/reshape | solution.py:99
  364.3 10.3 copy.499
  374.6 14.3 %reshape.2062 = bf16[4,2,512,2,4,128]{5,4,3,2,1,0:T(4,128)(2,1)} reshape(bf16[8,512,1024]{2,1,0:T(8,128)(2,1)} %all-gather.10.cloned.1.call-done) | data formatting | bytes 16777216 | tf_op jit(solution)/shard_map/reshape | solution.py:107
  388.8 23.7 %copy.507 = bf16[4,2,512,2,4,128]{5,1,3,4,2,0:T(2,128)(2,1)} copy(bf16[4,2,512,2,4,128]{5,4,3,2,1,0:T(4,128)(2,1)} %reshape.2062) | data formatting | bytes 16777216 | tf_op jit(solution)/shard_map/reshape | solution.py:107
  412.5 14.5 %reshape.2063 = bf16[2048,2048]{1,0:T(8,128)(2,1)} reshape(bf16[4,512,4,2,2,128]{5,4,3,2,1,0:T(2,128)(2,1)} %bitcast.357) | data formatting | bytes 16777216 | tf_op jit(solution)/shard_map/reshape | solution.py:108
  427.0 17.3 %multiply_convert_fusion.1 = (bf16[1024,2048]{1,0:T(8,128)(2,1)S(1)}, f32[1024,2048]{1,0:T(8,128)}) fusion(f32[2048]{0:T(1024)S(1)} %bitcast.485, bf16[1024,2048]{0,1:T(8,128)(2,1)} %maximum_dynamic-update-slice_fusion.1, bf16[2048,2048]{1,0:T(8,128)(2,1)} %bitcast.385), kind=kOutput, calls=%fused_computation.21 | convolution fusion | flops 8610906112 | bytes 25174016 | tf_op jit(solution)/shard_map/dot_general | solution.py:24
  456.1 5.0 collective-permute-done.22
  466.8 5.6 collective-permute-done.23
  479.3 5.0 fusion.130
  495.5 4.9 constant_dynamic-update-slice_fusion.23
  503.1 17.1 %collective-permute-done.27 = bf16[1024,512]{0,1:T(8,128)(2,1)S(1)} collective-permute-done((bf16[1024,512]{0,1:T(8,128)(2,1)S(1)}, bf16[1024,512]{0,1:T(8,128)(2,1)S(1)}, u32[]{:S(2)}, u32[]{:S(2)}) %collective-permute-start.27) | collective-permute-done | bytes 1048608 | tf_op jit(solution)/shard_map/ppermute | solution.py:33
  530.3 22.6 %convert_reduce_fusion = (f32[2048]{0:T(1024)}, bf16[1024,2048]{1,0:T(8,128)(2,1)}) fusion(f32[1024,2048]{1,0:T(8,128)} %get-tuple-element.175, f32[2048]{0:T(1024)S(1)} %bitcast.486, bf16[1024,2048]{0,1:T(8,128)(2,1)S(1)} %maximum_dynamic-update-slice_fusion.2, bf16[2048,2048]{1,0:T(8,128)(2,1)} %reshape.2063), kind=kOutput, calls=%fused_computation.19 | convolution fusion | flops 8638167040 | bytes 25182208 | tf_op jit(solution)/shard_map/dot_general | solution.py:24
  552.9 4.8 fusion.44
  576.6 5.8 collective-permute-done.36
  589.3 5.7 multiply_reduce_fusion.2
  607.0 12.7 %collective-permute-done.40 = bf16[1024,512]{0,1:T(8,128)(2,1)S(1)} collective-permute-done((bf16[1024,512]{0,1:T(8,128)(2,1)S(1)}, bf16[1024,512]{0,1:T(8,128)(2,1)S(1)}, u32[]{:S(2)}, u32[]{:S(2)}) %collective-permute-start.40) | collective-permute-done | bytes 1048608 | tf_op jit(solution)/shard_map/ppermute | solution.py:33
  622.9 6.0 collective-permute-done.42
  640.1 4.6 copy.459
  645.9 11.6 %multiply_reduce_fusion = (f32[4,1024]{1,0:T(4,128)S(1)}, f32[4,1024,1024]{1,2,0:T(8,128)}) fusion(f32[4,1024,1024]{1,2,0:T(8,128)} %get-tuple-element.171, f32[4,1024]{1,0:T(4,128)S(1)} %log_add_fusion, bf16[1024,4,128]{0,2,1:T(8,128)(2,1)S(1)} %bitcast.418, bf16[1024,4,3,128]{0,3,2,1:T(8,128)(2,1)} %bitcast.379), kind=kOutput, calls=%fused_computation.1 | convolution fusion | flops 1086320640 | bytes 35684352 | tf_op jit(solution)/shard_map/qhd,khd->hqk/dot_general | solution.py:249
  657.6 12.4 %multiply_convert_fusion = bf16[4,1024,1024]{1,2,0:T(8,128)(2,1)S(1)} fusion(f32[4,1024,1024]{1,2,0:T(8,128)} %get-tuple-element.178, f32[4,1024,1024]{1,2,0:T(8,128)} %get-tuple-element.171, f32[4,1024]{1,0:T(4,128)S(1)} %get-tuple-element.177, f32[4,1024]{1,0:T(4,128)S(1)} %log_add_fusion), kind=kLoop, calls=%fused_computation | loop fusion | flops 16777216 | bytes 41975808 | tf_op jit(solution)/shard_map/convert_element_type | solution.py:251
  675.5 8.1 fusion.83
  683.6 5.2 fusion.79
  692.6 10.9 %convolution_convert_fusion.2 = bf16[2048,1536]{1,0:T(8,128)(2,1)} fusion(bf16[1024,2048]{0,1:T(8,128)(2,1)} %maximum_dynamic-update-slice_fusion, bf16[1024,1536]{0,1:T(8,128)(2,1)S(1)} %bitcast.419), kind=kOutput, calls=%fused_computation.25 | convolution fusion | flops 6445596672 | bytes 13631488 | tf_op jit(solution)/shard_map/dot_general | solution.py:24
  703.6 11.8 %reshape.2069 = bf16[4,2,2,128,4,384]{5,4,3,2,1,0:T(4,128)(2,1)} reshape(bf16[2048,1536]{1,0:T(8,128)(2,1)} %convolution_convert_fusion.2) | data formatting | bytes 12582912 | tf_op jit(solution)/shard_map/reshape | solution.py:113
  715.4 6.7 copy.455
  722.2 14.1 %convolution_convert_fusion = bf16[2048,2048]{1,0:T(8,128)(2,1)} fusion(bf16[1024,2048]{1,0:T(8,128)(2,1)} %copy-done.92, bf16[1024,2048]{0,1:T(8,128)(2,1)} %copy-done.35), kind=kOutput, calls=%fused_computation.23 | convolution fusion | flops 8594128896 | bytes 16777216 | tf_op jit(solution)/shard_map/dot_general | solution.py:24
  736.3 14.3 %reshape.2082 = bf16[4,512,4,2,2,128]{5,4,3,2,1,0:T(2,128)(2,1)} reshape(bf16[2048,2048]{1,0:T(8,128)(2,1)} %convolution_convert_fusion) | data formatting | bytes 16777216 | tf_op jit(solution)/shard_map/reshape | solution.py:125
  750.6 21.1 %copy.463 = bf16[4,512,4,2,2,128]{1,5,2,3,4,0:T(8,128)(2,1)} copy(bf16[4,512,4,2,2,128]{5,4,3,2,1,0:T(2,128)(2,1)} %reshape.2082) | data formatting | bytes 16777216 | tf_op jit(solution)/shard_map/reshape | solution.py:125
  771.8 14.0 %convolution_convert_fusion.1 = bf16[2048,2048]{1,0:T(8,128)(2,1)} fusion(bf16[1024,2048]{0,1:T(8,128)(2,1)} %maximum_dynamic-update-slice_fusion.1, bf16[1024,2048]{1,0:T(8,128)(2,1)} %get-tuple-element.105), kind=kOutput, calls=%fused_computation.24 | convolution fusion | flops 8594128896 | bytes 16777216 | tf_op jit(solution)/shard_map/dot_general | solution.py:24
  785.8 14.7 %reshape.2079 = bf16[4,2,2,128,4,512]{5,4,3,2,1,0:T(4,128)(2,1)} reshape(bf16[2048,2048]{1,0:T(8,128)(2,1)} %convolution_convert_fusion.1) | data formatting | bytes 16777216 | tf_op jit(solution)/shard_map/reshape | solution.py:113
  800.5 8.7 copy.461
  835.9 5.5 collective-permute-done.45
  860.6 6.8 reduce.21
  869.4 5.3 all-to-all-start.13
  876.6 7.8 reduce.20
  888.1 23.3 %all-to-all-done.13 = bf16[4,2,65536]{2,1,0:T(2,128)(2,1)S(1)} async-done(((bf16[4,2,65536]{2,1,0:T(2,128)(2,1)}), bf16[4,2,65536]{2,1,0:T(2,128)(2,1)S(1)}, u32[]{:S(2)}, u32[]{:S(2)}) %all-to-all-start.13) | async-done | bytes 1048608 | tf_op jit(solution)/shard_map/all_to_all | solution.py:44
  922.1 18.8 %all-to-all-done.11 = bf16[4,2,65536]{2,1,0:T(2,128)(2,1)S(1)} async-done(((bf16[4,2,65536]{2,1,0:T(2,128)(2,1)}), bf16[4,2,65536]{2,1,0:T(2,128)(2,1)S(1)}, u32[]{:S(2)}, u32[]{:S(2)}) %all-to-all-start.11) | async-done | bytes 1048608 | tf_op jit(solution)/shard_map/all_to_all | solution.py:44
  974.1 5.1 collective-permute-done.56
  996.2 4.6 all-to-all-done.15
  1004.8 4.6 all-to-all-done.17
  1028.5 7.4 all-to-all-done.21
  1035.9 4.4 all-to-all-start.20
  1044.6 5.9 all-to-all-done.20
  (560 shorter events, 391.7 us)
Async XLA Ops:
  7.2 173.5 %all-gather.6.cloned.1.call-start = ((), (), s32[]{:S(2)}) async-start(), calls=%async_computation.26 | async-start | bytes 2359296 | tf_op jit(solution)/shard_map/all_gather | solution.py:105
  41.1 152.2 %all-gather.12.cloned.1.call-start = ((), (), s32[]{:S(2)}) async-start(), calls=%async_computation.33 | async-start | bytes 7077888 | tf_op jit(solution)/shard_map/all_gather | solution.py:97
  47.4 305.8 %all-gather.8.cloned.1.call-start = ((), (), s32[]{:S(2)}) async-start(), calls=%async_computation.27 | async-start | bytes 9437184 | tf_op jit(solution)/shard_map/all_gather | solution.py:97
  75.6 13.0 %all-to-all-start.8 = ((bf16[2,512,512]{2,1,0:T(8,128)(2,1)}), bf16[2,512,512]{2,1,0:T(8,128)(2,1)S(1)}, u32[]{:S(2)}, u32[]{:S(2)}) async-start(bf16[2,512,512]{2,1,0:T(8,128)(2,1)} %bitcast.57), calls=%async_computation.8 | async-start | bytes 2097152 | tf_op jit(solution)/shard_map/all_to_all | solution.py:104
  79.2 63.8 %collective-permute-start.4 = (s32[2,4]{1,0:T(2,128)S(1)}, s32[2,4]{1,0:T(2,128)S(1)}, u32[]{:S(2)}, u32[]{:S(2)}) collective-permute-start(s32[2,4]{1,0:T(2,128)S(1)} %copy-done.91), channel_id=1, source_target_pairs={{0,16},{1,17},{2,18},{3,19},{4,20},{5,21},{6,22},{7,23},{8,24},{9,... | collective-permute-start | bytes 104 | tf_op jit(solution)/shard_map/ppermute | solution.py:33
  88.5 46.9 %all-to-all-start.1 = ((bf16[4,1024,128]{2,1,0:T(8,128)(2,1)}), bf16[4,1024,128]{2,1,0:T(8,128)(2,1)S(1)}, u32[]{:S(2)}, u32[]{:S(2)}) async-start(bf16[4,1024,128]{2,1,0:T(8,128)(2,1)} %bitcast.2), calls=%async_computation.1 | async-start | bytes 2097152 | tf_op jit(solution)/shard_map/all_to_all | solution.py:39
  92.9 281.7 %all-gather.10.cloned.1.call-start = ((), (), s32[]{:S(2)}) async-start(), calls=%async_computation.28 | async-start | bytes 9437184 | tf_op jit(solution)/shard_map/all_gather | solution.py:105
  139.9 23.5 %collective-permute-start = (bf16[1024,512]{0,1:T(8,128)(2,1)S(1)}, bf16[1024,512]{0,1:T(8,128)(2,1)S(1)}, u32[]{:S(2)}, u32[]{:S(2)}) collective-permute-start(bf16[1024,512]{0,1:T(8,128)(2,1)S(1)} %bitcast.363), channel_id=1, source_target_pairs={{0,1},{1,0},{2,3},{3,2},{4,5},{5,4},{6,7},{7,6},{8,9},{9,8},{10,11... | collective-permute-start | bytes 3145736 | tf_op jit(solution)/shard_map/ppermute | solution.py:33
  141.5 24.6 %collective-permute-start.1 = (bf16[1024,512]{0,1:T(8,128)(2,1)S(1)}, bf16[1024,512]{0,1:T(8,128)(2,1)}, u32[]{:S(2)}, u32[]{:S(2)}) collective-permute-start(bf16[1024,512]{0,1:T(8,128)(2,1)S(1)} %bitcast.364), channel_id=1, source_target_pairs={{0,16},{1,17},{2,18},{3,19},{4,20},{5,21},{6,22},{7,23},{8,24},{9,... | collective-permute-start | bytes 3145736 | tf_op jit(solution)/shard_map/ppermute | solution.py:33
  164.3 12.0 %collective-permute-start.2 = (bf16[512,512]{0,1:T(8,128)(2,1)}, bf16[512,512]{0,1:T(8,128)(2,1)}, u32[]{:S(2)}, u32[]{:S(2)}) collective-permute-start(bf16[512,512]{0,1:T(8,128)(2,1)} %slice.316), channel_id=1, source_target_pairs={{0,16},{1,17},{2,18},{3,19},{4,20},{5,21},{6,22},{7,23},{8,24},{9,... | collective-permute-start | bytes 1572872 | tf_op jit(solution)/shard_map/ppermute | solution.py:33
  167.1 11.5 %collective-permute-start.3 = (bf16[512,512]{0,1:T(8,128)(2,1)S(1)}, bf16[512,512]{0,1:T(8,128)(2,1)S(1)}, u32[]{:S(2)}, u32[]{:S(2)}) collective-permute-start(bf16[512,512]{0,1:T(8,128)(2,1)S(1)} %slice.317), channel_id=1, source_target_pairs={{0,1},{1,0},{2,3},{3,2},{4,5},{5,4},{6,7},{7,6},{8,9},{9,8},{10,11... | collective-permute-start | bytes 1572872 | tf_op jit(solution)/shard_map/ppermute | solution.py:33
  246.6 14.9 %collective-permute-start.9 = (bf16[512,512]{0,1:T(8,128)(2,1)S(1)}, bf16[512,512]{0,1:T(8,128)(2,1)S(1)}, u32[]{:S(2)}, u32[]{:S(2)}) collective-permute-start(bf16[512,512]{0,1:T(8,128)(2,1)S(1)} %get-tuple-element.135), channel_id=1, source_target_pairs={{0,16},{1,17},{2,18},{3,19},{4,20},{5,21},{6,22},{7,23},{8,24},{9,... | collective-permute-start | bytes 1572872 | tf_op jit(solution)/shard_map/ppermute | solution.py:33
  248.3 28.4 %collective-permute-start.5 = (bf16[512,512]{0,1:T(8,128)(2,1)S(1)}, bf16[512,512]{0,1:T(8,128)(2,1)S(1)}, u32[]{:S(2)}, u32[]{:S(2)}) collective-permute-start(bf16[512,512]{0,1:T(8,128)(2,1)S(1)} %slice.498), channel_id=1, source_target_pairs={{0,1},{1,0},{2,3},{3,2},{4,5},{5,4},{6,7},{7,6},{8,9},{9,8},{10,11... | collective-permute-start | bytes 1572872 | tf_op jit(solution)/shard_map/ppermute | solution.py:33
  249.8 24.6 %collective-permute-start.6 = (bf16[512,512]{0,1:T(8,128)(2,1)S(1)}, bf16[512,512]{0,1:T(8,128)(2,1)S(1)}, u32[]{:S(2)}, u32[]{:S(2)}) collective-permute-start(bf16[512,512]{0,1:T(8,128)(2,1)S(1)} %get-tuple-element.134), channel_id=1, source_target_pairs={{0,1},{1,0},{2,3},{3,2},{4,5},{5,4},{6,7},{7,6},{8,9},{9,8},{10,11... | collective-permute-start | bytes 1572872 | tf_op jit(solution)/shard_map/ppermute | solution.py:33
  251.3 25.4 %collective-permute-start.8 = (bf16[512,512]{0,1:T(8,128)(2,1)S(1)}, bf16[512,512]{0,1:T(8,128)(2,1)S(1)}, u32[]{:S(2)}, u32[]{:S(2)}) collective-permute-start(bf16[512,512]{0,1:T(8,128)(2,1)S(1)} %slice.497), channel_id=1, source_target_pairs={{0,16},{1,17},{2,18},{3,19},{4,20},{5,21},{6,22},{7,23},{8,24},{9,... | collective-permute-start | bytes 1572872 | tf_op jit(solution)/shard_map/ppermute | solution.py:33
  261.7 19.8 %collective-permute-start.10 = (bf16[512,512]{0,1:T(8,128)(2,1)S(1)}, bf16[512,512]{0,1:T(8,128)(2,1)S(1)}, u32[]{:S(2)}, u32[]{:S(2)}) collective-permute-start(bf16[512,512]{0,1:T(8,128)(2,1)S(1)} %fusion.98), channel_id=1, source_target_pairs={{0,1},{1,0},{2,3},{3,2},{4,5},{5,4},{6,7},{7,6},{8,9},{9,8},{10,11... | collective-permute-start | bytes 1572872 | tf_op jit(solution)/shard_map/ppermute | solution.py:33
  274.6 9.2 collective-permute-start.7
  304.1 19.6 %collective-permute-start.14 = (bf16[1024,512]{0,1:T(8,128)(2,1)}, bf16[1024,512]{0,1:T(8,128)(2,1)}, u32[]{:S(2)}, u32[]{:S(2)}) collective-permute-start(bf16[1024,512]{0,1:T(8,128)(2,1)} %get-tuple-element.173), channel_id=1, source_target_pairs={{0,1},{1,0},{2,3},{3,2},{4,5},{5,4},{6,7},{7,6},{8,9},{9,8},{10,11... | collective-permute-start | bytes 3145736 | tf_op jit(solution)/shard_map/ppermute | solution.py:33
  304.4 26.4 %collective-permute-start.15 = (bf16[1024,512]{0,1:T(8,128)(2,1)}, bf16[1024,512]{0,1:T(8,128)(2,1)}, u32[]{:S(2)}, u32[]{:S(2)}) collective-permute-start(bf16[1024,512]{0,1:T(8,128)(2,1)} %get-tuple-element.173), channel_id=1, source_target_pairs={{0,16},{1,17},{2,18},{3,19},{4,20},{5,21},{6,22},{7,23},{8,24},{9,... | collective-permute-start | bytes 3145736 | tf_op jit(solution)/shard_map/ppermute | solution.py:33
  307.7 32.1 %all-to-all-start.9 = ((bf16[2048,2,128]{0,2,1:T(8,128)(2,1)}), bf16[2048,2,128]{0,2,1:T(8,128)(2,1)}, u32[]{:S(2)}, u32[]{:S(2)}) async-start(bf16[2048,2,128]{0,2,1:T(8,128)(2,1)} %bitcast.410), calls=%async_computation.9 | async-start | bytes 2097152 | tf_op jit(solution)/shard_map/all_to_all | solution.py:38
  325.6 25.4 %collective-permute-start.16 = (bf16[512,512]{0,1:T(8,128)(2,1)}, bf16[512,512]{0,1:T(8,128)(2,1)}, u32[]{:S(2)}, u32[]{:S(2)}) collective-permute-start(bf16[512,512]{0,1:T(8,128)(2,1)} %slice.336), channel_id=1, source_target_pairs={{0,16},{1,17},{2,18},{3,19},{4,20},{5,21},{6,22},{7,23},{8,24},{9,... | collective-permute-start | bytes 1572872 | tf_op jit(solution)/shard_map/ppermute | solution.py:33
  332.7 18.2 %collective-permute-start.17 = (bf16[512,512]{0,1:T(8,128)(2,1)}, bf16[512,512]{0,1:T(8,128)(2,1)}, u32[]{:S(2)}, u32[]{:S(2)}) collective-permute-start(bf16[512,512]{0,1:T(8,128)(2,1)} %slice.337), channel_id=1, source_target_pairs={{0,1},{1,0},{2,3},{3,2},{4,5},{5,4},{6,7},{7,6},{8,9},{9,8},{10,11... | collective-permute-start | bytes 1572872 | tf_op jit(solution)/shard_map/ppermute | solution.py:33
  342.1 137.2 %all-to-all-start.10 = ((bf16[4,1024,128]{2,1,0:T(8,128)(2,1)}), bf16[4,1024,128]{2,1,0:T(8,128)(2,1)}, u32[]{:S(2)}, u32[]{:S(2)}) async-start(bf16[4,1024,128]{2,1,0:T(8,128)(2,1)} %bitcast.408), calls=%async_computation.10 | async-start | bytes 2097152 | tf_op jit(solution)/shard_map/all_to_all | solution.py:39
  346.3 637.2 %reduce-scatter.7.cloned.1.call-start = ((), (), s32[]{:S(2)}) async-start(), calls=%async_computation.30 | async-start | bytes 2359296 | tf_op jit(solution)/shard_map/reduce_scatter | solution.py:127
  449.3 11.8 %collective-permute-start.22 = (bf16[512,512]{0,1:T(8,128)(2,1)S(1)}, bf16[512,512]{0,1:T(8,128)(2,1)S(1)}, u32[]{:S(2)}, u32[]{:S(2)}) collective-permute-start(bf16[512,512]{0,1:T(8,128)(2,1)S(1)} %get-tuple-element.133), channel_id=1, source_target_pairs={{0,16},{1,17},{2,18},{3,19},{4,20},{5,21},{6,22},{7,23},{8,24},{9,... | collective-permute-start | bytes 1572872 | tf_op jit(solution)/shard_map/ppermute | solution.py:33
  449.6 12.4 %collective-permute-start.19 = (bf16[512,512]{0,1:T(8,128)(2,1)S(1)}, bf16[512,512]{0,1:T(8,128)(2,1)S(1)}, u32[]{:S(2)}, u32[]{:S(2)}) collective-permute-start(bf16[512,512]{0,1:T(8,128)(2,1)S(1)} %get-tuple-element.132), channel_id=1, source_target_pairs={{0,1},{1,0},{2,3},{3,2},{4,5},{5,4},{6,7},{7,6},{8,9},{9,8},{10,11... | collective-permute-start | bytes 1572872 | tf_op jit(solution)/shard_map/ppermute | solution.py:33
  453.4 13.4 %collective-permute-start.18 = (bf16[512,512]{0,1:T(8,128)(2,1)S(1)}, bf16[512,512]{0,1:T(8,128)(2,1)S(1)}, u32[]{:S(2)}, u32[]{:S(2)}) collective-permute-start(bf16[512,512]{0,1:T(8,128)(2,1)S(1)} %slice.496), channel_id=1, source_target_pairs={{0,1},{1,0},{2,3},{3,2},{4,5},{5,4},{6,7},{7,6},{8,9},{9,8},{10,11... | collective-permute-start | bytes 1572872 | tf_op jit(solution)/shard_map/ppermute | solution.py:33
  454.3 12.5 %collective-permute-start.21 = (bf16[512,512]{0,1:T(8,128)(2,1)S(1)}, bf16[512,512]{0,1:T(8,128)(2,1)S(1)}, u32[]{:S(2)}, u32[]{:S(2)}) collective-permute-start(bf16[512,512]{0,1:T(8,128)(2,1)S(1)} %slice.495), channel_id=1, source_target_pairs={{0,16},{1,17},{2,18},{3,19},{4,20},{5,21},{6,22},{7,23},{8,24},{9,... | collective-permute-start | bytes 1572872 | tf_op jit(solution)/shard_map/ppermute | solution.py:33
  461.3 11.1 %collective-permute-start.23 = (bf16[512,512]{0,1:T(8,128)(2,1)S(1)}, bf16[512,512]{0,1:T(8,128)(2,1)S(1)}, u32[]{:S(2)}, u32[]{:S(2)}) collective-permute-start(bf16[512,512]{0,1:T(8,128)(2,1)S(1)} %fusion.94), channel_id=1, source_target_pairs={{0,1},{1,0},{2,3},{3,2},{4,5},{5,4},{6,7},{7,6},{8,9},{9,8},{10,11... | collective-permute-start | bytes 1572872 | tf_op jit(solution)/shard_map/ppermute | solution.py:33
  462.3 10.2 collective-permute-start.20
  484.3 9.2 collective-permute-start.24
  500.5 19.7 %collective-permute-start.27 = (bf16[1024,512]{0,1:T(8,128)(2,1)S(1)}, bf16[1024,512]{0,1:T(8,128)(2,1)S(1)}, u32[]{:S(2)}, u32[]{:S(2)}) collective-permute-start(bf16[1024,512]{0,1:T(8,128)(2,1)S(1)} %get-tuple-element.114), channel_id=1, source_target_pairs={{0,1},{1,0},{2,3},{3,2},{4,5},{5,4},{6,7},{7,6},{8,9},{9,8},{10,11... | collective-permute-start | bytes 3145736 | tf_op jit(solution)/shard_map/ppermute | solution.py:33
  501.3 19.6 %collective-permute-start.28 = (bf16[1024,512]{0,1:T(8,128)(2,1)S(1)}, bf16[1024,512]{0,1:T(8,128)(2,1)S(1)}, u32[]{:S(2)}, u32[]{:S(2)}) collective-permute-start(bf16[1024,512]{0,1:T(8,128)(2,1)S(1)} %get-tuple-element.114), channel_id=1, source_target_pairs={{0,16},{1,17},{2,18},{3,19},{4,20},{5,21},{6,22},{7,23},{8,24},{9,... | collective-permute-start | bytes 3145736 | tf_op jit(solution)/shard_map/ppermute | solution.py:33
  520.2 9.2 collective-permute-start.29
  520.9 9.2 collective-permute-start.30
  560.2 9.2 collective-permute-start.35
  561.8 9.3 collective-permute-start.32
  564.7 11.9 %collective-permute-start.31 = (bf16[512,512]{0,1:T(8,128)(2,1)S(1)}, bf16[512,512]{0,1:T(8,128)(2,1)S(1)}, u32[]{:S(2)}, u32[]{:S(2)}) collective-permute-start(bf16[512,512]{0,1:T(8,128)(2,1)S(1)} %slice.494), channel_id=1, source_target_pairs={{0,1},{1,0},{2,3},{3,2},{4,5},{5,4},{6,7},{7,6},{8,9},{9,8},{10,11... | collective-permute-start | bytes 1572872 | tf_op jit(solution)/shard_map/ppermute | solution.py:33
  566.4 10.2 collective-permute-start.34
  569.6 12.7 %collective-permute-start.36 = (bf16[512,512]{0,1:T(8,128)(2,1)S(1)}, bf16[512,512]{0,1:T(8,128)(2,1)S(1)}, u32[]{:S(2)}, u32[]{:S(2)}) collective-permute-start(bf16[512,512]{0,1:T(8,128)(2,1)S(1)} %fusion.90), channel_id=1, source_target_pairs={{0,1},{1,0},{2,3},{3,2},{4,5},{5,4},{6,7},{7,6},{8,9},{9,8},{10,11... | collective-permute-start | bytes 1572872 | tf_op jit(solution)/shard_map/ppermute | solution.py:33
  571.2 11.1 %collective-permute-start.33 = (bf16[512,512]{0,1:T(8,128)(2,1)S(1)}, bf16[512,512]{0,1:T(8,128)(2,1)S(1)}, u32[]{:S(2)}, u32[]{:S(2)}) collective-permute-start(bf16[512,512]{0,1:T(8,128)(2,1)S(1)} %fusion.92), channel_id=1, source_target_pairs={{0,16},{1,17},{2,18},{3,19},{4,20},{5,21},{6,22},{7,23},{8,24},{9,... | collective-permute-start | bytes 1572872 | tf_op jit(solution)/shard_map/ppermute | solution.py:33
  604.9 14.8 %collective-permute-start.40 = (bf16[1024,512]{0,1:T(8,128)(2,1)S(1)}, bf16[1024,512]{0,1:T(8,128)(2,1)S(1)}, u32[]{:S(2)}, u32[]{:S(2)}) collective-permute-start(bf16[1024,512]{0,1:T(8,128)(2,1)S(1)} %get-tuple-element.118), channel_id=1, source_target_pairs={{0,1},{1,0},{2,3},{3,2},{4,5},{5,4},{6,7},{7,6},{8,9},{9,8},{10,11... | collective-permute-start | bytes 3145736 | tf_op jit(solution)/shard_map/ppermute | solution.py:33
  605.4 14.9 %collective-permute-start.41 = (bf16[1024,512]{0,1:T(8,128)(2,1)S(1)}, bf16[1024,512]{0,1:T(8,128)(2,1)S(1)}, u32[]{:S(2)}, u32[]{:S(2)}) collective-permute-start(bf16[1024,512]{0,1:T(8,128)(2,1)S(1)} %get-tuple-element.118), channel_id=1, source_target_pairs={{0,16},{1,17},{2,18},{3,19},{4,20},{5,21},{6,22},{7,23},{8,24},{9,... | collective-permute-start | bytes 3145736 | tf_op jit(solution)/shard_map/ppermute | solution.py:33
  619.7 9.2 collective-permute-start.42
  620.4 9.2 collective-permute-start.43
  644.7 342.2 %reduce-scatter.5.cloned.1.call-start = ((), (), s32[]{:S(2)}) async-start(), calls=%async_computation.29 | async-start | bytes 7077888 | tf_op jit(solution)/shard_map/reduce_scatter | solution.py:115
  722.1 299.1 %reduce-scatter.11.cloned.1.call-start = ((), (), s32[]{:S(2)}) async-start(), calls=%async_computation.32 | async-start | bytes 9437184 | tf_op jit(solution)/shard_map/reduce_scatter | solution.py:127
  771.7 256.7 %reduce-scatter.9.cloned.1.call-start = ((), (), s32[]{:S(2)}) async-start(), calls=%async_computation.31 | async-start | bytes 9437184 | tf_op jit(solution)/shard_map/reduce_scatter | solution.py:115
  820.8 12.5 %collective-permute-start.48 = (bf16[512,512]{0,1:T(8,128)(2,1)S(1)}, bf16[512,512]{0,1:T(8,128)(2,1)S(1)}, u32[]{:S(2)}, u32[]{:S(2)}) collective-permute-start(bf16[512,512]{0,1:T(8,128)(2,1)S(1)} %get-tuple-element.129), channel_id=1, source_target_pairs={{0,16},{1,17},{2,18},{3,19},{4,20},{5,21},{6,22},{7,23},{8,24},{9,... | collective-permute-start | bytes 1572872 | tf_op jit(solution)/shard_map/ppermute | solution.py:33
  826.5 24.9 %collective-permute-start.44 = (bf16[512,512]{0,1:T(8,128)(2,1)}, bf16[512,512]{0,1:T(8,128)(2,1)}, u32[]{:S(2)}, u32[]{:S(2)}) collective-permute-start(bf16[512,512]{0,1:T(8,128)(2,1)} %slice.492), channel_id=1, source_target_pairs={{0,1},{1,0},{2,3},{3,2},{4,5},{5,4},{6,7},{7,6},{8,9},{9,8},{10,11... | collective-permute-start | bytes 1572872 | tf_op jit(solution)/shard_map/ppermute | solution.py:33
  826.9 14.6 %collective-permute-start.45 = (bf16[512,512]{0,1:T(8,128)(2,1)S(1)}, bf16[512,512]{0,1:T(8,128)(2,1)S(1)}, u32[]{:S(2)}, u32[]{:S(2)}) collective-permute-start(bf16[512,512]{0,1:T(8,128)(2,1)S(1)} %get-tuple-element.128), channel_id=1, source_target_pairs={{0,1},{1,0},{2,3},{3,2},{4,5},{5,4},{6,7},{7,6},{8,9},{9,8},{10,11... | collective-permute-start | bytes 1572872 | tf_op jit(solution)/shard_map/ppermute | solution.py:33
  832.7 18.7 %collective-permute-start.47 = (bf16[512,512]{0,1:T(8,128)(2,1)}, bf16[512,512]{0,1:T(8,128)(2,1)}, u32[]{:S(2)}, u32[]{:S(2)}) collective-permute-start(bf16[512,512]{0,1:T(8,128)(2,1)} %slice.491), channel_id=1, source_target_pairs={{0,16},{1,17},{2,18},{3,19},{4,20},{5,21},{6,22},{7,23},{8,24},{9,... | collective-permute-start | bytes 1572872 | tf_op jit(solution)/shard_map/ppermute | solution.py:33
  834.2 17.2 %collective-permute-start.49 = (bf16[512,512]{0,1:T(8,128)(2,1)}, bf16[512,512]{0,1:T(8,128)(2,1)}, u32[]{:S(2)}, u32[]{:S(2)}) collective-permute-start(bf16[512,512]{0,1:T(8,128)(2,1)} %fusion.84), channel_id=1, source_target_pairs={{0,1},{1,0},{2,3},{3,2},{4,5},{5,4},{6,7},{7,6},{8,9},{9,8},{10,11... | collective-permute-start | bytes 1572872 | tf_op jit(solution)/shard_map/ppermute | solution.py:33
  842.4 9.5 collective-permute-start.46
  843.5 25.9 %all-to-all-start.16 = ((f32[4,1,1536]{2,1,0:T(1,128)}), f32[4,1,1536]{2,1,0:T(1,128)S(1)}, u32[]{:S(2)}, u32[]{:S(2)}) async-start(f32[4,1,1536]{2,1,0:T(1,128)} %all_to_all.277), calls=%async_computation.17 | async-start | bytes 49152 | tf_op jit(solution)/shard_map/all_to_all | solution.py:276
  869.4 41.9 %all-to-all-start.13 = ((bf16[4,2,65536]{2,1,0:T(2,128)(2,1)}), bf16[4,2,65536]{2,1,0:T(2,128)(2,1)S(1)}, u32[]{:S(2)}, u32[]{:S(2)}) async-start(bf16[4,2,65536]{2,1,0:T(2,128)(2,1)} %reshape.2107), calls=%async_computation.13 | async-start | bytes 2097152 | tf_op jit(solution)/shard_map/all_to_all | solution.py:44
  912.4 28.6 %all-to-all-start.11 = ((bf16[4,2,65536]{2,1,0:T(2,128)(2,1)}), bf16[4,2,65536]{2,1,0:T(2,128)(2,1)S(1)}, u32[]{:S(2)}, u32[]{:S(2)}) async-start(bf16[4,2,65536]{2,1,0:T(2,128)(2,1)} %reshape.2105), calls=%async_computation.11 | async-start | bytes 2097152 | tf_op jit(solution)/shard_map/all_to_all | solution.py:44
  941.9 18.9 %all-to-all-start.14 = ((bf16[2,2048,128]{2,1,0:T(8,128)(2,1)}), bf16[2,2048,128]{2,1,0:T(8,128)(2,1)S(1)}, u32[]{:S(2)}, u32[]{:S(2)}) async-start(bf16[2,2048,128]{2,1,0:T(8,128)(2,1)} %bitcast.108), calls=%async_computation.14 | async-start | bytes 2097152 | tf_op jit(solution)/shard_map/all_to_all | solution.py:45
  954.3 10.0 collective-permute-start.53
  954.4 25.4 %collective-permute-start.50 = (f32[1536]{0:T(1024)S(1)}, f32[1536]{0:T(1024)S(1)}, u32[]{:S(2)}, u32[]{:S(2)}) collective-permute-start(f32[1536]{0:T(1024)S(1)} %reduce_sum.235), channel_id=1, source_target_pairs={{0,8},{1,9},{2,10},{3,11},{4,12},{5,13},{6,14},{7,15},{8,0},{9,1},... | collective-permute-start | bytes 18440 | tf_op jit(solution)/shard_map/ppermute | solution.py:33
  960.7 22.7 %all-to-all-start.12 = ((bf16[2,2048,128]{2,1,0:T(8,128)(2,1)}), bf16[2,2048,128]{2,1,0:T(8,128)(2,1)S(1)}, u32[]{:S(2)}, u32[]{:S(2)}) async-start(bf16[2,2048,128]{2,1,0:T(8,128)(2,1)} %bitcast.80), calls=%async_computation.12 | async-start | bytes 2097152 | tf_op jit(solution)/shard_map/all_to_all | solution.py:45
  1010.1 11.1 %all-to-all-start.18 = ((bf16[2,512,128]{2,1,0:T(8,128)(2,1)}), bf16[2,512,128]{2,1,0:T(8,128)(2,1)}, u32[]{:S(2)}, u32[]{:S(2)}) async-start(bf16[2,512,128]{2,1,0:T(8,128)(2,1)} %bitcast.124), calls=%async_computation.19 | async-start | bytes 524288 | tf_op jit(solution)/shard_map/all_to_all | solution.py:118
  1021.2 14.7 %all-to-all-start.21 = ((bf16[512,2,512]{0,2,1:T(8,128)(2,1)}), bf16[512,2,512]{0,2,1:T(8,128)(2,1)S(1)}, u32[]{:S(2)}, u32[]{:S(2)}) async-start(bf16[512,2,512]{0,2,1:T(8,128)(2,1)} %bitcast.429), calls=%async_computation.25 | async-start | bytes 2097152 | tf_op jit(solution)/shard_map/all_to_all | solution.py:128
  1035.9 14.6 %all-to-all-start.20 = ((bf16[2,512,512]{2,1,0:T(8,128)(2,1)}), bf16[2,512,512]{2,1,0:T(8,128)(2,1)}, u32[]{:S(2)}, u32[]{:S(2)}) async-start(bf16[2,512,512]{2,1,0:T(8,128)(2,1)} %bitcast.428), calls=%async_computation.23 | async-start | bytes 2097152 | tf_op jit(solution)/shard_map/all_to_all | solution.py:118
  (120 other events, 4308.7 us)
Sparse Core Ops, SparseCore 0:
  18.7 29.6 all-gather.5
  50.5 86.0 all-gather.11
  138.2 80.4 all-gather.7
  220.2 80.5 all-gather.9
  644.9 35.4 reduce-scatter.6
  722.2 69.4 reduce-scatter.4
  794.0 103.2 reduce-scatter.10
  899.6 110.3 reduce-scatter.8

commit v2 on v0

--- a/solution.py
+++ b/solution.py
@@ -1,14 +1,19 @@
+import functools
+
 import jax
 import jax.numpy as jnp
 from jax import lax
+from jax.experimental import pallas as pl
+from jax.experimental.pallas import tpu as pltpu
+from jax.sharding import Mesh
 from jax.sharding import PartitionSpec as P
 
 HD = 128
 LEN = 1024
-
-
 EPS = 1e-06
 NEGATIVE = -1000000000.0
+BF = jnp.bfloat16
+F32 = jnp.float32
 
 
 def segment_ids(lengths):
@@ -19,12 +24,700 @@
     return jnp.sum(hits, axis=2)
 
 
+AXES = ("y", "c", "z", "x")
+X_BIT, Z_LOW, Z_HIGH, C_BIT, Y_BIT = 1, 2, 4, 8, 16
+XY_BIT = X_BIT | Y_BIT
+QUARTER = 512
+HALF = LEN // 2
+WIDTH = 2048
+NN, NT, TN = ((1,), (0,)), ((1,), (1,)), ((0,), (0,))
+
+
+def swap(piece, mask):
+    return lax.ppermute(piece, AXES, [(i, i ^ mask) for i in range(32)])
+
+
+def dot(left, right, dims):
+    return lax.dot_general(left, right, (dims, ((), ())), preferred_element_type=F32)
+
+
+def call(body, grid, spot, ins, in_specs, outs, out_specs, scratch, flops, size):
+    return pl.pallas_call(
+        body,
+        grid_spec=pltpu.PrefetchScalarGridSpec(
+            num_scalar_prefetch=1, grid=grid, in_specs=in_specs, out_specs=out_specs, scratch_shapes=scratch
+        ),
+        out_shape=outs,
+        compiler_params=pltpu.CompilerParams(
+            dimension_semantics=("arbitrary",) * len(grid), vmem_limit_bytes=56 * 1024 * 1024
+        ),
+        cost_estimate=pl.CostEstimate(flops=flops, bytes_accessed=size, transcendentals=0),
+    )(spot, *ins)
+
+
+def shape_of(*shape, dtype=F32):
+    return jax.ShapeDtypeStruct(shape, dtype)
+
+
+def fixed(shape):
+    return pl.BlockSpec(shape, lambda *_: (0,) * len(shape))
+
+
+def pick(low, high, t):
+    return jnp.where(t == 0, low[...], high[...])
+
+
+SLOTS = (0, 2, 1, 3)
+
+
+def wide_body(by_rows, finish, count, spot, *refs):
+    pieces, weights, rest = refs[:8], refs[8], refs[9:]
+    extra, outs, kept = rest[: -1 - count], rest[-1 - count : -1], rest[-1]
+    t = pl.program_id(1)
+
+    @pl.when(t == 0)
+    def _():
+        for slot, mask in enumerate(SLOTS):
+            start = pl.multiple_of((spot[0] ^ mask) * 128, 128)
+            for block in range(4):
+                y, c = divmod(block, 2)
+                y = y ^ spot[1]
+                at = slot * QUARTER + block * 128
+                if by_rows:
+                    kept[:, at : at + 128] = weights[0, c, :, pl.ds(pl.multiple_of(y * 512 + start, 128), 128)]
+                else:
+                    kept[at : at + 128, :] = weights[0, c, y, pl.ds(start, 128), :]
+
+    total = None
+    for slot in range(4):
+        tile = pick(pieces[2 * slot], pieces[2 * slot + 1], t)
+        part = slice(slot * QUARTER, slot * QUARTER + QUARTER)
+        term = dot(tile, kept[:, part], NT) if by_rows else dot(tile, kept[part, :], NN)
+        total = term if total is None else total + term
+    finish(total, extra, outs)
+
+
+def wide(pieces, weights, spot, by_rows, finish, extra, count):
+    if by_rows:
+        n = weights.shape[1]
+        weights = weights.reshape(4, 2, n, 1024)
+        kept = pltpu.VMEM((n, WIDTH), BF)
+    else:
+        n = weights.shape[2]
+        weights = weights.reshape(4, 2, 2, 512, n)
+        kept = pltpu.VMEM((WIDTH, n), BF)
+    block = (1,) + weights.shape[1:]
+    tail = (0,) * (len(block) - 1)
+    bias = pl.BlockSpec((1, n), lambda z, t, *_: (0, z))
+    tile = pl.BlockSpec((HALF, n), lambda z, t, *_: (t, z))
+    return call(
+        functools.partial(wide_body, by_rows, finish, count),
+        (4, 2),
+        spot,
+        (*pieces, weights, *extra),
+        [fixed(p.shape) for p in pieces]
+        + [pl.BlockSpec(block, lambda z, t, *_: (z,) + tail)]
+        + [bias if e.shape[0] == 1 else tile for e in extra],
+        [shape_of(LEN, 4 * n, dtype=BF)] * count,
+        [tile] * count,
+        [kept],
+        2 * LEN * WIDTH * 4 * n,
+        2 * (LEN * WIDTH + WIDTH * 4 * n + LEN * 4 * n),
+    )
+
+
+def finish_bias(total, extra, outs):
+    outs[0][...] = (total + extra[0][...]).astype(BF)
+
+
+def finish_plain(total, extra, outs):
+    outs[0][...] = total.astype(BF)
+
+
+def finish_gelu(total, extra, outs):
+    pre = total + extra[0][...]
+    square = pre * pre
+    bend = jnp.tanh(0.7978845608028654 * pre * (1.0 + 0.044715 * square))
+    rise = 0.5 * (1.0 + bend)
+    outs[0][...] = (pre * rise).astype(BF)
+    slope = 0.7978845608028654 * (1.0 + 0.134145 * square)
+    outs[1][...] = (rise + 0.5 * pre * (1.0 - bend * bend) * slope).astype(BF)
+
+
+def finish_slope(total, extra, outs):
+    outs[0][...] = (total * extra[0][...].astype(F32)).astype(BF)
+
+
+def partial_body(by_rows, n, spot, local, *rest):
+    weights, (low, high) = rest[:-2], rest[-2:]
+    t = pl.program_id(0)
+    total = None
+    for z in range(4):
+        tile = local[:, z * n : (z + 1) * n]
+        if by_rows:
+            kept = jnp.concatenate([weights[y][z, c] for y in range(2) for c in range(2)], axis=1)
+            term = dot(tile, kept, NN)
+        else:
+            kept = jnp.concatenate([weights[0][z, c, y ^ spot[1]] for y in range(2) for c in range(2)], axis=0)
+            term = dot(tile, kept, NT)
+        total = term if total is None else total + term
+
+    @pl.when(t == 0)
+    def _():
+        low[...] = total.astype(low.dtype)
+
+    @pl.when(t == 1)
+    def _():
+        high[...] = total.astype(high.dtype)
+
+
+def partial(local, weights, spot, by_rows, mask, low, high):
+    n = local.shape[1] // 4
+    if by_rows:
+        weights = weights.reshape(4, 2, n, 1024)
+        specs = [
+            pl.BlockSpec((4, 2, n, 128), functools.partial(lambda y, t, p: (0, 0, 0, (y ^ p[1]) * 4 + (p[0] ^ mask)), y))
+            for y in range(2)
+        ]
+        ins = (weights, weights)
+    else:
+        weights = weights.reshape(4, 2, 2, 512, n)
+        specs = [pl.BlockSpec((4, 2, 2, 128, n), lambda t, p: (0, 0, 0, p[0] ^ mask, 0))]
+        ins = (weights,)
+    return call(
+        functools.partial(partial_body, by_rows, n),
+        (2,),
+        spot,
+        (local, *ins),
+        [pl.BlockSpec((HALF, 4 * n), lambda t, p: (t, 0))] + specs,
+        [shape_of(HALF, QUARTER, dtype=low), shape_of(HALF, QUARTER, dtype=high)],
+        [fixed((HALF, QUARTER))] * 2,
+        [],
+        2 * LEN * QUARTER * 4 * n,
+        2 * (LEN * 4 * n + QUARTER * 4 * n + LEN * QUARTER),
+    )
+
+
+def grad_body(by_rows, spot, *refs):
+    pieces, local, out = refs[:8], refs[8], refs[9]
+    for slot, mask in enumerate(SLOTS):
+        start = pl.multiple_of((spot[0] ^ mask) * 128, 128)
+
+        def term(piece, tile):
+            return dot(tile, piece, TN) if by_rows else dot(piece, tile, TN)
+
+        total = term(pieces[2 * slot][...], local[:HALF, :]) + term(pieces[2 * slot + 1][...], local[HALF:, :])
+        for block in range(4):
+            y, c = divmod(block, 2)
+            y = y ^ spot[1]
+            part = slice(block * 128, block * 128 + 128)
+            if by_rows:
+                out[0, c, :, pl.ds(pl.multiple_of(y * 512 + start, 128), 128)] = total[:, part].astype(BF)
+            else:
+                out[0, c, y, pl.ds(start, 128), :] = total[part, :].astype(BF)
+
+
+def grad(pieces, local, spot, by_rows):
+    n = local.shape[1] // 4
+    shape = (4, 2, n, 1024) if by_rows else (4, 2, 2, 512, n)
+    tail = (0,) * (len(shape) - 1)
+    out = call(
+        functools.partial(grad_body, by_rows),
+        (4,),
+        spot,
+        (*pieces, local),
+        [fixed(p.shape) for p in pieces] + [pl.BlockSpec((LEN, n), lambda z, *_: (0, z))],
+        shape_of(*shape, dtype=BF),
+        pl.BlockSpec((1,) + shape[1:], lambda z, *_: (z,) + tail),
+        [],
+        2 * LEN * WIDTH * 4 * n,
+        2 * (LEN * WIDTH + WIDTH * 4 * n + LEN * 4 * n),
+    )
+    return out.reshape(8, n, 1024) if by_rows else out.reshape(8, 1024, n)
+
+
+SCALE = HD ** (-0.5)
+LOG2E = 1.4426950408889634
+QUERY_BLOCK = 512
+
+
+def forward_body(spot, queries, whole, ids_row, ids_column, out, logsum):
+    scores = dot(whole[:, HD : 2 * HD], queries[:, :HD], NT)
+    scores = jnp.where(ids_column[...] == ids_row[...], scores, NEGATIVE)
+    peak = jnp.max(scores, axis=0, keepdims=True)
+    expo = jnp.exp2((scores - peak) * (SCALE * LOG2E))
+    total = jnp.sum(expo, axis=0, keepdims=True)
+    probs = (expo * (1.0 / total)).astype(BF)
+    mixed = dot(whole[:, 2 * HD :], probs, TN)
+    out[...] = mixed.T.astype(BF)
+    logsum[0] = peak * (SCALE * LOG2E) + jnp.log2(total)
+
+
+def head_specs():
+    return [
+        pl.BlockSpec((QUERY_BLOCK, 3 * HD), lambda h, q, p: (q, h)),
+        pl.BlockSpec((LEN, 3 * HD), lambda h, q, p: (0, h)),
+        pl.BlockSpec((1, QUERY_BLOCK), lambda h, q, p: (0, q)),
+        pl.BlockSpec((LEN, 1), lambda h, q, p: (0, 0)),
+    ]
+
+
+def attention(qkv, ids_row, ids_column, spot):
+    return call(
+        forward_body,
+        (4, LEN // QUERY_BLOCK),
+        spot,
+        (qkv, qkv, ids_row, ids_column),
+        head_specs(),
+        [shape_of(LEN, QUARTER, dtype=BF), shape_of(4, 1, LEN)],
+        [
+            pl.BlockSpec((QUERY_BLOCK, HD), lambda h, q, p: (q, h)),
+            pl.BlockSpec((1, 1, QUERY_BLOCK), lambda h, q, p: (h, 0, q)),
+        ],
+        [],
+        64 * LEN * LEN * HD,
+        LEN * 4 * HD * 8,
+    )
+
+
+def backward_body(spot, queries, whole, ids_row, ids_column, logsum, grad_out, out, grad_keys, grad_values):
+    q = pl.program_id(1)
+    block = queries.shape[0]
+    keys = whole[:, HD : 2 * HD]
+    values = whole[:, 2 * HD :]
+    scores = dot(keys, queries[:, :HD], NT) * (SCALE * LOG2E)
+    scores = jnp.where(ids_column[...] == ids_row[...], scores, NEGATIVE)
+    probs = jnp.exp2(scores - logsum[0])
+    grad_probs = dot(values, grad_out[...], NT)
+    inner = jnp.sum(probs * grad_probs, axis=0, keepdims=True)
+    grad_scores = (probs * (grad_probs - inner)).astype(BF)
+    back_query = dot(keys, grad_scores, TN)
+    out[pl.ds(q * block, block), :HD] = (back_query.T * SCALE).astype(BF)
+    back_key = dot(grad_scores, queries[:, :HD], NN)
+    back_value = dot(probs.astype(BF), grad_out[...], NN)
+
+    @pl.when(q == 0)
+    def _():
+        grad_keys[...] = back_key
+        grad_values[...] = back_value
+
+    @pl.when(q > 0)
+    def _():
+        grad_keys[...] += back_key
+        grad_values[...] += back_value
+
+    @pl.when(q == pl.num_programs(1) - 1)
+    def _():
+        out[:, HD : 2 * HD] = (grad_keys[...] * SCALE).astype(BF)
+        out[:, 2 * HD :] = grad_values[...].astype(BF)
+
+
+def attention_back(qkv, ids_row, ids_column, logsum, grad_heads, spot):
+    return call(
+        backward_body,
+        (4, LEN // QUERY_BLOCK),
+        spot,
+        (qkv, qkv, ids_row, ids_column, logsum, grad_heads),
+        head_specs()
+        + [
+            pl.BlockSpec((1, 1, QUERY_BLOCK), lambda h, q, p: (h, 0, q)),
+            pl.BlockSpec((QUERY_BLOCK, HD), lambda h, q, p: (q, h)),
+        ],
+        shape_of(LEN, 12 * HD, dtype=BF),
+        pl.BlockSpec((LEN, 3 * HD), lambda h, q, p: (0, h)),
+        [pltpu.VMEM((LEN, HD), F32), pltpu.VMEM((LEN, HD), F32)],
+        120 * LEN * LEN * HD,
+        LEN * 4 * HD * 16,
+    )
+
+
+def row_sum(value):
+    folded = value[:, :128] + value[:, 128:256] + value[:, 256:384] + value[:, 384:512]
+    return jnp.sum(folded.T, axis=0, keepdims=True)
+
+
+def rows_of(values):
+    rows = [row_sum(v) for v in values]
+    return jnp.concatenate(rows + [jnp.zeros_like(rows[0])] * (8 - len(rows)), axis=0)
+
+
+def columns_of(rows):
+    return rows.T
+
+
+def column_sums(values):
+    sums = [jnp.sum(v, axis=0, keepdims=True) for v in values]
+    return jnp.concatenate(sums + [jnp.zeros_like(sums[0])] * (8 - len(sums)), axis=0)
+
+
+def add_columns(ref, t, values):
+    sums = column_sums(values)
+
+    @pl.when(t == 0)
+    def _():
+        ref[...] = sums
+
+    @pl.when(t > 0)
+    def _():
+        ref[...] += sums
+
+
+def moments_of(stats):
+    total = (stats[0][...] + stats[1][...] + stats[2][...] + stats[3][...]) / WIDTH
+    mean = total[0:1]
+    return mean, lax.rsqrt(total[1:2] - mean * mean + EPS), total
+
+
+def summed(refs, t):
+    own, near, last = (pick(refs[2 * i], refs[2 * i + 1], t).astype(F32) for i in range(3))
+    return own + near + last
+
+
+HALVES = fixed((HALF, QUARTER))
+TILE = pl.BlockSpec((HALF, QUARTER), lambda t, p: (t, 0))
+STATS = pl.BlockSpec((8, HALF), lambda t, p: (0, t))
+VECTOR = fixed((1, QUARTER))
+SUMS = fixed((8, QUARTER))
+
+
+def elementwise(body, spot, ins, in_specs, outs, out_specs):
+    return call(body, (2,), spot, ins, in_specs, outs, out_specs, [], 20 * LEN * QUARTER, 16 * LEN * QUARTER)
+
+
+def norm_one_sums(spot, *refs):
+    parts, (stream, bias, resid, stats) = refs[:6], refs[6:]
+    attn = summed(parts, pl.program_id(0)) + bias[...]
+    total = stream[...].astype(F32) + attn
+    resid[...] = total
+    stats[...] = rows_of([total, total * total, attn * attn, jnp.square(stream[...].astype(F32))])
+
+
+def write_halves(t, low, high, value):
+    @pl.when(t == 0)
+    def _():
+        low[...] = value
+
+    @pl.when(t == 1)
+    def _():
+        high[...] = value
+
+
+def norm_one(spot, resid, s0, s1, s2, s3, gain, shift, low, high, moments):
+    mean, rstd, _ = moments_of((s0, s1, s2, s3))
+    rows = jnp.concatenate([mean, rstd] + [mean] * 6, axis=0)
+    moments[...] = rows
+    columns = columns_of(rows)
+    hidden = (resid[...] - columns[:, 0:1]) * columns[:, 1:2] * gain[...] + shift[...]
+    write_halves(pl.program_id(0), low, high, hidden.astype(BF))
+
+
+def norm_two_sums(spot, *refs):
+    parts = refs[:6]
+    bias, resid, moments, gain, shift, dy, gain_two, resid_two, stats = refs[6:]
+    ffn = summed(parts, pl.program_id(0)) + bias[...]
+    columns = columns_of(moments[...])
+    hidden = (resid[...] - columns[:, 0:1]) * columns[:, 1:2] * gain[...] + shift[...]
+    total = hidden + ffn
+    resid_two[...] = total
+    scaled = dy[...].astype(F32) * gain_two[...]
+    stats[...] = rows_of([total, total * total, scaled, scaled * total, ffn * ffn])
+
+
+def norm_two(spot, resid_two, s0, s1, s2, s3, dy, gain, shift, layer_out, grad_two, low, high, sums):
+    mean, rstd, total = moments_of((s0, s1, s2, s3))
+    mean_e = total[2:3]
+    along = rstd * (total[3:4] - mean * mean_e)
+    columns = columns_of(jnp.concatenate([mean, rstd, mean_e, along] + [mean] * 4, axis=0))
+    normed = (resid_two[...] - columns[:, 0:1]) * columns[:, 1:2]
+    upstream = dy[...].astype(F32)
+    layer_out[...] = (normed * gain[...] + shift[...]).astype(BF)
+    back = columns[:, 1:2] * (upstream * gain[...] - columns[:, 2:3] - normed * columns[:, 3:4])
+    grad_two[...] = back
+    rounded = back.astype(BF)
+    t = pl.program_id(0)
+    write_halves(t, low, high, rounded)
+    add_columns(sums, t, [upstream * normed, upstream, rounded.astype(F32)])
+
+
+def back_one_sums(spot, *refs):
+    parts = refs[:6]
+    grad_two, resid, moments, gain, grad_hidden, stats, sums = refs[6:]
+    t = pl.program_id(0)
+    upstream = summed(parts, t) + grad_two[...]
+    grad_hidden[...] = upstream
+    columns = columns_of(moments[...])
+    normed = (resid[...] - columns[:, 0:1]) * columns[:, 1:2]
+    scaled = upstream * gain[...]
+    stats[...] = rows_of([scaled, scaled * normed])
+    add_columns(sums, t, [upstream * normed, upstream])
+
+
+def back_one(spot, grad_hidden, s0, s1, s2, s3, resid, moments, gain, grad_one, low, high, sums):
+    total = (s0[...] + s1[...] + s2[...] + s3[...]) / WIDTH
+    means = columns_of(total)
+    columns = columns_of(moments[...])
+    normed = (resid[...] - columns[:, 0:1]) * columns[:, 1:2]
+    back = columns[:, 1:2] * (grad_hidden[...] * gain[...] - means[:, 0:1] - normed * means[:, 1:2])
+    grad_one[...] = back
+    rounded = back.astype(BF)
+    t = pl.program_id(0)
+    write_halves(t, low, high, rounded)
+    add_columns(sums, t, [rounded.astype(F32)])
+
+
+def finish_back(spot, *refs):
+    parts, (grad_one, out) = refs[:6], refs[6:]
+    out[...] = (summed(parts, pl.program_id(0)) + grad_one[...]).astype(BF)
+
+
+def pass_on(spot, first, second, third, fourth, low, high):
+    low[...] = (first[...] + second[...].astype(F32)).astype(BF)
+    high[...] = (third[...] + fourth[...].astype(F32)).astype(BF)
+
+
+def tie(value, *others):
+    return lax.optimization_barrier((value, *others))[0]
+
+
+def to_share(piece, yi):
+    own = lax.dynamic_slice_in_dim(piece, yi * 128, 128, 1)
+    other = swap(lax.dynamic_slice_in_dim(piece, (1 - yi) * 128, 128, 1), Y_BIT)
+    return own, other
+
+
+def to_share_rest(own, other, yi):
+    both = jnp.where(yi == 0, jnp.stack([own, other]), jnp.stack([other, own])).reshape(4, LEN, 128)
+    return lax.all_to_all(both, "z", 0, 2, tiled=True)[0]
+
+
+def from_share(share, yi):
+    parts = lax.all_to_all(share[None], "z", 2, 0, tiled=True).reshape(2, 2 * LEN, 128)
+    own = lax.dynamic_index_in_dim(parts, yi, 0, False)
+    other = swap(lax.dynamic_index_in_dim(parts, 1 - yi, 0, False), Y_BIT)
+    return own, other
+
+
+def side_by_side(own, other, yi, axis):
+    return jnp.where(yi == 0, jnp.concatenate([own, other], axis), jnp.concatenate([other, own], axis))
+
+
+def square_gather(low, high):
+    x_low = swap(low, X_BIT)
+    y_high = swap(high, Y_BIT)
+    x_high = swap(high, X_BIT)
+    y_low = swap(low, Y_BIT)
+    xy_low = swap(x_low, Y_BIT)
+    xy_high = swap(y_high, X_BIT)
+    return (low, high, x_low, x_high, y_low, y_high, xy_low, xy_high)
+
+
+def square_scatter(local, weights, spot, by_rows, before_own=()):
+    term = functools.partial(partial, local, weights, spot, by_rows)
+    far_low, far_high = term(3, BF, BF)
+    far_low = swap(far_low, X_BIT)
+    far_high = swap(far_high, Y_BIT)
+    near_low, x_high = term(2, BF, F32)
+    near_low = swap(near_low, X_BIT)
+    y_low, near_high = term(1, F32, BF)
+    near_high = swap(near_high, Y_BIT)
+    half = fixed((HALF, QUARTER))
+    last_low, last_high = call(
+        pass_on, (1,), spot, (y_low, far_low, x_high, far_high), [half] * 4, [shape_of(HALF, QUARTER, dtype=BF)] * 2,
+        [half] * 2, [], LEN * QUARTER, 8 * LEN * QUARTER,
+    )
+    last_low = swap(last_low, Y_BIT)
+    last_high = swap(last_high, X_BIT)
+    if before_own:
+        local = tie(local, *before_own)
+    own_low, own_high = partial(local, weights, spot, by_rows, 0, F32, F32)
+    return (own_low, own_high, near_low, near_high, last_low, last_high)
+
+
+def square_stats(stats):
+    return (stats, swap(stats, X_BIT), swap(stats, Y_BIT), swap(stats, XY_BIT))
+
+
+def halve_columns(pieces, yi):
+    n = pieces[0].shape[1] // 2
+    own = jnp.concatenate([lax.dynamic_slice_in_dim(p, yi * n, n, 1) for p in pieces], axis=1)
+    other = jnp.concatenate([lax.dynamic_slice_in_dim(p, (1 - yi) * n, n, 1) for p in pieces], axis=1)
+    return jnp.concatenate([own, swap(other, Y_BIT)], axis=0)
+
+
+def halve_rows(piece, yi):
+    n = piece.shape[0] // 2
+    own = lax.dynamic_slice_in_dim(piece, yi * n, n, 0)
+    other = lax.dynamic_slice_in_dim(piece, (1 - yi) * n, n, 0)
+    return jnp.concatenate([own, swap(other, Y_BIT)], axis=1)
+
+
+def gather_zc(piece):
+    return lax.all_gather(piece, ("z", "c"), axis=0)
+
+
+def scatter_zc(full):
+    return lax.psum_scatter(full, ("z", "c"), scatter_dimension=0)
+
+
+def restore_columns(piece, count, yi):
+    other = swap(piece[512:], Y_BIT)
+    n = piece.shape[1] // count
+    return [
+        side_by_side(piece[:512, i * n : (i + 1) * n], other[:, i * n : (i + 1) * n], yi, 1).astype(F32)
+        for i in range(count)
+    ]
+
+
+def restore_rows(piece, yi):
+    return side_by_side(piece[:, :512], swap(piece[:, 512:], Y_BIT), yi, 0).astype(F32)
+
+
+def square_device(
+    tokens, lengths, w_query, b_query, w_key, w_value, b_value, w_proj, b_proj, norm_gain, norm_shift,
+    w_up, b_up, w_down, b_down, final_gain, final_shift, cotangent,
+):
+    yi = lax.axis_index("y")
+    zi = lax.axis_index("z")
+    spot = jnp.stack([lax.axis_index("x") * 2 + yi, yi]).astype(jnp.int32)
+
+    token_own, token_other = to_share(tokens, yi)
+    half_qkv = halve_columns([w_query, w_key, w_value], yi)
+    half_proj = halve_rows(tie(w_proj, half_qkv), yi)
+    half_up = halve_columns([tie(w_up, half_proj)], yi)
+    half_down = halve_rows(tie(w_down, half_up), yi)
+    full_qkv = gather_zc(half_qkv)
+    token_share = to_share_rest(token_own, token_other, yi)
+    full_proj = gather_zc(half_proj)
+    full_up = gather_zc(half_up)
+    full_down = gather_zc(half_down)
+    dy_own, dy_other = to_share(tie(cotangent, half_down), yi)
+    dy = to_share_rest(dy_own, dy_other, yi)
+
+    both = side_by_side(lengths, swap(lengths, Y_BIT), yi, 0)
+    ids = segment_ids(lax.dynamic_slice_in_dim(both, zi, 1, 0))[0]
+    valid = (ids != lengths.shape[1] - 1).astype(F32)
+    ids_row, ids_column = ids[None], ids[:, None]
+
+    vectors = jnp.concatenate(
+        [v.reshape(2, -1) for v in (b_query, b_value, b_proj, norm_gain, norm_shift, b_down, final_gain, final_shift, b_up)],
+        axis=1,
+    )
+    vectors = lax.dynamic_slice_in_dim(vectors, yi, 1, 0)
+    vectors = lax.all_to_all(jnp.broadcast_to(vectors, (4, vectors.shape[1])), "z", 0, 0, tiled=True)
+    small = [vectors[:, i * 128 : (i + 1) * 128] for i in range(8)]
+    q_bias, v_bias = small[:2]
+    p_bias, n_gain, n_shift, d_bias, f_gain, f_shift = (v.reshape(1, QUARTER) for v in small[2:])
+    u_bias = vectors[:, 1024:].reshape(1, -1)
+    qkv_bias = jnp.stack([q_bias, jnp.zeros_like(q_bias), v_bias], axis=1).reshape(1, -1)
+
+    gathered = square_gather(token_share[:HALF], token_share[HALF:])
+    (qkv,) = wide(gathered, full_qkv, spot, False, finish_bias, (qkv_bias,), 1)
+    heads_out, logsum = attention(qkv, ids_row, ids_column, spot)
+    full = shape_of(LEN, QUARTER)
+    low_half = shape_of(HALF, QUARTER, dtype=BF)
+    stats_shape = shape_of(8, LEN)
+    sums_shape = shape_of(8, QUARTER)
+
+    parts = square_scatter(heads_out, full_proj, spot, True)
+    resid, stats_one = elementwise(
+        norm_one_sums, spot, (*parts, token_share, p_bias), [HALVES] * 6 + [TILE, VECTOR], [full, stats_shape], [TILE, STATS]
+    )
+    hidden_low, hidden_high, moments = elementwise(
+        norm_one, spot, (resid, *square_stats(stats_one), n_gain, n_shift), [TILE] + [STATS] * 4 + [VECTOR] * 2,
+        [low_half, low_half, stats_shape], [HALVES, HALVES, STATS],
+    )
+    hidden_wide = square_gather(hidden_low, hidden_high)
+    act, slope = wide(hidden_wide, full_up, spot, False, finish_gelu, (u_bias,), 2)
+    parts = square_scatter(act, full_down, spot, True)
+    resid_two, stats_two = elementwise(
+        norm_two_sums, spot, (*parts, d_bias, resid, moments, n_gain, n_shift, dy, f_gain),
+        [HALVES] * 6 + [VECTOR, TILE, STATS, VECTOR, VECTOR, TILE, VECTOR], [full, stats_shape], [TILE, STATS],
+    )
+    layer_share, grad_two, ffn_low, ffn_high, sums_two = elementwise(
+        norm_two, spot, (resid_two, *square_stats(stats_two), dy, f_gain, f_shift),
+        [TILE] + [STATS] * 4 + [TILE, VECTOR, VECTOR],
+        [shape_of(LEN, QUARTER, dtype=BF), full, low_half, low_half, sums_shape], [TILE, TILE, HALVES, HALVES, SUMS],
+    )
+    ffn_wide = square_gather(ffn_low, ffn_high)
+    layer_own, layer_other = from_share(layer_share, yi)
+    layer_out = side_by_side(layer_own, layer_other, yi, 1)
+
+    (grad_pre,) = wide(ffn_wide, full_down, spot, True, finish_slope, (slope,), 1)
+    grad_down = grad(ffn_wide, act, spot, True)
+    grad_up = grad(hidden_wide, grad_pre, spot, False)
+    parts = square_scatter(grad_pre, full_up, spot, False, (grad_down,))
+    sum_down = scatter_zc(grad_down)
+    grad_ubias = jnp.sum(grad_pre.astype(F32), axis=0)
+    grad_hidden, stats_back, sums_back = elementwise(
+        back_one_sums, spot, (*parts, grad_two, resid, moments, n_gain),
+        [HALVES] * 6 + [TILE, TILE, STATS, VECTOR], [full, stats_shape, sums_shape], [TILE, STATS, SUMS],
+    )
+    grad_one, attn_low, attn_high, sums_attn = elementwise(
+        back_one, spot, (grad_hidden, *square_stats(stats_back), resid, moments, n_gain),
+        [TILE] + [STATS] * 4 + [TILE, STATS, VECTOR],
+        [full, low_half, low_half, sums_shape], [TILE, HALVES, HALVES, SUMS],
+    )
+    attn_wide = square_gather(attn_low, attn_high)
+    sum_up = scatter_zc(grad_up)
+    (grad_heads,) = wide(attn_wide, full_proj, spot, True, finish_plain, (), 1)
+    grad_proj = grad(attn_wide, heads_out, spot, True)
+    grad_qkv = attention_back(qkv, ids_row, ids_column, logsum, tie(grad_heads, grad_up), spot)
+    sum_proj = scatter_zc(grad_proj)
+    grad_wqkv = grad(gathered, grad_qkv, spot, False)
+    parts = square_scatter(grad_qkv, full_qkv, spot, False, (grad_wqkv,))
+    sum_qkv = scatter_zc(grad_wqkv)
+    (back,) = elementwise(
+        finish_back, spot, (*parts, grad_one), [HALVES] * 6 + [TILE], [shape_of(LEN, QUARTER, dtype=BF)], [TILE]
+    )
+    back_own, back_other = from_share(back, yi)
+    grad_tokens = side_by_side(back_own, back_other, yi, 1).astype(F32)
+    sums_qkv = jnp.sum(grad_qkv.astype(F32), axis=0).reshape(4, 3, HD)
+
+    grad_down = restore_rows(sum_down, yi)
+    (grad_up,) = restore_columns(sum_up, 1, yi)
+    grad_proj = restore_rows(sum_proj, yi)
+    grad_query, grad_key, grad_value = restore_columns(sum_qkv, 3, yi)
+
+    sums = jnp.concatenate(
+        [
+            v.reshape(4, -1)
+            for v in (
+                sums_qkv[:, 0], sums_qkv[:, 2], sums_attn[0], sums_back[0], sums_back[1], sums_two[2], sums_two[0], sums_two[1],
+                grad_ubias,
+            )
+        ],
+        axis=1,
+    )
+    sums = jnp.sum(lax.all_to_all(sums, "z", 0, 0, tiled=True), axis=0)
+    sums = sums + swap(sums, C_BIT)
+    other = swap(sums, Y_BIT)
+    sums = jnp.where(yi == 0, jnp.stack([sums, other]), jnp.stack([other, sums]))
+    vecs = [sums[:, i * 128 : (i + 1) * 128].reshape(-1) for i in range(8)] + [sums[:, 1024:].reshape(-1)]
+
+    totals = jnp.stack(
+        [
+            jnp.sum(valid * stats_one[3]),
+            jnp.sum(valid * stats_one[2]),
+            jnp.sum(valid * stats_two[4]),
+            jnp.sum(valid) * QUARTER,
+        ]
+    )
+    for mask in (X_BIT, Z_LOW, Z_HIGH, C_BIT, Y_BIT):
+        totals = totals + swap(totals, mask)
+    norms = jnp.sqrt(totals[:3] / totals[3])
+    return (
+        layer_out, grad_tokens, grad_query, vecs[0], grad_key, grad_value, vecs[1], grad_proj, vecs[2], vecs[3], vecs[4],
+        grad_up, vecs[8], grad_down, vecs[5], vecs[6], vecs[7], norms,
+    )
+
+
 def gather_features(piece):
     return lax.all_gather(piece, "col", axis=1, tiled=True)
 
 
 def scatter_features(partial_sum):
-    return lax.psum_scatter(partial_sum, "col", scatter_dimension=1, tiled=True)
+    low = partial_sum.astype(jnp.bfloat16)
+    return lax.psum_scatter(low, "col", scatter_dimension=1, tiled=True).astype(F32)
 
 
 def row_totals(first, second):
@@ -298,50 +991,23 @@
     )
 
 
+def placements(row, col):
+    grid, turned, share = P(row, col), P(col, row), P(col)
+    args = (
+        grid, P(row, None), grid, share, grid, grid, share, turned, share, share, share, grid, share, turned, share, share, share, grid,
+    )
+    outs = (
+        grid, grid, grid, share, grid, grid, share, turned, share, share, share, grid, share, turned, share, share, share, P(),
+    )
+    return (args, outs)
+
+
 def solution(mesh):
-    placed = (
-        P("row", "col"),
-        P("row", None),
-        P("row", "col"),
-        P("col"),
-        P("row", "col"),
-        P("row", "col"),
-        P("col"),
-        P("col", "row"),
-        P("col"),
-        P("col"),
-        P("col"),
-        P("row", "col"),
-        P("col"),
-        P("col", "row"),
-        P("col"),
-        P("col"),
-        P("col"),
-        P("row", "col"),
-    )
-    return jax.shard_map(
-        per_device,
-        mesh=mesh,
-        in_specs=placed,
-        out_specs=(
-            P("row", "col"),
-            P("row", "col"),
-            P("row", "col"),
-            P("col"),
-            P("row", "col"),
-            P("row", "col"),
-            P("col"),
-            P("col", "row"),
-            P("col"),
-            P("col"),
-            P("col"),
-            P("row", "col"),
-            P("col"),
-            P("col", "row"),
-            P("col"),
-            P("col"),
-            P("col"),
-            P(),
-        ),
-        check_vma=False,
-    )
+    if mesh.shape["row"] == 4 and mesh.shape["col"] == 8:
+        mesh = Mesh(mesh.devices.reshape(2, 2, 4, 2), AXES)
+        args, outs = placements(("y", "c"), ("z", "x"))
+        body = square_device
+    else:
+        args, outs = placements("row", "col")
+        body = per_device
+    return jax.shard_map(body, mesh=mesh, in_specs=args, out_specs=outs, check_vma=False)

time: 2210 us -> 945 us (0.43)
  waiting for transfers between devices: 1680 us -> 397 us
  Pallas kernels: 0 us -> 298 us
  matrix products: 224 us -> 0 us
  blocking collectives: 190 us -> 0 us
  starting transfers between devices: 1.21 us -> 122 us
    reduce_scatter x10 -> x4, waiting for transfers between devices: 1150 us -> 79.9 us  [scatter_zc(): return lax.psum_scatter(full, ('z', 'c'), scatter_dimension=0)]
    all_gather x10 -> x4, waiting for transfers between devices: 524 us -> 24.5 us  [gather_zc(): return lax.all_gather(piece, ('z', 'c'), axis=0)]
    pallas_call x0 -> x37, Pallas kernels: none -> 298 us  [call(): pl.pallas_call(body, grid_spec=pltpu.PrefetchScalarGridSpec(num_scalar_pr...]
    ppermute x0 -> x77, waiting for transfers between devices: none -> 224 us  [swap(): return lax.ppermute(piece, AXES, [(i, i ^ mask) for i in range(32)])]
    dot_general x46 -> x0, matrix products: 224 us -> none  [the longest x1 20.8 us: per_device(): jnp.einsum('td,fd->tf', ffn_wide, full_down, preferred_element_type=jnp.f...]
    psum x6 -> x0, blocking collectives: 190 us -> none  [the longest x4 139 us: row_totals(): return lax.psum((first, second), 'col')]
    ppermute x0 -> x77, starting transfers between devices: none -> 95.2 us  [swap(): return lax.ppermute(piece, AXES, [(i, i ^ mask) for i in range(32)])]
    all_to_all x0 -> x6, waiting for transfers between devices: none -> 67.1 us  [the longest x2 39.4 us: to_share_rest(): return lax.all_to_all(both, 'z', 0, 2, tiled=True)[0]]
  transfers between devices with their start and end apart: 20 -> 91, of which waited for: 13 -> 45; matrix products, arithmetic and copies ran while one was open for 10% -> 9% of each run, Pallas kernels for 0% -> 26%
where the time goes in v2:
time: 945 us; the launch traced here: 933 us
  waiting for transfers between devices  397 us (42%)
  Pallas kernels  298 us (32%)
  starting transfers between devices  122 us (13%)
  local copies, waits for them, and re-layouts  56.7 us (6%)
  other arithmetic  41.8 us (4%)
  between operations  16.3 us (2%)
    pallas_call x37, Pallas kernels, call(): pl.pallas_call(body, grid_spec=pltpu.PrefetchScalarGridSpec(num_scalar_pr...  298 us
    ppermute x77, waiting for transfers between devices, swap(): return lax.ppermute(piece, AXES, [(i, i ^ mask) for i in range(32)])  224 us
    ppermute x77, starting transfers between devices, swap(): return lax.ppermute(piece, AXES, [(i, i ^ mask) for i in range(32)])  95.2 us
    reduce_scatter x4, waiting for transfers between devices, scatter_zc(): return lax.psum_scatter(full, ('z', 'c'), scatter_dimension=0)  79.9 us
    all_to_all x2, waiting for transfers between devices, to_share_rest(): return lax.all_to_all(both, 'z', 0, 2, tiled=True)[0]  39.4 us
    unnamed x178, local copies, waits for them, and re-layouts  28.1 us
    all_to_all x2, waiting for transfers between devices, from_share(): lax.all_to_all(share[None], 'z', 2, 0, tiled=True).reshape(2, 2 * LEN, 128)  27.7 us
    all_gather x4, waiting for transfers between devices, gather_zc(): return lax.all_gather(piece, ('z', 'c'), axis=0)  24.5 us
  transfers between devices with their start and end apart: 91, of which 45 were waited for; matrix products, arithmetic and copies ran while one was open for 9% of the time, Pallas kernels for 26%

profile of v2, /device:TPU:0, one launch (start us, length us, event | category | flops | bytes accessed | tf_op | source)
XLA Modules:
  0.0 933.0 jit_solution(3609863636495817943)
XLA Ops:
  12.5 9.1 collective-permute-done.7
  30.5 10.2 %collective-permute-done.25 = bf16[512,512]{1,0:T(8,128)(2,1)S(1)} collective-permute-done((bf16[512,512]{1,0:T(8,128)(2,1)S(1)}, bf16[512,512]{1,0:T(8,128)(2,1)S(1)}, u32[]{:S(2)}, u32[]{:S(2)}) %collective-permute-start.25) | collective-permute-done | bytes 524320 | tf_op jit(solution)/shard_map/ppermute | solution.py:37
  43.4 9.7 %collective-permute-done.26 = bf16[512,512]{1,0:T(8,128)(2,1)S(1)} collective-permute-done((bf16[512,512]{1,0:T(8,128)(2,1)S(1)}, bf16[512,512]{1,0:T(8,128)(2,1)S(1)}, u32[]{:S(2)}, u32[]{:S(2)}) %collective-permute-start.26) | collective-permute-done | bytes 524320 | tf_op jit(solution)/shard_map/ppermute | solution.py:37
  56.6 8.2 collective-permute-done
  70.3 39.4 %all-to-all-done = bf16[4,1024,128]{2,1,0:T(8,128)(2,1)S(1)} async-done(((bf16[4,1024,128]{2,1,0:T(8,128)(2,1)}), bf16[4,1024,128]{2,1,0:T(8,128)(2,1)S(1)}, u32[]{:S(2)}, u32[]{:S(2)}) %all-to-all-start) | async-done | bytes 1048608 | tf_op jit(solution)/shard_map/all_to_all | solution.py:490
  119.6 10.0 %collective-permute-done.1.refs_2_ = bf16[512,512]{1,0:T(8,128)(2,1)S(1)} collective-permute-done((bf16[512,512]{1,0:T(8,128)(2,1)S(1)}, bf16[512,512]{1,0:T(8,128)(2,1)S(1)}, u32[]{:S(2)}, u32[]{:S(2)}) %collective-permute-start.1) | collective-permute-done | bytes 524320 | tf_op jit(solution)/shard_map/ppermute | solution.py:37
  135.0 7.4 collective-permute-done.3.refs_4_
  142.4 9.3 %collective-permute-done.5.refs_6_ = bf16[512,512]{1,0:T(8,128)(2,1)} collective-permute-done((bf16[512,512]{1,0:T(8,128)(2,1)S(1)}, bf16[512,512]{1,0:T(8,128)(2,1)}, u32[]{:S(2)}, u32[]{:S(2)}) %collective-permute-start.5) | collective-permute-done | bytes 524320 | tf_op jit(solution)/shard_map/ppermute | solution.py:37
  151.8 15.8 %shard_map.313.queries.whole = bf16[1024,1536]{1,0:T(8,128)(2,1)} custom-call(s32[2]{0:T(128)} %pad_add_fusion.spot, bf16[512,512]{1,0:T(8,128)(2,1)} %bitcast.210, bf16[512,512]{1,0:T(8,128)(2,1)} %bitcast.206, bf16[512,512]{1,0:T(8,128)(2,1)} %copy-done.56, bf16[512,512]{1,0:T(8,128)(2,1)} %collective-permute-done.2.refs_3_, ...), custom_call_target="tpu_custom_call" | custom-call | flops 6442450944 | bytes 13631488 | tf_op jit(solution)/shard_map/pallas_call | solution.py:45
  167.6 12.9 %shard_map.314 = (bf16[1024,512]{1,0:T(8,128)(2,1)}, f32[4,1,1024]{2,1,0:T(1,128)}) custom-call(s32[2]{0:T(128)} %pad_add_fusion.spot, bf16[1024,1536]{1,0:T(8,128)(2,1)} %shard_map.313.queries.whole, bf16[1024,1536]{1,0:T(8,128)(2,1)} %shard_map.313.queries.whole, s32[1,1024]{1,0:T(1,128)} %bitcast.220, s32[1024,1]{1,0:T(8,128)} %copy.69.ids_column), custom_call_target="tpu_custom_call" | custom-call | flops 8589934592 | bytes 4194304 | tf_op jit(solution)/shard_map/pallas_call | solution.py:45
  186.9 4.5 shard_map.317
  192.0 4.6 shard_map.316
  209.7 4.7 shard_map.315
  214.5 5.7 collective-permute-done.14.refs_4_
  221.1 5.0 shard_map.320
  243.2 9.4 %collective-permute-done.19.refs_2_ = bf16[512,512]{1,0:T(8,128)(2,1)S(1)} collective-permute-done((bf16[512,512]{1,0:T(8,128)(2,1)}, bf16[512,512]{1,0:T(8,128)(2,1)S(1)}, u32[]{:S(2)}, u32[]{:S(2)}) %collective-permute-start.19) | collective-permute-done | bytes 524320 | tf_op jit(solution)/shard_map/ppermute | solution.py:37
  255.6 9.1 collective-permute-done.33
  265.9 4.4 all-to-all-start.2
  270.5 5.5 collective-permute-done.21.refs_4_
  276.1 5.7 collective-permute-done.23.refs_6_
  281.7 20.1 %shard_map.322 = (bf16[1024,2048]{1,0:T(8,128)(2,1)}, bf16[1024,2048]{1,0:T(8,128)(2,1)}) custom-call(s32[2]{0:T(128)} %pad_add_fusion.spot, bf16[512,512]{1,0:T(8,128)(2,1)} %get-tuple-element.102.refs_0_, bf16[512,512]{1,0:T(8,128)(2,1)} %get-tuple-element.103.refs_1_, bf16[512,512]{1,0:T(8,128)(2,1)} %copy-done.59, ...), custom_call_target="tpu_custom_call" | custom-call | flops 8589934592 | bytes 16777216 | tf_op jit(solution)/shard_map/pallas_call | solution.py:45
  301.8 24.5 %all-gather.15.cloned.1.call-done = bf16[4096,1024]{1,0:T(8,128)(2,1)} async-done(((bf16[512,1024]{1,0:T(8,128)(2,1)}), bf16[4096,1024]{1,0:T(8,128)(2,1)}) %all-gather.15.cloned.1.call-update) | async-done | bytes 8388624 | tf_op jit(solution)/shard_map/all_gather | solution.py:555
  326.3 6.5 shard_map.326
  335.7 6.6 shard_map.325
  342.9 6.7 shard_map.324
  359.6 6.8 shard_map.323
  375.0 6.2 shard_map.328
  388.1 6.0 shard_map.329
  398.1 11.0 %collective-permute-done.38.refs_2_ = bf16[512,512]{1,0:T(8,128)(2,1)S(1)} collective-permute-done((bf16[512,512]{1,0:T(8,128)(2,1)}, bf16[512,512]{1,0:T(8,128)(2,1)S(1)}, u32[]{:S(2)}, u32[]{:S(2)}) %collective-permute-start.38) | collective-permute-done | bytes 524320 | tf_op jit(solution)/shard_map/ppermute | solution.py:37
  412.1 9.8 %collective-permute-done.40.refs_4_ = bf16[512,512]{1,0:T(8,128)(2,1)S(1)} collective-permute-done((bf16[512,512]{1,0:T(8,128)(2,1)}, bf16[512,512]{1,0:T(8,128)(2,1)S(1)}, u32[]{:S(2)}, u32[]{:S(2)}) %collective-permute-start.40) | collective-permute-done | bytes 524320 | tf_op jit(solution)/shard_map/ppermute | solution.py:37
  421.8 6.7 collective-permute-done.42.refs_6_
  429.5 18.9 %shard_map.330.local.refs_8_ = bf16[1024,2048]{1,0:T(8,128)(2,1)} custom-call(s32[2]{0:T(128)} %pad_add_fusion.spot, bf16[512,512]{1,0:T(8,128)(2,1)} %get-tuple-element.123.refs_0_, bf16[512,512]{1,0:T(8,128)(2,1)} %get-tuple-element.124.refs_1_, bf16[512,512]{1,0:T(8,128)(2,1)} %copy-done.61, bf16[512,512]{1,0:T(8,128)(2,1)} %copy-done.64, ...), custom_call_target="tpu_custom_call" | custom-call | flops 8589934592 | bytes 16777216 | tf_op jit(solution)/shard_map/pallas_call | solution.py:45
  448.5 7.0 shard_map.335
  457.5 6.8 shard_map.334
  464.6 6.7 shard_map.333
  479.7 15.9 %shard_map.331 = bf16[4,2,512,1024]{3,2,1,0:T(8,128)(2,1)} custom-call(s32[2]{0:T(128)} %pad_add_fusion.spot, bf16[512,512]{1,0:T(8,128)(2,1)} %get-tuple-element.123.refs_0_, bf16[512,512]{1,0:T(8,128)(2,1)} %get-tuple-element.124.refs_1_, bf16[512,512]{1,0:T(8,128)(2,1)} %copy-done.61, bf16[512,512]{1,0:T(8,128)(2,1)} %copy-done.64, ...), custom_call_target="tpu_custom_call" | custom-call | flops 8589934592 | bytes 16777216 | tf_op jit(solution)/shard_map/pallas_call | solution.py:45
  495.6 6.9 shard_map.332
  503.8 6.6 shard_map.337
  518.2 5.7 shard_map.338
  527.9 11.0 %collective-permute-done.53.refs_2_ = bf16[512,512]{1,0:T(8,128)(2,1)S(1)} collective-permute-done((bf16[512,512]{1,0:T(8,128)(2,1)}, bf16[512,512]{1,0:T(8,128)(2,1)S(1)}, u32[]{:S(2)}, u32[]{:S(2)}) %collective-permute-start.53) | collective-permute-done | bytes 524320 | tf_op jit(solution)/shard_map/ppermute | solution.py:37
  541.0 6.4 collective-permute-done.55.refs_4_
  547.4 5.6 collective-permute-done.57.refs_6_
  554.6 7.3 shard_map.349
  562.0 14.2 %shard_map.340 = bf16[4,2,2,512,512]{4,3,2,1,0:T(8,128)(2,1)} custom-call(s32[2]{0:T(128)} %pad_add_fusion.spot, bf16[512,512]{1,0:T(8,128)(2,1)} %get-tuple-element.102.refs_0_, bf16[512,512]{1,0:T(8,128)(2,1)} %get-tuple-element.103.refs_1_, bf16[512,512]{1,0:T(8,128)(2,1)} %copy-done.59, bf16[512,512]{1,0:T(8,128)(2,1)} %collective-permute-done.20.refs_3_, ...), custom_call_target="tpu_custom_call" | custom-call | flops 8589934592 | bytes 16777216 | tf_op jit(solution)/shard_map/pallas_call | solution.py:45
  576.1 11.2 %shard_map.339.grad_out = bf16[1024,512]{1,0:T(8,128)(2,1)} custom-call(s32[2]{0:T(128)} %pad_add_fusion.spot, bf16[512,512]{1,0:T(8,128)(2,1)} %get-tuple-element.140.refs_0_, bf16[512,512]{1,0:T(8,128)(2,1)} %get-tuple-element.141.refs_1_, bf16[512,512]{1,0:T(8,128)(2,1)} %copy-done.67, bf16[512,512]{1,0:T(8,128)(2,1)} %copy-done.70, ...), custom_call_target="tpu_custom_call" | custom-call | flops 2147483648 | bytes 7340032 | tf_op jit(solution)/shard_map/pallas_call | solution.py:45
  587.4 18.3 %shard_map.341.refs_8_.local = bf16[1024,1536]{1,0:T(8,128)(2,1)} custom-call(s32[2]{0:T(128)} %pad_add_fusion.spot, bf16[1024,1536]{1,0:T(8,128)(2,1)} %shard_map.313.queries.whole, bf16[1024,1536]{1,0:T(8,128)(2,1)} %shard_map.313.queries.whole, s32[1,1024]{1,0:T(1,128)} %bitcast.221, s32[1024,1]{1,0:T(8,128)} %copy.69.ids_column, ...), custom_call_target="tpu_custom_call" | custom-call | flops 16106127360 | bytes 8388608 | tf_op jit(solution)/shard_map/pallas_call | solution.py:45
  605.6 13.8 %shard_map.342 = bf16[4,2,2,512,384]{4,3,2,1,0:T(8,128)(2,1)} custom-call(s32[2]{0:T(128)} %pad_add_fusion.spot, bf16[512,512]{1,0:T(8,128)(2,1)} %bitcast.211, bf16[512,512]{1,0:T(8,128)(2,1)} %bitcast.207, bf16[512,512]{1,0:T(8,128)(2,1)} %copy-done.56, bf16[512,512]{1,0:T(8,128)(2,1)} %collective-permute-done.2.refs_3_, ...), custom_call_target="tpu_custom_call" | custom-call | flops 6442450944 | bytes 13631488 | tf_op jit(solution)/shard_map/pallas_call | solution.py:45
  624.1 6.8 reduce.4
  646.8 27.7 %all-to-all-done.3 = bf16[4,2,65536]{2,1,0:T(2,128)(2,1)S(1)} async-done(((bf16[4,2,65536]{2,1,0:T(2,128)(2,1)}), bf16[4,2,65536]{2,1,0:T(2,128)(2,1)S(1)}, u32[]{:S(2)}, u32[]{:S(2)}) %all-to-all-start.3) | async-done | bytes 1048608 | tf_op jit(solution)/shard_map/all_to_all | solution.py:494
  684.2 6.2 shard_map.346
  692.1 6.4 shard_map.345
  700.3 6.5 shard_map.344
  714.2 5.7 all-to-all-start.5
  719.9 6.6 shard_map.343
  727.8 4.6 shard_map.348
  732.4 4.7 copy.75
  737.2 6.8 reduce.5
  746.0 5.5 all-to-all-start.4
  757.4 24.5 %collective-permute-done.73 = f32[4]{0:T(128)S(1)} collective-permute-done((f32[4]{0:T(128)S(1)}, f32[4]{0:T(128)S(1)}, u32[]{:S(2)}, u32[]{:S(2)}) %collective-permute-start.73) | collective-permute-done | bytes 48 | tf_op jit(solution)/shard_map/ppermute | solution.py:37
  783.9 4.6 collective-permute-start.74
  809.8 8.3 collective-permute-done.65
  821.9 6.2 collective-permute-done.66
  831.3 79.8 %reduce-scatter.9.cloned.1.call-done = bf16[1,1024,512]{2,1,0:T(8,128)(2,1)} async-done(((bf16[8,1024,512]{2,1,0:T(8,128)(2,1)}), bf16[1,1024,512]{2,1,0:T(8,128)(2,1)}) %reduce-scatter.9.cloned.1.call-update) | async-done | bytes 1048592 | tf_op jit(solution)/shard_map/reduce_scatter | solution.py:559
  918.1 5.8 collective-permute-done.70
  (425 shorter events, 236.1 us)
Async XLA Ops:
  7.2 144.6 %all-gather.9.cloned.1.call-start = ((), (), s32[]{:S(2)}) async-start(), calls=%async_computation.14 | async-start | bytes 7077888 | tf_op jit(solution)/shard_map/all_gather | solution.py:555
  22.6 157.8 %all-gather.11.cloned.1.call-start = ((), (), s32[]{:S(2)}) async-start(), calls=%async_computation.15 | async-start | bytes 2359296 | tf_op jit(solution)/shard_map/all_gather | solution.py:555
  28.5 253.2 %all-gather.13.cloned.1.call-start = ((), (), s32[]{:S(2)}) async-start(), calls=%async_computation.16 | async-start | bytes 9437184 | tf_op jit(solution)/shard_map/all_gather | solution.py:555
  41.8 284.5 %all-gather.15.cloned.1.call-start = ((), (), s32[]{:S(2)}) async-start(), calls=%async_computation.17 | async-start | bytes 9437184 | tf_op jit(solution)/shard_map/all_gather | solution.py:555
  55.6 62.7 %collective-permute-start.8 = (s32[2,4]{1,0:T(2,128)S(1)}, s32[2,4]{1,0:T(2,128)S(1)}, u32[]{:S(2)}, u32[]{:S(2)}) collective-permute-start(s32[2,4]{1,0:T(2,128)S(1)} %copy-done.55), channel_id=1, source_target_pairs={{0,16},{1,17},{2,18},{3,19},{4,20},{5,21},{6,22},{7,23},{8,24},{9,... | collective-permute-start | bytes 104 | tf_op jit(solution)/shard_map/ppermute | solution.py:37
  66.0 43.7 %all-to-all-start = ((bf16[4,1024,128]{2,1,0:T(8,128)(2,1)}), bf16[4,1024,128]{2,1,0:T(8,128)(2,1)S(1)}, u32[]{:S(2)}, u32[]{:S(2)}) async-start(bf16[4,1024,128]{2,1,0:T(8,128)(2,1)} %bitcast.4), calls=%async_computation | async-start | bytes 2097152 | tf_op jit(solution)/shard_map/all_to_all | solution.py:490
  110.3 23.4 %all-to-all-start.1 = ((f32[4,1,1536]{2,1,0:T(1,128)}), f32[4,1,1536]{2,1,0:T(1,128)S(1)}, u32[]{:S(2)}, u32[]{:S(2)}) async-start(f32[4,1,1536]{2,1,0:T(1,128)} %broadcast_in_dim.6), calls=%async_computation.1 | async-start | bytes 49152 | tf_op jit(solution)/shard_map/all_to_all | solution.py:606
  114.7 14.9 %collective-permute-start.1 = (bf16[512,512]{1,0:T(8,128)(2,1)S(1)}, bf16[512,512]{1,0:T(8,128)(2,1)S(1)}, u32[]{:S(2)}, u32[]{:S(2)}) collective-permute-start(bf16[512,512]{1,0:T(8,128)(2,1)S(1)} %bitcast.208), channel_id=1, source_target_pairs={{0,1},{1,0},{2,3},{3,2},{4,5},{5,4},{6,7},{7,6},{8,9},{9,8},{10,11... | collective-permute-start | bytes 1572872 | tf_op jit(solution)/shard_map/ppermute | solution.py:37
  116.2 15.0 %collective-permute-start.4 = (bf16[512,512]{1,0:T(8,128)(2,1)S(1)}, bf16[512,512]{1,0:T(8,128)(2,1)}, u32[]{:S(2)}, u32[]{:S(2)}) collective-permute-start(bf16[512,512]{1,0:T(8,128)(2,1)S(1)} %bitcast.204), channel_id=1, source_target_pairs={{0,16},{1,17},{2,18},{3,19},{4,20},{5,21},{6,22},{7,23},{8,24},{9,... | collective-permute-start | bytes 1572872 | tf_op jit(solution)/shard_map/ppermute | solution.py:37
  118.5 23.9 %collective-permute-start.3 = (bf16[512,512]{1,0:T(8,128)(2,1)S(1)}, bf16[512,512]{1,0:T(8,128)(2,1)}, u32[]{:S(2)}, u32[]{:S(2)}) collective-permute-start(bf16[512,512]{1,0:T(8,128)(2,1)S(1)} %bitcast.209), channel_id=1, source_target_pairs={{0,16},{1,17},{2,18},{3,19},{4,20},{5,21},{6,22},{7,23},{8,24},{9,... | collective-permute-start | bytes 1572872 | tf_op jit(solution)/shard_map/ppermute | solution.py:37
  119.1 23.4 %collective-permute-start.2 = (bf16[512,512]{1,0:T(8,128)(2,1)S(1)}, bf16[512,512]{1,0:T(8,128)(2,1)}, u32[]{:S(2)}, u32[]{:S(2)}) collective-permute-start(bf16[512,512]{1,0:T(8,128)(2,1)S(1)} %bitcast.205), channel_id=1, source_target_pairs={{0,1},{1,0},{2,3},{3,2},{4,5},{5,4},{6,7},{7,6},{8,9},{9,8},{10,11... | collective-permute-start | bytes 1572872 | tf_op jit(solution)/shard_map/ppermute | solution.py:37
  129.6 22.1 %collective-permute-start.5 = (bf16[512,512]{1,0:T(8,128)(2,1)S(1)}, bf16[512,512]{1,0:T(8,128)(2,1)}, u32[]{:S(2)}, u32[]{:S(2)}) collective-permute-start(bf16[512,512]{1,0:T(8,128)(2,1)S(1)} %collective-permute-done.1.refs_2_), channel_id=1, source_target_pairs={{0,16},{1,17},{2,18},{3,19},{4,20},{5,21},{6,22},{7,23},{8,24},{9,... | collective-permute-start | bytes 1572872 | tf_op jit(solution)/shard_map/ppermute | solution.py:37
  131.2 20.6 %collective-permute-start.6 = (bf16[512,512]{1,0:T(8,128)(2,1)}, bf16[512,512]{1,0:T(8,128)(2,1)}, u32[]{:S(2)}, u32[]{:S(2)}) collective-permute-start(bf16[512,512]{1,0:T(8,128)(2,1)} %collective-permute-done.4.refs_5_), channel_id=1, source_target_pairs={{0,1},{1,0},{2,3},{3,2},{4,5},{5,4},{6,7},{7,6},{8,9},{9,8},{10,11... | collective-permute-start | bytes 1572872 | tf_op jit(solution)/shard_map/ppermute | solution.py:37
  185.5 15.1 %collective-permute-start.13 = (bf16[512,512]{1,0:T(8,128)(2,1)}, bf16[512,512]{1,0:T(8,128)(2,1)S(1)}, u32[]{:S(2)}, u32[]{:S(2)}) collective-permute-start(bf16[512,512]{1,0:T(8,128)(2,1)} %get-tuple-element.97), channel_id=1, source_target_pairs={{0,16},{1,17},{2,18},{3,19},{4,20},{5,21},{6,22},{7,23},{8,24},{9,... | collective-permute-start | bytes 1572872 | tf_op jit(solution)/shard_map/ppermute | solution.py:37
  191.5 23.0 %collective-permute-start.11 = (bf16[512,512]{1,0:T(8,128)(2,1)}, bf16[512,512]{1,0:T(8,128)(2,1)S(1)}, u32[]{:S(2)}, u32[]{:S(2)}) collective-permute-start(bf16[512,512]{1,0:T(8,128)(2,1)} %get-tuple-element.93), channel_id=1, source_target_pairs={{0,16},{1,17},{2,18},{3,19},{4,20},{5,21},{6,22},{7,23},{8,24},{9,... | collective-permute-start | bytes 1572872 | tf_op jit(solution)/shard_map/ppermute | solution.py:37
  196.6 17.9 %collective-permute-start.10 = (bf16[512,512]{1,0:T(8,128)(2,1)}, bf16[512,512]{1,0:T(8,128)(2,1)S(1)}, u32[]{:S(2)}, u32[]{:S(2)}) collective-permute-start(bf16[512,512]{1,0:T(8,128)(2,1)} %get-tuple-element.92), channel_id=1, source_target_pairs={{0,1},{1,0},{2,3},{3,2},{4,5},{5,4},{6,7},{7,6},{8,9},{9,8},{10,11... | collective-permute-start | bytes 1572872 | tf_op jit(solution)/shard_map/ppermute | solution.py:37
  204.9 15.2 %collective-permute-start.14 = (bf16[512,512]{1,0:T(8,128)(2,1)}, bf16[512,512]{1,0:T(8,128)(2,1)S(1)}, u32[]{:S(2)}, u32[]{:S(2)}) collective-permute-start(bf16[512,512]{1,0:T(8,128)(2,1)} %get-tuple-element.98), channel_id=1, source_target_pairs={{0,16},{1,17},{2,18},{3,19},{4,20},{5,21},{6,22},{7,23},{8,24},{9,... | collective-permute-start | bytes 1572872 | tf_op jit(solution)/shard_map/ppermute | solution.py:37
  237.5 15.1 %collective-permute-start.19 = (bf16[512,512]{1,0:T(8,128)(2,1)}, bf16[512,512]{1,0:T(8,128)(2,1)S(1)}, u32[]{:S(2)}, u32[]{:S(2)}) collective-permute-start(bf16[512,512]{1,0:T(8,128)(2,1)} %get-tuple-element.102.refs_0_), channel_id=1, source_target_pairs={{0,1},{1,0},{2,3},{3,2},{4,5},{5,4},{6,7},{7,6},{8,9},{9,8},{10,11... | collective-permute-start | bytes 1572872 | tf_op jit(solution)/shard_map/ppermute | solution.py:37
  238.4 15.7 %collective-permute-start.22 = (bf16[512,512]{1,0:T(8,128)(2,1)}, bf16[512,512]{1,0:T(8,128)(2,1)S(1)}, u32[]{:S(2)}, u32[]{:S(2)}) collective-permute-start(bf16[512,512]{1,0:T(8,128)(2,1)} %get-tuple-element.103.refs_1_), channel_id=1, source_target_pairs={{0,16},{1,17},{2,18},{3,19},{4,20},{5,21},{6,22},{7,23},{8,24},{9,... | collective-permute-start | bytes 1572872 | tf_op jit(solution)/shard_map/ppermute | solution.py:37
  240.0 24.7 %collective-permute-start.33 = (bf16[2048,128]{1,0:T(8,128)(2,1)S(1)}, bf16[2048,128]{1,0:T(8,128)(2,1)S(1)}, u32[]{:S(2)}, u32[]{:S(2)}) collective-permute-start(bf16[2048,128]{1,0:T(8,128)(2,1)S(1)} %get-tuple-element.171), channel_id=1, source_target_pairs={{0,16},{1,17},{2,18},{3,19},{4,20},{5,21},{6,22},{7,23},{8,24},{9,... | collective-permute-start | bytes 1572872 | tf_op jit(solution)/shard_map/ppermute | solution.py:37
  240.6 35.5 %collective-permute-start.21 = (bf16[512,512]{1,0:T(8,128)(2,1)S(1)}, bf16[512,512]{1,0:T(8,128)(2,1)}, u32[]{:S(2)}, u32[]{:S(2)}) collective-permute-start(bf16[512,512]{1,0:T(8,128)(2,1)S(1)} %copy-done.57), channel_id=1, source_target_pairs={{0,16},{1,17},{2,18},{3,19},{4,20},{5,21},{6,22},{7,23},{8,24},{9,... | collective-permute-start | bytes 1572872 | tf_op jit(solution)/shard_map/ppermute | solution.py:37
  242.1 34.0 %collective-permute-start.20 = (bf16[512,512]{1,0:T(8,128)(2,1)S(1)}, bf16[512,512]{1,0:T(8,128)(2,1)}, u32[]{:S(2)}, u32[]{:S(2)}) collective-permute-start(bf16[512,512]{1,0:T(8,128)(2,1)S(1)} %copy-done.58), channel_id=1, source_target_pairs={{0,1},{1,0},{2,3},{3,2},{4,5},{5,4},{6,7},{7,6},{8,9},{9,8},{10,11... | collective-permute-start | bytes 1572872 | tf_op jit(solution)/shard_map/ppermute | solution.py:37
  252.6 29.1 %collective-permute-start.23 = (bf16[512,512]{1,0:T(8,128)(2,1)S(1)}, bf16[512,512]{1,0:T(8,128)(2,1)}, u32[]{:S(2)}, u32[]{:S(2)}) collective-permute-start(bf16[512,512]{1,0:T(8,128)(2,1)S(1)} %collective-permute-done.19.refs_2_), channel_id=1, source_target_pairs={{0,16},{1,17},{2,18},{3,19},{4,20},{5,21},{6,22},{7,23},{8,24},{9,... | collective-permute-start | bytes 1572872 | tf_op jit(solution)/shard_map/ppermute | solution.py:37
  254.1 27.6 %collective-permute-start.24 = (bf16[512,512]{1,0:T(8,128)(2,1)S(1)}, bf16[512,512]{1,0:T(8,128)(2,1)}, u32[]{:S(2)}, u32[]{:S(2)}) collective-permute-start(bf16[512,512]{1,0:T(8,128)(2,1)S(1)} %collective-permute-done.22.refs_5_), channel_id=1, source_target_pairs={{0,1},{1,0},{2,3},{3,2},{4,5},{5,4},{6,7},{7,6},{8,9},{9,8},{10,11... | collective-permute-start | bytes 1572872 | tf_op jit(solution)/shard_map/ppermute | solution.py:37
  265.9 91.7 %all-to-all-start.2 = ((bf16[4,1024,128]{2,1,0:T(8,128)(2,1)}), bf16[4,1024,128]{2,1,0:T(8,128)(2,1)S(1)}, u32[]{:S(2)}, u32[]{:S(2)}) async-start(bf16[4,1024,128]{2,1,0:T(8,128)(2,1)} %bitcast.31), calls=%async_computation.2 | async-start | bytes 2097152 | tf_op jit(solution)/shard_map/all_to_all | solution.py:490
  270.3 535.3 %reduce-scatter.7.cloned.1.call-start = ((), (), s32[]{:S(2)}) async-start(), calls=%async_computation.11 | async-start | bytes 2359296 | tf_op jit(solution)/shard_map/reduce_scatter | solution.py:559
  332.8 17.3 %collective-permute-start.29 = (bf16[512,512]{1,0:T(8,128)(2,1)}, bf16[512,512]{1,0:T(8,128)(2,1)S(1)}, u32[]{:S(2)}, u32[]{:S(2)}) collective-permute-start(bf16[512,512]{1,0:T(8,128)(2,1)} %get-tuple-element.112), channel_id=1, source_target_pairs={{0,1},{1,0},{2,3},{3,2},{4,5},{5,4},{6,7},{7,6},{8,9},{9,8},{10,11... | collective-permute-start | bytes 1572872 | tf_op jit(solution)/shard_map/ppermute | solution.py:37
  334.2 15.9 %collective-permute-start.30 = (bf16[512,512]{1,0:T(8,128)(2,1)}, bf16[512,512]{1,0:T(8,128)(2,1)S(1)}, u32[]{:S(2)}, u32[]{:S(2)}) collective-permute-start(bf16[512,512]{1,0:T(8,128)(2,1)} %get-tuple-element.114), channel_id=1, source_target_pairs={{0,16},{1,17},{2,18},{3,19},{4,20},{5,21},{6,22},{7,23},{8,24},{9,... | collective-permute-start | bytes 1572872 | tf_op jit(solution)/shard_map/ppermute | solution.py:37
  342.3 24.1 %collective-permute-start.28 = (bf16[512,512]{1,0:T(8,128)(2,1)}, bf16[512,512]{1,0:T(8,128)(2,1)S(1)}, u32[]{:S(2)}, u32[]{:S(2)}) collective-permute-start(bf16[512,512]{1,0:T(8,128)(2,1)} %get-tuple-element.110), channel_id=1, source_target_pairs={{0,16},{1,17},{2,18},{3,19},{4,20},{5,21},{6,22},{7,23},{8,24},{9,... | collective-permute-start | bytes 1572872 | tf_op jit(solution)/shard_map/ppermute | solution.py:37
  349.5 16.9 %collective-permute-start.27 = (bf16[512,512]{1,0:T(8,128)(2,1)}, bf16[512,512]{1,0:T(8,128)(2,1)S(1)}, u32[]{:S(2)}, u32[]{:S(2)}) collective-permute-start(bf16[512,512]{1,0:T(8,128)(2,1)} %get-tuple-element.109), channel_id=1, source_target_pairs={{0,1},{1,0},{2,3},{3,2},{4,5},{5,4},{6,7},{7,6},{8,9},{9,8},{10,11... | collective-permute-start | bytes 1572872 | tf_op jit(solution)/shard_map/ppermute | solution.py:37
  354.7 16.0 %collective-permute-start.31 = (bf16[512,512]{1,0:T(8,128)(2,1)}, bf16[512,512]{1,0:T(8,128)(2,1)S(1)}, u32[]{:S(2)}, u32[]{:S(2)}) collective-permute-start(bf16[512,512]{1,0:T(8,128)(2,1)} %get-tuple-element.115), channel_id=1, source_target_pairs={{0,16},{1,17},{2,18},{3,19},{4,20},{5,21},{6,22},{7,23},{8,24},{9,... | collective-permute-start | bytes 1572872 | tf_op jit(solution)/shard_map/ppermute | solution.py:37
  356.2 18.0 %collective-permute-start.32 = (bf16[512,512]{1,0:T(8,128)(2,1)}, bf16[512,512]{1,0:T(8,128)(2,1)S(1)}, u32[]{:S(2)}, u32[]{:S(2)}) collective-permute-start(bf16[512,512]{1,0:T(8,128)(2,1)} %get-tuple-element.116), channel_id=1, source_target_pairs={{0,1},{1,0},{2,3},{3,2},{4,5},{5,4},{6,7},{7,6},{8,9},{9,8},{10,11... | collective-permute-start | bytes 1572872 | tf_op jit(solution)/shard_map/ppermute | solution.py:37
  394.0 15.1 %collective-permute-start.38 = (bf16[512,512]{1,0:T(8,128)(2,1)}, bf16[512,512]{1,0:T(8,128)(2,1)S(1)}, u32[]{:S(2)}, u32[]{:S(2)}) collective-permute-start(bf16[512,512]{1,0:T(8,128)(2,1)} %get-tuple-element.123.refs_0_), channel_id=1, source_target_pairs={{0,1},{1,0},{2,3},{3,2},{4,5},{5,4},{6,7},{7,6},{8,9},{9,8},{10,11... | collective-permute-start | bytes 1572872 | tf_op jit(solution)/shard_map/ppermute | solution.py:37
  395.5 15.1 %collective-permute-start.41 = (bf16[512,512]{1,0:T(8,128)(2,1)}, bf16[512,512]{1,0:T(8,128)(2,1)S(1)}, u32[]{:S(2)}, u32[]{:S(2)}) collective-permute-start(bf16[512,512]{1,0:T(8,128)(2,1)} %get-tuple-element.124.refs_1_), channel_id=1, source_target_pairs={{0,16},{1,17},{2,18},{3,19},{4,20},{5,21},{6,22},{7,23},{8,24},{9,... | collective-permute-start | bytes 1572872 | tf_op jit(solution)/shard_map/ppermute | solution.py:37
  397.0 24.8 %collective-permute-start.40 = (bf16[512,512]{1,0:T(8,128)(2,1)}, bf16[512,512]{1,0:T(8,128)(2,1)S(1)}, u32[]{:S(2)}, u32[]{:S(2)}) collective-permute-start(bf16[512,512]{1,0:T(8,128)(2,1)} %get-tuple-element.123.refs_0_), channel_id=1, source_target_pairs={{0,16},{1,17},{2,18},{3,19},{4,20},{5,21},{6,22},{7,23},{8,24},{9,... | collective-permute-start | bytes 1572872 | tf_op jit(solution)/shard_map/ppermute | solution.py:37
  397.5 24.3 %collective-permute-start.39 = (bf16[512,512]{1,0:T(8,128)(2,1)}, bf16[512,512]{1,0:T(8,128)(2,1)S(1)}, u32[]{:S(2)}, u32[]{:S(2)}) collective-permute-start(bf16[512,512]{1,0:T(8,128)(2,1)} %get-tuple-element.124.refs_1_), channel_id=1, source_target_pairs={{0,1},{1,0},{2,3},{3,2},{4,5},{5,4},{6,7},{7,6},{8,9},{9,8},{10,11... | collective-permute-start | bytes 1572872 | tf_op jit(solution)/shard_map/ppermute | solution.py:37
  409.2 19.4 %collective-permute-start.42 = (bf16[512,512]{1,0:T(8,128)(2,1)S(1)}, bf16[512,512]{1,0:T(8,128)(2,1)S(1)}, u32[]{:S(2)}, u32[]{:S(2)}) collective-permute-start(bf16[512,512]{1,0:T(8,128)(2,1)S(1)} %collective-permute-done.38.refs_2_), channel_id=1, source_target_pairs={{0,16},{1,17},{2,18},{3,19},{4,20},{5,21},{6,22},{7,23},{8,24},{9,... | collective-permute-start | bytes 1572872 | tf_op jit(solution)/shard_map/ppermute | solution.py:37
  410.6 17.9 %collective-permute-start.43 = (bf16[512,512]{1,0:T(8,128)(2,1)S(1)}, bf16[512,512]{1,0:T(8,128)(2,1)S(1)}, u32[]{:S(2)}, u32[]{:S(2)}) collective-permute-start(bf16[512,512]{1,0:T(8,128)(2,1)S(1)} %collective-permute-done.41.refs_5_), channel_id=1, source_target_pairs={{0,1},{1,0},{2,3},{3,2},{4,5},{5,4},{6,7},{7,6},{8,9},{9,8},{10,11... | collective-permute-start | bytes 1572872 | tf_op jit(solution)/shard_map/ppermute | solution.py:37
  455.4 17.6 %collective-permute-start.46 = (bf16[512,512]{1,0:T(8,128)(2,1)}, bf16[512,512]{1,0:T(8,128)(2,1)S(1)}, u32[]{:S(2)}, u32[]{:S(2)}) collective-permute-start(bf16[512,512]{1,0:T(8,128)(2,1)} %get-tuple-element.132), channel_id=1, source_target_pairs={{0,1},{1,0},{2,3},{3,2},{4,5},{5,4},{6,7},{7,6},{8,9},{9,8},{10,11... | collective-permute-start | bytes 1572872 | tf_op jit(solution)/shard_map/ppermute | solution.py:37
  455.8 17.2 %collective-permute-start.47 = (bf16[512,512]{1,0:T(8,128)(2,1)}, bf16[512,512]{1,0:T(8,128)(2,1)S(1)}, u32[]{:S(2)}, u32[]{:S(2)}) collective-permute-start(bf16[512,512]{1,0:T(8,128)(2,1)} %get-tuple-element.134), channel_id=1, source_target_pairs={{0,16},{1,17},{2,18},{3,19},{4,20},{5,21},{6,22},{7,23},{8,24},{9,... | collective-permute-start | bytes 1572872 | tf_op jit(solution)/shard_map/ppermute | solution.py:37
  464.3 38.2 %collective-permute-start.45 = (bf16[512,512]{1,0:T(8,128)(2,1)}, bf16[512,512]{1,0:T(8,128)(2,1)S(1)}, u32[]{:S(2)}, u32[]{:S(2)}) collective-permute-start(bf16[512,512]{1,0:T(8,128)(2,1)} %get-tuple-element.130), channel_id=1, source_target_pairs={{0,16},{1,17},{2,18},{3,19},{4,20},{5,21},{6,22},{7,23},{8,24},{9,... | collective-permute-start | bytes 1572872 | tf_op jit(solution)/shard_map/ppermute | solution.py:37
  471.4 31.1 %collective-permute-start.44 = (bf16[512,512]{1,0:T(8,128)(2,1)}, bf16[512,512]{1,0:T(8,128)(2,1)S(1)}, u32[]{:S(2)}, u32[]{:S(2)}) collective-permute-start(bf16[512,512]{1,0:T(8,128)(2,1)} %get-tuple-element.129), channel_id=1, source_target_pairs={{0,1},{1,0},{2,3},{3,2},{4,5},{5,4},{6,7},{7,6},{8,9},{9,8},{10,11... | collective-permute-start | bytes 1572872 | tf_op jit(solution)/shard_map/ppermute | solution.py:37
  477.6 24.9 %collective-permute-start.48 = (bf16[512,512]{1,0:T(8,128)(2,1)}, bf16[512,512]{1,0:T(8,128)(2,1)S(1)}, u32[]{:S(2)}, u32[]{:S(2)}) collective-permute-start(bf16[512,512]{1,0:T(8,128)(2,1)} %get-tuple-element.135), channel_id=1, source_target_pairs={{0,16},{1,17},{2,18},{3,19},{4,20},{5,21},{6,22},{7,23},{8,24},{9,... | collective-permute-start | bytes 1572872 | tf_op jit(solution)/shard_map/ppermute | solution.py:37
  479.0 23.5 %collective-permute-start.49 = (bf16[512,512]{1,0:T(8,128)(2,1)}, bf16[512,512]{1,0:T(8,128)(2,1)S(1)}, u32[]{:S(2)}, u32[]{:S(2)}) collective-permute-start(bf16[512,512]{1,0:T(8,128)(2,1)} %get-tuple-element.136), channel_id=1, source_target_pairs={{0,1},{1,0},{2,3},{3,2},{4,5},{5,4},{6,7},{7,6},{8,9},{9,8},{10,11... | collective-permute-start | bytes 1572872 | tf_op jit(solution)/shard_map/ppermute | solution.py:37
  523.8 15.1 %collective-permute-start.53 = (bf16[512,512]{1,0:T(8,128)(2,1)}, bf16[512,512]{1,0:T(8,128)(2,1)S(1)}, u32[]{:S(2)}, u32[]{:S(2)}) collective-permute-start(bf16[512,512]{1,0:T(8,128)(2,1)} %get-tuple-element.140.refs_0_), channel_id=1, source_target_pairs={{0,1},{1,0},{2,3},{3,2},{4,5},{5,4},{6,7},{7,6},{8,9},{9,8},{10,11... | collective-permute-start | bytes 1572872 | tf_op jit(solution)/shard_map/ppermute | solution.py:37
  524.4 15.1 %collective-permute-start.56 = (bf16[512,512]{1,0:T(8,128)(2,1)}, bf16[512,512]{1,0:T(8,128)(2,1)S(1)}, u32[]{:S(2)}, u32[]{:S(2)}) collective-permute-start(bf16[512,512]{1,0:T(8,128)(2,1)} %get-tuple-element.141.refs_1_), channel_id=1, source_target_pairs={{0,16},{1,17},{2,18},{3,19},{4,20},{5,21},{6,22},{7,23},{8,24},{9,... | collective-permute-start | bytes 1572872 | tf_op jit(solution)/shard_map/ppermute | solution.py:37
  524.8 22.6 %collective-permute-start.55 = (bf16[512,512]{1,0:T(8,128)(2,1)}, bf16[512,512]{1,0:T(8,128)(2,1)S(1)}, u32[]{:S(2)}, u32[]{:S(2)}) collective-permute-start(bf16[512,512]{1,0:T(8,128)(2,1)} %get-tuple-element.140.refs_0_), channel_id=1, source_target_pairs={{0,16},{1,17},{2,18},{3,19},{4,20},{5,21},{6,22},{7,23},{8,24},{9,... | collective-permute-start | bytes 1572872 | tf_op jit(solution)/shard_map/ppermute | solution.py:37
  526.5 20.9 %collective-permute-start.54 = (bf16[512,512]{1,0:T(8,128)(2,1)}, bf16[512,512]{1,0:T(8,128)(2,1)S(1)}, u32[]{:S(2)}, u32[]{:S(2)}) collective-permute-start(bf16[512,512]{1,0:T(8,128)(2,1)} %get-tuple-element.141.refs_1_), channel_id=1, source_target_pairs={{0,1},{1,0},{2,3},{3,2},{4,5},{5,4},{6,7},{7,6},{8,9},{9,8},{10,11... | collective-permute-start | bytes 1572872 | tf_op jit(solution)/shard_map/ppermute | solution.py:37
  561.9 245.1 %reduce-scatter.5.cloned.1.call-start = ((), (), s32[]{:S(2)}) async-start(), calls=%async_computation.10 | async-start | bytes 7077888 | tf_op jit(solution)/shard_map/reduce_scatter | solution.py:559
  619.4 208.8 %reduce-scatter.11.cloned.1.call-start = ((), (), s32[]{:S(2)}) async-start(), calls=%async_computation.13 | async-start | bytes 9437184 | tf_op jit(solution)/shard_map/reduce_scatter | solution.py:559
  620.2 290.9 %reduce-scatter.9.cloned.1.call-start = ((), (), s32[]{:S(2)}) async-start(), calls=%async_computation.12 | async-start | bytes 9437184 | tf_op jit(solution)/shard_map/reduce_scatter | solution.py:559
  632.9 41.6 %all-to-all-start.3 = ((bf16[4,2,65536]{2,1,0:T(2,128)(2,1)}), bf16[4,2,65536]{2,1,0:T(2,128)(2,1)S(1)}, u32[]{:S(2)}, u32[]{:S(2)}) async-start(bf16[4,2,65536]{2,1,0:T(2,128)(2,1)} %reshape.286), calls=%async_computation.3 | async-start | bytes 2097152 | tf_op jit(solution)/shard_map/all_to_all | solution.py:494
  641.5 111.8 %collective-permute-start.72 = (f32[4]{0:T(128)S(1)}, f32[4]{0:T(128)S(1)}, u32[]{:S(2)}, u32[]{:S(2)}) collective-permute-start(f32[4]{0:T(128)S(1)} %pad_maximum_fusion.6), channel_id=1, source_target_pairs={{0,1},{1,0},{2,3},{3,2},{4,5},{5,4},{6,7},{7,6},{8,9},{9,8},{10,11... | collective-permute-start | bytes 56 | tf_op jit(solution)/shard_map/ppermute | solution.py:37
  690.4 17.0 %collective-permute-start.61 = (bf16[512,512]{1,0:T(8,128)(2,1)}, bf16[512,512]{1,0:T(8,128)(2,1)S(1)}, u32[]{:S(2)}, u32[]{:S(2)}) collective-permute-start(bf16[512,512]{1,0:T(8,128)(2,1)} %get-tuple-element.149), channel_id=1, source_target_pairs={{0,1},{1,0},{2,3},{3,2},{4,5},{5,4},{6,7},{7,6},{8,9},{9,8},{10,11... | collective-permute-start | bytes 1572872 | tf_op jit(solution)/shard_map/ppermute | solution.py:37
  691.9 15.5 %collective-permute-start.62 = (bf16[512,512]{1,0:T(8,128)(2,1)}, bf16[512,512]{1,0:T(8,128)(2,1)S(1)}, u32[]{:S(2)}, u32[]{:S(2)}) collective-permute-start(bf16[512,512]{1,0:T(8,128)(2,1)} %get-tuple-element.151), channel_id=1, source_target_pairs={{0,16},{1,17},{2,18},{3,19},{4,20},{5,21},{6,22},{7,23},{8,24},{9,... | collective-permute-start | bytes 1572872 | tf_op jit(solution)/shard_map/ppermute | solution.py:37
  698.5 28.0 %collective-permute-start.60 = (bf16[512,512]{1,0:T(8,128)(2,1)}, bf16[512,512]{1,0:T(8,128)(2,1)S(1)}, u32[]{:S(2)}, u32[]{:S(2)}) collective-permute-start(bf16[512,512]{1,0:T(8,128)(2,1)} %get-tuple-element.147), channel_id=1, source_target_pairs={{0,16},{1,17},{2,18},{3,19},{4,20},{5,21},{6,22},{7,23},{8,24},{9,... | collective-permute-start | bytes 1572872 | tf_op jit(solution)/shard_map/ppermute | solution.py:37
  706.7 19.8 %collective-permute-start.59 = (bf16[512,512]{1,0:T(8,128)(2,1)}, bf16[512,512]{1,0:T(8,128)(2,1)S(1)}, u32[]{:S(2)}, u32[]{:S(2)}) collective-permute-start(bf16[512,512]{1,0:T(8,128)(2,1)} %get-tuple-element.146), channel_id=1, source_target_pairs={{0,1},{1,0},{2,3},{3,2},{4,5},{5,4},{6,7},{7,6},{8,9},{9,8},{10,11... | collective-permute-start | bytes 1572872 | tf_op jit(solution)/shard_map/ppermute | solution.py:37
  714.2 31.8 %all-to-all-start.5 = ((f32[4,1,1536]{2,1,0:T(1,128)}), f32[4,1,1536]{2,1,0:T(1,128)S(1)}, u32[]{:S(2)}, u32[]{:S(2)}) async-start(f32[4,1,1536]{2,1,0:T(1,128)} %all_to_all.70), calls=%async_computation.6 | async-start | bytes 49152 | tf_op jit(solution)/shard_map/all_to_all | solution.py:691
  746.0 55.2 %all-to-all-start.4 = ((bf16[4,2,65536]{2,1,0:T(2,128)(2,1)}), bf16[4,2,65536]{2,1,0:T(2,128)(2,1)S(1)}, u32[]{:S(2)}, u32[]{:S(2)}) async-start(bf16[4,2,65536]{2,1,0:T(2,128)(2,1)} %reshape.288), calls=%async_computation.4 | async-start | bytes 2097152 | tf_op jit(solution)/shard_map/all_to_all | solution.py:494
  751.5 47.0 %collective-permute-start.37 = (bf16[2048,128]{1,0:T(8,128)(2,1)S(1)}, bf16[2048,128]{1,0:T(8,128)(2,1)S(1)}, u32[]{:S(2)}, u32[]{:S(2)}) collective-permute-start(bf16[2048,128]{1,0:T(8,128)(2,1)S(1)} %get-tuple-element.169), channel_id=1, source_target_pairs={{0,16},{1,17},{2,18},{3,19},{4,20},{5,21},{6,22},{7,23},{8,24},{9,... | collective-permute-start | bytes 1572872 | tf_op jit(solution)/shard_map/ppermute | solution.py:37
  755.4 26.5 %collective-permute-start.73 = (f32[4]{0:T(128)S(1)}, f32[4]{0:T(128)S(1)}, u32[]{:S(2)}, u32[]{:S(2)}) collective-permute-start(f32[4]{0:T(128)S(1)} %fusion.18), channel_id=1, source_target_pairs={{0,2},{1,3},{2,0},{3,1},{4,6},{5,7},{6,4},{7,5},{8,10},{9,11},{10,... | collective-permute-start | bytes 56 | tf_op jit(solution)/shard_map/ppermute | solution.py:37
  803.2 14.9 %collective-permute-start.65 = (bf16[2048,128]{1,0:T(8,128)(2,1)S(1)}, bf16[2048,128]{1,0:T(8,128)(2,1)S(1)}, u32[]{:S(2)}, u32[]{:S(2)}) collective-permute-start(bf16[2048,128]{1,0:T(8,128)(2,1)S(1)} %get-tuple-element.167), channel_id=1, source_target_pairs={{0,16},{1,17},{2,18},{3,19},{4,20},{5,21},{6,22},{7,23},{8,24},{9,... | collective-permute-start | bytes 1572872 | tf_op jit(solution)/shard_map/ppermute | solution.py:37
  808.0 20.1 %collective-permute-start.66 = (bf16[512,384]{1,0:T(8,128)(2,1)S(1)}, bf16[512,384]{1,0:T(8,128)(2,1)S(1)}, u32[]{:S(2)}, u32[]{:S(2)}) collective-permute-start(bf16[512,384]{1,0:T(8,128)(2,1)S(1)} %slice_bitcast_fusion.2), channel_id=1, source_target_pairs={{0,16},{1,17},{2,18},{3,19},{4,20},{5,21},{6,22},{7,23},{8,24},{9,... | collective-permute-start | bytes 1179656 | tf_op jit(solution)/shard_map/ppermute | solution.py:37
  829.5 87.0 %collective-permute-start.71 = (bf16[512,512]{1,0:T(8,128)(2,1)S(1)}, bf16[512,512]{1,0:T(8,128)(2,1)S(1)}, u32[]{:S(2)}, u32[]{:S(2)}) collective-permute-start(bf16[512,512]{1,0:T(8,128)(2,1)S(1)} %get-tuple-element.163), channel_id=1, source_target_pairs={{0,16},{1,17},{2,18},{3,19},{4,20},{5,21},{6,22},{7,23},{8,24},{9,... | collective-permute-start | bytes 1572872 | tf_op jit(solution)/shard_map/ppermute | solution.py:37
  (100 other events, 686.1 us)
Sparse Core Ops, SparseCore 0:
  22.8 86.6 all-gather.8
  111.6 27.1 all-gather.10
  140.5 81.5 all-gather.12
  223.5 102.7 all-gather.14
  562.0 33.3 reduce-scatter.6
  619.5 84.2 reduce-scatter.4
  706.1 109.8 reduce-scatter.10
  818.3 92.7 reduce-scatter.8

commit v3 on v2

--- a/solution.py
+++ b/solution.py
@@ -41,8 +41,23 @@
     return lax.dot_general(left, right, (dims, ((), ())), preferred_element_type=F32)
 
 
+def tie(value, *others):
+    return lax.optimization_barrier((value, *others))[0]
+
+
+class Order:
+    def __init__(self, value):
+        self.value = value
+
+    def after(self, *others):
+        self.value = tie(self.value, *others)
+
+
+MORE = 10
+
+
 def call(body, grid, spot, ins, in_specs, outs, out_specs, scratch, flops, size):
-    return pl.pallas_call(
+    result = pl.pallas_call(
         body,
         grid_spec=pltpu.PrefetchScalarGridSpec(
             num_scalar_prefetch=1, grid=grid, in_specs=in_specs, out_specs=out_specs, scratch_shapes=scratch
@@ -51,8 +66,10 @@
         compiler_params=pltpu.CompilerParams(
             dimension_semantics=("arbitrary",) * len(grid), vmem_limit_bytes=56 * 1024 * 1024
         ),
-        cost_estimate=pl.CostEstimate(flops=flops, bytes_accessed=size, transcendentals=0),
-    )(spot, *ins)
+        cost_estimate=pl.CostEstimate(flops=flops * MORE, bytes_accessed=size * MORE, transcendentals=0),
+    )(spot.value, *ins)
+    spot.after(result[0])
+    return result
 
 
 def shape_of(*shape, dtype=F32):
@@ -63,8 +80,8 @@
     return pl.BlockSpec(shape, lambda *_: (0,) * len(shape))
 
 
-def pick(low, high, t):
-    return jnp.where(t == 0, low[...], high[...])
+def pick(low, high, first):
+    return jnp.where(first, low[...], high[...])
 
 
 SLOTS = (0, 2, 1, 3)
@@ -90,14 +107,14 @@
 
     total = None
     for slot in range(4):
-        tile = pick(pieces[2 * slot], pieces[2 * slot + 1], t)
+        tile = pick(pieces[2 * slot], pieces[2 * slot + 1], t == 0)
         part = slice(slot * QUARTER, slot * QUARTER + QUARTER)
         term = dot(tile, kept[:, part], NT) if by_rows else dot(tile, kept[part, :], NN)
         total = term if total is None else total + term
     finish(total, extra, outs)
 
 
-def wide(pieces, weights, spot, by_rows, finish, extra, count):
+def wide(pieces, weights, spot, by_rows, finish, extra, count, sums=0):
     if by_rows:
         n = weights.shape[1]
         weights = weights.reshape(4, 2, n, 1024)
@@ -111,15 +128,15 @@
     bias = pl.BlockSpec((1, n), lambda z, t, *_: (0, z))
     tile = pl.BlockSpec((HALF, n), lambda z, t, *_: (t, z))
     return call(
-        functools.partial(wide_body, by_rows, finish, count),
+        functools.partial(wide_body, by_rows, finish, count + sums),
         (4, 2),
         spot,
         (*pieces, weights, *extra),
         [fixed(p.shape) for p in pieces]
         + [pl.BlockSpec(block, lambda z, t, *_: (z,) + tail)]
         + [bias if e.shape[0] == 1 else tile for e in extra],
-        [shape_of(LEN, 4 * n, dtype=BF)] * count,
-        [tile] * count,
+        [shape_of(LEN, 4 * n, dtype=BF)] * count + [shape_of(8, 4 * n)] * sums,
+        [tile] * count + [pl.BlockSpec((8, n), lambda z, t, *_: (0, z))] * sums,
         [kept],
         2 * LEN * WIDTH * 4 * n,
         2 * (LEN * WIDTH + WIDTH * 4 * n + LEN * 4 * n),
@@ -145,7 +162,9 @@
 
 
 def finish_slope(total, extra, outs):
-    outs[0][...] = (total * extra[0][...].astype(F32)).astype(BF)
+    rounded = (total * extra[0][...].astype(F32)).astype(BF)
+    outs[0][...] = rounded
+    add_columns(outs[1], pl.program_id(1), [rounded.astype(F32)])
 
 
 def partial_body(by_rows, n, spot, local, *rest):
@@ -198,7 +217,7 @@
     )
 
 
-def grad_body(by_rows, spot, *refs):
+def grad_whole_body(by_rows, spot, *refs):
     pieces, local, out = refs[:8], refs[8], refs[9]
     for slot, mask in enumerate(SLOTS):
         start = pl.multiple_of((spot[0] ^ mask) * 128, 128)
@@ -217,23 +236,121 @@
                 out[0, c, y, pl.ds(start, 128), :] = total[part, :].astype(BF)
 
 
-def grad(pieces, local, spot, by_rows):
+def grad_whole(pieces, local, spot, by_rows):
     n = local.shape[1] // 4
     shape = (4, 2, n, 1024) if by_rows else (4, 2, 2, 512, n)
     tail = (0,) * (len(shape) - 1)
-    out = call(
+    (out,) = call(
+        functools.partial(grad_whole_body, by_rows),
+        (4,),
+        spot,
+        (*pieces, local),
+        [fixed(p.shape) for p in pieces] + [pl.BlockSpec((LEN, n), lambda z, *_: (0, z))],
+        [shape_of(*shape, dtype=BF)],
+        [pl.BlockSpec((1,) + shape[1:], lambda z, *_: (z,) + tail)],
+        [],
+        2 * LEN * WIDTH * 4 * n,
+        2 * (LEN * WIDTH + WIDTH * 4 * n + LEN * 4 * n),
+    )
+    return out.reshape(8, n, 1024) if by_rows else out.reshape(8, 1024, n)
+
+
+def grad_body(by_rows, spot, *refs):
+    pieces, local, outs = refs[:8], refs[8], refs[9:]
+    order = [((y ^ spot[1]) * 2 + (c ^ spot[2])) * 128 for y in range(2) for c in range(2)]
+    order = [pl.ds(pl.multiple_of(at, 128), 128) for at in order]
+    for slot, mask in enumerate(SLOTS):
+        start = pl.multiple_of((spot[0] ^ mask) * 128, 128)
+        total = None
+        for part in range(2):
+            piece = jnp.concatenate([pieces[2 * slot + part][:, at] for at in order], axis=1)
+            tile = local[part * HALF : part * HALF + HALF, :]
+            term = dot(tile, piece, TN) if by_rows else dot(piece, tile, TN)
+            total = term if total is None else total + term
+        for block in range(4):
+            y, c = divmod(block, 2)
+            part = slice(block * 128, block * 128 + 128)
+            if by_rows:
+                outs[c][0, :, pl.ds(pl.multiple_of(y * 512 + start, 128), 128)] = total[:, part].astype(BF)
+            else:
+                outs[c][0, y, pl.ds(start, 128), :] = total[part, :].astype(BF)
+
+
+def grad(pieces, local, spot, by_rows):
+    n = local.shape[1] // 4
+    shape = (4, n, 1024) if by_rows else (4, 2, 512, n)
+    tail = (0,) * (len(shape) - 1)
+
+    def where(z, p):
+        far = z ^ p[3]
+        return ((far >> 1) | ((far & 1) << 1),) + tail
+
+    outs = call(
         functools.partial(grad_body, by_rows),
         (4,),
         spot,
         (*pieces, local),
         [fixed(p.shape) for p in pieces] + [pl.BlockSpec((LEN, n), lambda z, *_: (0, z))],
-        shape_of(*shape, dtype=BF),
-        pl.BlockSpec((1,) + shape[1:], lambda z, *_: (z,) + tail),
+        [shape_of(*shape, dtype=BF)] * 2,
+        [pl.BlockSpec((1,) + shape[1:], where)] * 2,
         [],
         2 * LEN * WIDTH * 4 * n,
         2 * (LEN * WIDTH + WIDTH * 4 * n + LEN * 4 * n),
     )
-    return out.reshape(8, n, 1024) if by_rows else out.reshape(8, 1024, n)
+    return [o if by_rows else o.reshape(4, 1024, n) for o in outs]
+
+
+def fold_body(spot, *refs):
+    count = len(refs) // 3
+    for i in range(count):
+        out = refs[2 * count + i]
+        out[...] = (refs[i][...].astype(F32) + refs[count + i][...].astype(F32)).astype(out.dtype)
+
+
+def fold(own, got, spot):
+    half, rows, width = own.shape[0] // 2, own.shape[1], own.shape[2]
+    step = min(rows, 512)
+    first = pl.BlockSpec((1, step, width), lambda i, t, p: (i, t, 0))
+    second = pl.BlockSpec((1, step, width), lambda i, t, p: (i + half, t, 0))
+    return call(
+        fold_body, (half, rows // step), spot, (own, own, got, got), [first, second] * 2,
+        [shape_of(half, rows, width, dtype=BF)] * 2, [first, first], [], 2 * half * rows * width, 12 * half * rows * width,
+    )
+
+
+def fold_last(own, got, spot, by_rows):
+    rows, width = own.shape[1:]
+    if by_rows:
+        shape = (rows, 512)
+        parts = [pl.BlockSpec((1, rows, 512), functools.partial(lambda y, i, p: (0, 0, y), y)) for y in range(2)]
+    else:
+        shape = (512, width)
+        parts = [pl.BlockSpec((1, 512, width), functools.partial(lambda y, i, p: (0, y, 0), y)) for y in range(2)]
+
+    def body(spot, a, b, c, d, keep, send):
+        keep[...] = a[0].astype(F32) + c[0].astype(F32)
+        send[...] = (b[0].astype(F32) + d[0].astype(F32)).astype(BF)
+
+    return call(
+        body, (1,), spot, (own, own, got, got), parts * 2, [shape_of(*shape), shape_of(*shape, dtype=BF)], [fixed(shape)] * 2,
+        [], rows * width, 6 * rows * width,
+    )
+
+
+class Sum:
+    def __init__(self, outs, spot, by_rows):
+        self.keep, self.send = outs
+        self.spot, self.by_rows = spot, by_rows
+
+    def go(self, mask):
+        self.got = swap(tie(self.send, self.spot.value), mask)
+
+    def step(self):
+        self.keep, self.send = fold(self.keep, self.got, self.spot)
+
+    def last(self):
+        self.keep, self.send = fold_last(self.keep, self.got, self.spot, self.by_rows)
+        return self.keep, swap(self.send, Y_BIT)
 
 
 SCALE = HD ** (-0.5)
@@ -280,7 +397,7 @@
     )
 
 
-def backward_body(spot, queries, whole, ids_row, ids_column, logsum, grad_out, out, grad_keys, grad_values):
+def backward_body(spot, queries, whole, ids_row, ids_column, logsum, grad_out, out, sums, grad_keys, grad_values):
     q = pl.program_id(1)
     block = queries.shape[0]
     keys = whole[:, HD : 2 * HD]
@@ -292,7 +409,9 @@
     inner = jnp.sum(probs * grad_probs, axis=0, keepdims=True)
     grad_scores = (probs * (grad_probs - inner)).astype(BF)
     back_query = dot(keys, grad_scores, TN)
-    out[pl.ds(q * block, block), :HD] = (back_query.T * SCALE).astype(BF)
+    back_query = (back_query.T * SCALE).astype(BF)
+    out[pl.ds(q * block, block), :HD] = back_query
+    add_columns(sums.at[:, :HD], q, [back_query.astype(F32)])
     back_key = dot(grad_scores, queries[:, :HD], NN)
     back_value = dot(probs.astype(BF), grad_out[...], NN)
 
@@ -309,7 +428,10 @@
     @pl.when(q == pl.num_programs(1) - 1)
     def _():
         out[:, HD : 2 * HD] = (grad_keys[...] * SCALE).astype(BF)
-        out[:, 2 * HD :] = grad_values[...].astype(BF)
+        rounded = grad_values[...].astype(BF)
+        out[:, 2 * HD :] = rounded
+        sums[:, HD : 2 * HD] = jnp.zeros((8, HD), F32)
+        sums[:, 2 * HD :] = column_sums([rounded.astype(F32)])
 
 
 def attention_back(qkv, ids_row, ids_column, logsum, grad_heads, spot):
@@ -323,8 +445,8 @@
             pl.BlockSpec((1, 1, QUERY_BLOCK), lambda h, q, p: (h, 0, q)),
             pl.BlockSpec((QUERY_BLOCK, HD), lambda h, q, p: (q, h)),
         ],
-        shape_of(LEN, 12 * HD, dtype=BF),
-        pl.BlockSpec((LEN, 3 * HD), lambda h, q, p: (0, h)),
+        [shape_of(LEN, 12 * HD, dtype=BF), shape_of(8, 12 * HD)],
+        [pl.BlockSpec((LEN, 3 * HD), lambda h, q, p: (0, h)), pl.BlockSpec((8, 3 * HD), lambda h, q, p: (0, h))],
         [pltpu.VMEM((LEN, HD), F32), pltpu.VMEM((LEN, HD), F32)],
         120 * LEN * LEN * HD,
         LEN * 4 * HD * 16,
@@ -369,35 +491,47 @@
 
 
 def summed(refs, t):
-    own, near, last = (pick(refs[2 * i], refs[2 * i + 1], t).astype(F32) for i in range(3))
+    own, near, last = (pick(refs[2 * i], refs[2 * i + 1], t < STEPS // 2).astype(F32) for i in range(3))
     return own + near + last
 
 
-HALVES = fixed((HALF, QUARTER))
-TILE = pl.BlockSpec((HALF, QUARTER), lambda t, p: (t, 0))
-STATS = pl.BlockSpec((8, HALF), lambda t, p: (0, t))
+STEP = 256
+STEPS = LEN // STEP
+LOW = pl.BlockSpec((STEP, QUARTER), lambda t, p: (jnp.minimum(t, STEPS // 2 - 1), 0))
+HIGH = pl.BlockSpec((STEP, QUARTER), lambda t, p: (jnp.maximum(t - STEPS // 2, 0), 0))
+PARTS = [LOW, HIGH] * 3
+TILE = pl.BlockSpec((STEP, QUARTER), lambda t, p: (t, 0))
+STATS = pl.BlockSpec((8, STEP), lambda t, p: (0, t))
 VECTOR = fixed((1, QUARTER))
 SUMS = fixed((8, QUARTER))
+BLOCKS = pl.BlockSpec((4, STEP, 128), lambda t, p: (0, t, 0))
 
 
 def elementwise(body, spot, ins, in_specs, outs, out_specs):
-    return call(body, (2,), spot, ins, in_specs, outs, out_specs, [], 20 * LEN * QUARTER, 16 * LEN * QUARTER)
+    return call(body, (STEPS,), spot, ins, in_specs, outs, out_specs, [], 20 * LEN * QUARTER, 16 * LEN * QUARTER)
+
+
+def write_blocks(out, value):
+    for z in range(4):
+        out[z] = value[:, z * 128 : z * 128 + 128].astype(BF)
 
 
 def norm_one_sums(spot, *refs):
-    parts, (stream, bias, resid, stats) = refs[:6], refs[6:]
-    attn = summed(parts, pl.program_id(0)) + bias[...]
-    total = stream[...].astype(F32) + attn
+    parts, (low, high, bias, resid, stats) = refs[:6], refs[6:]
+    t = pl.program_id(0)
+    attn = summed(parts, t) + bias[...]
+    stream = pick(low, high, t < STEPS // 2).astype(F32)
+    total = stream + attn
     resid[...] = total
-    stats[...] = rows_of([total, total * total, attn * attn, jnp.square(stream[...].astype(F32))])
+    stats[...] = rows_of([total, total * total, attn * attn, stream * stream])
 
 
 def write_halves(t, low, high, value):
-    @pl.when(t == 0)
+    @pl.when(t < STEPS // 2)
     def _():
         low[...] = value
 
-    @pl.when(t == 1)
+    @pl.when(t >= STEPS // 2)
     def _():
         high[...] = value
 
@@ -413,28 +547,29 @@
 
 def norm_two_sums(spot, *refs):
     parts = refs[:6]
-    bias, resid, moments, gain, shift, dy, gain_two, resid_two, stats = refs[6:]
-    ffn = summed(parts, pl.program_id(0)) + bias[...]
+    bias, resid, moments, gain, shift, dy_low, dy_high, gain_two, resid_two, stats = refs[6:]
+    t = pl.program_id(0)
+    ffn = summed(parts, t) + bias[...]
     columns = columns_of(moments[...])
     hidden = (resid[...] - columns[:, 0:1]) * columns[:, 1:2] * gain[...] + shift[...]
     total = hidden + ffn
     resid_two[...] = total
-    scaled = dy[...].astype(F32) * gain_two[...]
+    scaled = pick(dy_low, dy_high, t < STEPS // 2).astype(F32) * gain_two[...]
     stats[...] = rows_of([total, total * total, scaled, scaled * total, ffn * ffn])
 
 
-def norm_two(spot, resid_two, s0, s1, s2, s3, dy, gain, shift, layer_out, grad_two, low, high, sums):
+def norm_two(spot, resid_two, s0, s1, s2, s3, dy_low, dy_high, gain, shift, layer_out, grad_two, low, high, sums):
     mean, rstd, total = moments_of((s0, s1, s2, s3))
     mean_e = total[2:3]
     along = rstd * (total[3:4] - mean * mean_e)
     columns = columns_of(jnp.concatenate([mean, rstd, mean_e, along] + [mean] * 4, axis=0))
     normed = (resid_two[...] - columns[:, 0:1]) * columns[:, 1:2]
-    upstream = dy[...].astype(F32)
-    layer_out[...] = (normed * gain[...] + shift[...]).astype(BF)
+    t = pl.program_id(0)
+    upstream = pick(dy_low, dy_high, t < STEPS // 2).astype(F32)
+    write_blocks(layer_out, normed * gain[...] + shift[...])
     back = columns[:, 1:2] * (upstream * gain[...] - columns[:, 2:3] - normed * columns[:, 3:4])
     grad_two[...] = back
     rounded = back.astype(BF)
-    t = pl.program_id(0)
     write_halves(t, low, high, rounded)
     add_columns(sums, t, [upstream * normed, upstream, rounded.astype(F32)])
 
@@ -467,7 +602,7 @@
 
 def finish_back(spot, *refs):
     parts, (grad_one, out) = refs[:6], refs[6:]
-    out[...] = (summed(parts, pl.program_id(0)) + grad_one[...]).astype(BF)
+    write_blocks(out, summed(parts, pl.program_id(0)) + grad_one[...])
 
 
 def pass_on(spot, first, second, third, fourth, low, high):
@@ -475,23 +610,39 @@
     high[...] = (third[...] + fourth[...].astype(F32)).astype(BF)
 
 
-def tie(value, *others):
-    return lax.optimization_barrier((value, *others))[0]
-
-
-def to_share(piece, yi):
-    own = lax.dynamic_slice_in_dim(piece, yi * 128, 128, 1)
-    other = swap(lax.dynamic_slice_in_dim(piece, (1 - yi) * 128, 128, 1), Y_BIT)
-    return own, other
-
-
-def to_share_rest(own, other, yi):
-    both = jnp.where(yi == 0, jnp.stack([own, other]), jnp.stack([other, own])).reshape(4, LEN, 128)
-    return lax.all_to_all(both, "z", 0, 2, tiled=True)[0]
+def split_y(piece, yi):
+    return lax.dynamic_slice_in_dim(piece, yi * 128, 128, 1), lax.dynamic_slice_in_dim(piece, (1 - yi) * 128, 128, 1)
+
+
+def spread_z(own, other, yi, zi):
+    both = jnp.concatenate([own.reshape(2, LEN, 128), other.reshape(2, LEN, 128)], axis=0)
+    blocks = []
+    for mask, bits in ((0, 0), (1, Z_LOW), (2, Z_HIGH), (3, Z_LOW | Z_HIGH)):
+        block = lax.dynamic_index_in_dim(both, (zi ^ mask) ^ (yi * 2), 0, False)
+        blocks.append(swap(block, bits) if mask else block)
+    return blocks
+
+
+def assemble_body(spot, *refs):
+    blocks, (low, high) = refs[:4], refs[4:]
+    t = pl.program_id(0)
+    for out, when in ((low, t < STEPS // 2), (high, t >= STEPS // 2)):
+
+        @pl.when(when)
+        def _():
+            for mask, block in enumerate(blocks):
+                out[:, pl.ds(pl.multiple_of((spot[3] ^ mask) * 128, 128), 128)] = block[...]
+
+
+def assemble(blocks, spot):
+    half = shape_of(HALF, QUARTER, dtype=BF)
+    return elementwise(
+        assemble_body, spot, blocks, [pl.BlockSpec((STEP, 128), lambda t, p: (t, 0))] * 4, [half, half], [LOW, HIGH]
+    )
 
 
 def from_share(share, yi):
-    parts = lax.all_to_all(share[None], "z", 2, 0, tiled=True).reshape(2, 2 * LEN, 128)
+    parts = lax.all_to_all(share, "z", 0, 0, tiled=True).reshape(2, 2 * LEN, 128)
     own = lax.dynamic_index_in_dim(parts, yi, 0, False)
     other = swap(lax.dynamic_index_in_dim(parts, 1 - yi, 0, False), Y_BIT)
     return own, other
@@ -511,13 +662,14 @@
     return (low, high, x_low, x_high, y_low, y_high, xy_low, xy_high)
 
 
-def square_scatter(local, weights, spot, by_rows, before_own=()):
+def square_scatter(local, weights, spot, by_rows, first=lambda: None, between=lambda: None, after=lambda: None):
     term = functools.partial(partial, local, weights, spot, by_rows)
     far_low, far_high = term(3, BF, BF)
     far_low = swap(far_low, X_BIT)
     far_high = swap(far_high, Y_BIT)
     near_low, x_high = term(2, BF, F32)
     near_low = swap(near_low, X_BIT)
+    first()
     y_low, near_high = term(1, F32, BF)
     near_high = swap(near_high, Y_BIT)
     half = fixed((HALF, QUARTER))
@@ -527,9 +679,10 @@
     )
     last_low = swap(last_low, Y_BIT)
     last_high = swap(last_high, X_BIT)
-    if before_own:
-        local = tie(local, *before_own)
-    own_low, own_high = partial(local, weights, spot, by_rows, 0, F32, F32)
+    between()
+    spot.after(near_low, near_high)
+    own_low, own_high = term(0, F32, F32)
+    after()
     return (own_low, own_high, near_low, near_high, last_low, last_high)
 
 
@@ -537,18 +690,18 @@
     return (stats, swap(stats, X_BIT), swap(stats, Y_BIT), swap(stats, XY_BIT))
 
 
-def halve_columns(pieces, yi):
+def halve_columns(pieces, yi, *after):
     n = pieces[0].shape[1] // 2
     own = jnp.concatenate([lax.dynamic_slice_in_dim(p, yi * n, n, 1) for p in pieces], axis=1)
-    other = jnp.concatenate([lax.dynamic_slice_in_dim(p, (1 - yi) * n, n, 1) for p in pieces], axis=1)
-    return jnp.concatenate([own, swap(other, Y_BIT)], axis=0)
-
-
-def halve_rows(piece, yi):
+    send = tie(jnp.concatenate([lax.dynamic_slice_in_dim(p, (1 - yi) * n, n, 1) for p in pieces], axis=1), *after)
+    return jnp.concatenate([own, swap(send, Y_BIT)], axis=0), send
+
+
+def halve_rows(piece, yi, *after):
     n = piece.shape[0] // 2
     own = lax.dynamic_slice_in_dim(piece, yi * n, n, 0)
-    other = lax.dynamic_slice_in_dim(piece, (1 - yi) * n, n, 0)
-    return jnp.concatenate([own, swap(other, Y_BIT)], axis=1)
+    send = tie(lax.dynamic_slice_in_dim(piece, (1 - yi) * n, n, 0), *after)
+    return jnp.concatenate([own, swap(send, Y_BIT)], axis=1), send
 
 
 def gather_zc(piece):
@@ -559,17 +712,24 @@
     return lax.psum_scatter(full, ("z", "c"), scatter_dimension=0)
 
 
-def restore_columns(piece, count, yi):
-    other = swap(piece[512:], Y_BIT)
-    n = piece.shape[1] // count
+def exchange_columns(piece):
+    return piece[:512], swap(piece[512:], Y_BIT)
+
+
+def exchange_rows(piece):
+    return piece[:, :512], swap(piece[:, 512:], Y_BIT)
+
+
+def restore_columns(pair, count, yi):
+    own, other = pair
+    n = own.shape[1] // count
     return [
-        side_by_side(piece[:512, i * n : (i + 1) * n], other[:, i * n : (i + 1) * n], yi, 1).astype(F32)
-        for i in range(count)
+        side_by_side(own[:, i * n : (i + 1) * n].astype(F32), other[:, i * n : (i + 1) * n].astype(F32), yi, 1) for i in range(count)
     ]
 
 
-def restore_rows(piece, yi):
-    return side_by_side(piece[:, :512], swap(piece[:, 512:], Y_BIT), yi, 0).astype(F32)
+def restore_rows(pair, yi):
+    return side_by_side(pair[0].astype(F32), pair[1].astype(F32), yi, 0)
 
 
 def square_device(
@@ -578,26 +738,11 @@
 ):
     yi = lax.axis_index("y")
     zi = lax.axis_index("z")
-    spot = jnp.stack([lax.axis_index("x") * 2 + yi, yi]).astype(jnp.int32)
-
-    token_own, token_other = to_share(tokens, yi)
-    half_qkv = halve_columns([w_query, w_key, w_value], yi)
-    half_proj = halve_rows(tie(w_proj, half_qkv), yi)
-    half_up = halve_columns([tie(w_up, half_proj)], yi)
-    half_down = halve_rows(tie(w_down, half_up), yi)
-    full_qkv = gather_zc(half_qkv)
-    token_share = to_share_rest(token_own, token_other, yi)
-    full_proj = gather_zc(half_proj)
-    full_up = gather_zc(half_up)
-    full_down = gather_zc(half_down)
-    dy_own, dy_other = to_share(tie(cotangent, half_down), yi)
-    dy = to_share_rest(dy_own, dy_other, yi)
-
-    both = side_by_side(lengths, swap(lengths, Y_BIT), yi, 0)
-    ids = segment_ids(lax.dynamic_slice_in_dim(both, zi, 1, 0))[0]
-    valid = (ids != lengths.shape[1] - 1).astype(F32)
-    ids_row, ids_column = ids[None], ids[:, None]
-
+    spot = Order(jnp.stack([lax.axis_index("x") * 2 + yi, yi, lax.axis_index("c"), zi]).astype(jnp.int32))
+
+    token_own, token_send = split_y(tokens, yi)
+    token_other = swap(token_send, Y_BIT)
+    half_qkv, sent = halve_columns([w_query, w_key, w_value], yi, token_send)
     vectors = jnp.concatenate(
         [v.reshape(2, -1) for v in (b_query, b_value, b_proj, norm_gain, norm_shift, b_down, final_gain, final_shift, b_up)],
         axis=1,
@@ -610,7 +755,21 @@
     u_bias = vectors[:, 1024:].reshape(1, -1)
     qkv_bias = jnp.stack([q_bias, jnp.zeros_like(q_bias), v_bias], axis=1).reshape(1, -1)
 
-    gathered = square_gather(token_share[:HALF], token_share[HALF:])
+    both = side_by_side(lengths, swap(lengths, Y_BIT), yi, 0)
+    ids = segment_ids(lax.dynamic_slice_in_dim(both, zi, 1, 0))[0]
+    valid = (ids != lengths.shape[1] - 1).astype(F32)
+    ids_row, ids_column = ids[None], ids[:, None]
+
+    full_qkv = gather_zc(tie(half_qkv, vectors))
+    token_blocks = spread_z(token_own, token_other, yi, zi)
+    half_proj, sent = halve_rows(w_proj, yi, sent)
+    half_up, sent = halve_columns([w_up], yi, sent)
+    half_down, sent = halve_rows(w_down, yi, sent)
+    token_low, token_high = assemble(token_blocks, spot)
+    gathered = square_gather(token_low, token_high)
+    full_proj = gather_zc(tie(half_proj, token_low))
+    full_up = gather_zc(tie(half_up, token_low))
+    full_down = gather_zc(tie(half_down, token_low))
     (qkv,) = wide(gathered, full_qkv, spot, False, finish_bias, (qkv_bias,), 1)
     heads_out, logsum = attention(qkv, ids_row, ids_column, spot)
     full = shape_of(LEN, QUARTER)
@@ -620,91 +779,103 @@
 
     parts = square_scatter(heads_out, full_proj, spot, True)
     resid, stats_one = elementwise(
-        norm_one_sums, spot, (*parts, token_share, p_bias), [HALVES] * 6 + [TILE, VECTOR], [full, stats_shape], [TILE, STATS]
+        norm_one_sums, spot, (*parts, token_low, token_high, p_bias), PARTS + [LOW, HIGH, VECTOR], [full, stats_shape], [TILE, STATS]
     )
     hidden_low, hidden_high, moments = elementwise(
         norm_one, spot, (resid, *square_stats(stats_one), n_gain, n_shift), [TILE] + [STATS] * 4 + [VECTOR] * 2,
-        [low_half, low_half, stats_shape], [HALVES, HALVES, STATS],
+        [low_half, low_half, stats_shape], [LOW, HIGH, STATS],
     )
     hidden_wide = square_gather(hidden_low, hidden_high)
+    dy_own, dy_send = split_y(tie(cotangent, hidden_low), yi)
+    dy_other = swap(dy_send, Y_BIT)
     act, slope = wide(hidden_wide, full_up, spot, False, finish_gelu, (u_bias,), 2)
-    parts = square_scatter(act, full_down, spot, True)
+    dy_blocks = spread_z(tie(dy_own, full_down), dy_other, yi, zi)
+    dy_halves = []
+    parts = square_scatter(act, full_down, spot, True, between=lambda: dy_halves.extend(assemble(dy_blocks, spot)))
     resid_two, stats_two = elementwise(
-        norm_two_sums, spot, (*parts, d_bias, resid, moments, n_gain, n_shift, dy, f_gain),
-        [HALVES] * 6 + [VECTOR, TILE, STATS, VECTOR, VECTOR, TILE, VECTOR], [full, stats_shape], [TILE, STATS],
+        norm_two_sums, spot, (*parts, d_bias, resid, moments, n_gain, n_shift, *dy_halves, f_gain),
+        PARTS + [VECTOR, TILE, STATS, VECTOR, VECTOR, LOW, HIGH, VECTOR], [full, stats_shape], [TILE, STATS],
     )
     layer_share, grad_two, ffn_low, ffn_high, sums_two = elementwise(
-        norm_two, spot, (resid_two, *square_stats(stats_two), dy, f_gain, f_shift),
-        [TILE] + [STATS] * 4 + [TILE, VECTOR, VECTOR],
-        [shape_of(LEN, QUARTER, dtype=BF), full, low_half, low_half, sums_shape], [TILE, TILE, HALVES, HALVES, SUMS],
+        norm_two, spot, (resid_two, *square_stats(stats_two), *dy_halves, f_gain, f_shift),
+        [TILE] + [STATS] * 4 + [LOW, HIGH, VECTOR, VECTOR],
+        [shape_of(4, LEN, 128, dtype=BF), full, low_half, low_half, sums_shape], [BLOCKS, TILE, LOW, HIGH, SUMS],
     )
     ffn_wide = square_gather(ffn_low, ffn_high)
     layer_own, layer_other = from_share(layer_share, yi)
     layer_out = side_by_side(layer_own, layer_other, yi, 1)
 
-    (grad_pre,) = wide(ffn_wide, full_down, spot, True, finish_slope, (slope,), 1)
-    grad_down = grad(ffn_wide, act, spot, True)
-    grad_up = grad(hidden_wide, grad_pre, spot, False)
-    parts = square_scatter(grad_pre, full_up, spot, False, (grad_down,))
-    sum_down = scatter_zc(grad_down)
-    grad_ubias = jnp.sum(grad_pre.astype(F32), axis=0)
+    spot.after(layer_own)
+    grad_down = scatter_zc(grad_whole(ffn_wide, act, spot, True))
+    grad_pre, sums_up = wide(ffn_wide, full_down, spot, True, finish_slope, (slope,), 1, 1)
+    up = []
+    parts = square_scatter(
+        grad_pre, full_up, spot, False, between=lambda: up.append(grad_whole(hidden_wide, grad_pre, spot, False))
+    )
+    grad_up = scatter_zc(up[0])
     grad_hidden, stats_back, sums_back = elementwise(
         back_one_sums, spot, (*parts, grad_two, resid, moments, n_gain),
-        [HALVES] * 6 + [TILE, TILE, STATS, VECTOR], [full, stats_shape, sums_shape], [TILE, STATS, SUMS],
+        PARTS + [TILE, TILE, STATS, VECTOR], [full, stats_shape, sums_shape], [TILE, STATS, SUMS],
     )
     grad_one, attn_low, attn_high, sums_attn = elementwise(
         back_one, spot, (grad_hidden, *square_stats(stats_back), resid, moments, n_gain),
         [TILE] + [STATS] * 4 + [TILE, STATS, VECTOR],
-        [full, low_half, low_half, sums_shape], [TILE, HALVES, HALVES, SUMS],
+        [full, low_half, low_half, sums_shape], [TILE, LOW, HIGH, SUMS],
     )
     attn_wide = square_gather(attn_low, attn_high)
-    sum_up = scatter_zc(grad_up)
+    spot.after(grad_down)
     (grad_heads,) = wide(attn_wide, full_proj, spot, True, finish_plain, (), 1)
-    grad_proj = grad(attn_wide, heads_out, spot, True)
-    grad_qkv = attention_back(qkv, ids_row, ids_column, logsum, tie(grad_heads, grad_up), spot)
-    sum_proj = scatter_zc(grad_proj)
-    grad_wqkv = grad(gathered, grad_qkv, spot, False)
-    parts = square_scatter(grad_qkv, full_qkv, spot, False, (grad_wqkv,))
-    sum_qkv = scatter_zc(grad_wqkv)
-    (back,) = elementwise(
-        finish_back, spot, (*parts, grad_one), [HALVES] * 6 + [TILE], [shape_of(LEN, QUARTER, dtype=BF)], [TILE]
-    )
-    back_own, back_other = from_share(back, yi)
-    grad_tokens = side_by_side(back_own, back_other, yi, 1).astype(F32)
-    sums_qkv = jnp.sum(grad_qkv.astype(F32), axis=0).reshape(4, 3, HD)
-
-    grad_down = restore_rows(sum_down, yi)
-    (grad_up,) = restore_columns(sum_up, 1, yi)
-    grad_proj = restore_rows(sum_proj, yi)
-    grad_query, grad_key, grad_value = restore_columns(sum_qkv, 3, yi)
-
+    grad_qkv, sums_qkv = attention_back(qkv, ids_row, ids_column, logsum, grad_heads, spot)
+    qkv_sum = Sum(grad(gathered, grad_qkv, spot, False), spot, False)
+    qkv_sum.go(C_BIT)
+
+    totals = jnp.stack([stats_one[3] * valid, stats_one[2] * valid, stats_two[4] * valid, valid * QUARTER])
+    totals = jnp.pad(jnp.sum(totals, axis=1)[None], ((0, 3), (0, 124)))
     sums = jnp.concatenate(
         [
             v.reshape(4, -1)
             for v in (
-                sums_qkv[:, 0], sums_qkv[:, 2], sums_attn[0], sums_back[0], sums_back[1], sums_two[2], sums_two[0], sums_two[1],
-                grad_ubias,
+                *(sums_qkv[0].reshape(4, 3, HD)[:, i] for i in (0, 2)),
+                sums_attn[0], sums_back[0], sums_back[1], sums_two[2], sums_two[0], sums_two[1], sums_up[0], totals,
             )
         ],
         axis=1,
     )
-    sums = jnp.sum(lax.all_to_all(sums, "z", 0, 0, tiled=True), axis=0)
-    sums = sums + swap(sums, C_BIT)
-    other = swap(sums, Y_BIT)
+    for mask in (C_BIT, Z_LOW, Z_HIGH):
+        sums = sums + swap(sums, mask)
+    proj = []
+
+    def first():
+        qkv_sum.step()
+        qkv_sum.go(Z_LOW)
+
+    def between():
+        proj.append(scatter_zc(grad_whole(attn_wide, heads_out, spot, True)))
+
+    parts = square_scatter(grad_qkv, full_qkv, spot, False, first=first, between=between)
+    (grad_proj,) = proj
+    spot.after(grad_up)
+    (back,) = elementwise(
+        finish_back, spot, (*parts, grad_one), PARTS + [TILE], [shape_of(4, LEN, 128, dtype=BF)], [BLOCKS]
+    )
+    down, up, proj = exchange_rows(grad_down), exchange_columns(grad_up), exchange_rows(grad_proj)
+    qkv_sum.step()
+    qkv_sum.go(Z_HIGH)
+    back_own, back_other = from_share(back, yi)
+    qkv_sum = qkv_sum.last()
+    last = qkv_sum[0]
+    totals = sums[0, 1536:] + swap(sums[0, 1536:], Y_BIT)
+    totals = totals + tie(swap(totals, X_BIT), last)
+    norms = jnp.sqrt(totals[:3] / totals[3])
+    sums = lax.dynamic_index_in_dim(sums, zi, 0, False)
+    other = tie(swap(sums, Y_BIT), last)
     sums = jnp.where(yi == 0, jnp.stack([sums, other]), jnp.stack([other, sums]))
-    vecs = [sums[:, i * 128 : (i + 1) * 128].reshape(-1) for i in range(8)] + [sums[:, 1024:].reshape(-1)]
-
-    totals = jnp.stack(
-        [
-            jnp.sum(valid * stats_one[3]),
-            jnp.sum(valid * stats_one[2]),
-            jnp.sum(valid * stats_two[4]),
-            jnp.sum(valid) * QUARTER,
-        ]
-    )
-    for mask in (X_BIT, Z_LOW, Z_HIGH, C_BIT, Y_BIT):
-        totals = totals + swap(totals, mask)
-    norms = jnp.sqrt(totals[:3] / totals[3])
+    vecs = [sums[:, i * 128 : (i + 1) * 128].reshape(-1) for i in range(8)] + [sums[:, 1024:1536].reshape(-1)]
+    grad_tokens = side_by_side(back_own, tie(back_other, last), yi, 1).astype(F32)
+    grad_down = restore_rows(down, yi)
+    (grad_up,) = restore_columns(up, 1, yi)
+    grad_proj = restore_rows((proj[0], tie(proj[1], last)), yi)
+    grad_query, grad_key, grad_value = restore_columns(qkv_sum, 3, yi)
     return (
         layer_out, grad_tokens, grad_query, vecs[0], grad_key, grad_value, vecs[1], grad_proj, vecs[2], vecs[3], vecs[4],
         grad_up, vecs[8], grad_down, vecs[5], vecs[6], vecs[7], norms,

time: 945 us -> 835 us (0.88)
  waiting for transfers between devices: 397 us -> 299 us
  Pallas kernels: 298 us -> 330 us
  local copies, waits for them, and re-layouts: 56.7 us -> 36.4 us
  other arithmetic: 41.8 us -> 25.7 us
  starting transfers between devices: 122 us -> 111 us
  blocking collectives: 0 us -> 10.3 us
    reduce_scatter x4 -> x3, waiting for transfers between devices: 79.9 us -> 0.02 us  [scatter_zc(): return lax.psum_scatter(full, ('z', 'c'), scatter_dimension=0)]
    all_to_all x6 -> x2, waiting for transfers between devices: 67.1 us -> 5.46 us  [from_share(): lax.all_to_all(share, 'z', 0, 0, tiled=True).reshape(2, 2 * LEN, 128)]
    ppermute x77 -> x85, waiting for transfers between devices: 224 us -> 284 us  [swap(): return lax.ppermute(piece, AXES, [(i, i ^ mask) for i in range(32)])]
    pallas_call x37 -> x42, Pallas kernels: 298 us -> 330 us  [call(): pl.pallas_call(body, grid_spec=pltpu.PrefetchScalarGridSpec(num_scalar_pr...]
    all_to_all x6 -> x2, starting transfers between devices: 26.8 us -> 10.1 us  [from_share(): lax.all_to_all(share, 'z', 0, 0, tiled=True).reshape(2, 2 * LEN, 128)]
    all_gather x4, waiting for transfers between devices: 24.5 us -> 9.71 us  [gather_zc(): return lax.all_gather(piece, ('z', 'c'), axis=0)]
    unnamed x2 -> x0, other arithmetic: 13.6 us -> none
    all_to_all x0 -> x1, blocking collectives: none -> 10.3 us  [square_device(): lax.all_to_all(jnp.broadcast_to(vectors, (4, vectors.shape[1])), 'z', 0,...]
  transfers between devices with their start and end apart: 91 -> 94, of which waited for: 45 -> 45; matrix products, arithmetic and copies ran while one was open for 9% -> 5% of each run, Pallas kernels for 26% -> 34%
where the time goes in v3:
time: 835 us; the launch traced here: 828 us
  Pallas kernels  330 us (40%)
  waiting for transfers between devices  299 us (36%)
  starting transfers between devices  111 us (13%)
  local copies, waits for them, and re-layouts  36.4 us (4%)
  other arithmetic  25.7 us (3%)
  between operations  15.4 us (2%)
  blocking collectives  10.3 us (1%)
    pallas_call x42, Pallas kernels, call(): pl.pallas_call(body, grid_spec=pltpu.PrefetchScalarGridSpec(num_scalar_pr...  330 us
    ppermute x85, waiting for transfers between devices, swap(): return lax.ppermute(piece, AXES, [(i, i ^ mask) for i in range(32)])  284 us
    ppermute x85, starting transfers between devices, swap(): return lax.ppermute(piece, AXES, [(i, i ^ mask) for i in range(32)])  101 us
    unnamed x208, local copies, waits for them, and re-layouts  18.1 us
  transfers between devices with their start and end apart: 94, of which 45 were waited for; matrix products, arithmetic and copies ran while one was open for 5% of the time, Pallas kernels for 34%

profile of v3, /device:TPU:0, one launch (start us, length us, event | category | flops | bytes accessed | tf_op | source)
XLA Modules:
  0.0 828.3 jit_solution(17104719139154917771)
XLA Ops:
  13.2 10.3 %all_to_all.19 = f32[4,1,1536]{2,1,0:T(1,128)S(1)} all-to-all(f32[4,1,1536]{2,1,0:T(1,128)S(1)} %broadcast_in_dim.4), channel_id=1, replica_groups=mesh['y'=2,'c'=2,'z'=4,'x'=2] {'z'}, dimensions={0} | all-to-all | bytes 49152 | tf_op jit(solution)/shard_map/all_to_all | solution.py:751
  25.7 11.4 %collective-permute-done = bf16[2048,128]{1,0:T(8,128)(2,1)S(1)} collective-permute-done((bf16[2048,128]{1,0:T(8,128)(2,1)S(1)}, bf16[2048,128]{1,0:T(8,128)(2,1)S(1)}, u32[]{:S(2)}, u32[]{:S(2)}) %collective-permute-start) | collective-permute-done | bytes 524320 | tf_op jit(solution)/shard_map/ppermute | solution.py:37
  49.5 5.6 collective-permute-done.3.refs_3_
  55.1 10.3 %collective-permute-done.1.refs_1_ = bf16[1024,128]{1,0:T(8,128)(2,1)S(1)} collective-permute-done((bf16[1024,128]{1,0:T(8,128)(2,1)}, bf16[1024,128]{1,0:T(8,128)(2,1)S(1)}, u32[]{:S(2)}, u32[]{:S(2)}) %collective-permute-start.1) | collective-permute-done | bytes 262176 | tf_op jit(solution)/shard_map/ppermute | solution.py:37
  65.4 25.9 %collective-permute-done.2.refs_2_ = bf16[1024,128]{1,0:T(8,128)(2,1)S(1)} collective-permute-done((bf16[1024,128]{1,0:T(8,128)(2,1)S(1)}, bf16[1024,128]{1,0:T(8,128)(2,1)S(1)}, u32[]{:S(2)}, u32[]{:S(2)}) %collective-permute-start.2) | collective-permute-done | bytes 262176 | tf_op jit(solution)/shard_map/ppermute | solution.py:37
  91.9 4.2 shard_map.313
  98.0 8.5 %collective-permute-done.28 = bf16[512,512]{1,0:T(8,128)(2,1)S(1)} collective-permute-done((bf16[512,512]{1,0:T(8,128)(2,1)S(1)}, bf16[512,512]{1,0:T(8,128)(2,1)S(1)}, u32[]{:S(2)}, u32[]{:S(2)}) %collective-permute-start.28) | collective-permute-done | bytes 524320 | tf_op jit(solution)/shard_map/ppermute | solution.py:37
  116.3 19.7 %collective-permute-done.7.refs_5_ = bf16[512,512]{1,0:T(8,128)(2,1)} collective-permute-done((bf16[512,512]{1,0:T(8,128)(2,1)S(1)}, bf16[512,512]{1,0:T(8,128)(2,1)}, u32[]{:S(2)}, u32[]{:S(2)}) %collective-permute-start.7) | collective-permute-done | bytes 524320 | tf_op jit(solution)/shard_map/ppermute | solution.py:37
  140.1 6.2 collective-permute-done.6.refs_4_
  146.3 5.6 collective-permute-done.8.refs_6_
  151.9 16.0 %shard_map.314.queries.whole = bf16[1024,1536]{1,0:T(8,128)(2,1)} custom-call(s32[4]{0:T(128)} %pad_add_fusion.spot, bf16[512,512]{1,0:T(8,128)(2,1)} %get-tuple-element.161.refs_0_.refs_6_, bf16[512,512]{1,0:T(8,128)(2,1)} %get-tuple-element.163.refs_1_.refs_7_, bf16[512,512]{1,0:T(8,128)(2,1)} %collective-permute-done.4.refs_2_, ...), custom_call_target="tpu_custom_call" | custom-call | flops 64424509440 | bytes 136314880 | tf_op jit(solution)/shard_map/pallas_call | solution.py:60
  167.9 12.9 %shard_map.315 = (bf16[1024,512]{1,0:T(8,128)(2,1)}, f32[4,1,1024]{2,1,0:T(1,128)}) custom-call(s32[4]{0:T(128)} %pad_add_fusion.spot, bf16[1024,1536]{1,0:T(8,128)(2,1)} %shard_map.314.queries.whole, bf16[1024,1536]{1,0:T(8,128)(2,1)} %shard_map.314.queries.whole, s32[1,1024]{1,0:T(1,128)} %bitcast.141, s32[1024,1]{1,0:T(8,128)} %copy.46.ids_column), custom_call_target="tpu_custom_call" | custom-call | flops 85899345920 | bytes 41943040 | tf_op jit(solution)/shard_map/pallas_call | solution.py:60
  180.9 4.3 shard_map.316
  186.8 4.5 shard_map.317
  193.1 4.5 shard_map.318
  198.3 8.3 collective-permute-done.14.fourth
  216.8 4.7 shard_map.320
  223.2 5.8 shard_map.321
  236.8 5.1 shard_map.322
  246.0 11.0 %collective-permute-done.25.refs_5_ = bf16[512,512]{1,0:T(8,128)(2,1)S(1)} collective-permute-done((bf16[512,512]{1,0:T(8,128)(2,1)}, bf16[512,512]{1,0:T(8,128)(2,1)S(1)}, u32[]{:S(2)}, u32[]{:S(2)}) %collective-permute-start.25) | collective-permute-done | bytes 524320 | tf_op jit(solution)/shard_map/ppermute | solution.py:37
  271.1 4.8 collective-permute-done.26.refs_6_
  276.7 20.3 %shard_map.323 = (bf16[1024,2048]{1,0:T(8,128)(2,1)}, bf16[1024,2048]{1,0:T(8,128)(2,1)}) custom-call(s32[4]{0:T(128)} %pad_add_fusion.spot, bf16[512,512]{1,0:T(8,128)(2,1)} %get-tuple-element.190.refs_0_, bf16[512,512]{1,0:T(8,128)(2,1)} %get-tuple-element.192.refs_1_, bf16[512,512]{1,0:T(8,128)(2,1)} %copy-done.72, bf16[512,512]{1,0:T(8,128)(2,1)} %copy-done.73, ...), custom_call_target="tpu_custom_call" | custom-call | flops 85899345920 | bytes 167772160 | tf_op jit(solution)/shard_map/pallas_call | solution.py:60
  297.0 9.7 %all-gather.15.cloned.1.call-done = bf16[4096,1024]{1,0:T(8,128)(2,1)} async-done(((bf16[512,1024]{1,0:T(8,128)(2,1)}), bf16[4096,1024]{1,0:T(8,128)(2,1)}) %all-gather.15.cloned.1.call-update) | async-done | bytes 8388624 | tf_op jit(solution)/shard_map/all_gather | solution.py:708
  306.7 6.5 shard_map.324
  314.7 6.7 shard_map.325
  323.4 6.8 shard_map.326
  332.9 4.0 collective-permute-start.35
  345.8 4.7 collective-permute-done.33.refs_1_
  350.5 5.8 collective-permute-done.34.refs_2_
  357.0 4.2 shard_map.328
  362.7 6.8 shard_map.329
  373.6 6.6 shard_map.330
  388.3 6.5 shard_map.331
  394.8 5.5 all-to-all-start.1
  404.5 10.8 %collective-permute-done.44.refs_2_ = bf16[512,512]{1,0:T(8,128)(2,1)S(1)} collective-permute-done((bf16[512,512]{1,0:T(8,128)(2,1)S(1)}, bf16[512,512]{1,0:T(8,128)(2,1)S(1)}, u32[]{:S(2)}, u32[]{:S(2)}) %collective-permute-start.44) | collective-permute-done | bytes 524320 | tf_op jit(solution)/shard_map/ppermute | solution.py:37
  417.3 5.5 all-to-all-done.1
  427.3 6.3 collective-permute-done.48.refs_6_
  433.6 15.9 %shard_map.332 = bf16[4,2,512,1024]{3,2,1,0:T(8,128)(2,1)} custom-call(s32[4]{0:T(128)} %pad_add_fusion.spot, bf16[512,512]{1,0:T(8,128)(2,1)} %get-tuple-element.227.refs_0_, bf16[512,512]{1,0:T(8,128)(2,1)} %get-tuple-element.228.refs_1_, bf16[512,512]{1,0:T(8,128)(2,1)} %copy-done.86, bf16[512,512]{1,0:T(8,128)(2,1)} %collective-permute-done.45.refs_3_, ...), custom_call_target="tpu_custom_call" | custom-call | flops 85899345920 | bytes 167772160 | tf_op jit(solution)/shard_map/pallas_call | solution.py:60
  449.5 19.3 %shard_map.333 = (bf16[1024,2048]{1,0:T(8,128)(2,1)}, f32[8,2048]{1,0:T(8,128)}) custom-call(s32[4]{0:T(128)} %pad_add_fusion.spot, bf16[512,512]{1,0:T(8,128)(2,1)} %get-tuple-element.227.refs_0_, bf16[512,512]{1,0:T(8,128)(2,1)} %get-tuple-element.228.refs_1_, bf16[512,512]{1,0:T(8,128)(2,1)} %copy-done.86, ...), custom_call_target="tpu_custom_call" | custom-call | flops 85899345920 | bytes 167772160 | tf_op jit(solution)/shard_map/pallas_call | solution.py:60
  468.8 7.0 shard_map.334
  476.9 6.7 shard_map.335
  485.7 6.8 shard_map.336
  493.5 4.5 collective-permute-done.51.fourth
  506.0 14.0 %shard_map.338 = bf16[4,2,2,512,512]{4,3,2,1,0:T(8,128)(2,1)} custom-call(s32[4]{0:T(128)} %pad_add_fusion.spot, bf16[512,512]{1,0:T(8,128)(2,1)} %get-tuple-element.190.refs_0_, bf16[512,512]{1,0:T(8,128)(2,1)} %get-tuple-element.192.refs_1_, bf16[512,512]{1,0:T(8,128)(2,1)} %copy-done.72, bf16[512,512]{1,0:T(8,128)(2,1)} %copy-done.73, ...), custom_call_target="tpu_custom_call" | custom-call | flops 85899345920 | bytes 167772160 | tf_op jit(solution)/shard_map/pallas_call | solution.py:60
  520.1 6.9 shard_map.339
  528.0 6.8 shard_map.340
  541.7 6.3 shard_map.341
  553.6 7.6 collective-permute-done.59.refs_2_
  573.3 5.6 collective-permute-done.63.refs_6_
  580.6 11.4 %shard_map.342.grad_out = bf16[1024,512]{1,0:T(8,128)(2,1)} custom-call(s32[4]{0:T(128)} %pad_add_fusion.spot, bf16[512,512]{1,0:T(8,128)(2,1)} %get-tuple-element.257.refs_0_, bf16[512,512]{1,0:T(8,128)(2,1)} %get-tuple-element.258.refs_1_, bf16[512,512]{1,0:T(8,128)(2,1)} %copy-done.77, bf16[512,512]{1,0:T(8,128)(2,1)} %copy-done.80, ...), custom_call_target="tpu_custom_call" | custom-call | flops 21474836480 | bytes 73400320 | tf_op jit(solution)/shard_map/pallas_call | solution.py:60
  591.9 23.2 %shard_map.343 = (bf16[1024,1536]{1,0:T(8,128)(2,1)}, f32[8,1536]{1,0:T(8,128)}) custom-call(s32[4]{0:T(128)} %pad_add_fusion.spot, bf16[1024,1536]{1,0:T(8,128)(2,1)} %shard_map.314.queries.whole, bf16[1024,1536]{1,0:T(8,128)(2,1)} %shard_map.314.queries.whole, s32[1,1024]{1,0:T(1,128)} %bitcast.142, s32[1024,1]{1,0:T(8,128)} %copy.46.ids_column, ...), custom_call_target="tpu_custom_call" | custom-call | flops 161061273600 | bytes 83886080 | tf_op jit(solution)/shard_map/pallas_call | solution.py:60
  615.1 13.9 %shard_map.344 = (bf16[4,2,512,384]{3,2,1,0:T(8,128)(2,1)}, bf16[4,2,512,384]{3,2,1,0:T(8,128)(2,1)}) custom-call(s32[4]{0:T(128)} %pad_add_fusion.spot, bf16[512,512]{1,0:T(8,128)(2,1)} %get-tuple-element.161.refs_0_.refs_6_, bf16[512,512]{1,0:T(8,128)(2,1)} %get-tuple-element.163.refs_1_.refs_7_, bf16[512,512]{1,0:T(8,128)(2,1)} %collective-permute-done.4.refs_2_, ...), custom_call_target="tpu_custom_call" | custom-call | flops 64424509440 | bytes 136314880 | tf_op jit(solution)/shard_map/pallas_call | solution.py:60
  629.2 6.2 shard_map.345
  637.8 6.4 shard_map.346
  648.1 5.6 shard_map.347
  653.7 6.5 shard_map.348
  666.6 7.3 shard_map.350
  675.3 14.1 %collective-permute-done.69.refs_3_ = bf16[512,512]{1,0:T(8,128)(2,1)S(1)} collective-permute-done((bf16[512,512]{1,0:T(8,128)(2,1)S(1)}, bf16[512,512]{1,0:T(8,128)(2,1)S(1)}, u32[]{:S(2)}, u32[]{:S(2)}) %collective-permute-start.69) | collective-permute-done | bytes 524320 | tf_op jit(solution)/shard_map/ppermute | solution.py:37
  690.9 6.6 shard_map.351
  698.5 5.6 shard_map.352
  704.1 4.6 all-to-all-start.2
  715.6 36.6 %collective-permute-done.78 = f32[4,1664]{1,0:T(4,128)S(1)} collective-permute-done((f32[4,1664]{1,0:T(4,128)S(1)}, f32[4,1664]{1,0:T(4,128)S(1)}, u32[]{:S(2)}, u32[]{:S(2)}) %collective-permute-start.78) | collective-permute-done | bytes 26656 | tf_op jit(solution)/shard_map/ppermute | solution.py:37
  775.9 22.7 %collective-permute-done.74.c.d = bf16[1,1024,384]{2,1,0:T(8,128)(2,1)S(1)} collective-permute-done((bf16[1,1024,384]{2,1,0:T(8,128)(2,1)}, bf16[1,1024,384]{2,1,0:T(8,128)(2,1)S(1)}, u32[]{:S(2)}, u32[]{:S(2)}) %collective-permute-start.74) | collective-permute-done | bytes 786464 | tf_op jit(solution)/shard_map/ppermute | solution.py:37
  808.9 4.6 collective-permute-done.75
  (452 shorter events, 223.9 us)
Async XLA Ops:
  7.2 144.7 %all-gather.9.cloned.1.call-start = ((), (), s32[]{:S(2)}) async-start(), calls=%async_computation.9 | async-start | bytes 7077888 | tf_op jit(solution)/shard_map/all_gather | solution.py:708
  25.1 155.8 %all-gather.11.cloned.1.call-start = ((), (), s32[]{:S(2)}) async-start(), calls=%async_computation.10 | async-start | bytes 2359296 | tf_op jit(solution)/shard_map/all_gather | solution.py:708
  38.3 16.8 %collective-permute-start.3 = (bf16[1024,128]{1,0:T(8,128)(2,1)}, bf16[1024,128]{1,0:T(8,128)(2,1)S(1)}, u32[]{:S(2)}, u32[]{:S(2)}) collective-permute-start(bf16[1024,128]{1,0:T(8,128)(2,1)} %get-tuple-element.324), channel_id=1, source_target_pairs={{0,6},{1,7},{2,4},{3,5},{4,2},{5,3},{6,0},{7,1},{8,14},{9,15},{10,... | collective-permute-start | bytes 786440 | tf_op jit(solution)/shard_map/ppermute | solution.py:37
  41.0 24.4 %collective-permute-start.1 = (bf16[1024,128]{1,0:T(8,128)(2,1)}, bf16[1024,128]{1,0:T(8,128)(2,1)S(1)}, u32[]{:S(2)}, u32[]{:S(2)}) collective-permute-start(bf16[1024,128]{1,0:T(8,128)(2,1)} %get-tuple-element.326), channel_id=1, source_target_pairs={{0,2},{1,3},{2,0},{3,1},{4,6},{5,7},{6,4},{7,5},{8,10},{9,11},{10,... | collective-permute-start | bytes 786440 | tf_op jit(solution)/shard_map/ppermute | solution.py:37
  41.0 50.3 %collective-permute-start.2 = (bf16[1024,128]{1,0:T(8,128)(2,1)S(1)}, bf16[1024,128]{1,0:T(8,128)(2,1)S(1)}, u32[]{:S(2)}, u32[]{:S(2)}) collective-permute-start(bf16[1024,128]{1,0:T(8,128)(2,1)S(1)} %get-tuple-element.327), channel_id=1, source_target_pairs={{0,4},{1,5},{2,6},{3,7},{4,0},{5,1},{6,2},{7,3},{8,12},{9,13},{10,... | collective-permute-start | bytes 786440 | tf_op jit(solution)/shard_map/ppermute | solution.py:37
  96.1 179.7 %all-gather.13.cloned.1.call-start = ((), (), s32[]{:S(2)}) async-start(), calls=%async_computation.11 | async-start | bytes 9437184 | tf_op jit(solution)/shard_map/all_gather | solution.py:708
  107.6 199.1 %all-gather.15.cloned.1.call-start = ((), (), s32[]{:S(2)}) async-start(), calls=%async_computation.12 | async-start | bytes 9437184 | tf_op jit(solution)/shard_map/all_gather | solution.py:708
  109.8 29.1 %collective-permute-start.29 = (bf16[512,512]{1,0:T(8,128)(2,1)S(1)}, bf16[512,512]{1,0:T(8,128)(2,1)S(1)}, u32[]{:S(2)}, u32[]{:S(2)}) collective-permute-start(bf16[512,512]{1,0:T(8,128)(2,1)S(1)} %get-tuple-element.197), channel_id=1, source_target_pairs={{0,16},{1,17},{2,18},{3,19},{4,20},{5,21},{6,22},{7,23},{8,24},{9,... | collective-permute-start | bytes 1572872 | tf_op jit(solution)/shard_map/ppermute | solution.py:37
  109.9 27.6 %collective-permute-start.4 = (bf16[512,512]{1,0:T(8,128)(2,1)S(1)}, bf16[512,512]{1,0:T(8,128)(2,1)}, u32[]{:S(2)}, u32[]{:S(2)}) collective-permute-start(bf16[512,512]{1,0:T(8,128)(2,1)S(1)} %copy-done.9), channel_id=1, source_target_pairs={{0,1},{1,0},{2,3},{3,2},{4,5},{5,4},{6,7},{7,6},{8,9},{9,8},{10,11... | collective-permute-start | bytes 1572872 | tf_op jit(solution)/shard_map/ppermute | solution.py:37
  111.5 24.5 %collective-permute-start.7 = (bf16[512,512]{1,0:T(8,128)(2,1)S(1)}, bf16[512,512]{1,0:T(8,128)(2,1)}, u32[]{:S(2)}, u32[]{:S(2)}) collective-permute-start(bf16[512,512]{1,0:T(8,128)(2,1)S(1)} %copy-done.10), channel_id=1, source_target_pairs={{0,16},{1,17},{2,18},{3,19},{4,20},{5,21},{6,22},{7,23},{8,24},{9,... | collective-permute-start | bytes 1572872 | tf_op jit(solution)/shard_map/ppermute | solution.py:37
  114.8 25.3 %collective-permute-start.5 = (bf16[512,512]{1,0:T(8,128)(2,1)S(1)}, bf16[512,512]{1,0:T(8,128)(2,1)}, u32[]{:S(2)}, u32[]{:S(2)}) collective-permute-start(bf16[512,512]{1,0:T(8,128)(2,1)S(1)} %copy-done.10), channel_id=1, source_target_pairs={{0,1},{1,0},{2,3},{3,2},{4,5},{5,4},{6,7},{7,6},{8,9},{9,8},{10,11... | collective-permute-start | bytes 1572872 | tf_op jit(solution)/shard_map/ppermute | solution.py:37
  115.3 31.0 %collective-permute-start.6 = (bf16[512,512]{1,0:T(8,128)(2,1)S(1)}, bf16[512,512]{1,0:T(8,128)(2,1)}, u32[]{:S(2)}, u32[]{:S(2)}) collective-permute-start(bf16[512,512]{1,0:T(8,128)(2,1)S(1)} %copy-done.9), channel_id=1, source_target_pairs={{0,16},{1,17},{2,18},{3,19},{4,20},{5,21},{6,22},{7,23},{8,24},{9,... | collective-permute-start | bytes 1572872 | tf_op jit(solution)/shard_map/ppermute | solution.py:37
  185.2 21.4 %collective-permute-start.13 = (bf16[512,512]{1,0:T(8,128)(2,1)}, bf16[512,512]{1,0:T(8,128)(2,1)S(1)}, u32[]{:S(2)}, u32[]{:S(2)}) collective-permute-start(bf16[512,512]{1,0:T(8,128)(2,1)} %get-tuple-element.171), channel_id=1, source_target_pairs={{0,1},{1,0},{2,3},{3,2},{4,5},{5,4},{6,7},{7,6},{8,9},{9,8},{10,11... | collective-permute-start | bytes 1572872 | tf_op jit(solution)/shard_map/ppermute | solution.py:37
  191.3 22.6 %collective-permute-start.15 = (bf16[512,512]{1,0:T(8,128)(2,1)}, bf16[512,512]{1,0:T(8,128)(2,1)S(1)}, u32[]{:S(2)}, u32[]{:S(2)}) collective-permute-start(bf16[512,512]{1,0:T(8,128)(2,1)} %get-tuple-element.173), channel_id=1, source_target_pairs={{0,1},{1,0},{2,3},{3,2},{4,5},{5,4},{6,7},{7,6},{8,9},{9,8},{10,11... | collective-permute-start | bytes 1572872 | tf_op jit(solution)/shard_map/ppermute | solution.py:37
  197.6 19.2 %collective-permute-start.16 = (bf16[512,512]{1,0:T(8,128)(2,1)}, bf16[512,512]{1,0:T(8,128)(2,1)S(1)}, u32[]{:S(2)}, u32[]{:S(2)}) collective-permute-start(bf16[512,512]{1,0:T(8,128)(2,1)} %get-tuple-element.181), channel_id=1, source_target_pairs={{0,16},{1,17},{2,18},{3,19},{4,20},{5,21},{6,22},{7,23},{8,24},{9,... | collective-permute-start | bytes 1572872 | tf_op jit(solution)/shard_map/ppermute | solution.py:37
  241.9 15.1 %collective-permute-start.25 = (bf16[512,512]{1,0:T(8,128)(2,1)}, bf16[512,512]{1,0:T(8,128)(2,1)S(1)}, u32[]{:S(2)}, u32[]{:S(2)}) collective-permute-start(bf16[512,512]{1,0:T(8,128)(2,1)} %get-tuple-element.192.refs_1_), channel_id=1, source_target_pairs={{0,16},{1,17},{2,18},{3,19},{4,20},{5,21},{6,22},{7,23},{8,24},{9,... | collective-permute-start | bytes 1572872 | tf_op jit(solution)/shard_map/ppermute | solution.py:37
  243.1 15.1 %collective-permute-start.22 = (bf16[512,512]{1,0:T(8,128)(2,1)}, bf16[512,512]{1,0:T(8,128)(2,1)S(1)}, u32[]{:S(2)}, u32[]{:S(2)}) collective-permute-start(bf16[512,512]{1,0:T(8,128)(2,1)} %get-tuple-element.190.refs_0_), channel_id=1, source_target_pairs={{0,1},{1,0},{2,3},{3,2},{4,5},{5,4},{6,7},{7,6},{8,9},{9,8},{10,11... | collective-permute-start | bytes 1572872 | tf_op jit(solution)/shard_map/ppermute | solution.py:37
  243.7 21.8 %collective-permute-start.23 = (bf16[512,512]{1,0:T(8,128)(2,1)}, bf16[512,512]{1,0:T(8,128)(2,1)S(1)}, u32[]{:S(2)}, u32[]{:S(2)}) collective-permute-start(bf16[512,512]{1,0:T(8,128)(2,1)} %get-tuple-element.192.refs_1_), channel_id=1, source_target_pairs={{0,1},{1,0},{2,3},{3,2},{4,5},{5,4},{6,7},{7,6},{8,9},{9,8},{10,11... | collective-permute-start | bytes 1572872 | tf_op jit(solution)/shard_map/ppermute | solution.py:37
  245.1 23.1 %collective-permute-start.24 = (bf16[512,512]{1,0:T(8,128)(2,1)}, bf16[512,512]{1,0:T(8,128)(2,1)S(1)}, u32[]{:S(2)}, u32[]{:S(2)}) collective-permute-start(bf16[512,512]{1,0:T(8,128)(2,1)} %get-tuple-element.190.refs_0_), channel_id=1, source_target_pairs={{0,16},{1,17},{2,18},{3,19},{4,20},{5,21},{6,22},{7,23},{8,24},{9,... | collective-permute-start | bytes 1572872 | tf_op jit(solution)/shard_map/ppermute | solution.py:37
  258.2 17.7 %collective-permute-start.26 = (bf16[512,512]{1,0:T(8,128)(2,1)S(1)}, bf16[512,512]{1,0:T(8,128)(2,1)S(1)}, u32[]{:S(2)}, u32[]{:S(2)}) collective-permute-start(bf16[512,512]{1,0:T(8,128)(2,1)S(1)} %collective-permute-done.22.refs_2_), channel_id=1, source_target_pairs={{0,16},{1,17},{2,18},{3,19},{4,20},{5,21},{6,22},{7,23},{8,24},{9,... | collective-permute-start | bytes 1572872 | tf_op jit(solution)/shard_map/ppermute | solution.py:37
  261.4 69.3 %collective-permute-start.32 = (bf16[2048,128]{1,0:T(8,128)(2,1)}, bf16[2048,128]{1,0:T(8,128)(2,1)}, u32[]{:S(2)}, u32[]{:S(2)}) collective-permute-start(bf16[2048,128]{1,0:T(8,128)(2,1)} %get-tuple-element.318), channel_id=1, source_target_pairs={{0,16},{1,17},{2,18},{3,19},{4,20},{5,21},{6,22},{7,23},{8,24},{9,... | collective-permute-start | bytes 1572872 | tf_op jit(solution)/shard_map/ppermute | solution.py:37
  313.2 24.0 %collective-permute-start.30 = (bf16[512,512]{1,0:T(8,128)(2,1)}, bf16[512,512]{1,0:T(8,128)(2,1)S(1)}, u32[]{:S(2)}, u32[]{:S(2)}) collective-permute-start(bf16[512,512]{1,0:T(8,128)(2,1)} %get-tuple-element.199), channel_id=1, source_target_pairs={{0,1},{1,0},{2,3},{3,2},{4,5},{5,4},{6,7},{7,6},{8,9},{9,8},{10,11... | collective-permute-start | bytes 1572872 | tf_op jit(solution)/shard_map/ppermute | solution.py:37
  321.3 41.3 %collective-permute-start.36 = (bf16[512,512]{1,0:T(8,128)(2,1)}, bf16[512,512]{1,0:T(8,128)(2,1)S(1)}, u32[]{:S(2)}, u32[]{:S(2)}) collective-permute-start(bf16[512,512]{1,0:T(8,128)(2,1)} %get-tuple-element.201), channel_id=1, source_target_pairs={{0,1},{1,0},{2,3},{3,2},{4,5},{5,4},{6,7},{7,6},{8,9},{9,8},{10,11... | collective-permute-start | bytes 1572872 | tf_op jit(solution)/shard_map/ppermute | solution.py:37
  321.9 15.0 %collective-permute-start.31 = (bf16[512,512]{1,0:T(8,128)(2,1)S(1)}, bf16[512,512]{1,0:T(8,128)(2,1)S(1)}, u32[]{:S(2)}, u32[]{:S(2)}) collective-permute-start(bf16[512,512]{1,0:T(8,128)(2,1)S(1)} %copy-done.90), channel_id=1, source_target_pairs={{0,16},{1,17},{2,18},{3,19},{4,20},{5,21},{6,22},{7,23},{8,24},{9,... | collective-permute-start | bytes 1572872 | tf_op jit(solution)/shard_map/ppermute | solution.py:37
  330.2 32.5 %collective-permute-start.37 = (bf16[512,512]{1,0:T(8,128)(2,1)}, bf16[512,512]{1,0:T(8,128)(2,1)S(1)}, u32[]{:S(2)}, u32[]{:S(2)}) collective-permute-start(bf16[512,512]{1,0:T(8,128)(2,1)} %get-tuple-element.213), channel_id=1, source_target_pairs={{0,16},{1,17},{2,18},{3,19},{4,20},{5,21},{6,22},{7,23},{8,24},{9,... | collective-permute-start | bytes 1572872 | tf_op jit(solution)/shard_map/ppermute | solution.py:37
  337.2 19.1 %collective-permute-start.34 = (bf16[1024,128]{1,0:T(8,128)(2,1)S(1)}, bf16[1024,128]{1,0:T(8,128)(2,1)S(1)}, u32[]{:S(2)}, u32[]{:S(2)}) collective-permute-start(bf16[1024,128]{1,0:T(8,128)(2,1)S(1)} %get-tuple-element.317), channel_id=1, source_target_pairs={{0,4},{1,5},{2,6},{3,7},{4,0},{5,1},{6,2},{7,3},{8,12},{9,13},{10,... | collective-permute-start | bytes 786440 | tf_op jit(solution)/shard_map/ppermute | solution.py:37
  344.1 28.5 %collective-permute-start.38 = (bf16[512,512]{1,0:T(8,128)(2,1)}, bf16[512,512]{1,0:T(8,128)(2,1)S(1)}, u32[]{:S(2)}, u32[]{:S(2)}) collective-permute-start(bf16[512,512]{1,0:T(8,128)(2,1)} %get-tuple-element.207), channel_id=1, source_target_pairs={{0,16},{1,17},{2,18},{3,19},{4,20},{5,21},{6,22},{7,23},{8,24},{9,... | collective-permute-start | bytes 1572872 | tf_op jit(solution)/shard_map/ppermute | solution.py:37
  394.8 28.0 %all-to-all-start.1 = ((bf16[4,1024,128]{2,1,0:T(8,128)(2,1)}), bf16[4,1024,128]{2,1,0:T(8,128)(2,1)S(1)}, u32[]{:S(2)}, u32[]{:S(2)}) async-start(bf16[4,1024,128]{2,1,0:T(8,128)(2,1)} %get-tuple-element.224), calls=%async_computation.1 | async-start | bytes 2097152 | tf_op jit(solution)/shard_map/all_to_all | solution.py:645
  400.3 171.1 %reduce-scatter.4.cloned.1.call-start = ((), (), s32[]{:S(2)}) async-start(), calls=%async_computation.6 | async-start | bytes 9437184 | tf_op jit(solution)/shard_map/reduce_scatter | solution.py:712
  400.4 14.9 %collective-permute-start.44 = (bf16[512,512]{1,0:T(8,128)(2,1)S(1)}, bf16[512,512]{1,0:T(8,128)(2,1)S(1)}, u32[]{:S(2)}, u32[]{:S(2)}) collective-permute-start(bf16[512,512]{1,0:T(8,128)(2,1)S(1)} %copy-done.83), channel_id=1, source_target_pairs={{0,1},{1,0},{2,3},{3,2},{4,5},{5,4},{6,7},{7,6},{8,9},{9,8},{10,11... | collective-permute-start | bytes 1572872 | tf_op jit(solution)/shard_map/ppermute | solution.py:37
  401.1 15.7 %collective-permute-start.47 = (bf16[512,512]{1,0:T(8,128)(2,1)S(1)}, bf16[512,512]{1,0:T(8,128)(2,1)S(1)}, u32[]{:S(2)}, u32[]{:S(2)}) collective-permute-start(bf16[512,512]{1,0:T(8,128)(2,1)S(1)} %copy-done.84), channel_id=1, source_target_pairs={{0,16},{1,17},{2,18},{3,19},{4,20},{5,21},{6,22},{7,23},{8,24},{9,... | collective-permute-start | bytes 1572872 | tf_op jit(solution)/shard_map/ppermute | solution.py:37
  402.4 24.9 %collective-permute-start.46 = (bf16[512,512]{1,0:T(8,128)(2,1)S(1)}, bf16[512,512]{1,0:T(8,128)(2,1)}, u32[]{:S(2)}, u32[]{:S(2)}) collective-permute-start(bf16[512,512]{1,0:T(8,128)(2,1)S(1)} %copy-done.83), channel_id=1, source_target_pairs={{0,16},{1,17},{2,18},{3,19},{4,20},{5,21},{6,22},{7,23},{8,24},{9,... | collective-permute-start | bytes 1572872 | tf_op jit(solution)/shard_map/ppermute | solution.py:37
  403.1 24.2 %collective-permute-start.45 = (bf16[512,512]{1,0:T(8,128)(2,1)S(1)}, bf16[512,512]{1,0:T(8,128)(2,1)}, u32[]{:S(2)}, u32[]{:S(2)}) collective-permute-start(bf16[512,512]{1,0:T(8,128)(2,1)S(1)} %copy-done.84), channel_id=1, source_target_pairs={{0,1},{1,0},{2,3},{3,2},{4,5},{5,4},{6,7},{7,6},{8,9},{9,8},{10,11... | collective-permute-start | bytes 1572872 | tf_op jit(solution)/shard_map/ppermute | solution.py:37
  415.3 18.3 %collective-permute-start.48 = (bf16[512,512]{1,0:T(8,128)(2,1)S(1)}, bf16[512,512]{1,0:T(8,128)(2,1)}, u32[]{:S(2)}, u32[]{:S(2)}) collective-permute-start(bf16[512,512]{1,0:T(8,128)(2,1)S(1)} %collective-permute-done.44.refs_2_), channel_id=1, source_target_pairs={{0,16},{1,17},{2,18},{3,19},{4,20},{5,21},{6,22},{7,23},{8,24},{9,... | collective-permute-start | bytes 1572872 | tf_op jit(solution)/shard_map/ppermute | solution.py:37
  416.8 16.8 %collective-permute-start.49 = (bf16[512,512]{1,0:T(8,128)(2,1)S(1)}, bf16[512,512]{1,0:T(8,128)(2,1)}, u32[]{:S(2)}, u32[]{:S(2)}) collective-permute-start(bf16[512,512]{1,0:T(8,128)(2,1)S(1)} %collective-permute-done.47.refs_5_), channel_id=1, source_target_pairs={{0,1},{1,0},{2,3},{3,2},{4,5},{5,4},{6,7},{7,6},{8,9},{9,8},{10,11... | collective-permute-start | bytes 1572872 | tf_op jit(solution)/shard_map/ppermute | solution.py:37
  468.8 283.4 %reduce-scatter.8.cloned.1.call-start = ((), (), s32[]{:S(2)}) async-start(), calls=%async_computation.8 | async-start | bytes 9437184 | tf_op jit(solution)/shard_map/reduce_scatter | solution.py:712
  475.8 22.1 %collective-permute-start.50 = (bf16[512,512]{1,0:T(8,128)(2,1)}, bf16[512,512]{1,0:T(8,128)(2,1)S(1)}, u32[]{:S(2)}, u32[]{:S(2)}) collective-permute-start(bf16[512,512]{1,0:T(8,128)(2,1)} %get-tuple-element.233), channel_id=1, source_target_pairs={{0,1},{1,0},{2,3},{3,2},{4,5},{5,4},{6,7},{7,6},{8,9},{9,8},{10,11... | collective-permute-start | bytes 1572872 | tf_op jit(solution)/shard_map/ppermute | solution.py:37
  483.6 36.5 %collective-permute-start.52 = (bf16[512,512]{1,0:T(8,128)(2,1)}, bf16[512,512]{1,0:T(8,128)(2,1)S(1)}, u32[]{:S(2)}, u32[]{:S(2)}) collective-permute-start(bf16[512,512]{1,0:T(8,128)(2,1)} %get-tuple-element.235), channel_id=1, source_target_pairs={{0,1},{1,0},{2,3},{3,2},{4,5},{5,4},{6,7},{7,6},{8,9},{9,8},{10,11... | collective-permute-start | bytes 1572872 | tf_op jit(solution)/shard_map/ppermute | solution.py:37
  492.5 27.6 %collective-permute-start.53 = (bf16[512,512]{1,0:T(8,128)(2,1)}, bf16[512,512]{1,0:T(8,128)(2,1)S(1)}, u32[]{:S(2)}, u32[]{:S(2)}) collective-permute-start(bf16[512,512]{1,0:T(8,128)(2,1)} %get-tuple-element.244), channel_id=1, source_target_pairs={{0,16},{1,17},{2,18},{3,19},{4,20},{5,21},{6,22},{7,23},{8,24},{9,... | collective-permute-start | bytes 1572872 | tf_op jit(solution)/shard_map/ppermute | solution.py:37
  502.6 24.5 %collective-permute-start.54 = (bf16[512,512]{1,0:T(8,128)(2,1)}, bf16[512,512]{1,0:T(8,128)(2,1)S(1)}, u32[]{:S(2)}, u32[]{:S(2)}) collective-permute-start(bf16[512,512]{1,0:T(8,128)(2,1)} %get-tuple-element.241), channel_id=1, source_target_pairs={{0,16},{1,17},{2,18},{3,19},{4,20},{5,21},{6,22},{7,23},{8,24},{9,... | collective-permute-start | bytes 1572872 | tf_op jit(solution)/shard_map/ppermute | solution.py:37
  503.7 23.4 %collective-permute-start.55 = (bf16[512,512]{1,0:T(8,128)(2,1)}, bf16[512,512]{1,0:T(8,128)(2,1)S(1)}, u32[]{:S(2)}, u32[]{:S(2)}) collective-permute-start(bf16[512,512]{1,0:T(8,128)(2,1)} %get-tuple-element.249), channel_id=1, source_target_pairs={{0,1},{1,0},{2,3},{3,2},{4,5},{5,4},{6,7},{7,6},{8,9},{9,8},{10,11... | collective-permute-start | bytes 1572872 | tf_op jit(solution)/shard_map/ppermute | solution.py:37
  549.8 15.1 %collective-permute-start.62 = (bf16[512,512]{1,0:T(8,128)(2,1)}, bf16[512,512]{1,0:T(8,128)(2,1)S(1)}, u32[]{:S(2)}, u32[]{:S(2)}) collective-permute-start(bf16[512,512]{1,0:T(8,128)(2,1)} %get-tuple-element.258.refs_1_), channel_id=1, source_target_pairs={{0,16},{1,17},{2,18},{3,19},{4,20},{5,21},{6,22},{7,23},{8,24},{9,... | collective-permute-start | bytes 1572872 | tf_op jit(solution)/shard_map/ppermute | solution.py:37
  552.0 21.3 %collective-permute-start.61 = (bf16[512,512]{1,0:T(8,128)(2,1)}, bf16[512,512]{1,0:T(8,128)(2,1)S(1)}, u32[]{:S(2)}, u32[]{:S(2)}) collective-permute-start(bf16[512,512]{1,0:T(8,128)(2,1)} %get-tuple-element.257.refs_0_), channel_id=1, source_target_pairs={{0,16},{1,17},{2,18},{3,19},{4,20},{5,21},{6,22},{7,23},{8,24},{9,... | collective-permute-start | bytes 1572872 | tf_op jit(solution)/shard_map/ppermute | solution.py:37
  553.4 19.9 %collective-permute-start.60 = (bf16[512,512]{1,0:T(8,128)(2,1)}, bf16[512,512]{1,0:T(8,128)(2,1)S(1)}, u32[]{:S(2)}, u32[]{:S(2)}) collective-permute-start(bf16[512,512]{1,0:T(8,128)(2,1)} %get-tuple-element.258.refs_1_), channel_id=1, source_target_pairs={{0,1},{1,0},{2,3},{3,2},{4,5},{5,4},{6,7},{7,6},{8,9},{9,8},{10,11... | collective-permute-start | bytes 1572872 | tf_op jit(solution)/shard_map/ppermute | solution.py:37
  561.2 17.6 %collective-permute-start.63 = (bf16[512,512]{1,0:T(8,128)(2,1)S(1)}, bf16[512,512]{1,0:T(8,128)(2,1)S(1)}, u32[]{:S(2)}, u32[]{:S(2)}) collective-permute-start(bf16[512,512]{1,0:T(8,128)(2,1)S(1)} %collective-permute-done.59.refs_2_), channel_id=1, source_target_pairs={{0,16},{1,17},{2,18},{3,19},{4,20},{5,21},{6,22},{7,23},{8,24},{9,... | collective-permute-start | bytes 1572872 | tf_op jit(solution)/shard_map/ppermute | solution.py:37
  566.6 142.1 %collective-permute-start.43 = (bf16[2048,128]{1,0:T(8,128)(2,1)}, bf16[2048,128]{1,0:T(8,128)(2,1)}, u32[]{:S(2)}, u32[]{:S(2)}) collective-permute-start(bf16[2048,128]{1,0:T(8,128)(2,1)} %get-tuple-element.313), channel_id=1, source_target_pairs={{0,16},{1,17},{2,18},{3,19},{4,20},{5,21},{6,22},{7,23},{8,24},{9,... | collective-permute-start | bytes 1572872 | tf_op jit(solution)/shard_map/ppermute | solution.py:37
  568.7 245.6 %reduce-scatter.6.cloned.1.call-start = ((), (), s32[]{:S(2)}) async-start(), calls=%async_computation.7 | async-start | bytes 2359296 | tf_op jit(solution)/shard_map/reduce_scatter | solution.py:712
  629.1 17.3 %collective-permute-start.65 = (bf16[4,1024,384]{2,1,0:T(8,128)(2,1)}, bf16[4,1024,384]{2,1,0:T(8,128)(2,1)S(1)}, u32[]{:S(2)}, u32[]{:S(2)}) collective-permute-start(bf16[4,1024,384]{2,1,0:T(8,128)(2,1)} %bitcast.181), channel_id=1, source_target_pairs={{0,8},{1,9},{2,10},{3,11},{4,12},{5,13},{6,14},{7,15},{8,0},{9,1},... | collective-permute-start | bytes 9437192 | tf_op jit(solution)/shard_map/ppermute | solution.py:37
  635.4 24.8 %collective-permute-start.66 = (bf16[512,512]{1,0:T(8,128)(2,1)}, bf16[512,512]{1,0:T(8,128)(2,1)}, u32[]{:S(2)}, u32[]{:S(2)}) collective-permute-start(bf16[512,512]{1,0:T(8,128)(2,1)} %get-tuple-element.265), channel_id=1, source_target_pairs={{0,1},{1,0},{2,3},{3,2},{4,5},{5,4},{6,7},{7,6},{8,9},{9,8},{10,11... | collective-permute-start | bytes 1572872 | tf_op jit(solution)/shard_map/ppermute | solution.py:37
  644.2 29.7 %collective-permute-start.68 = (bf16[512,512]{1,0:T(8,128)(2,1)}, bf16[512,512]{1,0:T(8,128)(2,1)}, u32[]{:S(2)}, u32[]{:S(2)}) collective-permute-start(bf16[512,512]{1,0:T(8,128)(2,1)} %get-tuple-element.267), channel_id=1, source_target_pairs={{0,1},{1,0},{2,3},{3,2},{4,5},{5,4},{6,7},{7,6},{8,9},{9,8},{10,11... | collective-permute-start | bytes 1572872 | tf_op jit(solution)/shard_map/ppermute | solution.py:37
  645.2 14.9 %collective-permute-start.67 = (bf16[512,512]{1,0:T(8,128)(2,1)S(1)}, bf16[512,512]{1,0:T(8,128)(2,1)S(1)}, u32[]{:S(2)}, u32[]{:S(2)}) collective-permute-start(bf16[512,512]{1,0:T(8,128)(2,1)S(1)} %copy-done.85), channel_id=1, source_target_pairs={{0,16},{1,17},{2,18},{3,19},{4,20},{5,21},{6,22},{7,23},{8,24},{9,... | collective-permute-start | bytes 1572872 | tf_op jit(solution)/shard_map/ppermute | solution.py:37
  646.4 65.0 %collective-permute-start.77 = (f32[4,1664]{1,0:T(4,128)S(1)}, f32[4,1664]{1,0:T(4,128)S(1)}, u32[]{:S(2)}, u32[]{:S(2)}) collective-permute-start(f32[4,1664]{1,0:T(4,128)S(1)} %add.95), channel_id=1, source_target_pairs={{0,2},{1,3},{2,0},{3,1},{4,6},{5,7},{6,4},{7,5},{8,10},{9,11},{10,... | collective-permute-start | bytes 79880 | tf_op jit(solution)/shard_map/ppermute | solution.py:37
  664.5 33.0 %collective-permute-start.70 = (bf16[512,512]{1,0:T(8,128)(2,1)}, bf16[512,512]{1,0:T(8,128)(2,1)S(1)}, u32[]{:S(2)}, u32[]{:S(2)}) collective-permute-start(bf16[512,512]{1,0:T(8,128)(2,1)} %get-tuple-element.277), channel_id=1, source_target_pairs={{0,16},{1,17},{2,18},{3,19},{4,20},{5,21},{6,22},{7,23},{8,24},{9,... | collective-permute-start | bytes 1572872 | tf_op jit(solution)/shard_map/ppermute | solution.py:37
  665.4 23.9 %collective-permute-start.69 = (bf16[512,512]{1,0:T(8,128)(2,1)S(1)}, bf16[512,512]{1,0:T(8,128)(2,1)S(1)}, u32[]{:S(2)}, u32[]{:S(2)}) collective-permute-start(bf16[512,512]{1,0:T(8,128)(2,1)S(1)} %copy-done.89), channel_id=1, source_target_pairs={{0,16},{1,17},{2,18},{3,19},{4,20},{5,21},{6,22},{7,23},{8,24},{9,... | collective-permute-start | bytes 1572872 | tf_op jit(solution)/shard_map/ppermute | solution.py:37
  674.9 22.6 %collective-permute-start.71 = (bf16[512,512]{1,0:T(8,128)(2,1)S(1)}, bf16[512,512]{1,0:T(8,128)(2,1)S(1)}, u32[]{:S(2)}, u32[]{:S(2)}) collective-permute-start(bf16[512,512]{1,0:T(8,128)(2,1)S(1)} %copy-done.88), channel_id=1, source_target_pairs={{0,1},{1,0},{2,3},{3,2},{4,5},{5,4},{6,7},{7,6},{8,9},{9,8},{10,11... | collective-permute-start | bytes 1572872 | tf_op jit(solution)/shard_map/ppermute | solution.py:37
  689.4 67.9 %collective-permute-start.73 = (bf16[2,1024,384]{2,1,0:T(8,128)(2,1)}, bf16[2,1024,384]{2,1,0:T(8,128)(2,1)S(1)}, u32[]{:S(2)}, u32[]{:S(2)}) collective-permute-start(bf16[2,1024,384]{2,1,0:T(8,128)(2,1)} %get-tuple-element.288), channel_id=1, source_target_pairs={{0,2},{1,3},{2,0},{3,1},{4,6},{5,7},{6,4},{7,5},{8,10},{9,11},{10,... | collective-permute-start | bytes 4718600 | tf_op jit(solution)/shard_map/ppermute | solution.py:37
  704.1 68.9 %all-to-all-start.2 = ((bf16[4,1024,128]{2,1,0:T(8,128)(2,1)}), bf16[4,1024,128]{2,1,0:T(8,128)(2,1)}, u32[]{:S(2)}, u32[]{:S(2)}) async-start(bf16[4,1024,128]{2,1,0:T(8,128)(2,1)} %shard_map.352), calls=%async_computation.3 | async-start | bytes 2097152 | tf_op jit(solution)/shard_map/all_to_all | solution.py:645
  711.3 40.8 %collective-permute-start.78 = (f32[4,1664]{1,0:T(4,128)S(1)}, f32[4,1664]{1,0:T(4,128)S(1)}, u32[]{:S(2)}, u32[]{:S(2)}) collective-permute-start(f32[4,1664]{1,0:T(4,128)S(1)} %add.96), channel_id=1, source_target_pairs={{0,4},{1,5},{2,6},{3,7},{4,0},{5,1},{6,2},{7,3},{8,12},{9,13},{10,... | collective-permute-start | bytes 79880 | tf_op jit(solution)/shard_map/ppermute | solution.py:37
  714.4 54.0 %collective-permute-start.82 = (bf16[512,512]{1,0:T(8,128)(2,1)S(1)}, bf16[512,512]{1,0:T(8,128)(2,1)}, u32[]{:S(2)}, u32[]{:S(2)}) collective-permute-start(bf16[512,512]{1,0:T(8,128)(2,1)S(1)} %get-tuple-element.307), channel_id=1, source_target_pairs={{0,16},{1,17},{2,18},{3,19},{4,20},{5,21},{6,22},{7,23},{8,24},{9,... | collective-permute-start | bytes 1572872 | tf_op jit(solution)/shard_map/ppermute | solution.py:37
  753.6 17.6 %collective-permute-start.81 = (bf16[512,512]{1,0:T(8,128)(2,1)S(1)}, bf16[512,512]{1,0:T(8,128)(2,1)S(1)}, u32[]{:S(2)}, u32[]{:S(2)}) collective-permute-start(bf16[512,512]{1,0:T(8,128)(2,1)S(1)} %get-tuple-element.309), channel_id=1, source_target_pairs={{0,16},{1,17},{2,18},{3,19},{4,20},{5,21},{6,22},{7,23},{8,24},{9,... | collective-permute-start | bytes 1572872 | tf_op jit(solution)/shard_map/ppermute | solution.py:37
  755.7 46.9 %collective-permute-start.79 = (f32[1664]{0:T(1024)S(1)}, f32[1664]{0:T(1024)S(1)}, u32[]{:S(2)}, u32[]{:S(2)}) collective-permute-start(f32[1664]{0:T(1024)S(1)} %get-tuple-element.304), channel_id=1, source_target_pairs={{0,16},{1,17},{2,18},{3,19},{4,20},{5,21},{6,22},{7,23},{8,24},{9,... | collective-permute-start | bytes 19976 | tf_op jit(solution)/shard_map/ppermute | solution.py:37
  761.9 36.6 %collective-permute-start.74 = (bf16[1,1024,384]{2,1,0:T(8,128)(2,1)}, bf16[1,1024,384]{2,1,0:T(8,128)(2,1)S(1)}, u32[]{:S(2)}, u32[]{:S(2)}) collective-permute-start(bf16[1,1024,384]{2,1,0:T(8,128)(2,1)} %get-tuple-element.292), channel_id=1, source_target_pairs={{0,4},{1,5},{2,6},{3,7},{4,0},{5,1},{6,2},{7,3},{8,12},{9,13},{10,... | collective-permute-start | bytes 2359304 | tf_op jit(solution)/shard_map/ppermute | solution.py:37
  766.7 36.5 %collective-permute-start.84 = (f32[128]{0:T(128)S(1)}, f32[128]{0:T(128)S(1)}, u32[]{:S(2)}, u32[]{:S(2)}) collective-permute-start(f32[128]{0:T(128)S(1)} %fusion.20), channel_id=1, source_target_pairs={{0,1},{1,0},{2,3},{3,2},{4,5},{5,4},{6,7},{7,6},{8,9},{9,8},{10,11... | collective-permute-start | bytes 1544 | tf_op jit(solution)/shard_map/ppermute | solution.py:37
  774.3 32.8 %collective-permute-start.72 = (bf16[2048,128]{1,0:T(8,128)(2,1)S(1)}, bf16[2048,128]{1,0:T(8,128)(2,1)S(1)}, u32[]{:S(2)}, u32[]{:S(2)}) collective-permute-start(bf16[2048,128]{1,0:T(8,128)(2,1)S(1)} %get-tuple-element.311), channel_id=1, source_target_pairs={{0,16},{1,17},{2,18},{3,19},{4,20},{5,21},{6,22},{7,23},{8,24},{9,... | collective-permute-start | bytes 1572872 | tf_op jit(solution)/shard_map/ppermute | solution.py:37
  (123 other events, 1030.3 us)
Sparse Core Ops, SparseCore 0:
  25.2 86.1 all-gather.8
  113.6 27.7 all-gather.10
  143.0 81.5 all-gather.12
  226.1 80.5 all-gather.14
  468.9 90.4 reduce-scatter.3
  568.8 92.0 reduce-scatter.7
  674.0 42.7 reduce-scatter.5

commit v4 on v3

--- a/solution.py
+++ b/solution.py
@@ -53,7 +53,7 @@
         self.value = tie(self.value, *others)
 
 
-MORE = 10
+LESS = 4
 
 
 def call(body, grid, spot, ins, in_specs, outs, out_specs, scratch, flops, size):
@@ -66,7 +66,7 @@
         compiler_params=pltpu.CompilerParams(
             dimension_semantics=("arbitrary",) * len(grid), vmem_limit_bytes=56 * 1024 * 1024
         ),
-        cost_estimate=pl.CostEstimate(flops=flops * MORE, bytes_accessed=size * MORE, transcendentals=0),
+        cost_estimate=pl.CostEstimate(flops=flops // LESS, bytes_accessed=size // LESS, transcendentals=0),
     )(spot.value, *ins)
     spot.after(result[0])
     return result
@@ -87,7 +87,7 @@
 SLOTS = (0, 2, 1, 3)
 
 
-def wide_body(by_rows, finish, count, spot, *refs):
+def wide_body(by_rows, finish, count, several, spot, *refs):
     pieces, weights, rest = refs[:8], refs[8], refs[9:]
     extra, outs, kept = rest[: -1 - count], rest[-1 - count : -1], rest[-1]
     t = pl.program_id(1)
@@ -100,10 +100,13 @@
                 y, c = divmod(block, 2)
                 y = y ^ spot[1]
                 at = slot * QUARTER + block * 128
-                if by_rows:
-                    kept[:, at : at + 128] = weights[0, c, :, pl.ds(pl.multiple_of(y * 512 + start, 128), 128)]
-                else:
-                    kept[at : at + 128, :] = weights[0, c, y, pl.ds(start, 128), :]
+                for z in range(several):
+                    if by_rows:
+                        n = weights.shape[2]
+                        part = weights[z, c, :, pl.ds(pl.multiple_of(y * 512 + start, 128), 128)]
+                        kept[z * n : z * n + n, at : at + 128] = part
+                    else:
+                        kept[at : at + 128, :] = weights[0, c, y, pl.ds(start, 128), :]
 
     total = None
     for slot in range(4):
@@ -118,28 +121,32 @@
     if by_rows:
         n = weights.shape[1]
         weights = weights.reshape(4, 2, n, 1024)
-        kept = pltpu.VMEM((n, WIDTH), BF)
+        several = 4 if n < 256 else 1
+        kept = pltpu.VMEM((several * n, WIDTH), BF)
     else:
         n = weights.shape[2]
         weights = weights.reshape(4, 2, 2, 512, n)
+        several = 1
         kept = pltpu.VMEM((WIDTH, n), BF)
-    block = (1,) + weights.shape[1:]
+    block = (several,) + weights.shape[1:]
     tail = (0,) * (len(block) - 1)
+    total = 4 * n
+    n = several * n
     bias = pl.BlockSpec((1, n), lambda z, t, *_: (0, z))
     tile = pl.BlockSpec((HALF, n), lambda z, t, *_: (t, z))
     return call(
-        functools.partial(wide_body, by_rows, finish, count + sums),
-        (4, 2),
+        functools.partial(wide_body, by_rows, finish, count + sums, several),
+        (4 // several, 2),
         spot,
         (*pieces, weights, *extra),
         [fixed(p.shape) for p in pieces]
         + [pl.BlockSpec(block, lambda z, t, *_: (z,) + tail)]
         + [bias if e.shape[0] == 1 else tile for e in extra],
-        [shape_of(LEN, 4 * n, dtype=BF)] * count + [shape_of(8, 4 * n)] * sums,
+        [shape_of(LEN, total, dtype=BF)] * count + [shape_of(8, total)] * sums,
         [tile] * count + [pl.BlockSpec((8, n), lambda z, t, *_: (0, z))] * sums,
         [kept],
-        2 * LEN * WIDTH * 4 * n,
-        2 * (LEN * WIDTH + WIDTH * 4 * n + LEN * 4 * n),
+        2 * LEN * WIDTH * total,
+        2 * (LEN * WIDTH + WIDTH * total + LEN * total),
     )
 
 
@@ -255,102 +262,53 @@
     return out.reshape(8, n, 1024) if by_rows else out.reshape(8, 1024, n)
 
 
-def grad_body(by_rows, spot, *refs):
-    pieces, local, outs = refs[:8], refs[8], refs[9:]
-    order = [((y ^ spot[1]) * 2 + (c ^ spot[2])) * 128 for y in range(2) for c in range(2)]
-    order = [pl.ds(pl.multiple_of(at, 128), 128) for at in order]
+def place_pair_body(spot, own, other, query, key, value, proj):
+    for side, part in ((spot[1], own), (1 - spot[1], other)):
+        at = pl.ds(pl.multiple_of(side * 128, 128), 128)
+        for i, out in enumerate((query, key, value)):
+            out[:, at] = part[:, i * 128 : i * 128 + 128].astype(F32)
+        proj[at, :] = part[:, 384:].astype(F32).T
+
+
+def place_pair(own, other, spot):
+    grid = [shape_of(512, 256)] * 3 + [shape_of(256, 512)]
+    return call(
+        place_pair_body, (1,), spot, (own, other), [fixed((512, 512))] * 2, grid, [fixed(g.shape) for g in grid], [],
+        2 * 512 * 512, 8 * 512 * 512,
+    )
+
+
+def grad_pair_body(spot, *refs):
+    out = refs[18]
     for slot, mask in enumerate(SLOTS):
         start = pl.multiple_of((spot[0] ^ mask) * 128, 128)
-        total = None
-        for part in range(2):
-            piece = jnp.concatenate([pieces[2 * slot + part][:, at] for at in order], axis=1)
-            tile = local[part * HALF : part * HALF + HALF, :]
-            term = dot(tile, piece, TN) if by_rows else dot(piece, tile, TN)
-            total = term if total is None else total + term
-        for block in range(4):
-            y, c = divmod(block, 2)
-            part = slice(block * 128, block * 128 + 128)
-            if by_rows:
-                outs[c][0, :, pl.ds(pl.multiple_of(y * 512 + start, 128), 128)] = total[:, part].astype(BF)
-            else:
-                outs[c][0, y, pl.ds(start, 128), :] = total[part, :].astype(BF)
-
-
-def grad(pieces, local, spot, by_rows):
-    n = local.shape[1] // 4
-    shape = (4, n, 1024) if by_rows else (4, 2, 512, n)
-    tail = (0,) * (len(shape) - 1)
-
-    def where(z, p):
-        far = z ^ p[3]
-        return ((far >> 1) | ((far & 1) << 1),) + tail
-
-    outs = call(
-        functools.partial(grad_body, by_rows),
+        at = 0
+        for pieces, local in ((refs[:8], refs[8]), (refs[9:17], refs[17])):
+            total = dot(pieces[2 * slot][...], local[:HALF, :], TN) + dot(pieces[2 * slot + 1][...], local[HALF:, :], TN)
+            n = local.shape[1]
+            for block in range(4):
+                y, c = divmod(block, 2)
+                out[0, c, y ^ spot[1], pl.ds(start, 128), at : at + n] = total[block * 128 : block * 128 + 128, :].astype(BF)
+            at += n
+
+
+def grad_pair(first, first_local, second, second_local, spot):
+    sizes = [local.shape[1] // 4 for local in (first_local, second_local)]
+    n = sum(sizes)
+    specs = [fixed(p.shape) for p in first]
+    (out,) = call(
+        grad_pair_body,
         (4,),
         spot,
-        (*pieces, local),
-        [fixed(p.shape) for p in pieces] + [pl.BlockSpec((LEN, n), lambda z, *_: (0, z))],
-        [shape_of(*shape, dtype=BF)] * 2,
-        [pl.BlockSpec((1,) + shape[1:], where)] * 2,
+        (*first, first_local, *second, second_local),
+        specs + [pl.BlockSpec((LEN, sizes[0]), lambda z, *_: (0, z))] + specs + [pl.BlockSpec((LEN, sizes[1]), lambda z, *_: (0, z))],
+        [shape_of(4, 2, 2, 512, n, dtype=BF)],
+        [pl.BlockSpec((1, 2, 2, 512, n), lambda z, *_: (z, 0, 0, 0, 0))],
         [],
         2 * LEN * WIDTH * 4 * n,
-        2 * (LEN * WIDTH + WIDTH * 4 * n + LEN * 4 * n),
-    )
-    return [o if by_rows else o.reshape(4, 1024, n) for o in outs]
-
-
-def fold_body(spot, *refs):
-    count = len(refs) // 3
-    for i in range(count):
-        out = refs[2 * count + i]
-        out[...] = (refs[i][...].astype(F32) + refs[count + i][...].astype(F32)).astype(out.dtype)
-
-
-def fold(own, got, spot):
-    half, rows, width = own.shape[0] // 2, own.shape[1], own.shape[2]
-    step = min(rows, 512)
-    first = pl.BlockSpec((1, step, width), lambda i, t, p: (i, t, 0))
-    second = pl.BlockSpec((1, step, width), lambda i, t, p: (i + half, t, 0))
-    return call(
-        fold_body, (half, rows // step), spot, (own, own, got, got), [first, second] * 2,
-        [shape_of(half, rows, width, dtype=BF)] * 2, [first, first], [], 2 * half * rows * width, 12 * half * rows * width,
-    )
-
-
-def fold_last(own, got, spot, by_rows):
-    rows, width = own.shape[1:]
-    if by_rows:
-        shape = (rows, 512)
-        parts = [pl.BlockSpec((1, rows, 512), functools.partial(lambda y, i, p: (0, 0, y), y)) for y in range(2)]
-    else:
-        shape = (512, width)
-        parts = [pl.BlockSpec((1, 512, width), functools.partial(lambda y, i, p: (0, y, 0), y)) for y in range(2)]
-
-    def body(spot, a, b, c, d, keep, send):
-        keep[...] = a[0].astype(F32) + c[0].astype(F32)
-        send[...] = (b[0].astype(F32) + d[0].astype(F32)).astype(BF)
-
-    return call(
-        body, (1,), spot, (own, own, got, got), parts * 2, [shape_of(*shape), shape_of(*shape, dtype=BF)], [fixed(shape)] * 2,
-        [], rows * width, 6 * rows * width,
-    )
-
-
-class Sum:
-    def __init__(self, outs, spot, by_rows):
-        self.keep, self.send = outs
-        self.spot, self.by_rows = spot, by_rows
-
-    def go(self, mask):
-        self.got = swap(tie(self.send, self.spot.value), mask)
-
-    def step(self):
-        self.keep, self.send = fold(self.keep, self.got, self.spot)
-
-    def last(self):
-        self.keep, self.send = fold_last(self.keep, self.got, self.spot, self.by_rows)
-        return self.keep, swap(self.send, Y_BIT)
+        2 * (2 * LEN * WIDTH + WIDTH * 4 * n + LEN * 4 * n),
+    )
+    return out.reshape(8, 1024, n)
 
 
 SCALE = HD ** (-0.5)
@@ -614,12 +572,12 @@
     return lax.dynamic_slice_in_dim(piece, yi * 128, 128, 1), lax.dynamic_slice_in_dim(piece, (1 - yi) * 128, 128, 1)
 
 
-def spread_z(own, other, yi, zi):
+def spread_z(own, other, yi, zi, *after):
     both = jnp.concatenate([own.reshape(2, LEN, 128), other.reshape(2, LEN, 128)], axis=0)
     blocks = []
     for mask, bits in ((0, 0), (1, Z_LOW), (2, Z_HIGH), (3, Z_LOW | Z_HIGH)):
         block = lax.dynamic_index_in_dim(both, (zi ^ mask) ^ (yi * 2), 0, False)
-        blocks.append(swap(block, bits) if mask else block)
+        blocks.append(swap(tie(block, *after), bits) if mask else block)
     return blocks
 
 
@@ -634,6 +592,17 @@
                 out[:, pl.ds(pl.multiple_of((spot[3] ^ mask) * 128, 128), 128)] = block[...]
 
 
+def assemble_whole_body(spot, blocks, low, high):
+    t = pl.program_id(0)
+    whole = jnp.concatenate([blocks[z] for z in range(4)], axis=1)
+    write_halves(t, low, high, whole)
+
+
+def assemble_whole(blocks, spot):
+    half = shape_of(HALF, QUARTER, dtype=BF)
+    return elementwise(assemble_whole_body, spot, (blocks,), [BLOCKS], [half, half], [LOW, HIGH])
+
+
 def assemble(blocks, spot):
     half = shape_of(HALF, QUARTER, dtype=BF)
     return elementwise(
@@ -641,11 +610,13 @@
     )
 
 
-def from_share(share, yi):
-    parts = lax.all_to_all(share, "z", 0, 0, tiled=True).reshape(2, 2 * LEN, 128)
+def from_share(share):
+    return lax.all_to_all(share, "z", 0, 0, tiled=True).reshape(2, 2 * LEN, 128)
+
+
+def swap_y(parts, yi):
     own = lax.dynamic_index_in_dim(parts, yi, 0, False)
-    other = swap(lax.dynamic_index_in_dim(parts, 1 - yi, 0, False), Y_BIT)
-    return own, other
+    return own, swap(lax.dynamic_index_in_dim(parts, 1 - yi, 0, False), Y_BIT)
 
 
 def side_by_side(own, other, yi, axis):
@@ -662,7 +633,7 @@
     return (low, high, x_low, x_high, y_low, y_high, xy_low, xy_high)
 
 
-def square_scatter(local, weights, spot, by_rows, first=lambda: None, between=lambda: None, after=lambda: None):
+def square_scatter(local, weights, spot, by_rows, first=lambda: None, middle=lambda: None, between=lambda: None, after=lambda: None):
     term = functools.partial(partial, local, weights, spot, by_rows)
     far_low, far_high = term(3, BF, BF)
     far_low = swap(far_low, X_BIT)
@@ -672,6 +643,7 @@
     first()
     y_low, near_high = term(1, F32, BF)
     near_high = swap(near_high, Y_BIT)
+    middle()
     half = fixed((HALF, QUARTER))
     last_low, last_high = call(
         pass_on, (1,), spot, (y_low, far_low, x_high, far_high), [half] * 4, [shape_of(HALF, QUARTER, dtype=BF)] * 2,
@@ -720,12 +692,11 @@
     return piece[:, :512], swap(piece[:, 512:], Y_BIT)
 
 
-def restore_columns(pair, count, yi):
+def restore_columns(pair, yi, begin=0, n=None):
     own, other = pair
-    n = own.shape[1] // count
-    return [
-        side_by_side(own[:, i * n : (i + 1) * n].astype(F32), other[:, i * n : (i + 1) * n].astype(F32), yi, 1) for i in range(count)
-    ]
+    n = n or own.shape[1]
+    own, other = own[:, begin : begin + n], other[:, begin : begin + n]
+    return side_by_side(own.astype(F32), other.astype(F32), yi, 1)
 
 
 def restore_rows(pair, yi):
@@ -765,6 +736,7 @@
     half_proj, sent = halve_rows(w_proj, yi, sent)
     half_up, sent = halve_columns([w_up], yi, sent)
     half_down, sent = halve_rows(w_down, yi, sent)
+    spot.after(vectors, half_proj)
     token_low, token_high = assemble(token_blocks, spot)
     gathered = square_gather(token_low, token_high)
     full_proj = gather_zc(tie(half_proj, token_low))
@@ -789,9 +761,16 @@
     dy_own, dy_send = split_y(tie(cotangent, hidden_low), yi)
     dy_other = swap(dy_send, Y_BIT)
     act, slope = wide(hidden_wide, full_up, spot, False, finish_gelu, (u_bias,), 2)
-    dy_blocks = spread_z(tie(dy_own, full_down), dy_other, yi, zi)
-    dy_halves = []
-    parts = square_scatter(act, full_down, spot, True, between=lambda: dy_halves.extend(assemble(dy_blocks, spot)))
+    dy = side_by_side(dy_own.reshape(2, LEN, 128), dy_other.reshape(2, LEN, 128), yi, 0)
+    dy_blocks, dy_halves = [], []
+
+    def first():
+        dy_blocks.append(lax.all_to_all(tie(dy, spot.value), "z", 0, 0, tiled=True))
+
+    def after():
+        dy_halves.extend(assemble_whole(dy_blocks[0], spot))
+
+    parts = square_scatter(act, full_down, spot, True, first=first, after=after)
     resid_two, stats_two = elementwise(
         norm_two_sums, spot, (*parts, d_bias, resid, moments, n_gain, n_shift, *dy_halves, f_gain),
         PARTS + [VECTOR, TILE, STATS, VECTOR, VECTOR, LOW, HIGH, VECTOR], [full, stats_shape], [TILE, STATS],
@@ -802,17 +781,17 @@
         [shape_of(4, LEN, 128, dtype=BF), full, low_half, low_half, sums_shape], [BLOCKS, TILE, LOW, HIGH, SUMS],
     )
     ffn_wide = square_gather(ffn_low, ffn_high)
-    layer_own, layer_other = from_share(layer_share, yi)
-    layer_out = side_by_side(layer_own, layer_other, yi, 1)
-
-    spot.after(layer_own)
-    grad_down = scatter_zc(grad_whole(ffn_wide, act, spot, True))
+    down = grad_whole(ffn_wide, act, spot, True)
+    grad_down = scatter_zc(down)
+    layer_parts = from_share(tie(layer_share, down))
     grad_pre, sums_up = wide(ffn_wide, full_down, spot, True, finish_slope, (slope,), 1, 1)
     up = []
-    parts = square_scatter(
-        grad_pre, full_up, spot, False, between=lambda: up.append(grad_whole(hidden_wide, grad_pre, spot, False))
-    )
-    grad_up = scatter_zc(up[0])
+
+    def after():
+        spot.after(layer_parts)
+        up.append(grad_whole(hidden_wide, grad_pre, spot, False))
+
+    parts = square_scatter(grad_pre, full_up, spot, False, after=after)
     grad_hidden, stats_back, sums_back = elementwise(
         back_one_sums, spot, (*parts, grad_two, resid, moments, n_gain),
         PARTS + [TILE, TILE, STATS, VECTOR], [full, stats_shape, sums_shape], [TILE, STATS, SUMS],
@@ -823,59 +802,55 @@
         [full, low_half, low_half, sums_shape], [TILE, LOW, HIGH, SUMS],
     )
     attn_wide = square_gather(attn_low, attn_high)
+    grad_up = scatter_zc(tie(up[0], spot.value))
     spot.after(grad_down)
     (grad_heads,) = wide(attn_wide, full_proj, spot, True, finish_plain, (), 1)
+    layer_own, layer_other = swap_y(tie(layer_parts, grad_heads), yi)
+    down = exchange_rows(tie(grad_down, grad_heads))
     grad_qkv, sums_qkv = attention_back(qkv, ids_row, ids_column, logsum, grad_heads, spot)
-    qkv_sum = Sum(grad(gathered, grad_qkv, spot, False), spot, False)
-    qkv_sum.go(C_BIT)
-
-    totals = jnp.stack([stats_one[3] * valid, stats_one[2] * valid, stats_two[4] * valid, valid * QUARTER])
-    totals = jnp.pad(jnp.sum(totals, axis=1)[None], ((0, 3), (0, 124)))
-    sums = jnp.concatenate(
-        [
-            v.reshape(4, -1)
-            for v in (
-                *(sums_qkv[0].reshape(4, 3, HD)[:, i] for i in (0, 2)),
-                sums_attn[0], sums_back[0], sums_back[1], sums_two[2], sums_two[0], sums_two[1], sums_up[0], totals,
-            )
-        ],
-        axis=1,
-    )
-    for mask in (C_BIT, Z_LOW, Z_HIGH):
-        sums = sums + swap(sums, mask)
-    proj = []
-
-    def first():
-        qkv_sum.step()
-        qkv_sum.go(Z_LOW)
+    spot.after(layer_other, down[1])
+    sum_last = scatter_zc(grad_pair(gathered, grad_qkv, attn_wide, heads_out, spot))
+
+    kept = []
 
     def between():
-        proj.append(scatter_zc(grad_whole(attn_wide, heads_out, spot, True)))
-
-    parts = square_scatter(grad_qkv, full_qkv, spot, False, first=first, between=between)
-    (grad_proj,) = proj
-    spot.after(grad_up)
+        totals = jnp.stack([tie(stats_one[3], spot.value) * valid, stats_one[2] * valid, stats_two[4] * valid, valid * QUARTER])
+        totals = jnp.pad(jnp.sum(totals, axis=1)[None], ((0, 3), (0, 124)))
+        vector_sums = jnp.concatenate(
+            [
+                v.reshape(4, -1)
+                for v in (
+                    *(tie(sums_qkv[0], spot.value).reshape(4, 3, HD)[:, i] for i in (0, 2)),
+                    sums_attn[0], sums_back[0], sums_back[1], sums_two[2], sums_two[0], sums_two[1], sums_up[0], totals,
+                )
+            ],
+            axis=1,
+        )
+        kept.append((vector_sums, swap(vector_sums, C_BIT)))
+
+    parts = square_scatter(grad_qkv, full_qkv, spot, False, between=between)
     (back,) = elementwise(
         finish_back, spot, (*parts, grad_one), PARTS + [TILE], [shape_of(4, LEN, 128, dtype=BF)], [BLOCKS]
     )
-    down, up, proj = exchange_rows(grad_down), exchange_columns(grad_up), exchange_rows(grad_proj)
-    qkv_sum.step()
-    qkv_sum.go(Z_HIGH)
-    back_own, back_other = from_share(back, yi)
-    qkv_sum = qkv_sum.last()
-    last = qkv_sum[0]
+    back_parts = from_share(back)
+    up = exchange_columns(tie(grad_up, back))
+    sums = kept[0][0] + tie(kept[0][1], back)
+    sums = sums + tie(swap(sums, Z_LOW), up[1])
+    back_own, back_other = swap_y(back_parts, yi)
+    sums = sums + tie(swap(sums, Z_HIGH), back_other)
+    last = swap(sum_last[512:], Y_BIT)
     totals = sums[0, 1536:] + swap(sums[0, 1536:], Y_BIT)
-    totals = totals + tie(swap(totals, X_BIT), last)
+    totals = totals + swap(totals, X_BIT)
     norms = jnp.sqrt(totals[:3] / totals[3])
     sums = lax.dynamic_index_in_dim(sums, zi, 0, False)
-    other = tie(swap(sums, Y_BIT), last)
+    other = swap(sums, Y_BIT)
     sums = jnp.where(yi == 0, jnp.stack([sums, other]), jnp.stack([other, sums]))
     vecs = [sums[:, i * 128 : (i + 1) * 128].reshape(-1) for i in range(8)] + [sums[:, 1024:1536].reshape(-1)]
-    grad_tokens = side_by_side(back_own, tie(back_other, last), yi, 1).astype(F32)
-    grad_down = restore_rows(down, yi)
-    (grad_up,) = restore_columns(up, 1, yi)
-    grad_proj = restore_rows((proj[0], tie(proj[1], last)), yi)
-    grad_query, grad_key, grad_value = restore_columns(qkv_sum, 3, yi)
+    layer_out = side_by_side(tie(layer_own, back), layer_other, yi, 1)
+    grad_tokens = side_by_side(back_own, back_other, yi, 1).astype(F32)
+    grad_down = restore_rows((tie(down[0], back), down[1]), yi)
+    grad_up = restore_columns(up, yi)
+    grad_query, grad_key, grad_value, grad_proj = place_pair(sum_last, last, spot)
     return (
         layer_out, grad_tokens, grad_query, vecs[0], grad_key, grad_value, vecs[1], grad_proj, vecs[2], vecs[3], vecs[4],
         grad_up, vecs[8], grad_down, vecs[5], vecs[6], vecs[7], norms,

time: 835 us -> 767 us (0.919)
  waiting for transfers between devices: 299 us -> 269 us
  Pallas kernels: 330 us -> 316 us
  starting transfers between devices: 111 us -> 99.9 us
    ppermute x85 -> x78, waiting for transfers between devices: 284 us -> 223 us  [swap(): return lax.ppermute(piece, AXES, [(i, i ^ mask) for i in range(32)])]
    all_to_all x2 -> x3, waiting for transfers between devices: 5.46 us -> 29.4 us  [the longest x2 29.4 us: from_share(): return lax.all_to_all(share, 'z', 0, 0, tiled=True).reshape(2, 2 * LEN, 128)]
    ppermute x85 -> x78, starting transfers between devices: 101 us -> 84.5 us  [swap(): return lax.ppermute(piece, AXES, [(i, i ^ mask) for i in range(32)])]
    pallas_call x42 -> x39, Pallas kernels: 330 us -> 316 us  [call(): pl.pallas_call(body, grid_spec=pltpu.PrefetchScalarGridSpec(num_scalar_pr...]
    unnamed x208 -> x188, local copies, waits for them, and re-layouts: 18.1 us -> 16.6 us
  transfers between devices with their start and end apart: 94 -> 88, of which waited for: 45 -> 49; matrix products, arithmetic and copies ran while one was open for 5% -> 4% of each run, Pallas kernels for 34% -> 36%
where the time goes in v4:
time: 767 us; the launch traced here: 760 us
  Pallas kernels  316 us (41%)
  waiting for transfers between devices  269 us (35%)
  starting transfers between devices  99.9 us (13%)
  local copies, waits for them, and re-layouts  30.4 us (4%)
  other arithmetic  19.4 us (3%)
  between operations  15.3 us (2%)
  blocking collectives  10.3 us (1%)
    pallas_call x39, Pallas kernels, call(): pl.pallas_call(body, grid_spec=pltpu.PrefetchScalarGridSpec(num_scalar_pr...  316 us
    ppermute x78, waiting for transfers between devices, swap(): return lax.ppermute(piece, AXES, [(i, i ^ mask) for i in range(32)])  223 us
    ppermute x78, starting transfers between devices, swap(): return lax.ppermute(piece, AXES, [(i, i ^ mask) for i in range(32)])  84.5 us
    all_to_all x2, waiting for transfers between devices, from_share(): return lax.all_to_all(share, 'z', 0, 0, tiled=True).reshape(2, 2 * LEN, 128)  29.4 us
    unnamed x188, local copies, waits for them, and re-layouts  16.6 us
  transfers between devices with their start and end apart: 88, of which 49 were waited for; matrix products, arithmetic and copies ran while one was open for 4% of the time, Pallas kernels for 36%

profile of v4, /device:TPU:0, one launch (start us, length us, event | category | flops | bytes accessed | tf_op | source)
XLA Modules:
  0.0 760.5 jit_solution(6680322337004822597)
XLA Ops:
  13.2 10.3 %all_to_all.24 = f32[4,1,1536]{2,1,0:T(1,128)S(1)} all-to-all(f32[4,1,1536]{2,1,0:T(1,128)S(1)} %broadcast_in_dim.4), channel_id=1, replica_groups=mesh['y'=2,'c'=2,'z'=4,'x'=2] {'z'}, dimensions={0} | all-to-all | bytes 49152 | tf_op jit(solution)/shard_map/all_to_all | solution.py:722
  25.7 11.4 %collective-permute-done.1 = bf16[2048,128]{1,0:T(8,128)(2,1)S(1)} collective-permute-done((bf16[2048,128]{1,0:T(8,128)(2,1)S(1)}, bf16[2048,128]{1,0:T(8,128)(2,1)S(1)}, u32[]{:S(2)}, u32[]{:S(2)}) %collective-permute-start.1) | collective-permute-done | bytes 524320 | tf_op jit(solution)/shard_map/ppermute | solution.py:37
  43.9 3.8 collective-permute-done
  48.4 6.5 collective-permute-done.4.refs_3_
  54.9 9.9 %collective-permute-done.2.refs_1_ = bf16[1024,128]{1,0:T(8,128)(2,1)} collective-permute-done((bf16[1024,128]{1,0:T(8,128)(2,1)S(1)}, bf16[1024,128]{1,0:T(8,128)(2,1)}, u32[]{:S(2)}, u32[]{:S(2)}) %collective-permute-start.2) | collective-permute-done | bytes 262176 | tf_op jit(solution)/shard_map/ppermute | solution.py:37
  64.8 26.5 %collective-permute-done.3.refs_2_ = bf16[1024,128]{1,0:T(8,128)(2,1)} collective-permute-done((bf16[1024,128]{1,0:T(8,128)(2,1)S(1)}, bf16[1024,128]{1,0:T(8,128)(2,1)}, u32[]{:S(2)}, u32[]{:S(2)}) %collective-permute-start.3) | collective-permute-done | bytes 262176 | tf_op jit(solution)/shard_map/ppermute | solution.py:37
  91.2 4.2 shard_map.313
  97.3 9.2 %collective-permute-done.28 = bf16[512,512]{1,0:T(8,128)(2,1)S(1)} collective-permute-done((bf16[512,512]{1,0:T(8,128)(2,1)S(1)}, bf16[512,512]{1,0:T(8,128)(2,1)S(1)}, u32[]{:S(2)}, u32[]{:S(2)}) %collective-permute-start.28) | collective-permute-done | bytes 524320 | tf_op jit(solution)/shard_map/ppermute | solution.py:37
  109.3 9.5 %collective-permute-done.29 = bf16[512,512]{1,0:T(8,128)(2,1)S(1)} collective-permute-done((bf16[512,512]{1,0:T(8,128)(2,1)S(1)}, bf16[512,512]{1,0:T(8,128)(2,1)S(1)}, u32[]{:S(2)}, u32[]{:S(2)}) %collective-permute-start.29) | collective-permute-done | bytes 524320 | tf_op jit(solution)/shard_map/ppermute | solution.py:37
  123.7 8.3 %collective-permute-done.12 = s32[2,4]{1,0:T(2,128)S(1)} collective-permute-done((s32[2,4]{1,0:T(2,128)S(1)}, s32[2,4]{1,0:T(2,128)S(1)}, u32[]{:S(2)}, u32[]{:S(2)}) %collective-permute-start.12) | collective-permute-done | bytes 64 | tf_op jit(solution)/shard_map/ppermute | solution.py:37
  139.2 8.2 %collective-permute-done.6.refs_3_ = bf16[512,512]{1,0:T(8,128)(2,1)S(1)} collective-permute-done((bf16[512,512]{1,0:T(8,128)(2,1)S(1)}, bf16[512,512]{1,0:T(8,128)(2,1)S(1)}, u32[]{:S(2)}, u32[]{:S(2)}) %collective-permute-start.6) | collective-permute-done | bytes 524320 | tf_op jit(solution)/shard_map/ppermute | solution.py:37
  147.4 5.7 collective-permute-done.10.refs_7_
  153.1 15.8 %shard_map.314.queries.whole = bf16[1024,1536]{1,0:T(8,128)(2,1)} custom-call(s32[4]{0:T(128)} %pad_add_fusion.spot, bf16[512,512]{1,0:T(8,128)(2,1)} %get-tuple-element.164.refs_0_.refs_6_, bf16[512,512]{1,0:T(8,128)(2,1)} %get-tuple-element.166.refs_1_.refs_7_, bf16[512,512]{1,0:T(8,128)(2,1)} %copy-done.4, bf16[512,512]{1,0:T(8,128)(2,1)} %copy-done.5, ...), custom_call_target="tpu_custom_call" | custom-call | flops 1610612736 | bytes 3407872 | tf_op jit(solution)/shard_map/pallas_call | solution.py:60
  169.0 12.9 %shard_map.315 = (bf16[1024,512]{1,0:T(8,128)(2,1)}, f32[4,1,1024]{2,1,0:T(1,128)}) custom-call(s32[4]{0:T(128)} %pad_add_fusion.spot, bf16[1024,1536]{1,0:T(8,128)(2,1)} %shard_map.314.queries.whole, bf16[1024,1536]{1,0:T(8,128)(2,1)} %shard_map.314.queries.whole, s32[1,1024]{1,0:T(1,128)} %bitcast.153, s32[1024,1]{1,0:T(8,128)} %copy.44.ids_column), custom_call_target="tpu_custom_call" | custom-call | flops 2147483648 | bytes 1048576 | tf_op jit(solution)/shard_map/pallas_call | solution.py:60
  181.9 4.4 shard_map.316
  188.5 4.5 shard_map.317
  193.6 4.5 shard_map.318
  212.5 4.7 shard_map.320
  219.0 5.8 shard_map.321
  232.5 5.1 shard_map.322
  243.0 9.8 %collective-permute-done.25.refs_5_ = bf16[512,512]{1,0:T(8,128)(2,1)S(1)} collective-permute-done((bf16[512,512]{1,0:T(8,128)(2,1)}, bf16[512,512]{1,0:T(8,128)(2,1)S(1)}, u32[]{:S(2)}, u32[]{:S(2)}) %collective-permute-start.25) | collective-permute-done | bytes 524320 | tf_op jit(solution)/shard_map/ppermute | solution.py:37
  255.7 8.3 %collective-permute-done.34 = bf16[2048,128]{1,0:T(8,128)(2,1)S(1)} collective-permute-done((bf16[2048,128]{1,0:T(8,128)(2,1)S(1)}, bf16[2048,128]{1,0:T(8,128)(2,1)S(1)}, u32[]{:S(2)}, u32[]{:S(2)}) %collective-permute-start.34) | collective-permute-done | bytes 524320 | tf_op jit(solution)/shard_map/ppermute | solution.py:37
  265.2 6.7 collective-permute-done.24.refs_4_
  272.8 4.8 collective-permute-done.26.refs_6_
  277.7 20.3 %shard_map.323 = (bf16[1024,2048]{1,0:T(8,128)(2,1)}, bf16[1024,2048]{1,0:T(8,128)(2,1)}) custom-call(s32[4]{0:T(128)} %pad_add_fusion.spot, bf16[512,512]{1,0:T(8,128)(2,1)} %get-tuple-element.191.refs_0_, bf16[512,512]{1,0:T(8,128)(2,1)} %get-tuple-element.193.refs_1_, bf16[512,512]{1,0:T(8,128)(2,1)} %copy-done.10, bf16[512,512]{1,0:T(8,128)(2,1)} %copy-done.11, ...), custom_call_target="tpu_custom_call" | custom-call | flops 2147483648 | bytes 4194304 | tf_op jit(solution)/shard_map/pallas_call | solution.py:60
  298.0 8.7 %all-gather.15.cloned.1.call-done = bf16[4096,1024]{1,0:T(8,128)(2,1)} async-done(((bf16[512,1024]{1,0:T(8,128)(2,1)}), bf16[4096,1024]{1,0:T(8,128)(2,1)}) %all-gather.15.cloned.1.call-update) | async-done | bytes 8388624 | tf_op jit(solution)/shard_map/all_gather | solution.py:680
  306.7 6.5 shard_map.324
  313.2 6.7 shard_map.325
  319.8 5.3 all-to-all-start.1
  329.1 6.6 shard_map.326
  347.2 6.0 collective-permute-done.32.refs_2_
  353.1 6.9 shard_map.328
  361.0 4.2 shard_map.329
  366.2 6.6 shard_map.330
  379.4 6.5 shard_map.331
  390.1 11.0 %collective-permute-done.40.refs_2_ = bf16[512,512]{1,0:T(8,128)(2,1)S(1)} collective-permute-done((bf16[512,512]{1,0:T(8,128)(2,1)}, bf16[512,512]{1,0:T(8,128)(2,1)S(1)}, u32[]{:S(2)}, u32[]{:S(2)}) %collective-permute-start.40) | collective-permute-done | bytes 524320 | tf_op jit(solution)/shard_map/ppermute | solution.py:37
  403.1 9.0 %collective-permute-done.42.refs_4_ = bf16[512,512]{1,0:T(8,128)(2,1)S(1)} collective-permute-done((bf16[512,512]{1,0:T(8,128)(2,1)}, bf16[512,512]{1,0:T(8,128)(2,1)S(1)}, u32[]{:S(2)}, u32[]{:S(2)}) %collective-permute-start.42) | collective-permute-done | bytes 524320 | tf_op jit(solution)/shard_map/ppermute | solution.py:37
  412.2 5.6 collective-permute-done.44.refs_6_
  419.5 15.9 %shard_map.332 = bf16[4,2,512,1024]{3,2,1,0:T(8,128)(2,1)} custom-call(s32[4]{0:T(128)} %pad_add_fusion.spot, bf16[512,512]{1,0:T(8,128)(2,1)} %get-tuple-element.227.refs_0_, bf16[512,512]{1,0:T(8,128)(2,1)} %get-tuple-element.228.refs_1_, bf16[512,512]{1,0:T(8,128)(2,1)} %copy-done.14, bf16[512,512]{1,0:T(8,128)(2,1)} %copy-done.17, ...), custom_call_target="tpu_custom_call" | custom-call | flops 2147483648 | bytes 4194304 | tf_op jit(solution)/shard_map/pallas_call | solution.py:60
  435.4 4.5 all-to-all-start.2
  440.3 19.9 %shard_map.333 = (bf16[1024,2048]{1,0:T(8,128)(2,1)}, f32[8,2048]{1,0:T(8,128)}) custom-call(s32[4]{0:T(128)} %pad_add_fusion.spot, bf16[512,512]{1,0:T(8,128)(2,1)} %get-tuple-element.227.refs_0_, bf16[512,512]{1,0:T(8,128)(2,1)} %get-tuple-element.228.refs_1_, bf16[512,512]{1,0:T(8,128)(2,1)} %copy-done.14, bf16[512,512]{1,0:T(8,128)(2,1)} %copy-done.17, ...), custom_call_target="tpu_custom_call" | custom-call | flops 2147483648 | bytes 4194304 | tf_op jit(solution)/shard_map/pallas_call | solution.py:60
  460.2 6.6 shard_map.334
  469.2 6.8 shard_map.335
  476.1 6.8 shard_map.336
  485.3 3.6 shard_map.337
  495.4 7.0 shard_map.338
  502.4 14.0 %shard_map.339 = bf16[4,2,2,512,512]{4,3,2,1,0:T(8,128)(2,1)} custom-call(s32[4]{0:T(128)} %pad_add_fusion.spot, bf16[512,512]{1,0:T(8,128)(2,1)} %get-tuple-element.191.refs_0_, bf16[512,512]{1,0:T(8,128)(2,1)} %get-tuple-element.193.refs_1_, bf16[512,512]{1,0:T(8,128)(2,1)} %copy-done.10, bf16[512,512]{1,0:T(8,128)(2,1)} %copy-done.11, ...), custom_call_target="tpu_custom_call" | custom-call | flops 2147483648 | bytes 4194304 | tf_op jit(solution)/shard_map/pallas_call | solution.py:60
  517.5 6.9 shard_map.340
  531.7 6.2 shard_map.341
  543.0 8.8 %collective-permute-done.55.refs_2_.refs_11_ = bf16[512,512]{1,0:T(8,128)(2,1)S(1)} collective-permute-done((bf16[512,512]{1,0:T(8,128)(2,1)S(1)}, bf16[512,512]{1,0:T(8,128)(2,1)S(1)}, u32[]{:S(2)}, u32[]{:S(2)}) %collective-permute-start.55) | collective-permute-done | bytes 524320 | tf_op jit(solution)/shard_map/ppermute | solution.py:37
  553.5 4.5 collective-permute-done.57.refs_4_.refs_13_
  558.0 7.6 %collective-permute-done.59.refs_6_.refs_15_ = bf16[512,512]{1,0:T(8,128)(2,1)} collective-permute-done((bf16[512,512]{1,0:T(8,128)(2,1)S(1)}, bf16[512,512]{1,0:T(8,128)(2,1)}, u32[]{:S(2)}, u32[]{:S(2)}) %collective-permute-start.59) | collective-permute-done | bytes 524320 | tf_op jit(solution)/shard_map/ppermute | solution.py:37
  565.6 7.8 %shard_map.342.grad_out = bf16[1024,512]{1,0:T(8,128)(2,1)} custom-call(s32[4]{0:T(128)} %pad_add_fusion.spot, bf16[512,512]{1,0:T(8,128)(2,1)} %get-tuple-element.259.refs_0_.refs_9_, bf16[512,512]{1,0:T(8,128)(2,1)} %get-tuple-element.260.refs_1_.refs_10_, bf16[512,512]{1,0:T(8,128)(2,1)} %copy-done.23, ...), custom_call_target="tpu_custom_call" | custom-call | flops 536870912 | bytes 1835008 | tf_op jit(solution)/shard_map/pallas_call | solution.py:60
  576.5 23.2 %shard_map.343 = (bf16[1024,1536]{1,0:T(8,128)(2,1)}, f32[8,1536]{1,0:T(8,128)}) custom-call(s32[4]{0:T(128)} %pad_add_fusion.spot, bf16[1024,1536]{1,0:T(8,128)(2,1)} %shard_map.314.queries.whole, bf16[1024,1536]{1,0:T(8,128)(2,1)} %shard_map.314.queries.whole, s32[1,1024]{1,0:T(1,128)} %bitcast.154, s32[1024,1]{1,0:T(8,128)} %copy.44.ids_column, ...), custom_call_target="tpu_custom_call" | custom-call | flops 4026531840 | bytes 2097152 | tf_op jit(solution)/shard_map/pallas_call | solution.py:60
  599.7 19.9 %shard_map.344 = bf16[4,2,2,512,512]{4,3,2,1,0:T(8,128)(2,1)} custom-call(s32[4]{0:T(128)} %pad_add_fusion.spot, bf16[512,512]{1,0:T(8,128)(2,1)} %get-tuple-element.164.refs_0_.refs_6_, bf16[512,512]{1,0:T(8,128)(2,1)} %get-tuple-element.166.refs_1_.refs_7_, bf16[512,512]{1,0:T(8,128)(2,1)} %copy-done.4, bf16[512,512]{1,0:T(8,128)(2,1)} %copy-done.5, ...), custom_call_target="tpu_custom_call" | custom-call | flops 2147483648 | bytes 5242880 | tf_op jit(solution)/shard_map/pallas_call | solution.py:60
  619.7 6.3 shard_map.345
  629.0 6.4 shard_map.346
  636.3 6.4 shard_map.347
  654.5 6.6 shard_map.349
  662.2 5.9 shard_map.350
  668.1 4.8 all-to-all-start.3
  679.5 29.4 %all-to-all-done.3 = bf16[4,1024,128]{2,1,0:T(8,128)(2,1)} async-done(((bf16[4,1024,128]{2,1,0:T(8,128)(2,1)}), bf16[4,1024,128]{2,1,0:T(8,128)(2,1)}, u32[]{:S(2)}, u32[]{:S(2)}) %all-to-all-start.3) | async-done | bytes 1048608 | tf_op jit(solution)/shard_map/all_to_all | solution.py:614
  729.1 7.6 reduce-scatter.6.cloned.1.call-done
  740.5 8.8 %collective-permute-done.70.other = bf16[512,512]{1,0:T(8,128)(2,1)S(1)} collective-permute-done((bf16[512,512]{1,0:T(8,128)(2,1)S(1)}, bf16[512,512]{1,0:T(8,128)(2,1)S(1)}, u32[]{:S(2)}, u32[]{:S(2)}) %collective-permute-start.70) | collective-permute-done | bytes 524320 | tf_op jit(solution)/shard_map/ppermute | solution.py:37
  (412 shorter events, 182.3 us)
Async XLA Ops:
  7.2 145.9 %all-gather.9.cloned.1.call-start = ((), (), s32[]{:S(2)}) async-start(), calls=%async_computation.10 | async-start | bytes 7077888 | tf_op jit(solution)/shard_map/all_gather | solution.py:680
  9.9 14.2 %collective-permute-start.11 = (bf16[512,384]{1,0:T(8,128)(2,1)S(1)}, bf16[512,384]{1,0:T(8,128)(2,1)S(1)}, u32[]{:S(2)}, u32[]{:S(2)}) collective-permute-start(bf16[512,384]{1,0:T(8,128)(2,1)S(1)} %pad_maximum_fusion.3), channel_id=1, source_target_pairs={{0,16},{1,17},{2,18},{3,19},{4,20},{5,21},{6,22},{7,23},{8,24},{9,... | collective-permute-start | bytes 1179656 | tf_op jit(solution)/shard_map/ppermute | solution.py:37
  25.1 156.8 %all-gather.11.cloned.1.call-start = ((), (), s32[]{:S(2)}) async-start(), calls=%async_computation.11 | async-start | bytes 2359296 | tf_op jit(solution)/shard_map/all_gather | solution.py:680
  25.2 12.0 %collective-permute-start.1 = (bf16[2048,128]{1,0:T(8,128)(2,1)S(1)}, bf16[2048,128]{1,0:T(8,128)(2,1)S(1)}, u32[]{:S(2)}, u32[]{:S(2)}) collective-permute-start(bf16[2048,128]{1,0:T(8,128)(2,1)S(1)} %get-tuple-element.325), channel_id=1, source_target_pairs={{0,16},{1,17},{2,18},{3,19},{4,20},{5,21},{6,22},{7,23},{8,24},{9,... | collective-permute-start | bytes 1572872 | tf_op jit(solution)/shard_map/ppermute | solution.py:37
  38.3 16.7 %collective-permute-start.4 = (bf16[1024,128]{1,0:T(8,128)(2,1)S(1)}, bf16[1024,128]{1,0:T(8,128)(2,1)}, u32[]{:S(2)}, u32[]{:S(2)}) collective-permute-start(bf16[1024,128]{1,0:T(8,128)(2,1)S(1)} %get-tuple-element.320), channel_id=1, source_target_pairs={{0,6},{1,7},{2,4},{3,5},{4,2},{5,3},{6,0},{7,1},{8,14},{9,15},{10,... | collective-permute-start | bytes 786440 | tf_op jit(solution)/shard_map/ppermute | solution.py:37
  40.9 23.9 %collective-permute-start.2 = (bf16[1024,128]{1,0:T(8,128)(2,1)S(1)}, bf16[1024,128]{1,0:T(8,128)(2,1)}, u32[]{:S(2)}, u32[]{:S(2)}) collective-permute-start(bf16[1024,128]{1,0:T(8,128)(2,1)S(1)} %get-tuple-element.322), channel_id=1, source_target_pairs={{0,2},{1,3},{2,0},{3,1},{4,6},{5,7},{6,4},{7,5},{8,10},{9,11},{10,... | collective-permute-start | bytes 786440 | tf_op jit(solution)/shard_map/ppermute | solution.py:37
  40.9 50.4 %collective-permute-start.3 = (bf16[1024,128]{1,0:T(8,128)(2,1)S(1)}, bf16[1024,128]{1,0:T(8,128)(2,1)}, u32[]{:S(2)}, u32[]{:S(2)}) collective-permute-start(bf16[1024,128]{1,0:T(8,128)(2,1)S(1)} %get-tuple-element.323), channel_id=1, source_target_pairs={{0,4},{1,5},{2,6},{3,7},{4,0},{5,1},{6,2},{7,3},{8,12},{9,13},{10,... | collective-permute-start | bytes 786440 | tf_op jit(solution)/shard_map/ppermute | solution.py:37
  95.5 182.2 %all-gather.13.cloned.1.call-start = ((), (), s32[]{:S(2)}) async-start(), calls=%async_computation.12 | async-start | bytes 9437184 | tf_op jit(solution)/shard_map/all_gather | solution.py:680
  107.5 199.2 %all-gather.15.cloned.1.call-start = ((), (), s32[]{:S(2)}) async-start(), calls=%async_computation.13 | async-start | bytes 9437184 | tf_op jit(solution)/shard_map/all_gather | solution.py:680
  120.0 15.6 %collective-permute-start.8 = (bf16[512,512]{1,0:T(8,128)(2,1)S(1)}, bf16[512,512]{1,0:T(8,128)(2,1)S(1)}, u32[]{:S(2)}, u32[]{:S(2)}) collective-permute-start(bf16[512,512]{1,0:T(8,128)(2,1)S(1)} %copy-done.1), channel_id=1, source_target_pairs={{0,16},{1,17},{2,18},{3,19},{4,20},{5,21},{6,22},{7,23},{8,24},{9,... | collective-permute-start | bytes 1572872 | tf_op jit(solution)/shard_map/ppermute | solution.py:37
  121.4 14.5 %collective-permute-start.5 = (bf16[512,512]{1,0:T(8,128)(2,1)S(1)}, bf16[512,512]{1,0:T(8,128)(2,1)S(1)}, u32[]{:S(2)}, u32[]{:S(2)}) collective-permute-start(bf16[512,512]{1,0:T(8,128)(2,1)S(1)} %copy-done), channel_id=1, source_target_pairs={{0,1},{1,0},{2,3},{3,2},{4,5},{5,4},{6,7},{7,6},{8,9},{9,8},{10,11... | collective-permute-start | bytes 1572872 | tf_op jit(solution)/shard_map/ppermute | solution.py:37
  132.2 15.2 %collective-permute-start.6 = (bf16[512,512]{1,0:T(8,128)(2,1)S(1)}, bf16[512,512]{1,0:T(8,128)(2,1)S(1)}, u32[]{:S(2)}, u32[]{:S(2)}) collective-permute-start(bf16[512,512]{1,0:T(8,128)(2,1)S(1)} %copy-done.1), channel_id=1, source_target_pairs={{0,1},{1,0},{2,3},{3,2},{4,5},{5,4},{6,7},{7,6},{8,9},{9,8},{10,11... | collective-permute-start | bytes 1572872 | tf_op jit(solution)/shard_map/ppermute | solution.py:37
  134.6 12.8 %collective-permute-start.7 = (bf16[512,512]{1,0:T(8,128)(2,1)S(1)}, bf16[512,512]{1,0:T(8,128)(2,1)S(1)}, u32[]{:S(2)}, u32[]{:S(2)}) collective-permute-start(bf16[512,512]{1,0:T(8,128)(2,1)S(1)} %copy-done), channel_id=1, source_target_pairs={{0,16},{1,17},{2,18},{3,19},{4,20},{5,21},{6,22},{7,23},{8,24},{9,... | collective-permute-start | bytes 1572872 | tf_op jit(solution)/shard_map/ppermute | solution.py:37
  135.6 17.5 %collective-permute-start.10 = (bf16[512,512]{1,0:T(8,128)(2,1)S(1)}, bf16[512,512]{1,0:T(8,128)(2,1)}, u32[]{:S(2)}, u32[]{:S(2)}) collective-permute-start(bf16[512,512]{1,0:T(8,128)(2,1)S(1)} %collective-permute-done.8.refs_5_), channel_id=1, source_target_pairs={{0,1},{1,0},{2,3},{3,2},{4,5},{5,4},{6,7},{7,6},{8,9},{9,8},{10,11... | collective-permute-start | bytes 1572872 | tf_op jit(solution)/shard_map/ppermute | solution.py:37
  135.8 17.3 %collective-permute-start.9 = (bf16[512,512]{1,0:T(8,128)(2,1)S(1)}, bf16[512,512]{1,0:T(8,128)(2,1)}, u32[]{:S(2)}, u32[]{:S(2)}) collective-permute-start(bf16[512,512]{1,0:T(8,128)(2,1)S(1)} %collective-permute-done.5.refs_2_), channel_id=1, source_target_pairs={{0,16},{1,17},{2,18},{3,19},{4,20},{5,21},{6,22},{7,23},{8,24},{9,... | collective-permute-start | bytes 1572872 | tf_op jit(solution)/shard_map/ppermute | solution.py:37
  186.2 13.1 %collective-permute-start.14 = (bf16[512,512]{1,0:T(8,128)(2,1)}, bf16[512,512]{1,0:T(8,128)(2,1)S(1)}, u32[]{:S(2)}, u32[]{:S(2)}) collective-permute-start(bf16[512,512]{1,0:T(8,128)(2,1)} %get-tuple-element.179), channel_id=1, source_target_pairs={{0,16},{1,17},{2,18},{3,19},{4,20},{5,21},{6,22},{7,23},{8,24},{9,... | collective-permute-start | bytes 1572872 | tf_op jit(solution)/shard_map/ppermute | solution.py:37
  187.0 14.0 %collective-permute-start.13 = (bf16[512,512]{1,0:T(8,128)(2,1)}, bf16[512,512]{1,0:T(8,128)(2,1)S(1)}, u32[]{:S(2)}, u32[]{:S(2)}) collective-permute-start(bf16[512,512]{1,0:T(8,128)(2,1)} %get-tuple-element.172), channel_id=1, source_target_pairs={{0,1},{1,0},{2,3},{3,2},{4,5},{5,4},{6,7},{7,6},{8,9},{9,8},{10,11... | collective-permute-start | bytes 1572872 | tf_op jit(solution)/shard_map/ppermute | solution.py:37
  193.1 19.1 %collective-permute-start.15 = (bf16[512,512]{1,0:T(8,128)(2,1)}, bf16[512,512]{1,0:T(8,128)(2,1)S(1)}, u32[]{:S(2)}, u32[]{:S(2)}) collective-permute-start(bf16[512,512]{1,0:T(8,128)(2,1)} %get-tuple-element.174), channel_id=1, source_target_pairs={{0,1},{1,0},{2,3},{3,2},{4,5},{5,4},{6,7},{7,6},{8,9},{9,8},{10,11... | collective-permute-start | bytes 1572872 | tf_op jit(solution)/shard_map/ppermute | solution.py:37
  198.1 14.4 %collective-permute-start.16 = (bf16[512,512]{1,0:T(8,128)(2,1)}, bf16[512,512]{1,0:T(8,128)(2,1)S(1)}, u32[]{:S(2)}, u32[]{:S(2)}) collective-permute-start(bf16[512,512]{1,0:T(8,128)(2,1)} %get-tuple-element.182), channel_id=1, source_target_pairs={{0,16},{1,17},{2,18},{3,19},{4,20},{5,21},{6,22},{7,23},{8,24},{9,... | collective-permute-start | bytes 1572872 | tf_op jit(solution)/shard_map/ppermute | solution.py:37
  205.4 12.3 %collective-permute-start.18 = (bf16[512,512]{1,0:T(8,128)(2,1)}, bf16[512,512]{1,0:T(8,128)(2,1)S(1)}, u32[]{:S(2)}, u32[]{:S(2)}) collective-permute-start(bf16[512,512]{1,0:T(8,128)(2,1)} %get-tuple-element.187), channel_id=1, source_target_pairs={{0,1},{1,0},{2,3},{3,2},{4,5},{5,4},{6,7},{7,6},{8,9},{9,8},{10,11... | collective-permute-start | bytes 1572872 | tf_op jit(solution)/shard_map/ppermute | solution.py:37
  237.6 15.1 %collective-permute-start.25 = (bf16[512,512]{1,0:T(8,128)(2,1)}, bf16[512,512]{1,0:T(8,128)(2,1)S(1)}, u32[]{:S(2)}, u32[]{:S(2)}) collective-permute-start(bf16[512,512]{1,0:T(8,128)(2,1)} %get-tuple-element.193.refs_1_), channel_id=1, source_target_pairs={{0,16},{1,17},{2,18},{3,19},{4,20},{5,21},{6,22},{7,23},{8,24},{9,... | collective-permute-start | bytes 1572872 | tf_op jit(solution)/shard_map/ppermute | solution.py:37
  238.8 15.1 %collective-permute-start.22 = (bf16[512,512]{1,0:T(8,128)(2,1)}, bf16[512,512]{1,0:T(8,128)(2,1)S(1)}, u32[]{:S(2)}, u32[]{:S(2)}) collective-permute-start(bf16[512,512]{1,0:T(8,128)(2,1)} %get-tuple-element.191.refs_0_), channel_id=1, source_target_pairs={{0,1},{1,0},{2,3},{3,2},{4,5},{5,4},{6,7},{7,6},{8,9},{9,8},{10,11... | collective-permute-start | bytes 1572872 | tf_op jit(solution)/shard_map/ppermute | solution.py:37
  240.1 24.0 %collective-permute-start.34 = (bf16[2048,128]{1,0:T(8,128)(2,1)S(1)}, bf16[2048,128]{1,0:T(8,128)(2,1)S(1)}, u32[]{:S(2)}, u32[]{:S(2)}) collective-permute-start(bf16[2048,128]{1,0:T(8,128)(2,1)S(1)} %get-tuple-element.315), channel_id=1, source_target_pairs={{0,16},{1,17},{2,18},{3,19},{4,20},{5,21},{6,22},{7,23},{8,24},{9,... | collective-permute-start | bytes 1572872 | tf_op jit(solution)/shard_map/ppermute | solution.py:37
  240.6 24.6 %collective-permute-start.23 = (bf16[512,512]{1,0:T(8,128)(2,1)S(1)}, bf16[512,512]{1,0:T(8,128)(2,1)S(1)}, u32[]{:S(2)}, u32[]{:S(2)}) collective-permute-start(bf16[512,512]{1,0:T(8,128)(2,1)S(1)} %copy-done.8), channel_id=1, source_target_pairs={{0,1},{1,0},{2,3},{3,2},{4,5},{5,4},{6,7},{7,6},{8,9},{9,8},{10,11... | collective-permute-start | bytes 1572872 | tf_op jit(solution)/shard_map/ppermute | solution.py:37
  241.9 30.0 %collective-permute-start.24 = (bf16[512,512]{1,0:T(8,128)(2,1)S(1)}, bf16[512,512]{1,0:T(8,128)(2,1)S(1)}, u32[]{:S(2)}, u32[]{:S(2)}) collective-permute-start(bf16[512,512]{1,0:T(8,128)(2,1)S(1)} %copy-done.7), channel_id=1, source_target_pairs={{0,16},{1,17},{2,18},{3,19},{4,20},{5,21},{6,22},{7,23},{8,24},{9,... | collective-permute-start | bytes 1572872 | tf_op jit(solution)/shard_map/ppermute | solution.py:37
  252.8 19.2 %collective-permute-start.27 = (bf16[512,512]{1,0:T(8,128)(2,1)S(1)}, bf16[512,512]{1,0:T(8,128)(2,1)S(1)}, u32[]{:S(2)}, u32[]{:S(2)}) collective-permute-start(bf16[512,512]{1,0:T(8,128)(2,1)S(1)} %collective-permute-done.25.refs_5_), channel_id=1, source_target_pairs={{0,1},{1,0},{2,3},{3,2},{4,5},{5,4},{6,7},{7,6},{8,9},{9,8},{10,11... | collective-permute-start | bytes 1572872 | tf_op jit(solution)/shard_map/ppermute | solution.py:37
  253.9 23.8 %collective-permute-start.26 = (bf16[512,512]{1,0:T(8,128)(2,1)S(1)}, bf16[512,512]{1,0:T(8,128)(2,1)}, u32[]{:S(2)}, u32[]{:S(2)}) collective-permute-start(bf16[512,512]{1,0:T(8,128)(2,1)S(1)} %collective-permute-done.22.refs_2_), channel_id=1, source_target_pairs={{0,16},{1,17},{2,18},{3,19},{4,20},{5,21},{6,22},{7,23},{8,24},{9,... | collective-permute-start | bytes 1572872 | tf_op jit(solution)/shard_map/ppermute | solution.py:37
  319.8 40.2 %all-to-all-start.1 = ((bf16[4,1024,128]{2,1,0:T(8,128)(2,1)}), bf16[4,1024,128]{2,1,0:T(8,128)(2,1)S(1)}, u32[]{:S(2)}, u32[]{:S(2)}) async-start(bf16[4,1024,128]{2,1,0:T(8,128)(2,1)} %maximum_select_fusion.2), calls=%async_computation.1 | async-start | bytes 2097152 | tf_op jit(solution)/shard_map/all_to_all | solution.py:768
  325.2 228.3 %reduce-scatter.4.cloned.1.call-start = ((), (), s32[]{:S(2)}) async-start(), calls=%async_computation.7 | async-start | bytes 9437184 | tf_op jit(solution)/shard_map/reduce_scatter | solution.py:684
  325.2 14.3 %collective-permute-start.31 = (bf16[512,512]{1,0:T(8,128)(2,1)S(1)}, bf16[512,512]{1,0:T(8,128)(2,1)S(1)}, u32[]{:S(2)}, u32[]{:S(2)}) collective-permute-start(bf16[512,512]{1,0:T(8,128)(2,1)S(1)} %copy-done.82), channel_id=1, source_target_pairs={{0,16},{1,17},{2,18},{3,19},{4,20},{5,21},{6,22},{7,23},{8,24},{9,... | collective-permute-start | bytes 1572872 | tf_op jit(solution)/shard_map/ppermute | solution.py:37
  327.0 14.9 %collective-permute-start.30 = (bf16[512,512]{1,0:T(8,128)(2,1)S(1)}, bf16[512,512]{1,0:T(8,128)(2,1)S(1)}, u32[]{:S(2)}, u32[]{:S(2)}) collective-permute-start(bf16[512,512]{1,0:T(8,128)(2,1)S(1)} %copy-done.81), channel_id=1, source_target_pairs={{0,1},{1,0},{2,3},{3,2},{4,5},{5,4},{6,7},{7,6},{8,9},{9,8},{10,11... | collective-permute-start | bytes 1572872 | tf_op jit(solution)/shard_map/ppermute | solution.py:37
  327.4 25.8 %collective-permute-start.32 = (bf16[512,512]{1,0:T(8,128)(2,1)}, bf16[512,512]{1,0:T(8,128)(2,1)S(1)}, u32[]{:S(2)}, u32[]{:S(2)}) collective-permute-start(bf16[512,512]{1,0:T(8,128)(2,1)} %get-tuple-element.202), channel_id=1, source_target_pairs={{0,1},{1,0},{2,3},{3,2},{4,5},{5,4},{6,7},{7,6},{8,9},{9,8},{10,11... | collective-permute-start | bytes 1572872 | tf_op jit(solution)/shard_map/ppermute | solution.py:37
  335.7 17.4 %collective-permute-start.33 = (bf16[512,512]{1,0:T(8,128)(2,1)}, bf16[512,512]{1,0:T(8,128)(2,1)S(1)}, u32[]{:S(2)}, u32[]{:S(2)}) collective-permute-start(bf16[512,512]{1,0:T(8,128)(2,1)} %get-tuple-element.210), channel_id=1, source_target_pairs={{0,16},{1,17},{2,18},{3,19},{4,20},{5,21},{6,22},{7,23},{8,24},{9,... | collective-permute-start | bytes 1572872 | tf_op jit(solution)/shard_map/ppermute | solution.py:37
  346.3 18.9 %collective-permute-start.36 = (bf16[512,512]{1,0:T(8,128)(2,1)}, bf16[512,512]{1,0:T(8,128)(2,1)S(1)}, u32[]{:S(2)}, u32[]{:S(2)}) collective-permute-start(bf16[512,512]{1,0:T(8,128)(2,1)} %get-tuple-element.219), channel_id=1, source_target_pairs={{0,1},{1,0},{2,3},{3,2},{4,5},{5,4},{6,7},{7,6},{8,9},{9,8},{10,11... | collective-permute-start | bytes 1572872 | tf_op jit(solution)/shard_map/ppermute | solution.py:37
  346.6 18.6 %collective-permute-start.35 = (bf16[512,512]{1,0:T(8,128)(2,1)}, bf16[512,512]{1,0:T(8,128)(2,1)S(1)}, u32[]{:S(2)}, u32[]{:S(2)}) collective-permute-start(bf16[512,512]{1,0:T(8,128)(2,1)} %get-tuple-element.208), channel_id=1, source_target_pairs={{0,16},{1,17},{2,18},{3,19},{4,20},{5,21},{6,22},{7,23},{8,24},{9,... | collective-permute-start | bytes 1572872 | tf_op jit(solution)/shard_map/ppermute | solution.py:37
  386.0 15.1 %collective-permute-start.40 = (bf16[512,512]{1,0:T(8,128)(2,1)}, bf16[512,512]{1,0:T(8,128)(2,1)S(1)}, u32[]{:S(2)}, u32[]{:S(2)}) collective-permute-start(bf16[512,512]{1,0:T(8,128)(2,1)} %get-tuple-element.227.refs_0_), channel_id=1, source_target_pairs={{0,1},{1,0},{2,3},{3,2},{4,5},{5,4},{6,7},{7,6},{8,9},{9,8},{10,11... | collective-permute-start | bytes 1572872 | tf_op jit(solution)/shard_map/ppermute | solution.py:37
  387.7 15.1 %collective-permute-start.43 = (bf16[512,512]{1,0:T(8,128)(2,1)}, bf16[512,512]{1,0:T(8,128)(2,1)S(1)}, u32[]{:S(2)}, u32[]{:S(2)}) collective-permute-start(bf16[512,512]{1,0:T(8,128)(2,1)} %get-tuple-element.228.refs_1_), channel_id=1, source_target_pairs={{0,16},{1,17},{2,18},{3,19},{4,20},{5,21},{6,22},{7,23},{8,24},{9,... | collective-permute-start | bytes 1572872 | tf_op jit(solution)/shard_map/ppermute | solution.py:37
  388.0 24.1 %collective-permute-start.42 = (bf16[512,512]{1,0:T(8,128)(2,1)}, bf16[512,512]{1,0:T(8,128)(2,1)S(1)}, u32[]{:S(2)}, u32[]{:S(2)}) collective-permute-start(bf16[512,512]{1,0:T(8,128)(2,1)} %get-tuple-element.227.refs_0_), channel_id=1, source_target_pairs={{0,16},{1,17},{2,18},{3,19},{4,20},{5,21},{6,22},{7,23},{8,24},{9,... | collective-permute-start | bytes 1572872 | tf_op jit(solution)/shard_map/ppermute | solution.py:37
  389.8 22.4 %collective-permute-start.41 = (bf16[512,512]{1,0:T(8,128)(2,1)}, bf16[512,512]{1,0:T(8,128)(2,1)S(1)}, u32[]{:S(2)}, u32[]{:S(2)}) collective-permute-start(bf16[512,512]{1,0:T(8,128)(2,1)} %get-tuple-element.228.refs_1_), channel_id=1, source_target_pairs={{0,1},{1,0},{2,3},{3,2},{4,5},{5,4},{6,7},{7,6},{8,9},{9,8},{10,11... | collective-permute-start | bytes 1572872 | tf_op jit(solution)/shard_map/ppermute | solution.py:37
  401.1 16.7 %collective-permute-start.44 = (bf16[512,512]{1,0:T(8,128)(2,1)S(1)}, bf16[512,512]{1,0:T(8,128)(2,1)S(1)}, u32[]{:S(2)}, u32[]{:S(2)}) collective-permute-start(bf16[512,512]{1,0:T(8,128)(2,1)S(1)} %collective-permute-done.40.refs_2_), channel_id=1, source_target_pairs={{0,16},{1,17},{2,18},{3,19},{4,20},{5,21},{6,22},{7,23},{8,24},{9,... | collective-permute-start | bytes 1572872 | tf_op jit(solution)/shard_map/ppermute | solution.py:37
  402.8 15.0 %collective-permute-start.45 = (bf16[512,512]{1,0:T(8,128)(2,1)S(1)}, bf16[512,512]{1,0:T(8,128)(2,1)S(1)}, u32[]{:S(2)}, u32[]{:S(2)}) collective-permute-start(bf16[512,512]{1,0:T(8,128)(2,1)S(1)} %collective-permute-done.43.refs_5_), channel_id=1, source_target_pairs={{0,1},{1,0},{2,3},{3,2},{4,5},{5,4},{6,7},{7,6},{8,9},{9,8},{10,11... | collective-permute-start | bytes 1572872 | tf_op jit(solution)/shard_map/ppermute | solution.py:37
  435.4 67.0 %all-to-all-start.2 = ((bf16[4,1024,128]{2,1,0:T(8,128)(2,1)}), bf16[4,1024,128]{2,1,0:T(8,128)(2,1)S(1)}, u32[]{:S(2)}, u32[]{:S(2)}) async-start(bf16[4,1024,128]{2,1,0:T(8,128)(2,1)} %get-tuple-element.229), calls=%async_computation.2 | async-start | bytes 2097152 | tf_op jit(solution)/shard_map/all_to_all | solution.py:614
  439.9 236.7 %reduce-scatter.8.cloned.1.call-start = ((), (), s32[]{:S(2)}) async-start(), calls=%async_computation.9 | async-start | bytes 9437184 | tf_op jit(solution)/shard_map/reduce_scatter | solution.py:684
  466.7 17.6 %collective-permute-start.47 = (bf16[512,512]{1,0:T(8,128)(2,1)}, bf16[512,512]{1,0:T(8,128)(2,1)S(1)}, u32[]{:S(2)}, u32[]{:S(2)}) collective-permute-start(bf16[512,512]{1,0:T(8,128)(2,1)} %get-tuple-element.241), channel_id=1, source_target_pairs={{0,16},{1,17},{2,18},{3,19},{4,20},{5,21},{6,22},{7,23},{8,24},{9,... | collective-permute-start | bytes 1572872 | tf_op jit(solution)/shard_map/ppermute | solution.py:37
  467.3 17.0 %collective-permute-start.46 = (bf16[512,512]{1,0:T(8,128)(2,1)}, bf16[512,512]{1,0:T(8,128)(2,1)S(1)}, u32[]{:S(2)}, u32[]{:S(2)}) collective-permute-start(bf16[512,512]{1,0:T(8,128)(2,1)} %get-tuple-element.234), channel_id=1, source_target_pairs={{0,1},{1,0},{2,3},{3,2},{4,5},{5,4},{6,7},{7,6},{8,9},{9,8},{10,11... | collective-permute-start | bytes 1572872 | tf_op jit(solution)/shard_map/ppermute | solution.py:37
  475.9 16.2 %collective-permute-start.48 = (bf16[512,512]{1,0:T(8,128)(2,1)}, bf16[512,512]{1,0:T(8,128)(2,1)S(1)}, u32[]{:S(2)}, u32[]{:S(2)}) collective-permute-start(bf16[512,512]{1,0:T(8,128)(2,1)} %get-tuple-element.236), channel_id=1, source_target_pairs={{0,1},{1,0},{2,3},{3,2},{4,5},{5,4},{6,7},{7,6},{8,9},{9,8},{10,11... | collective-permute-start | bytes 1572872 | tf_op jit(solution)/shard_map/ppermute | solution.py:37
  482.9 12.5 %collective-permute-start.49 = (bf16[512,512]{1,0:T(8,128)(2,1)}, bf16[512,512]{1,0:T(8,128)(2,1)S(1)}, u32[]{:S(2)}, u32[]{:S(2)}) collective-permute-start(bf16[512,512]{1,0:T(8,128)(2,1)} %get-tuple-element.244), channel_id=1, source_target_pairs={{0,16},{1,17},{2,18},{3,19},{4,20},{5,21},{6,22},{7,23},{8,24},{9,... | collective-permute-start | bytes 1572872 | tf_op jit(solution)/shard_map/ppermute | solution.py:37
  488.9 27.6 %collective-permute-start.51 = (bf16[512,512]{1,0:T(8,128)(2,1)}, bf16[512,512]{1,0:T(8,128)(2,1)S(1)}, u32[]{:S(2)}, u32[]{:S(2)}) collective-permute-start(bf16[512,512]{1,0:T(8,128)(2,1)} %get-tuple-element.251), channel_id=1, source_target_pairs={{0,1},{1,0},{2,3},{3,2},{4,5},{5,4},{6,7},{7,6},{8,9},{9,8},{10,11... | collective-permute-start | bytes 1572872 | tf_op jit(solution)/shard_map/ppermute | solution.py:37
  490.6 25.9 %collective-permute-start.50 = (bf16[512,512]{1,0:T(8,128)(2,1)}, bf16[512,512]{1,0:T(8,128)(2,1)S(1)}, u32[]{:S(2)}, u32[]{:S(2)}) collective-permute-start(bf16[512,512]{1,0:T(8,128)(2,1)} %get-tuple-element.242), channel_id=1, source_target_pairs={{0,16},{1,17},{2,18},{3,19},{4,20},{5,21},{6,22},{7,23},{8,24},{9,... | collective-permute-start | bytes 1572872 | tf_op jit(solution)/shard_map/ppermute | solution.py:37
  537.9 198.7 %reduce-scatter.6.cloned.1.call-start = ((), (), s32[]{:S(2)}) async-start(), calls=%async_computation.8 | async-start | bytes 9437184 | tf_op jit(solution)/shard_map/reduce_scatter | solution.py:684
  538.9 12.9 %collective-permute-start.55 = (bf16[512,512]{1,0:T(8,128)(2,1)S(1)}, bf16[512,512]{1,0:T(8,128)(2,1)S(1)}, u32[]{:S(2)}, u32[]{:S(2)}) collective-permute-start(bf16[512,512]{1,0:T(8,128)(2,1)S(1)} %copy-done.21), channel_id=1, source_target_pairs={{0,1},{1,0},{2,3},{3,2},{4,5},{5,4},{6,7},{7,6},{8,9},{9,8},{10,11... | collective-permute-start | bytes 1572872 | tf_op jit(solution)/shard_map/ppermute | solution.py:37
  540.3 12.5 %collective-permute-start.58 = (bf16[512,512]{1,0:T(8,128)(2,1)S(1)}, bf16[512,512]{1,0:T(8,128)(2,1)S(1)}, u32[]{:S(2)}, u32[]{:S(2)}) collective-permute-start(bf16[512,512]{1,0:T(8,128)(2,1)S(1)} %copy-done.22), channel_id=1, source_target_pairs={{0,16},{1,17},{2,18},{3,19},{4,20},{5,21},{6,22},{7,23},{8,24},{9,... | collective-permute-start | bytes 1572872 | tf_op jit(solution)/shard_map/ppermute | solution.py:37
  541.3 16.6 %collective-permute-start.57 = (bf16[512,512]{1,0:T(8,128)(2,1)S(1)}, bf16[512,512]{1,0:T(8,128)(2,1)}, u32[]{:S(2)}, u32[]{:S(2)}) collective-permute-start(bf16[512,512]{1,0:T(8,128)(2,1)S(1)} %copy-done.21), channel_id=1, source_target_pairs={{0,16},{1,17},{2,18},{3,19},{4,20},{5,21},{6,22},{7,23},{8,24},{9,... | collective-permute-start | bytes 1572872 | tf_op jit(solution)/shard_map/ppermute | solution.py:37
  542.4 15.6 %collective-permute-start.56 = (bf16[512,512]{1,0:T(8,128)(2,1)S(1)}, bf16[512,512]{1,0:T(8,128)(2,1)}, u32[]{:S(2)}, u32[]{:S(2)}) collective-permute-start(bf16[512,512]{1,0:T(8,128)(2,1)S(1)} %copy-done.22), channel_id=1, source_target_pairs={{0,1},{1,0},{2,3},{3,2},{4,5},{5,4},{6,7},{7,6},{8,9},{9,8},{10,11... | collective-permute-start | bytes 1572872 | tf_op jit(solution)/shard_map/ppermute | solution.py:37
  551.8 13.8 %collective-permute-start.59 = (bf16[512,512]{1,0:T(8,128)(2,1)S(1)}, bf16[512,512]{1,0:T(8,128)(2,1)}, u32[]{:S(2)}, u32[]{:S(2)}) collective-permute-start(bf16[512,512]{1,0:T(8,128)(2,1)S(1)} %collective-permute-done.55.refs_2_.refs_11_), channel_id=1, source_target_pairs={{0,16},{1,17},{2,18},{3,19},{4,20},{5,21},{6,22},{7,23},{8,24},{9,... | collective-permute-start | bytes 1572872 | tf_op jit(solution)/shard_map/ppermute | solution.py:37
  552.8 12.8 %collective-permute-start.60 = (bf16[512,512]{1,0:T(8,128)(2,1)S(1)}, bf16[512,512]{1,0:T(8,128)(2,1)}, u32[]{:S(2)}, u32[]{:S(2)}) collective-permute-start(bf16[512,512]{1,0:T(8,128)(2,1)S(1)} %collective-permute-done.58.refs_5_.refs_14_), channel_id=1, source_target_pairs={{0,1},{1,0},{2,3},{3,2},{4,5},{5,4},{6,7},{7,6},{8,9},{9,8},{10,11... | collective-permute-start | bytes 1572872 | tf_op jit(solution)/shard_map/ppermute | solution.py:37
  574.3 25.4 %collective-permute-start.61 = (bf16[2048,128]{1,0:T(8,128)(2,1)S(1)}, bf16[2048,128]{1,0:T(8,128)(2,1)S(1)}, u32[]{:S(2)}, u32[]{:S(2)}) collective-permute-start(bf16[2048,128]{1,0:T(8,128)(2,1)S(1)} %get-tuple-element.313), channel_id=1, source_target_pairs={{0,16},{1,17},{2,18},{3,19},{4,20},{5,21},{6,22},{7,23},{8,24},{9,... | collective-permute-start | bytes 1572872 | tf_op jit(solution)/shard_map/ppermute | solution.py:37
  575.4 24.2 %collective-permute-start.62 = (bf16[512,512]{1,0:T(8,128)(2,1)S(1)}, bf16[512,512]{1,0:T(8,128)(2,1)S(1)}, u32[]{:S(2)}, u32[]{:S(2)}) collective-permute-start(bf16[512,512]{1,0:T(8,128)(2,1)S(1)} %get-tuple-element.307), channel_id=1, source_target_pairs={{0,16},{1,17},{2,18},{3,19},{4,20},{5,21},{6,22},{7,23},{8,24},{9,... | collective-permute-start | bytes 1572872 | tf_op jit(solution)/shard_map/ppermute | solution.py:37
  626.0 19.4 %collective-permute-start.64 = (bf16[512,512]{1,0:T(8,128)(2,1)}, bf16[512,512]{1,0:T(8,128)(2,1)S(1)}, u32[]{:S(2)}, u32[]{:S(2)}) collective-permute-start(bf16[512,512]{1,0:T(8,128)(2,1)} %get-tuple-element.276), channel_id=1, source_target_pairs={{0,16},{1,17},{2,18},{3,19},{4,20},{5,21},{6,22},{7,23},{8,24},{9,... | collective-permute-start | bytes 1572872 | tf_op jit(solution)/shard_map/ppermute | solution.py:37
  627.0 18.4 %collective-permute-start.63 = (bf16[512,512]{1,0:T(8,128)(2,1)}, bf16[512,512]{1,0:T(8,128)(2,1)S(1)}, u32[]{:S(2)}, u32[]{:S(2)}) collective-permute-start(bf16[512,512]{1,0:T(8,128)(2,1)} %get-tuple-element.269), channel_id=1, source_target_pairs={{0,1},{1,0},{2,3},{3,2},{4,5},{5,4},{6,7},{7,6},{8,9},{9,8},{10,11... | collective-permute-start | bytes 1572872 | tf_op jit(solution)/shard_map/ppermute | solution.py:37
  635.4 19.0 %collective-permute-start.65 = (bf16[512,512]{1,0:T(8,128)(2,1)}, bf16[512,512]{1,0:T(8,128)(2,1)S(1)}, u32[]{:S(2)}, u32[]{:S(2)}) collective-permute-start(bf16[512,512]{1,0:T(8,128)(2,1)} %get-tuple-element.271), channel_id=1, source_target_pairs={{0,1},{1,0},{2,3},{3,2},{4,5},{5,4},{6,7},{7,6},{8,9},{9,8},{10,11... | collective-permute-start | bytes 1572872 | tf_op jit(solution)/shard_map/ppermute | solution.py:37
  668.1 40.8 %all-to-all-start.3 = ((bf16[4,1024,128]{2,1,0:T(8,128)(2,1)}), bf16[4,1024,128]{2,1,0:T(8,128)(2,1)}, u32[]{:S(2)}, u32[]{:S(2)}) async-start(bf16[4,1024,128]{2,1,0:T(8,128)(2,1)} %shard_map.350), calls=%async_computation.4 | async-start | bytes 2097152 | tf_op jit(solution)/shard_map/all_to_all | solution.py:614
  674.3 40.0 %collective-permute-start.72 = (f32[4,1664]{1,0:T(4,128)S(1)}, f32[4,1664]{1,0:T(4,128)S(1)}, u32[]{:S(2)}, u32[]{:S(2)}) collective-permute-start(f32[4,1664]{1,0:T(4,128)S(1)} %add.91), channel_id=1, source_target_pairs={{0,2},{1,3},{2,0},{3,1},{4,6},{5,7},{6,4},{7,5},{8,10},{9,11},{10,... | collective-permute-start | bytes 79880 | tf_op jit(solution)/shard_map/ppermute | solution.py:37
  678.7 35.6 %collective-permute-start.73 = (bf16[512,512]{1,0:T(8,128)(2,1)}, bf16[512,512]{1,0:T(8,128)(2,1)}, u32[]{:S(2)}, u32[]{:S(2)}) collective-permute-start(bf16[512,512]{1,0:T(8,128)(2,1)} %get-tuple-element.309), channel_id=1, source_target_pairs={{0,16},{1,17},{2,18},{3,19},{4,20},{5,21},{6,22},{7,23},{8,24},{9,... | collective-permute-start | bytes 1572872 | tf_op jit(solution)/shard_map/ppermute | solution.py:37
  (107 other events, 791.7 us)
Sparse Core Ops, SparseCore 0:
  25.2 86.1 all-gather.8
  113.6 27.8 all-gather.10
  143.0 81.5 all-gather.12
  226.1 80.5 all-gather.14
  435.5 98.3 reduce-scatter.3
  538.0 90.3 reduce-scatter.7
  630.7 105.9 reduce-scatter.5

commit v5 on v4

--- a/solution.py
+++ b/solution.py
@@ -102,11 +102,10 @@
                 at = slot * QUARTER + block * 128
                 for z in range(several):
                     if by_rows:
-                        n = weights.shape[2]
-                        part = weights[z, c, :, pl.ds(pl.multiple_of(y * 512 + start, 128), 128)]
-                        kept[z * n : z * n + n, at : at + 128] = part
+                        kept[:, at : at + 128] = weights[0, c, :, pl.ds(pl.multiple_of(y * 512 + start, 128), 128)]
                     else:
-                        kept[at : at + 128, :] = weights[0, c, y, pl.ds(start, 128), :]
+                        n = weights.shape[4]
+                        kept[at : at + 128, z * n : z * n + n] = weights[z, c, y, pl.ds(start, 128), :]
 
     total = None
     for slot in range(4):
@@ -117,19 +116,20 @@
     finish(total, extra, outs)
 
 
-def wide(pieces, weights, spot, by_rows, finish, extra, count, sums=0):
+def wide(pieces, weights, spot, by_rows, finish, extra, count, sums=0, n=None, lane=0):
+    several = 1
     if by_rows:
         n = weights.shape[1]
         weights = weights.reshape(4, 2, n, 1024)
+        kept = pltpu.VMEM((n, WIDTH), BF)
+        block = (1, 2, n, 1024)
+    else:
+        n = n or weights.shape[2]
+        weights = weights.reshape(4, 2, 2, 512, weights.shape[2])
         several = 4 if n < 256 else 1
-        kept = pltpu.VMEM((several * n, WIDTH), BF)
-    else:
-        n = weights.shape[2]
-        weights = weights.reshape(4, 2, 2, 512, n)
-        several = 1
-        kept = pltpu.VMEM((WIDTH, n), BF)
-    block = (several,) + weights.shape[1:]
-    tail = (0,) * (len(block) - 1)
+        kept = pltpu.VMEM((WIDTH, several * n), BF)
+        block = (several, 2, 2, 512, n)
+    tail = (0,) * (len(block) - 2) + (lane,)
     total = 4 * n
     n = several * n
     bias = pl.BlockSpec((1, n), lambda z, t, *_: (0, z))
@@ -197,7 +197,7 @@
         high[...] = total.astype(high.dtype)
 
 
-def partial(local, weights, spot, by_rows, mask, low, high):
+def partial(local, weights, spot, by_rows, lane, mask, low, high):
     n = local.shape[1] // 4
     if by_rows:
         weights = weights.reshape(4, 2, n, 1024)
@@ -207,8 +207,8 @@
         ]
         ins = (weights, weights)
     else:
-        weights = weights.reshape(4, 2, 2, 512, n)
-        specs = [pl.BlockSpec((4, 2, 2, 128, n), lambda t, p: (0, 0, 0, p[0] ^ mask, 0))]
+        weights = weights.reshape(4, 2, 2, 512, weights.shape[2])
+        specs = [pl.BlockSpec((4, 2, 2, 128, n), lambda t, p: (0, 0, 0, p[0] ^ mask, lane))]
         ins = (weights,)
     return call(
         functools.partial(partial_body, by_rows, n),
@@ -276,6 +276,19 @@
         place_pair_body, (1,), spot, (own, other), [fixed((512, 512))] * 2, grid, [fixed(g.shape) for g in grid], [],
         2 * 512 * 512, 8 * 512 * 512,
     )
+
+
+def turn_body(spot, piece, out):
+    out[...] = piece[...].T
+
+
+def turn(piece, spot):
+    rows, width = piece.shape
+    (out,) = call(
+        turn_body, (1,), spot, (piece,), [fixed(piece.shape)], [shape_of(width, rows, dtype=BF)], [fixed((width, rows))], [],
+        rows * width, 4 * rows * width,
+    )
+    return out
 
 
 def grad_pair_body(spot, *refs):
@@ -474,6 +487,10 @@
         out[z] = value[:, z * 128 : z * 128 + 128].astype(BF)
 
 
+def whole_of(blocks):
+    return jnp.concatenate([blocks[z] for z in range(4)], axis=1).astype(F32)
+
+
 def norm_one_sums(spot, *refs):
     parts, (low, high, bias, resid, stats) = refs[:6], refs[6:]
     t = pl.program_id(0)
@@ -505,25 +522,25 @@
 
 def norm_two_sums(spot, *refs):
     parts = refs[:6]
-    bias, resid, moments, gain, shift, dy_low, dy_high, gain_two, resid_two, stats = refs[6:]
+    bias, resid, moments, gain, shift, dy, gain_two, resid_two, stats = refs[6:]
     t = pl.program_id(0)
     ffn = summed(parts, t) + bias[...]
     columns = columns_of(moments[...])
     hidden = (resid[...] - columns[:, 0:1]) * columns[:, 1:2] * gain[...] + shift[...]
     total = hidden + ffn
     resid_two[...] = total
-    scaled = pick(dy_low, dy_high, t < STEPS // 2).astype(F32) * gain_two[...]
+    scaled = whole_of(dy) * gain_two[...]
     stats[...] = rows_of([total, total * total, scaled, scaled * total, ffn * ffn])
 
 
-def norm_two(spot, resid_two, s0, s1, s2, s3, dy_low, dy_high, gain, shift, layer_out, grad_two, low, high, sums):
+def norm_two(spot, resid_two, s0, s1, s2, s3, dy, gain, shift, layer_out, grad_two, low, high, sums):
     mean, rstd, total = moments_of((s0, s1, s2, s3))
     mean_e = total[2:3]
     along = rstd * (total[3:4] - mean * mean_e)
     columns = columns_of(jnp.concatenate([mean, rstd, mean_e, along] + [mean] * 4, axis=0))
     normed = (resid_two[...] - columns[:, 0:1]) * columns[:, 1:2]
     t = pl.program_id(0)
-    upstream = pick(dy_low, dy_high, t < STEPS // 2).astype(F32)
+    upstream = whole_of(dy)
     write_blocks(layer_out, normed * gain[...] + shift[...])
     back = columns[:, 1:2] * (upstream * gain[...] - columns[:, 2:3] - normed * columns[:, 3:4])
     grad_two[...] = back
@@ -592,17 +609,6 @@
                 out[:, pl.ds(pl.multiple_of((spot[3] ^ mask) * 128, 128), 128)] = block[...]
 
 
-def assemble_whole_body(spot, blocks, low, high):
-    t = pl.program_id(0)
-    whole = jnp.concatenate([blocks[z] for z in range(4)], axis=1)
-    write_halves(t, low, high, whole)
-
-
-def assemble_whole(blocks, spot):
-    half = shape_of(HALF, QUARTER, dtype=BF)
-    return elementwise(assemble_whole_body, spot, (blocks,), [BLOCKS], [half, half], [LOW, HIGH])
-
-
 def assemble(blocks, spot):
     half = shape_of(HALF, QUARTER, dtype=BF)
     return elementwise(
@@ -633,8 +639,8 @@
     return (low, high, x_low, x_high, y_low, y_high, xy_low, xy_high)
 
 
-def square_scatter(local, weights, spot, by_rows, first=lambda: None, middle=lambda: None, between=lambda: None, after=lambda: None):
-    term = functools.partial(partial, local, weights, spot, by_rows)
+def square_scatter(local, weights, spot, by_rows, lane=0, first=lambda: None, middle=lambda: None, between=lambda: None, after=lambda: None):
+    term = functools.partial(partial, local, weights, spot, by_rows, lane)
     far_low, far_high = term(3, BF, BF)
     far_low = swap(far_low, X_BIT)
     far_high = swap(far_high, Y_BIT)
@@ -713,7 +719,7 @@
 
     token_own, token_send = split_y(tokens, yi)
     token_other = swap(token_send, Y_BIT)
-    half_qkv, sent = halve_columns([w_query, w_key, w_value], yi, token_send)
+    half_qkv, sent = halve_columns([w_query, w_key, w_value, turn(w_proj, spot)], yi, token_send)
     vectors = jnp.concatenate(
         [v.reshape(2, -1) for v in (b_query, b_value, b_proj, norm_gain, norm_shift, b_down, final_gain, final_shift, b_up)],
         axis=1,
@@ -733,23 +739,22 @@
 
     full_qkv = gather_zc(tie(half_qkv, vectors))
     token_blocks = spread_z(token_own, token_other, yi, zi)
-    half_proj, sent = halve_rows(w_proj, yi, sent)
     half_up, sent = halve_columns([w_up], yi, sent)
-    half_down, sent = halve_rows(w_down, yi, sent)
-    spot.after(vectors, half_proj)
+    spot.after(vectors, half_up)
     token_low, token_high = assemble(token_blocks, spot)
     gathered = square_gather(token_low, token_high)
-    full_proj = gather_zc(tie(half_proj, token_low))
     full_up = gather_zc(tie(half_up, token_low))
-    full_down = gather_zc(tie(half_down, token_low))
-    (qkv,) = wide(gathered, full_qkv, spot, False, finish_bias, (qkv_bias,), 1)
+    (qkv,) = wide(gathered, full_qkv, spot, False, finish_bias, (qkv_bias,), 1, n=384)
+    half_down, sent = halve_rows(tie(w_down, qkv), yi)
     heads_out, logsum = attention(qkv, ids_row, ids_column, spot)
+    spot.after(half_down)
+    full_down = gather_zc(half_down)
     full = shape_of(LEN, QUARTER)
     low_half = shape_of(HALF, QUARTER, dtype=BF)
     stats_shape = shape_of(8, LEN)
     sums_shape = shape_of(8, QUARTER)
 
-    parts = square_scatter(heads_out, full_proj, spot, True)
+    parts = square_scatter(heads_out, full_qkv, spot, False, 3)
     resid, stats_one = elementwise(
         norm_one_sums, spot, (*parts, token_low, token_high, p_bias), PARTS + [LOW, HIGH, VECTOR], [full, stats_shape], [TILE, STATS]
     )
@@ -762,22 +767,15 @@
     dy_other = swap(dy_send, Y_BIT)
     act, slope = wide(hidden_wide, full_up, spot, False, finish_gelu, (u_bias,), 2)
     dy = side_by_side(dy_own.reshape(2, LEN, 128), dy_other.reshape(2, LEN, 128), yi, 0)
-    dy_blocks, dy_halves = [], []
-
-    def first():
-        dy_blocks.append(lax.all_to_all(tie(dy, spot.value), "z", 0, 0, tiled=True))
-
-    def after():
-        dy_halves.extend(assemble_whole(dy_blocks[0], spot))
-
-    parts = square_scatter(act, full_down, spot, True, first=first, after=after)
+    dy = lax.all_to_all(tie(dy, act), "z", 0, 0, tiled=True)
+    parts = square_scatter(act, full_down, spot, True)
     resid_two, stats_two = elementwise(
-        norm_two_sums, spot, (*parts, d_bias, resid, moments, n_gain, n_shift, *dy_halves, f_gain),
-        PARTS + [VECTOR, TILE, STATS, VECTOR, VECTOR, LOW, HIGH, VECTOR], [full, stats_shape], [TILE, STATS],
+        norm_two_sums, spot, (*parts, d_bias, resid, moments, n_gain, n_shift, dy, f_gain),
+        PARTS + [VECTOR, TILE, STATS, VECTOR, VECTOR, BLOCKS, VECTOR], [full, stats_shape], [TILE, STATS],
     )
     layer_share, grad_two, ffn_low, ffn_high, sums_two = elementwise(
-        norm_two, spot, (resid_two, *square_stats(stats_two), *dy_halves, f_gain, f_shift),
-        [TILE] + [STATS] * 4 + [LOW, HIGH, VECTOR, VECTOR],
+        norm_two, spot, (resid_two, *square_stats(stats_two), dy, f_gain, f_shift),
+        [TILE] + [STATS] * 4 + [BLOCKS, VECTOR, VECTOR],
         [shape_of(4, LEN, 128, dtype=BF), full, low_half, low_half, sums_shape], [BLOCKS, TILE, LOW, HIGH, SUMS],
     )
     ffn_wide = square_gather(ffn_low, ffn_high)
@@ -804,7 +802,7 @@
     attn_wide = square_gather(attn_low, attn_high)
     grad_up = scatter_zc(tie(up[0], spot.value))
     spot.after(grad_down)
-    (grad_heads,) = wide(attn_wide, full_proj, spot, True, finish_plain, (), 1)
+    (grad_heads,) = wide(attn_wide, full_qkv, spot, False, finish_plain, (), 1, n=128, lane=3)
     layer_own, layer_other = swap_y(tie(layer_parts, grad_heads), yi)
     down = exchange_rows(tie(grad_down, grad_heads))
     grad_qkv, sums_qkv = attention_back(qkv, ids_row, ids_column, logsum, grad_heads, spot)

time: 767 us -> 747 us (0.974)
  waiting for transfers between devices: 269 us -> 254 us
    all_gather x4 -> x3, waiting for transfers between devices: 8.75 us -> 0.04 us  [gather_zc(): return lax.all_gather(piece, ('z', 'c'), axis=0)]
    ppermute x78 -> x77, waiting for transfers between devices: 223 us -> 218 us  [swap(): return lax.ppermute(piece, AXES, [(i, i ^ mask) for i in range(32)])]
    ppermute x78 -> x77, starting transfers between devices: 84.5 us -> 82.3 us  [swap(): return lax.ppermute(piece, AXES, [(i, i ^ mask) for i in range(32)])]
  transfers between devices with their start and end apart: 88 -> 86, of which waited for: 49 -> 45; matrix products, arithmetic and copies ran while one was open for 4% -> 4% of each run, Pallas kernels for 36% -> 38%
where the time goes in v5:
time: 747 us; the launch traced here: 741 us
  Pallas kernels  316 us (42%)
  waiting for transfers between devices  254 us (34%)
  starting transfers between devices  96.2 us (13%)
  local copies, waits for them, and re-layouts  29.8 us (4%)
  other arithmetic  19.8 us (3%)
  between operations  15.4 us (2%)
  blocking collectives  10.3 us (1%)
    pallas_call x39, Pallas kernels, call(): pl.pallas_call(body, grid_spec=pltpu.PrefetchScalarGridSpec(num_scalar_pr...  316 us
    ppermute x77, waiting for transfers between devices, swap(): return lax.ppermute(piece, AXES, [(i, i ^ mask) for i in range(32)])  218 us
    ppermute x77, starting transfers between devices, swap(): return lax.ppermute(piece, AXES, [(i, i ^ mask) for i in range(32)])  82.3 us
    all_to_all x2, waiting for transfers between devices, from_share(): return lax.all_to_all(share, 'z', 0, 0, tiled=True).reshape(2, 2 * LEN, 128)  29.3 us
    unnamed x188, local copies, waits for them, and re-layouts  16.1 us
  transfers between devices with their start and end apart: 86, of which 45 were waited for; matrix products, arithmetic and copies ran while one was open for 4% of the time, Pallas kernels for 38%

profile of v5, /device:TPU:0, one launch (start us, length us, event | category | flops | bytes accessed | tf_op | source)
XLA Modules:
  0.0 741.3 jit_solution(10582775239407604977)
XLA Ops:
  15.4 10.3 %all_to_all.24 = f32[4,1,1536]{2,1,0:T(1,128)S(1)} all-to-all(f32[4,1,1536]{2,1,0:T(1,128)S(1)} %broadcast_in_dim.4), channel_id=1, replica_groups=mesh['y'=2,'c'=2,'z'=4,'x'=2] {'z'}, dimensions={0} | all-to-all | bytes 49152 | tf_op jit(solution)/shard_map/all_to_all | solution.py:728
  32.3 11.9 %collective-permute-done.1 = bf16[2048,128]{1,0:T(8,128)(2,1)S(1)} collective-permute-done((bf16[2048,128]{1,0:T(8,128)(2,1)S(1)}, bf16[2048,128]{1,0:T(8,128)(2,1)S(1)}, u32[]{:S(2)}, u32[]{:S(2)}) %collective-permute-start.1) | collective-permute-done | bytes 524320 | tf_op jit(solution)/shard_map/ppermute | solution.py:37
  45.3 3.8 collective-permute-start.4
  49.7 4.0 collective-permute-done
  54.8 7.1 collective-permute-done.4.refs_3_
  61.9 10.8 %collective-permute-done.2.refs_1_ = bf16[1024,128]{1,0:T(8,128)(2,1)S(1)} collective-permute-done((bf16[1024,128]{1,0:T(8,128)(2,1)S(1)}, bf16[1024,128]{1,0:T(8,128)(2,1)S(1)}, u32[]{:S(2)}, u32[]{:S(2)}) %collective-permute-start.2) | collective-permute-done | bytes 262176 | tf_op jit(solution)/shard_map/ppermute | solution.py:37
  72.7 26.1 %collective-permute-done.3.refs_2_ = bf16[1024,128]{1,0:T(8,128)(2,1)S(1)} collective-permute-done((bf16[1024,128]{1,0:T(8,128)(2,1)S(1)}, bf16[1024,128]{1,0:T(8,128)(2,1)S(1)}, u32[]{:S(2)}, u32[]{:S(2)}) %collective-permute-start.3) | collective-permute-done | bytes 262176 | tf_op jit(solution)/shard_map/ppermute | solution.py:37
  99.5 4.2 shard_map.314
  108.1 11.0 %collective-permute-done.8.refs_5_ = bf16[512,512]{1,0:T(8,128)(2,1)S(1)} collective-permute-done((bf16[512,512]{1,0:T(8,128)(2,1)}, bf16[512,512]{1,0:T(8,128)(2,1)S(1)}, u32[]{:S(2)}, u32[]{:S(2)}) %collective-permute-start.8) | collective-permute-done | bytes 524320 | tf_op jit(solution)/shard_map/ppermute | solution.py:37
  123.4 7.7 %collective-permute-done.6.refs_3_ = bf16[512,512]{1,0:T(8,128)(2,1)S(1)} collective-permute-done((bf16[512,512]{1,0:T(8,128)(2,1)}, bf16[512,512]{1,0:T(8,128)(2,1)S(1)}, u32[]{:S(2)}, u32[]{:S(2)}) %collective-permute-start.6) | collective-permute-done | bytes 524320 | tf_op jit(solution)/shard_map/ppermute | solution.py:37
  131.1 5.6 collective-permute-done.10.refs_7_
  137.7 16.1 %shard_map.315.queries.whole = bf16[1024,1536]{1,0:T(8,128)(2,1)} custom-call(s32[4]{0:T(128)} %pad_add_fusion.spot, bf16[512,512]{1,0:T(8,128)(2,1)} %get-tuple-element.161.refs_0_.refs_6_, bf16[512,512]{1,0:T(8,128)(2,1)} %get-tuple-element.163.refs_1_.refs_7_, bf16[512,512]{1,0:T(8,128)(2,1)} %copy-done.2, bf16[512,512]{1,0:T(8,128)(2,1)} %copy-done.3, ...), custom_call_target="tpu_custom_call" | custom-call | flops 1610612736 | bytes 3407872 | tf_op jit(solution)/shard_map/pallas_call | solution.py:60
  154.6 11.0 %collective-permute-done.13 = bf16[512,512]{1,0:T(8,128)(2,1)S(1)} collective-permute-done((bf16[512,512]{1,0:T(8,128)(2,1)S(1)}, bf16[512,512]{1,0:T(8,128)(2,1)S(1)}, u32[]{:S(2)}, u32[]{:S(2)}) %collective-permute-start.13) | collective-permute-done | bytes 524320 | tf_op jit(solution)/shard_map/ppermute | solution.py:37
  171.8 13.1 %shard_map.316 = (bf16[1024,512]{1,0:T(8,128)(2,1)}, f32[4,1,1024]{2,1,0:T(1,128)}) custom-call(s32[4]{0:T(128)} %pad_add_fusion.spot, bf16[1024,1536]{1,0:T(8,128)(2,1)} %shard_map.315.queries.whole, bf16[1024,1536]{1,0:T(8,128)(2,1)} %shard_map.315.queries.whole, s32[1,1024]{1,0:T(1,128)} %bitcast.148, s32[1024,1]{1,0:T(8,128)} %copy.44.ids_column), custom_call_target="tpu_custom_call" | custom-call | flops 2147483648 | bytes 1048576 | tf_op jit(solution)/shard_map/pallas_call | solution.py:60
  184.8 4.5 shard_map.317
  192.3 4.6 shard_map.318
  197.4 4.6 shard_map.319
  206.7 3.6 shard_map.320
  212.2 4.9 collective-permute-done.16.refs_2_
  217.1 4.8 shard_map.321
  225.0 6.3 shard_map.322
  239.0 5.1 shard_map.323
  248.6 10.7 %collective-permute-done.26.refs_5_ = bf16[512,512]{1,0:T(8,128)(2,1)S(1)} collective-permute-done((bf16[512,512]{1,0:T(8,128)(2,1)}, bf16[512,512]{1,0:T(8,128)(2,1)S(1)}, u32[]{:S(2)}, u32[]{:S(2)}) %collective-permute-start.26) | collective-permute-done | bytes 524320 | tf_op jit(solution)/shard_map/ppermute | solution.py:37
  261.9 8.6 %collective-permute-done.35 = bf16[2048,128]{1,0:T(8,128)(2,1)S(1)} collective-permute-done((bf16[2048,128]{1,0:T(8,128)(2,1)S(1)}, bf16[2048,128]{1,0:T(8,128)(2,1)S(1)}, u32[]{:S(2)}, u32[]{:S(2)}) %collective-permute-start.35) | collective-permute-done | bytes 524320 | tf_op jit(solution)/shard_map/ppermute | solution.py:37
  271.7 8.8 %collective-permute-done.25.refs_4_ = bf16[512,512]{1,0:T(8,128)(2,1)S(1)} collective-permute-done((bf16[512,512]{1,0:T(8,128)(2,1)S(1)}, bf16[512,512]{1,0:T(8,128)(2,1)S(1)}, u32[]{:S(2)}, u32[]{:S(2)}) %collective-permute-start.25) | collective-permute-done | bytes 524320 | tf_op jit(solution)/shard_map/ppermute | solution.py:37
  280.5 5.7 collective-permute-done.27.refs_6_
  286.2 20.2 %shard_map.324 = (bf16[1024,2048]{1,0:T(8,128)(2,1)}, bf16[1024,2048]{1,0:T(8,128)(2,1)}) custom-call(s32[4]{0:T(128)} %pad_add_fusion.spot, bf16[512,512]{1,0:T(8,128)(2,1)} %get-tuple-element.189.refs_0_, bf16[512,512]{1,0:T(8,128)(2,1)} %get-tuple-element.191.refs_1_, bf16[512,512]{1,0:T(8,128)(2,1)} %copy-done.10, bf16[512,512]{1,0:T(8,128)(2,1)} %copy-done.11, ...), custom_call_target="tpu_custom_call" | custom-call | flops 2147483648 | bytes 4194304 | tf_op jit(solution)/shard_map/pallas_call | solution.py:60
  310.3 6.5 shard_map.325
  317.7 6.7 shard_map.326
  325.7 6.7 shard_map.327
  339.7 5.4 collective-permute-done.32.refs_3_
  345.1 6.8 shard_map.329
  353.3 6.6 shard_map.330
  367.9 6.6 shard_map.331
  378.6 10.8 %collective-permute-done.39.refs_2_ = bf16[512,512]{1,0:T(8,128)(2,1)S(1)} collective-permute-done((bf16[512,512]{1,0:T(8,128)(2,1)}, bf16[512,512]{1,0:T(8,128)(2,1)S(1)}, u32[]{:S(2)}, u32[]{:S(2)}) %collective-permute-start.39) | collective-permute-done | bytes 524320 | tf_op jit(solution)/shard_map/ppermute | solution.py:37
  390.9 3.9 collective-permute-done.41.refs_4_
  395.1 5.3 collective-permute-done.43.refs_6_
  402.1 15.9 %shard_map.332 = bf16[4,2,512,1024]{3,2,1,0:T(8,128)(2,1)} custom-call(s32[4]{0:T(128)} %pad_add_fusion.spot, bf16[512,512]{1,0:T(8,128)(2,1)} %get-tuple-element.219.refs_0_, bf16[512,512]{1,0:T(8,128)(2,1)} %get-tuple-element.220.refs_1_, bf16[512,512]{1,0:T(8,128)(2,1)} %copy-done.13, bf16[512,512]{1,0:T(8,128)(2,1)} %copy-done.16, ...), custom_call_target="tpu_custom_call" | custom-call | flops 2147483648 | bytes 4194304 | tf_op jit(solution)/shard_map/pallas_call | solution.py:60
  418.0 4.5 all-to-all-start.2
  422.9 20.2 %shard_map.333 = (bf16[1024,2048]{1,0:T(8,128)(2,1)}, f32[8,2048]{1,0:T(8,128)}) custom-call(s32[4]{0:T(128)} %pad_add_fusion.spot, bf16[512,512]{1,0:T(8,128)(2,1)} %get-tuple-element.219.refs_0_, bf16[512,512]{1,0:T(8,128)(2,1)} %get-tuple-element.220.refs_1_, bf16[512,512]{1,0:T(8,128)(2,1)} %copy-done.13, bf16[512,512]{1,0:T(8,128)(2,1)} %copy-done.16, ...), custom_call_target="tpu_custom_call" | custom-call | flops 2147483648 | bytes 4194304 | tf_op jit(solution)/shard_map/pallas_call | solution.py:60
  443.1 6.7 shard_map.334
  452.6 6.8 shard_map.335
  460.1 6.8 shard_map.336
  468.4 3.6 shard_map.337
  476.3 7.0 shard_map.338
  483.2 14.1 %shard_map.339 = bf16[4,2,2,512,512]{4,3,2,1,0:T(8,128)(2,1)} custom-call(s32[4]{0:T(128)} %pad_add_fusion.spot, bf16[512,512]{1,0:T(8,128)(2,1)} %get-tuple-element.189.refs_0_, bf16[512,512]{1,0:T(8,128)(2,1)} %get-tuple-element.191.refs_1_, bf16[512,512]{1,0:T(8,128)(2,1)} %copy-done.10, bf16[512,512]{1,0:T(8,128)(2,1)} %copy-done.11, ...), custom_call_target="tpu_custom_call" | custom-call | flops 2147483648 | bytes 4194304 | tf_op jit(solution)/shard_map/pallas_call | solution.py:60
  498.3 6.9 shard_map.340
  513.2 6.3 shard_map.341
  524.6 8.7 %collective-permute-done.54.refs_2_.refs_11_ = bf16[512,512]{1,0:T(8,128)(2,1)S(1)} collective-permute-done((bf16[512,512]{1,0:T(8,128)(2,1)S(1)}, bf16[512,512]{1,0:T(8,128)(2,1)S(1)}, u32[]{:S(2)}, u32[]{:S(2)}) %collective-permute-start.54) | collective-permute-done | bytes 524320 | tf_op jit(solution)/shard_map/ppermute | solution.py:37
  535.1 4.3 collective-permute-done.56.refs_4_.refs_13_
  539.4 7.9 %collective-permute-done.58.refs_6_.refs_15_ = bf16[512,512]{1,0:T(8,128)(2,1)} collective-permute-done((bf16[512,512]{1,0:T(8,128)(2,1)S(1)}, bf16[512,512]{1,0:T(8,128)(2,1)}, u32[]{:S(2)}, u32[]{:S(2)}) %collective-permute-start.58) | collective-permute-done | bytes 524320 | tf_op jit(solution)/shard_map/ppermute | solution.py:37
  547.3 7.5 %shard_map.342.grad_out = bf16[1024,512]{1,0:T(8,128)(2,1)} custom-call(s32[4]{0:T(128)} %pad_add_fusion.spot, bf16[512,512]{1,0:T(8,128)(2,1)} %get-tuple-element.251.refs_0_.refs_9_, bf16[512,512]{1,0:T(8,128)(2,1)} %get-tuple-element.252.refs_1_.refs_10_, bf16[512,512]{1,0:T(8,128)(2,1)} %copy-done.22, ...), custom_call_target="tpu_custom_call" | custom-call | flops 536870912 | bytes 1835008 | tf_op jit(solution)/shard_map/pallas_call | solution.py:60
  557.9 23.1 %shard_map.343 = (bf16[1024,1536]{1,0:T(8,128)(2,1)}, f32[8,1536]{1,0:T(8,128)}) custom-call(s32[4]{0:T(128)} %pad_add_fusion.spot, bf16[1024,1536]{1,0:T(8,128)(2,1)} %shard_map.315.queries.whole, bf16[1024,1536]{1,0:T(8,128)(2,1)} %shard_map.315.queries.whole, s32[1,1024]{1,0:T(1,128)} %bitcast.149, s32[1024,1]{1,0:T(8,128)} %copy.44.ids_column, ...), custom_call_target="tpu_custom_call" | custom-call | flops 4026531840 | bytes 2097152 | tf_op jit(solution)/shard_map/pallas_call | solution.py:60
  581.0 19.9 %shard_map.344 = bf16[4,2,2,512,512]{4,3,2,1,0:T(8,128)(2,1)} custom-call(s32[4]{0:T(128)} %pad_add_fusion.spot, bf16[512,512]{1,0:T(8,128)(2,1)} %get-tuple-element.161.refs_0_.refs_6_, bf16[512,512]{1,0:T(8,128)(2,1)} %get-tuple-element.163.refs_1_.refs_7_, bf16[512,512]{1,0:T(8,128)(2,1)} %copy-done.2, bf16[512,512]{1,0:T(8,128)(2,1)} %copy-done.3, ...), custom_call_target="tpu_custom_call" | custom-call | flops 2147483648 | bytes 5242880 | tf_op jit(solution)/shard_map/pallas_call | solution.py:60
  601.0 6.4 shard_map.345
  611.0 6.4 shard_map.346
  617.9 6.4 shard_map.347
  627.8 3.7 shard_map.348
  636.7 6.6 shard_map.349
  644.4 5.6 shard_map.350
  650.0 4.8 all-to-all-start.3
  661.3 29.3 %all-to-all-done.3 = bf16[4,1024,128]{2,1,0:T(8,128)(2,1)} async-done(((bf16[4,1024,128]{2,1,0:T(8,128)(2,1)}), bf16[4,1024,128]{2,1,0:T(8,128)(2,1)}, u32[]{:S(2)}, u32[]{:S(2)}) %all-to-all-start.3) | async-done | bytes 1048608 | tf_op jit(solution)/shard_map/all_to_all | solution.py:620
  710.7 6.8 reduce-scatter.6.cloned.1.call-done
  721.4 8.8 %collective-permute-done.69.other = bf16[512,512]{1,0:T(8,128)(2,1)S(1)} collective-permute-done((bf16[512,512]{1,0:T(8,128)(2,1)S(1)}, bf16[512,512]{1,0:T(8,128)(2,1)S(1)}, u32[]{:S(2)}, u32[]{:S(2)}) %collective-permute-start.69) | collective-permute-done | bytes 524320 | tf_op jit(solution)/shard_map/ppermute | solution.py:37
  (406 shorter events, 171.0 us)
Async XLA Ops:
  7.2 129.5 %all-gather.7.cloned.1.call-start = ((), (), s32[]{:S(2)}) async-start(), calls=%async_computation.10 | async-start | bytes 9437184 | tf_op jit(solution)/shard_map/all_gather | solution.py:686
  12.1 15.1 %collective-permute-start.11 = (bf16[512,512]{1,0:T(8,128)(2,1)S(1)}, bf16[512,512]{1,0:T(8,128)(2,1)}, u32[]{:S(2)}, u32[]{:S(2)}) collective-permute-start(bf16[512,512]{1,0:T(8,128)(2,1)S(1)} %pad_maximum_fusion.3), channel_id=1, source_target_pairs={{0,16},{1,17},{2,18},{3,19},{4,20},{5,21},{6,22},{7,23},{8,24},{9,... | collective-permute-start | bytes 1572872 | tf_op jit(solution)/shard_map/ppermute | solution.py:37
  29.3 242.4 %all-gather.9.cloned.1.call-start = ((), (), s32[]{:S(2)}) async-start(), calls=%async_computation.11 | async-start | bytes 9437184 | tf_op jit(solution)/shard_map/all_gather | solution.py:686
  29.3 14.9 %collective-permute-start.1 = (bf16[2048,128]{1,0:T(8,128)(2,1)S(1)}, bf16[2048,128]{1,0:T(8,128)(2,1)S(1)}, u32[]{:S(2)}, u32[]{:S(2)}) collective-permute-start(bf16[2048,128]{1,0:T(8,128)(2,1)S(1)} %get-tuple-element.315), channel_id=1, source_target_pairs={{0,16},{1,17},{2,18},{3,19},{4,20},{5,21},{6,22},{7,23},{8,24},{9,... | collective-permute-start | bytes 1572872 | tf_op jit(solution)/shard_map/ppermute | solution.py:37
  32.0 21.7 %collective-permute-start = (bf16[512,512]{1,0:T(8,128)(2,1)}, bf16[512,512]{1,0:T(8,128)(2,1)S(1)}, u32[]{:S(2)}, u32[]{:S(2)}) collective-permute-start(bf16[512,512]{1,0:T(8,128)(2,1)} %get-tuple-element.159), channel_id=1, source_target_pairs={{0,16},{1,17},{2,18},{3,19},{4,20},{5,21},{6,22},{7,23},{8,24},{9,... | collective-permute-start | bytes 1572872 | tf_op jit(solution)/shard_map/ppermute | solution.py:37
  45.3 16.6 %collective-permute-start.4 = (bf16[1024,128]{1,0:T(8,128)(2,1)S(1)}, bf16[1024,128]{1,0:T(8,128)(2,1)S(1)}, u32[]{:S(2)}, u32[]{:S(2)}) collective-permute-start(bf16[1024,128]{1,0:T(8,128)(2,1)S(1)} %get-tuple-element.310), channel_id=1, source_target_pairs={{0,6},{1,7},{2,4},{3,5},{4,2},{5,3},{6,0},{7,1},{8,14},{9,15},{10,... | collective-permute-start | bytes 786440 | tf_op jit(solution)/shard_map/ppermute | solution.py:37
  49.2 23.5 %collective-permute-start.2 = (bf16[1024,128]{1,0:T(8,128)(2,1)S(1)}, bf16[1024,128]{1,0:T(8,128)(2,1)S(1)}, u32[]{:S(2)}, u32[]{:S(2)}) collective-permute-start(bf16[1024,128]{1,0:T(8,128)(2,1)S(1)} %get-tuple-element.312), channel_id=1, source_target_pairs={{0,2},{1,3},{2,0},{3,1},{4,6},{5,7},{6,4},{7,5},{8,10},{9,11},{10,... | collective-permute-start | bytes 786440 | tf_op jit(solution)/shard_map/ppermute | solution.py:37
  49.2 49.6 %collective-permute-start.3 = (bf16[1024,128]{1,0:T(8,128)(2,1)S(1)}, bf16[1024,128]{1,0:T(8,128)(2,1)S(1)}, u32[]{:S(2)}, u32[]{:S(2)}) collective-permute-start(bf16[1024,128]{1,0:T(8,128)(2,1)S(1)} %get-tuple-element.313), channel_id=1, source_target_pairs={{0,4},{1,5},{2,6},{3,7},{4,0},{5,1},{6,2},{7,3},{8,12},{9,13},{10,... | collective-permute-start | bytes 786440 | tf_op jit(solution)/shard_map/ppermute | solution.py:37
  103.7 206.6 %all-gather.11.cloned.1.call-start = ((), (), s32[]{:S(2)}) async-start(), calls=%async_computation.12 | async-start | bytes 9437184 | tf_op jit(solution)/shard_map/all_gather | solution.py:686
  103.9 15.1 %collective-permute-start.8 = (bf16[512,512]{1,0:T(8,128)(2,1)}, bf16[512,512]{1,0:T(8,128)(2,1)S(1)}, u32[]{:S(2)}, u32[]{:S(2)}) collective-permute-start(bf16[512,512]{1,0:T(8,128)(2,1)} %get-tuple-element.163.refs_1_.refs_7_), channel_id=1, source_target_pairs={{0,16},{1,17},{2,18},{3,19},{4,20},{5,21},{6,22},{7,23},{8,24},{9,... | collective-permute-start | bytes 1572872 | tf_op jit(solution)/shard_map/ppermute | solution.py:37
  105.4 15.1 %collective-permute-start.5 = (bf16[512,512]{1,0:T(8,128)(2,1)}, bf16[512,512]{1,0:T(8,128)(2,1)S(1)}, u32[]{:S(2)}, u32[]{:S(2)}) collective-permute-start(bf16[512,512]{1,0:T(8,128)(2,1)} %get-tuple-element.161.refs_0_.refs_6_), channel_id=1, source_target_pairs={{0,1},{1,0},{2,3},{3,2},{4,5},{5,4},{6,7},{7,6},{8,9},{9,8},{10,11... | collective-permute-start | bytes 1572872 | tf_op jit(solution)/shard_map/ppermute | solution.py:37
  106.9 24.1 %collective-permute-start.6 = (bf16[512,512]{1,0:T(8,128)(2,1)}, bf16[512,512]{1,0:T(8,128)(2,1)S(1)}, u32[]{:S(2)}, u32[]{:S(2)}) collective-permute-start(bf16[512,512]{1,0:T(8,128)(2,1)} %get-tuple-element.163.refs_1_.refs_7_), channel_id=1, source_target_pairs={{0,1},{1,0},{2,3},{3,2},{4,5},{5,4},{6,7},{7,6},{8,9},{9,8},{10,11... | collective-permute-start | bytes 1572872 | tf_op jit(solution)/shard_map/ppermute | solution.py:37
  107.5 23.6 %collective-permute-start.7 = (bf16[512,512]{1,0:T(8,128)(2,1)}, bf16[512,512]{1,0:T(8,128)(2,1)S(1)}, u32[]{:S(2)}, u32[]{:S(2)}) collective-permute-start(bf16[512,512]{1,0:T(8,128)(2,1)} %get-tuple-element.161.refs_0_.refs_6_), channel_id=1, source_target_pairs={{0,16},{1,17},{2,18},{3,19},{4,20},{5,21},{6,22},{7,23},{8,24},{9,... | collective-permute-start | bytes 1572872 | tf_op jit(solution)/shard_map/ppermute | solution.py:37
  119.1 17.6 %collective-permute-start.10 = (bf16[512,512]{1,0:T(8,128)(2,1)S(1)}, bf16[512,512]{1,0:T(8,128)(2,1)S(1)}, u32[]{:S(2)}, u32[]{:S(2)}) collective-permute-start(bf16[512,512]{1,0:T(8,128)(2,1)S(1)} %collective-permute-done.8.refs_5_), channel_id=1, source_target_pairs={{0,1},{1,0},{2,3},{3,2},{4,5},{5,4},{6,7},{7,6},{8,9},{9,8},{10,11... | collective-permute-start | bytes 1572872 | tf_op jit(solution)/shard_map/ppermute | solution.py:37
  120.5 16.2 %collective-permute-start.9 = (bf16[512,512]{1,0:T(8,128)(2,1)S(1)}, bf16[512,512]{1,0:T(8,128)(2,1)S(1)}, u32[]{:S(2)}, u32[]{:S(2)}) collective-permute-start(bf16[512,512]{1,0:T(8,128)(2,1)S(1)} %collective-permute-done.5.refs_2_), channel_id=1, source_target_pairs={{0,16},{1,17},{2,18},{3,19},{4,20},{5,21},{6,22},{7,23},{8,24},{9,... | collective-permute-start | bytes 1572872 | tf_op jit(solution)/shard_map/ppermute | solution.py:37
  189.3 13.3 %collective-permute-start.15 = (bf16[512,512]{1,0:T(8,128)(2,1)}, bf16[512,512]{1,0:T(8,128)(2,1)S(1)}, u32[]{:S(2)}, u32[]{:S(2)}) collective-permute-start(bf16[512,512]{1,0:T(8,128)(2,1)} %get-tuple-element.177), channel_id=1, source_target_pairs={{0,16},{1,17},{2,18},{3,19},{4,20},{5,21},{6,22},{7,23},{8,24},{9,... | collective-permute-start | bytes 1572872 | tf_op jit(solution)/shard_map/ppermute | solution.py:37
  190.8 15.1 %collective-permute-start.14 = (bf16[512,512]{1,0:T(8,128)(2,1)}, bf16[512,512]{1,0:T(8,128)(2,1)S(1)}, u32[]{:S(2)}, u32[]{:S(2)}) collective-permute-start(bf16[512,512]{1,0:T(8,128)(2,1)} %get-tuple-element.170), channel_id=1, source_target_pairs={{0,1},{1,0},{2,3},{3,2},{4,5},{5,4},{6,7},{7,6},{8,9},{9,8},{10,11... | collective-permute-start | bytes 1572872 | tf_op jit(solution)/shard_map/ppermute | solution.py:37
  196.9 20.2 %collective-permute-start.16 = (bf16[512,512]{1,0:T(8,128)(2,1)}, bf16[512,512]{1,0:T(8,128)(2,1)S(1)}, u32[]{:S(2)}, u32[]{:S(2)}) collective-permute-start(bf16[512,512]{1,0:T(8,128)(2,1)} %get-tuple-element.172), channel_id=1, source_target_pairs={{0,1},{1,0},{2,3},{3,2},{4,5},{5,4},{6,7},{7,6},{8,9},{9,8},{10,11... | collective-permute-start | bytes 1572872 | tf_op jit(solution)/shard_map/ppermute | solution.py:37
  202.0 15.1 %collective-permute-start.17 = (bf16[512,512]{1,0:T(8,128)(2,1)}, bf16[512,512]{1,0:T(8,128)(2,1)S(1)}, u32[]{:S(2)}, u32[]{:S(2)}) collective-permute-start(bf16[512,512]{1,0:T(8,128)(2,1)} %get-tuple-element.180), channel_id=1, source_target_pairs={{0,16},{1,17},{2,18},{3,19},{4,20},{5,21},{6,22},{7,23},{8,24},{9,... | collective-permute-start | bytes 1572872 | tf_op jit(solution)/shard_map/ppermute | solution.py:37
  210.2 13.8 %collective-permute-start.19 = (bf16[512,512]{1,0:T(8,128)(2,1)}, bf16[512,512]{1,0:T(8,128)(2,1)S(1)}, u32[]{:S(2)}, u32[]{:S(2)}) collective-permute-start(bf16[512,512]{1,0:T(8,128)(2,1)} %get-tuple-element.185), channel_id=1, source_target_pairs={{0,1},{1,0},{2,3},{3,2},{4,5},{5,4},{6,7},{7,6},{8,9},{9,8},{10,11... | collective-permute-start | bytes 1572872 | tf_op jit(solution)/shard_map/ppermute | solution.py:37
  211.7 12.3 %collective-permute-start.18 = (bf16[512,512]{1,0:T(8,128)(2,1)}, bf16[512,512]{1,0:T(8,128)(2,1)S(1)}, u32[]{:S(2)}, u32[]{:S(2)}) collective-permute-start(bf16[512,512]{1,0:T(8,128)(2,1)} %get-tuple-element.178), channel_id=1, source_target_pairs={{0,16},{1,17},{2,18},{3,19},{4,20},{5,21},{6,22},{7,23},{8,24},{9,... | collective-permute-start | bytes 1572872 | tf_op jit(solution)/shard_map/ppermute | solution.py:37
  244.2 15.1 %collective-permute-start.26 = (bf16[512,512]{1,0:T(8,128)(2,1)}, bf16[512,512]{1,0:T(8,128)(2,1)S(1)}, u32[]{:S(2)}, u32[]{:S(2)}) collective-permute-start(bf16[512,512]{1,0:T(8,128)(2,1)} %get-tuple-element.191.refs_1_), channel_id=1, source_target_pairs={{0,16},{1,17},{2,18},{3,19},{4,20},{5,21},{6,22},{7,23},{8,24},{9,... | collective-permute-start | bytes 1572872 | tf_op jit(solution)/shard_map/ppermute | solution.py:37
  244.4 15.5 %collective-permute-start.23 = (bf16[512,512]{1,0:T(8,128)(2,1)}, bf16[512,512]{1,0:T(8,128)(2,1)S(1)}, u32[]{:S(2)}, u32[]{:S(2)}) collective-permute-start(bf16[512,512]{1,0:T(8,128)(2,1)} %get-tuple-element.189.refs_0_), channel_id=1, source_target_pairs={{0,1},{1,0},{2,3},{3,2},{4,5},{5,4},{6,7},{7,6},{8,9},{9,8},{10,11... | collective-permute-start | bytes 1572872 | tf_op jit(solution)/shard_map/ppermute | solution.py:37
  245.1 25.4 %collective-permute-start.35 = (bf16[2048,128]{1,0:T(8,128)(2,1)S(1)}, bf16[2048,128]{1,0:T(8,128)(2,1)S(1)}, u32[]{:S(2)}, u32[]{:S(2)}) collective-permute-start(bf16[2048,128]{1,0:T(8,128)(2,1)S(1)} %get-tuple-element.307), channel_id=1, source_target_pairs={{0,16},{1,17},{2,18},{3,19},{4,20},{5,21},{6,22},{7,23},{8,24},{9,... | collective-permute-start | bytes 1572872 | tf_op jit(solution)/shard_map/ppermute | solution.py:37
  247.0 24.6 %collective-permute-start.24 = (bf16[512,512]{1,0:T(8,128)(2,1)S(1)}, bf16[512,512]{1,0:T(8,128)(2,1)S(1)}, u32[]{:S(2)}, u32[]{:S(2)}) collective-permute-start(bf16[512,512]{1,0:T(8,128)(2,1)S(1)} %copy-done.8), channel_id=1, source_target_pairs={{0,1},{1,0},{2,3},{3,2},{4,5},{5,4},{6,7},{7,6},{8,9},{9,8},{10,11... | collective-permute-start | bytes 1572872 | tf_op jit(solution)/shard_map/ppermute | solution.py:37
  248.4 32.1 %collective-permute-start.25 = (bf16[512,512]{1,0:T(8,128)(2,1)S(1)}, bf16[512,512]{1,0:T(8,128)(2,1)S(1)}, u32[]{:S(2)}, u32[]{:S(2)}) collective-permute-start(bf16[512,512]{1,0:T(8,128)(2,1)S(1)} %copy-done.7), channel_id=1, source_target_pairs={{0,16},{1,17},{2,18},{3,19},{4,20},{5,21},{6,22},{7,23},{8,24},{9,... | collective-permute-start | bytes 1572872 | tf_op jit(solution)/shard_map/ppermute | solution.py:37
  259.3 21.2 %collective-permute-start.28 = (bf16[512,512]{1,0:T(8,128)(2,1)S(1)}, bf16[512,512]{1,0:T(8,128)(2,1)}, u32[]{:S(2)}, u32[]{:S(2)}) collective-permute-start(bf16[512,512]{1,0:T(8,128)(2,1)S(1)} %collective-permute-done.26.refs_5_), channel_id=1, source_target_pairs={{0,1},{1,0},{2,3},{3,2},{4,5},{5,4},{6,7},{7,6},{8,9},{9,8},{10,11... | collective-permute-start | bytes 1572872 | tf_op jit(solution)/shard_map/ppermute | solution.py:37
  259.9 26.3 %collective-permute-start.27 = (bf16[512,512]{1,0:T(8,128)(2,1)S(1)}, bf16[512,512]{1,0:T(8,128)(2,1)}, u32[]{:S(2)}, u32[]{:S(2)}) collective-permute-start(bf16[512,512]{1,0:T(8,128)(2,1)S(1)} %collective-permute-done.23.refs_2_), channel_id=1, source_target_pairs={{0,16},{1,17},{2,18},{3,19},{4,20},{5,21},{6,22},{7,23},{8,24},{9,... | collective-permute-start | bytes 1572872 | tf_op jit(solution)/shard_map/ppermute | solution.py:37
  306.5 45.5 %all-to-all-start.1 = ((bf16[4,1024,128]{2,1,0:T(8,128)(2,1)}), bf16[4,1024,128]{2,1,0:T(8,128)(2,1)S(1)}, u32[]{:S(2)}, u32[]{:S(2)}) async-start(bf16[4,1024,128]{2,1,0:T(8,128)(2,1)} %maximum_select_fusion.2), calls=%async_computation.1 | async-start | bytes 2097152 | tf_op jit(solution)/shard_map/all_to_all | solution.py:770
  310.0 225.2 %reduce-scatter.4.cloned.1.call-start = ((), (), s32[]{:S(2)}) async-start(), calls=%async_computation.7 | async-start | bytes 9437184 | tf_op jit(solution)/shard_map/reduce_scatter | solution.py:690
  316.8 17.4 %collective-permute-start.30 = (bf16[512,512]{1,0:T(8,128)(2,1)}, bf16[512,512]{1,0:T(8,128)(2,1)S(1)}, u32[]{:S(2)}, u32[]{:S(2)}) collective-permute-start(bf16[512,512]{1,0:T(8,128)(2,1)} %get-tuple-element.202), channel_id=1, source_target_pairs={{0,16},{1,17},{2,18},{3,19},{4,20},{5,21},{6,22},{7,23},{8,24},{9,... | collective-permute-start | bytes 1572872 | tf_op jit(solution)/shard_map/ppermute | solution.py:37
  317.0 17.1 %collective-permute-start.29 = (bf16[512,512]{1,0:T(8,128)(2,1)}, bf16[512,512]{1,0:T(8,128)(2,1)S(1)}, u32[]{:S(2)}, u32[]{:S(2)}) collective-permute-start(bf16[512,512]{1,0:T(8,128)(2,1)} %get-tuple-element.195), channel_id=1, source_target_pairs={{0,1},{1,0},{2,3},{3,2},{4,5},{5,4},{6,7},{7,6},{8,9},{9,8},{10,11... | collective-permute-start | bytes 1572872 | tf_op jit(solution)/shard_map/ppermute | solution.py:37
  324.3 15.4 %collective-permute-start.31 = (bf16[512,512]{1,0:T(8,128)(2,1)}, bf16[512,512]{1,0:T(8,128)(2,1)S(1)}, u32[]{:S(2)}, u32[]{:S(2)}) collective-permute-start(bf16[512,512]{1,0:T(8,128)(2,1)} %get-tuple-element.197), channel_id=1, source_target_pairs={{0,1},{1,0},{2,3},{3,2},{4,5},{5,4},{6,7},{7,6},{8,9},{9,8},{10,11... | collective-permute-start | bytes 1572872 | tf_op jit(solution)/shard_map/ppermute | solution.py:37
  332.4 12.7 %collective-permute-start.32 = (bf16[512,512]{1,0:T(8,128)(2,1)}, bf16[512,512]{1,0:T(8,128)(2,1)S(1)}, u32[]{:S(2)}, u32[]{:S(2)}) collective-permute-start(bf16[512,512]{1,0:T(8,128)(2,1)} %get-tuple-element.205), channel_id=1, source_target_pairs={{0,16},{1,17},{2,18},{3,19},{4,20},{5,21},{6,22},{7,23},{8,24},{9,... | collective-permute-start | bytes 1572872 | tf_op jit(solution)/shard_map/ppermute | solution.py:37
  338.7 13.2 %collective-permute-start.34 = (bf16[512,512]{1,0:T(8,128)(2,1)}, bf16[512,512]{1,0:T(8,128)(2,1)S(1)}, u32[]{:S(2)}, u32[]{:S(2)}) collective-permute-start(bf16[512,512]{1,0:T(8,128)(2,1)} %get-tuple-element.210), channel_id=1, source_target_pairs={{0,1},{1,0},{2,3},{3,2},{4,5},{5,4},{6,7},{7,6},{8,9},{9,8},{10,11... | collective-permute-start | bytes 1572872 | tf_op jit(solution)/shard_map/ppermute | solution.py:37
  339.3 12.7 %collective-permute-start.33 = (bf16[512,512]{1,0:T(8,128)(2,1)}, bf16[512,512]{1,0:T(8,128)(2,1)S(1)}, u32[]{:S(2)}, u32[]{:S(2)}) collective-permute-start(bf16[512,512]{1,0:T(8,128)(2,1)} %get-tuple-element.203), channel_id=1, source_target_pairs={{0,16},{1,17},{2,18},{3,19},{4,20},{5,21},{6,22},{7,23},{8,24},{9,... | collective-permute-start | bytes 1572872 | tf_op jit(solution)/shard_map/ppermute | solution.py:37
  374.5 14.9 %collective-permute-start.39 = (bf16[512,512]{1,0:T(8,128)(2,1)}, bf16[512,512]{1,0:T(8,128)(2,1)S(1)}, u32[]{:S(2)}, u32[]{:S(2)}) collective-permute-start(bf16[512,512]{1,0:T(8,128)(2,1)} %get-tuple-element.219.refs_0_), channel_id=1, source_target_pairs={{0,1},{1,0},{2,3},{3,2},{4,5},{5,4},{6,7},{7,6},{8,9},{9,8},{10,11... | collective-permute-start | bytes 1572872 | tf_op jit(solution)/shard_map/ppermute | solution.py:37
  375.1 14.6 %collective-permute-start.42 = (bf16[512,512]{1,0:T(8,128)(2,1)}, bf16[512,512]{1,0:T(8,128)(2,1)S(1)}, u32[]{:S(2)}, u32[]{:S(2)}) collective-permute-start(bf16[512,512]{1,0:T(8,128)(2,1)} %get-tuple-element.220.refs_1_), channel_id=1, source_target_pairs={{0,16},{1,17},{2,18},{3,19},{4,20},{5,21},{6,22},{7,23},{8,24},{9,... | collective-permute-start | bytes 1572872 | tf_op jit(solution)/shard_map/ppermute | solution.py:37
  375.8 19.0 %collective-permute-start.41 = (bf16[512,512]{1,0:T(8,128)(2,1)}, bf16[512,512]{1,0:T(8,128)(2,1)S(1)}, u32[]{:S(2)}, u32[]{:S(2)}) collective-permute-start(bf16[512,512]{1,0:T(8,128)(2,1)} %get-tuple-element.219.refs_0_), channel_id=1, source_target_pairs={{0,16},{1,17},{2,18},{3,19},{4,20},{5,21},{6,22},{7,23},{8,24},{9,... | collective-permute-start | bytes 1572872 | tf_op jit(solution)/shard_map/ppermute | solution.py:37
  377.1 18.0 %collective-permute-start.40 = (bf16[512,512]{1,0:T(8,128)(2,1)}, bf16[512,512]{1,0:T(8,128)(2,1)S(1)}, u32[]{:S(2)}, u32[]{:S(2)}) collective-permute-start(bf16[512,512]{1,0:T(8,128)(2,1)} %get-tuple-element.220.refs_1_), channel_id=1, source_target_pairs={{0,1},{1,0},{2,3},{3,2},{4,5},{5,4},{6,7},{7,6},{8,9},{9,8},{10,11... | collective-permute-start | bytes 1572872 | tf_op jit(solution)/shard_map/ppermute | solution.py:37
  418.0 65.2 %all-to-all-start.2 = ((bf16[4,1024,128]{2,1,0:T(8,128)(2,1)}), bf16[4,1024,128]{2,1,0:T(8,128)(2,1)S(1)}, u32[]{:S(2)}, u32[]{:S(2)}) async-start(bf16[4,1024,128]{2,1,0:T(8,128)(2,1)} %get-tuple-element.221), calls=%async_computation.2 | async-start | bytes 2097152 | tf_op jit(solution)/shard_map/all_to_all | solution.py:620
  422.5 236.1 %reduce-scatter.8.cloned.1.call-start = ((), (), s32[]{:S(2)}) async-start(), calls=%async_computation.9 | async-start | bytes 9437184 | tf_op jit(solution)/shard_map/reduce_scatter | solution.py:690
  449.8 17.6 %collective-permute-start.46 = (bf16[512,512]{1,0:T(8,128)(2,1)}, bf16[512,512]{1,0:T(8,128)(2,1)S(1)}, u32[]{:S(2)}, u32[]{:S(2)}) collective-permute-start(bf16[512,512]{1,0:T(8,128)(2,1)} %get-tuple-element.233), channel_id=1, source_target_pairs={{0,16},{1,17},{2,18},{3,19},{4,20},{5,21},{6,22},{7,23},{8,24},{9,... | collective-permute-start | bytes 1572872 | tf_op jit(solution)/shard_map/ppermute | solution.py:37
  451.3 16.1 %collective-permute-start.45 = (bf16[512,512]{1,0:T(8,128)(2,1)}, bf16[512,512]{1,0:T(8,128)(2,1)S(1)}, u32[]{:S(2)}, u32[]{:S(2)}) collective-permute-start(bf16[512,512]{1,0:T(8,128)(2,1)} %get-tuple-element.226), channel_id=1, source_target_pairs={{0,1},{1,0},{2,3},{3,2},{4,5},{5,4},{6,7},{7,6},{8,9},{9,8},{10,11... | collective-permute-start | bytes 1572872 | tf_op jit(solution)/shard_map/ppermute | solution.py:37
  459.4 15.4 %collective-permute-start.47 = (bf16[512,512]{1,0:T(8,128)(2,1)}, bf16[512,512]{1,0:T(8,128)(2,1)S(1)}, u32[]{:S(2)}, u32[]{:S(2)}) collective-permute-start(bf16[512,512]{1,0:T(8,128)(2,1)} %get-tuple-element.228), channel_id=1, source_target_pairs={{0,1},{1,0},{2,3},{3,2},{4,5},{5,4},{6,7},{7,6},{8,9},{9,8},{10,11... | collective-permute-start | bytes 1572872 | tf_op jit(solution)/shard_map/ppermute | solution.py:37
  472.0 25.3 %collective-permute-start.50 = (bf16[512,512]{1,0:T(8,128)(2,1)}, bf16[512,512]{1,0:T(8,128)(2,1)S(1)}, u32[]{:S(2)}, u32[]{:S(2)}) collective-permute-start(bf16[512,512]{1,0:T(8,128)(2,1)} %get-tuple-element.243), channel_id=1, source_target_pairs={{0,1},{1,0},{2,3},{3,2},{4,5},{5,4},{6,7},{7,6},{8,9},{9,8},{10,11... | collective-permute-start | bytes 1572872 | tf_op jit(solution)/shard_map/ppermute | solution.py:37
  473.4 23.9 %collective-permute-start.49 = (bf16[512,512]{1,0:T(8,128)(2,1)}, bf16[512,512]{1,0:T(8,128)(2,1)S(1)}, u32[]{:S(2)}, u32[]{:S(2)}) collective-permute-start(bf16[512,512]{1,0:T(8,128)(2,1)} %get-tuple-element.234), channel_id=1, source_target_pairs={{0,16},{1,17},{2,18},{3,19},{4,20},{5,21},{6,22},{7,23},{8,24},{9,... | collective-permute-start | bytes 1572872 | tf_op jit(solution)/shard_map/ppermute | solution.py:37
  519.6 197.9 %reduce-scatter.6.cloned.1.call-start = ((), (), s32[]{:S(2)}) async-start(), calls=%async_computation.8 | async-start | bytes 9437184 | tf_op jit(solution)/shard_map/reduce_scatter | solution.py:690
  520.6 12.8 %collective-permute-start.54 = (bf16[512,512]{1,0:T(8,128)(2,1)S(1)}, bf16[512,512]{1,0:T(8,128)(2,1)S(1)}, u32[]{:S(2)}, u32[]{:S(2)}) collective-permute-start(bf16[512,512]{1,0:T(8,128)(2,1)S(1)} %copy-done.20), channel_id=1, source_target_pairs={{0,1},{1,0},{2,3},{3,2},{4,5},{5,4},{6,7},{7,6},{8,9},{9,8},{10,11... | collective-permute-start | bytes 1572872 | tf_op jit(solution)/shard_map/ppermute | solution.py:37
  521.2 13.2 %collective-permute-start.57 = (bf16[512,512]{1,0:T(8,128)(2,1)S(1)}, bf16[512,512]{1,0:T(8,128)(2,1)S(1)}, u32[]{:S(2)}, u32[]{:S(2)}) collective-permute-start(bf16[512,512]{1,0:T(8,128)(2,1)S(1)} %copy-done.21), channel_id=1, source_target_pairs={{0,16},{1,17},{2,18},{3,19},{4,20},{5,21},{6,22},{7,23},{8,24},{9,... | collective-permute-start | bytes 1572872 | tf_op jit(solution)/shard_map/ppermute | solution.py:37
  522.6 16.8 %collective-permute-start.56 = (bf16[512,512]{1,0:T(8,128)(2,1)S(1)}, bf16[512,512]{1,0:T(8,128)(2,1)}, u32[]{:S(2)}, u32[]{:S(2)}) collective-permute-start(bf16[512,512]{1,0:T(8,128)(2,1)S(1)} %copy-done.20), channel_id=1, source_target_pairs={{0,16},{1,17},{2,18},{3,19},{4,20},{5,21},{6,22},{7,23},{8,24},{9,... | collective-permute-start | bytes 1572872 | tf_op jit(solution)/shard_map/ppermute | solution.py:37
  523.3 16.2 %collective-permute-start.55 = (bf16[512,512]{1,0:T(8,128)(2,1)S(1)}, bf16[512,512]{1,0:T(8,128)(2,1)}, u32[]{:S(2)}, u32[]{:S(2)}) collective-permute-start(bf16[512,512]{1,0:T(8,128)(2,1)S(1)} %copy-done.21), channel_id=1, source_target_pairs={{0,1},{1,0},{2,3},{3,2},{4,5},{5,4},{6,7},{7,6},{8,9},{9,8},{10,11... | collective-permute-start | bytes 1572872 | tf_op jit(solution)/shard_map/ppermute | solution.py:37
  533.4 14.0 %collective-permute-start.58 = (bf16[512,512]{1,0:T(8,128)(2,1)S(1)}, bf16[512,512]{1,0:T(8,128)(2,1)}, u32[]{:S(2)}, u32[]{:S(2)}) collective-permute-start(bf16[512,512]{1,0:T(8,128)(2,1)S(1)} %collective-permute-done.54.refs_2_.refs_11_), channel_id=1, source_target_pairs={{0,16},{1,17},{2,18},{3,19},{4,20},{5,21},{6,22},{7,23},{8,24},{9,... | collective-permute-start | bytes 1572872 | tf_op jit(solution)/shard_map/ppermute | solution.py:37
  534.4 12.9 %collective-permute-start.59 = (bf16[512,512]{1,0:T(8,128)(2,1)S(1)}, bf16[512,512]{1,0:T(8,128)(2,1)}, u32[]{:S(2)}, u32[]{:S(2)}) collective-permute-start(bf16[512,512]{1,0:T(8,128)(2,1)S(1)} %collective-permute-done.57.refs_5_.refs_14_), channel_id=1, source_target_pairs={{0,1},{1,0},{2,3},{3,2},{4,5},{5,4},{6,7},{7,6},{8,9},{9,8},{10,11... | collective-permute-start | bytes 1572872 | tf_op jit(solution)/shard_map/ppermute | solution.py:37
  555.8 25.3 %collective-permute-start.60 = (bf16[2048,128]{1,0:T(8,128)(2,1)S(1)}, bf16[2048,128]{1,0:T(8,128)(2,1)S(1)}, u32[]{:S(2)}, u32[]{:S(2)}) collective-permute-start(bf16[2048,128]{1,0:T(8,128)(2,1)S(1)} %get-tuple-element.305), channel_id=1, source_target_pairs={{0,16},{1,17},{2,18},{3,19},{4,20},{5,21},{6,22},{7,23},{8,24},{9,... | collective-permute-start | bytes 1572872 | tf_op jit(solution)/shard_map/ppermute | solution.py:37
  557.1 23.9 %collective-permute-start.61 = (bf16[512,512]{1,0:T(8,128)(2,1)S(1)}, bf16[512,512]{1,0:T(8,128)(2,1)S(1)}, u32[]{:S(2)}, u32[]{:S(2)}) collective-permute-start(bf16[512,512]{1,0:T(8,128)(2,1)S(1)} %get-tuple-element.299), channel_id=1, source_target_pairs={{0,16},{1,17},{2,18},{3,19},{4,20},{5,21},{6,22},{7,23},{8,24},{9,... | collective-permute-start | bytes 1572872 | tf_op jit(solution)/shard_map/ppermute | solution.py:37
  607.4 19.5 %collective-permute-start.63 = (bf16[512,512]{1,0:T(8,128)(2,1)}, bf16[512,512]{1,0:T(8,128)(2,1)S(1)}, u32[]{:S(2)}, u32[]{:S(2)}) collective-permute-start(bf16[512,512]{1,0:T(8,128)(2,1)} %get-tuple-element.268), channel_id=1, source_target_pairs={{0,16},{1,17},{2,18},{3,19},{4,20},{5,21},{6,22},{7,23},{8,24},{9,... | collective-permute-start | bytes 1572872 | tf_op jit(solution)/shard_map/ppermute | solution.py:37
  608.6 18.3 %collective-permute-start.62 = (bf16[512,512]{1,0:T(8,128)(2,1)}, bf16[512,512]{1,0:T(8,128)(2,1)S(1)}, u32[]{:S(2)}, u32[]{:S(2)}) collective-permute-start(bf16[512,512]{1,0:T(8,128)(2,1)} %get-tuple-element.261), channel_id=1, source_target_pairs={{0,1},{1,0},{2,3},{3,2},{4,5},{5,4},{6,7},{7,6},{8,9},{9,8},{10,11... | collective-permute-start | bytes 1572872 | tf_op jit(solution)/shard_map/ppermute | solution.py:37
  617.4 19.2 %collective-permute-start.64 = (bf16[512,512]{1,0:T(8,128)(2,1)}, bf16[512,512]{1,0:T(8,128)(2,1)S(1)}, u32[]{:S(2)}, u32[]{:S(2)}) collective-permute-start(bf16[512,512]{1,0:T(8,128)(2,1)} %get-tuple-element.263), channel_id=1, source_target_pairs={{0,1},{1,0},{2,3},{3,2},{4,5},{5,4},{6,7},{7,6},{8,9},{9,8},{10,11... | collective-permute-start | bytes 1572872 | tf_op jit(solution)/shard_map/ppermute | solution.py:37
  624.4 12.3 %collective-permute-start.65 = (bf16[512,512]{1,0:T(8,128)(2,1)}, bf16[512,512]{1,0:T(8,128)(2,1)S(1)}, u32[]{:S(2)}, u32[]{:S(2)}) collective-permute-start(bf16[512,512]{1,0:T(8,128)(2,1)} %get-tuple-element.271), channel_id=1, source_target_pairs={{0,16},{1,17},{2,18},{3,19},{4,20},{5,21},{6,22},{7,23},{8,24},{9,... | collective-permute-start | bytes 1572872 | tf_op jit(solution)/shard_map/ppermute | solution.py:37
  631.5 11.9 %collective-permute-start.67 = (bf16[512,512]{1,0:T(8,128)(2,1)}, bf16[512,512]{1,0:T(8,128)(2,1)S(1)}, u32[]{:S(2)}, u32[]{:S(2)}) collective-permute-start(bf16[512,512]{1,0:T(8,128)(2,1)} %get-tuple-element.276), channel_id=1, source_target_pairs={{0,1},{1,0},{2,3},{3,2},{4,5},{5,4},{6,7},{7,6},{8,9},{9,8},{10,11... | collective-permute-start | bytes 1572872 | tf_op jit(solution)/shard_map/ppermute | solution.py:37
  650.0 40.6 %all-to-all-start.3 = ((bf16[4,1024,128]{2,1,0:T(8,128)(2,1)}), bf16[4,1024,128]{2,1,0:T(8,128)(2,1)}, u32[]{:S(2)}, u32[]{:S(2)}) async-start(bf16[4,1024,128]{2,1,0:T(8,128)(2,1)} %shard_map.350), calls=%async_computation.4 | async-start | bytes 2097152 | tf_op jit(solution)/shard_map/all_to_all | solution.py:620
  656.3 39.6 %collective-permute-start.71 = (f32[4,1664]{1,0:T(4,128)S(1)}, f32[4,1664]{1,0:T(4,128)S(1)}, u32[]{:S(2)}, u32[]{:S(2)}) collective-permute-start(f32[4,1664]{1,0:T(4,128)S(1)} %add.91), channel_id=1, source_target_pairs={{0,2},{1,3},{2,0},{3,1},{4,6},{5,7},{6,4},{7,5},{8,10},{9,11},{10,... | collective-permute-start | bytes 79880 | tf_op jit(solution)/shard_map/ppermute | solution.py:37
  660.7 35.2 %collective-permute-start.72 = (bf16[512,512]{1,0:T(8,128)(2,1)}, bf16[512,512]{1,0:T(8,128)(2,1)}, u32[]{:S(2)}, u32[]{:S(2)}) collective-permute-start(bf16[512,512]{1,0:T(8,128)(2,1)} %get-tuple-element.301), channel_id=1, source_target_pairs={{0,16},{1,17},{2,18},{3,19},{4,20},{5,21},{6,22},{7,23},{8,24},{9,... | collective-permute-start | bytes 1572872 | tf_op jit(solution)/shard_map/ppermute | solution.py:37
  (105 other events, 633.0 us)
Sparse Core Ops, SparseCore 0:
  29.4 105.7 all-gather.6
  136.8 80.4 all-gather.8
  218.9 80.5 all-gather.10
  418.1 98.3 reduce-scatter.3
  519.7 89.6 reduce-scatter.7
  611.5 105.9 reduce-scatter.5

commit v6 on v5

--- a/solution.py
+++ b/solution.py
@@ -737,7 +737,7 @@
     valid = (ids != lengths.shape[1] - 1).astype(F32)
     ids_row, ids_column = ids[None], ids[:, None]
 
-    full_qkv = gather_zc(tie(half_qkv, vectors))
+    full_qkv = gather_zc(half_qkv)
     token_blocks = spread_z(token_own, token_other, yi, zi)
     half_up, sent = halve_columns([w_up], yi, sent)
     spot.after(vectors, half_up)

time: 747 us -> 743 us (level)
  blocking collectives: 10.3 us -> 0 us
    all_to_all x0 -> x1, waiting for transfers between devices: none -> 44.1 us  [square_device(): lax.all_to_all(jnp.broadcast_to(vectors, (4, vectors.shape[1])), 'z', 0,...]
    ppermute x77, waiting for transfers between devices: 218 us -> 174 us  [swap(): return lax.ppermute(piece, AXES, [(i, i ^ mask) for i in range(32)])]
    all_to_all x1 -> x0, blocking collectives: 10.3 us -> none  [square_device(): lax.all_to_all(jnp.broadcast_to(vectors, (4, vectors.shape[1])), 'z', 0,...]
  transfers between devices with their start and end apart: 86 -> 87, of which waited for: 45 -> 41; matrix products, arithmetic and copies ran while one was open for 4% -> 4% of each run, Pallas kernels for 38% -> 38%
where the time goes in v6:
time: 743 us; the launch traced here: 737 us
  Pallas kernels  315 us (42%)
  waiting for transfers between devices  254 us (34%)
  starting transfers between devices  102 us (14%)
  local copies, waits for them, and re-layouts  30.8 us (4%)
  other arithmetic  18.8 us (3%)
  between operations  15.4 us (2%)
    pallas_call x39, Pallas kernels, call(): pl.pallas_call(body, grid_spec=pltpu.PrefetchScalarGridSpec(num_scalar_pr...  315 us
    ppermute x77, waiting for transfers between devices, swap(): return lax.ppermute(piece, AXES, [(i, i ^ mask) for i in range(32)])  174 us
    ppermute x77, starting transfers between devices, swap(): return lax.ppermute(piece, AXES, [(i, i ^ mask) for i in range(32)])  83.7 us
    all_to_all x1, waiting for transfers between devices, square_device(): lax.all_to_all(jnp.broadcast_to(vectors, (4, vectors.shape[1])), 'z', 0,...  44.1 us
    all_to_all x2, waiting for transfers between devices, from_share(): return lax.all_to_all(share, 'z', 0, 0, tiled=True).reshape(2, 2 * LEN, 128)  29.1 us
    unnamed x188, local copies, waits for them, and re-layouts  16.5 us
  transfers between devices with their start and end apart: 87, of which 41 were waited for; matrix products, arithmetic and copies ran while one was open for 4% of the time, Pallas kernels for 38%

profile of v6, /device:TPU:0, one launch (start us, length us, event | category | flops | bytes accessed | tf_op | source)
XLA Modules:
  0.0 736.7 jit_solution(11793941362051968770)
XLA Ops:
  15.1 11.9 %collective-permute-done.11 = bf16[512,512]{1,0:T(8,128)(2,1)S(1)} collective-permute-done((bf16[512,512]{1,0:T(8,128)(2,1)S(1)}, bf16[512,512]{1,0:T(8,128)(2,1)S(1)}, u32[]{:S(2)}, u32[]{:S(2)}) %collective-permute-start.11) | collective-permute-done | bytes 524320 | tf_op jit(solution)/shard_map/ppermute | solution.py:37
  31.3 11.7 %collective-permute-done.1 = bf16[2048,128]{1,0:T(8,128)(2,1)S(1)} collective-permute-done((bf16[2048,128]{1,0:T(8,128)(2,1)S(1)}, bf16[2048,128]{1,0:T(8,128)(2,1)S(1)}, u32[]{:S(2)}, u32[]{:S(2)}) %collective-permute-start.1) | collective-permute-done | bytes 524320 | tf_op jit(solution)/shard_map/ppermute | solution.py:37
  44.1 3.8 collective-permute-start.4
  49.2 5.1 all-to-all-start
  54.3 44.1 %all-to-all-done = f32[4,1,1536]{2,1,0:T(1,128)S(1)} async-done(((f32[4,1,1536]{2,1,0:T(1,128)}), f32[4,1,1536]{2,1,0:T(1,128)S(1)}, u32[]{:S(2)}, u32[]{:S(2)}) %all-to-all-start) | async-done | bytes 24608 | tf_op jit(solution)/shard_map/all_to_all | solution.py:728
  100.3 4.2 shard_map.314
  108.9 11.0 %collective-permute-done.8.refs_5_ = bf16[512,512]{1,0:T(8,128)(2,1)S(1)} collective-permute-done((bf16[512,512]{1,0:T(8,128)(2,1)}, bf16[512,512]{1,0:T(8,128)(2,1)S(1)}, u32[]{:S(2)}, u32[]{:S(2)}) %collective-permute-start.8) | collective-permute-done | bytes 524320 | tf_op jit(solution)/shard_map/ppermute | solution.py:37
  124.2 7.8 %collective-permute-done.6.refs_3_ = bf16[512,512]{1,0:T(8,128)(2,1)S(1)} collective-permute-done((bf16[512,512]{1,0:T(8,128)(2,1)}, bf16[512,512]{1,0:T(8,128)(2,1)S(1)}, u32[]{:S(2)}, u32[]{:S(2)}) %collective-permute-start.6) | collective-permute-done | bytes 524320 | tf_op jit(solution)/shard_map/ppermute | solution.py:37
  132.0 5.6 collective-permute-done.10.refs_7_
  138.6 16.4 %shard_map.315.queries.whole = bf16[1024,1536]{1,0:T(8,128)(2,1)} custom-call(s32[4]{0:T(128)} %pad_add_fusion.spot, bf16[512,512]{1,0:T(8,128)(2,1)} %get-tuple-element.160.refs_0_.refs_6_, bf16[512,512]{1,0:T(8,128)(2,1)} %get-tuple-element.162.refs_1_.refs_7_, bf16[512,512]{1,0:T(8,128)(2,1)} %copy-done.2, bf16[512,512]{1,0:T(8,128)(2,1)} %copy-done.3, ...), custom_call_target="tpu_custom_call" | custom-call | flops 1610612736 | bytes 3407872 | tf_op jit(solution)/shard_map/pallas_call | solution.py:60
  155.3 9.6 %collective-permute-done.13 = bf16[512,512]{1,0:T(8,128)(2,1)S(1)} collective-permute-done((bf16[512,512]{1,0:T(8,128)(2,1)S(1)}, bf16[512,512]{1,0:T(8,128)(2,1)S(1)}, u32[]{:S(2)}, u32[]{:S(2)}) %collective-permute-start.13) | collective-permute-done | bytes 524320 | tf_op jit(solution)/shard_map/ppermute | solution.py:37
  171.2 12.9 %shard_map.316 = (bf16[1024,512]{1,0:T(8,128)(2,1)}, f32[4,1,1024]{2,1,0:T(1,128)}) custom-call(s32[4]{0:T(128)} %pad_add_fusion.spot, bf16[1024,1536]{1,0:T(8,128)(2,1)} %shard_map.315.queries.whole, bf16[1024,1536]{1,0:T(8,128)(2,1)} %shard_map.315.queries.whole, s32[1,1024]{1,0:T(1,128)} %bitcast.148, s32[1024,1]{1,0:T(8,128)} %copy.44.ids_column), custom_call_target="tpu_custom_call" | custom-call | flops 2147483648 | bytes 1048576 | tf_op jit(solution)/shard_map/pallas_call | solution.py:60
  184.1 4.5 shard_map.317
  191.5 4.6 shard_map.318
  196.7 4.6 shard_map.319
  205.8 3.6 shard_map.320
  211.4 4.8 collective-permute-done.16.refs_2_
  216.2 4.8 shard_map.321
  223.0 6.2 shard_map.322
  236.8 5.1 shard_map.323
  246.5 10.6 %collective-permute-done.26.refs_5_ = bf16[512,512]{1,0:T(8,128)(2,1)S(1)} collective-permute-done((bf16[512,512]{1,0:T(8,128)(2,1)}, bf16[512,512]{1,0:T(8,128)(2,1)S(1)}, u32[]{:S(2)}, u32[]{:S(2)}) %collective-permute-start.26) | collective-permute-done | bytes 524320 | tf_op jit(solution)/shard_map/ppermute | solution.py:37
  259.7 8.6 %collective-permute-done.35 = bf16[2048,128]{1,0:T(8,128)(2,1)S(1)} collective-permute-done((bf16[2048,128]{1,0:T(8,128)(2,1)S(1)}, bf16[2048,128]{1,0:T(8,128)(2,1)S(1)}, u32[]{:S(2)}, u32[]{:S(2)}) %collective-permute-start.35) | collective-permute-done | bytes 524320 | tf_op jit(solution)/shard_map/ppermute | solution.py:37
  269.5 7.4 %collective-permute-done.25.refs_4_ = bf16[512,512]{1,0:T(8,128)(2,1)S(1)} collective-permute-done((bf16[512,512]{1,0:T(8,128)(2,1)S(1)}, bf16[512,512]{1,0:T(8,128)(2,1)S(1)}, u32[]{:S(2)}, u32[]{:S(2)}) %collective-permute-start.25) | collective-permute-done | bytes 524320 | tf_op jit(solution)/shard_map/ppermute | solution.py:37
  276.8 5.7 collective-permute-done.27.refs_6_
  282.6 20.1 %shard_map.324 = (bf16[1024,2048]{1,0:T(8,128)(2,1)}, bf16[1024,2048]{1,0:T(8,128)(2,1)}) custom-call(s32[4]{0:T(128)} %pad_add_fusion.spot, bf16[512,512]{1,0:T(8,128)(2,1)} %get-tuple-element.187.refs_0_, bf16[512,512]{1,0:T(8,128)(2,1)} %get-tuple-element.189.refs_1_, bf16[512,512]{1,0:T(8,128)(2,1)} %copy-done.10, bf16[512,512]{1,0:T(8,128)(2,1)} %copy-done.11, ...), custom_call_target="tpu_custom_call" | custom-call | flops 2147483648 | bytes 4194304 | tf_op jit(solution)/shard_map/pallas_call | solution.py:60
  302.7 4.2 all-to-all-start.1
  307.2 6.5 shard_map.325
  316.2 6.7 shard_map.326
  323.5 6.6 shard_map.327
  332.1 3.6 shard_map.328
  341.7 6.8 shard_map.329
  349.8 6.6 shard_map.330
  364.1 6.6 shard_map.331
  374.7 10.5 %collective-permute-done.39.refs_2_ = bf16[512,512]{1,0:T(8,128)(2,1)S(1)} collective-permute-done((bf16[512,512]{1,0:T(8,128)(2,1)}, bf16[512,512]{1,0:T(8,128)(2,1)S(1)}, u32[]{:S(2)}, u32[]{:S(2)}) %collective-permute-start.39) | collective-permute-done | bytes 524320 | tf_op jit(solution)/shard_map/ppermute | solution.py:37
  387.3 4.7 collective-permute-done.41.refs_4_
  392.0 5.6 collective-permute-done.43.refs_6_
  399.3 15.9 %shard_map.332 = bf16[4,2,512,1024]{3,2,1,0:T(8,128)(2,1)} custom-call(s32[4]{0:T(128)} %pad_add_fusion.spot, bf16[512,512]{1,0:T(8,128)(2,1)} %get-tuple-element.217.refs_0_, bf16[512,512]{1,0:T(8,128)(2,1)} %get-tuple-element.218.refs_1_, bf16[512,512]{1,0:T(8,128)(2,1)} %copy-done.13, bf16[512,512]{1,0:T(8,128)(2,1)} %copy-done.16, ...), custom_call_target="tpu_custom_call" | custom-call | flops 2147483648 | bytes 4194304 | tf_op jit(solution)/shard_map/pallas_call | solution.py:60
  415.2 3.5 all-to-all-start.2
  419.2 19.6 %shard_map.333 = (bf16[1024,2048]{1,0:T(8,128)(2,1)}, f32[8,2048]{1,0:T(8,128)}) custom-call(s32[4]{0:T(128)} %pad_add_fusion.spot, bf16[512,512]{1,0:T(8,128)(2,1)} %get-tuple-element.217.refs_0_, bf16[512,512]{1,0:T(8,128)(2,1)} %get-tuple-element.218.refs_1_, bf16[512,512]{1,0:T(8,128)(2,1)} %copy-done.13, bf16[512,512]{1,0:T(8,128)(2,1)} %copy-done.16, ...), custom_call_target="tpu_custom_call" | custom-call | flops 2147483648 | bytes 4194304 | tf_op jit(solution)/shard_map/pallas_call | solution.py:60
  438.8 6.6 shard_map.334
  447.5 6.8 shard_map.335
  455.7 6.8 shard_map.336
  464.0 3.6 shard_map.337
  471.8 7.0 shard_map.338
  478.8 14.1 %shard_map.339 = bf16[4,2,2,512,512]{4,3,2,1,0:T(8,128)(2,1)} custom-call(s32[4]{0:T(128)} %pad_add_fusion.spot, bf16[512,512]{1,0:T(8,128)(2,1)} %get-tuple-element.187.refs_0_, bf16[512,512]{1,0:T(8,128)(2,1)} %get-tuple-element.189.refs_1_, bf16[512,512]{1,0:T(8,128)(2,1)} %copy-done.10, bf16[512,512]{1,0:T(8,128)(2,1)} %copy-done.11, ...), custom_call_target="tpu_custom_call" | custom-call | flops 2147483648 | bytes 4194304 | tf_op jit(solution)/shard_map/pallas_call | solution.py:60
  493.9 6.9 shard_map.340
  508.2 6.3 shard_map.341
  519.6 9.0 %collective-permute-done.54.refs_2_.refs_11_ = bf16[512,512]{1,0:T(8,128)(2,1)S(1)} collective-permute-done((bf16[512,512]{1,0:T(8,128)(2,1)S(1)}, bf16[512,512]{1,0:T(8,128)(2,1)S(1)}, u32[]{:S(2)}, u32[]{:S(2)}) %collective-permute-start.54) | collective-permute-done | bytes 524320 | tf_op jit(solution)/shard_map/ppermute | solution.py:37
  530.6 3.9 collective-permute-done.56.refs_4_.refs_13_
  534.6 7.7 %collective-permute-done.58.refs_6_.refs_15_ = bf16[512,512]{1,0:T(8,128)(2,1)} collective-permute-done((bf16[512,512]{1,0:T(8,128)(2,1)S(1)}, bf16[512,512]{1,0:T(8,128)(2,1)}, u32[]{:S(2)}, u32[]{:S(2)}) %collective-permute-start.58) | collective-permute-done | bytes 524320 | tf_op jit(solution)/shard_map/ppermute | solution.py:37
  542.3 7.5 %shard_map.342.grad_out = bf16[1024,512]{1,0:T(8,128)(2,1)} custom-call(s32[4]{0:T(128)} %pad_add_fusion.spot, bf16[512,512]{1,0:T(8,128)(2,1)} %get-tuple-element.249.refs_0_.refs_9_, bf16[512,512]{1,0:T(8,128)(2,1)} %get-tuple-element.250.refs_1_.refs_10_, bf16[512,512]{1,0:T(8,128)(2,1)} %copy-done.22, ...), custom_call_target="tpu_custom_call" | custom-call | flops 536870912 | bytes 1835008 | tf_op jit(solution)/shard_map/pallas_call | solution.py:60
  553.4 23.1 %shard_map.343 = (bf16[1024,1536]{1,0:T(8,128)(2,1)}, f32[8,1536]{1,0:T(8,128)}) custom-call(s32[4]{0:T(128)} %pad_add_fusion.spot, bf16[1024,1536]{1,0:T(8,128)(2,1)} %shard_map.315.queries.whole, bf16[1024,1536]{1,0:T(8,128)(2,1)} %shard_map.315.queries.whole, s32[1,1024]{1,0:T(1,128)} %bitcast.149, s32[1024,1]{1,0:T(8,128)} %copy.44.ids_column, ...), custom_call_target="tpu_custom_call" | custom-call | flops 4026531840 | bytes 2097152 | tf_op jit(solution)/shard_map/pallas_call | solution.py:60
  576.5 19.9 %shard_map.344 = bf16[4,2,2,512,512]{4,3,2,1,0:T(8,128)(2,1)} custom-call(s32[4]{0:T(128)} %pad_add_fusion.spot, bf16[512,512]{1,0:T(8,128)(2,1)} %get-tuple-element.160.refs_0_.refs_6_, bf16[512,512]{1,0:T(8,128)(2,1)} %get-tuple-element.162.refs_1_.refs_7_, bf16[512,512]{1,0:T(8,128)(2,1)} %copy-done.2, bf16[512,512]{1,0:T(8,128)(2,1)} %copy-done.3, ...), custom_call_target="tpu_custom_call" | custom-call | flops 2147483648 | bytes 5242880 | tf_op jit(solution)/shard_map/pallas_call | solution.py:60
  596.5 6.4 shard_map.345
  605.9 6.4 shard_map.346
  613.8 6.4 shard_map.347
  623.4 3.6 shard_map.348
  631.5 6.7 shard_map.349
  639.3 5.6 shard_map.350
  644.9 4.7 all-to-all-start.3
  656.5 29.1 %all-to-all-done.3 = bf16[4,1024,128]{2,1,0:T(8,128)(2,1)} async-done(((bf16[4,1024,128]{2,1,0:T(8,128)(2,1)}), bf16[4,1024,128]{2,1,0:T(8,128)(2,1)}, u32[]{:S(2)}, u32[]{:S(2)}) %all-to-all-start.3) | async-done | bytes 1048608 | tf_op jit(solution)/shard_map/all_to_all | solution.py:620
  705.7 7.2 reduce-scatter.6.cloned.1.call-done
  716.7 8.8 %collective-permute-done.69.other = bf16[512,512]{1,0:T(8,128)(2,1)S(1)} collective-permute-done((bf16[512,512]{1,0:T(8,128)(2,1)S(1)}, bf16[512,512]{1,0:T(8,128)(2,1)S(1)}, u32[]{:S(2)}, u32[]{:S(2)}) %collective-permute-start.69) | collective-permute-done | bytes 524320 | tf_op jit(solution)/shard_map/ppermute | solution.py:37
  726.4 3.3 shard_map.351
  (407 shorter events, 162.0 us)
Async XLA Ops:
  7.2 130.4 %all-gather.7.cloned.1.call-start = ((), (), s32[]{:S(2)}) async-start(), calls=%async_computation.10 | async-start | bytes 9437184 | tf_op jit(solution)/shard_map/all_gather | solution.py:686
  12.0 15.0 %collective-permute-start.11 = (bf16[512,512]{1,0:T(8,128)(2,1)S(1)}, bf16[512,512]{1,0:T(8,128)(2,1)S(1)}, u32[]{:S(2)}, u32[]{:S(2)}) collective-permute-start(bf16[512,512]{1,0:T(8,128)(2,1)S(1)} %pad_maximum_fusion.3), channel_id=1, source_target_pairs={{0,16},{1,17},{2,18},{3,19},{4,20},{5,21},{6,22},{7,23},{8,24},{9,... | collective-permute-start | bytes 1572872 | tf_op jit(solution)/shard_map/ppermute | solution.py:37
  28.1 14.9 %collective-permute-start.1 = (bf16[2048,128]{1,0:T(8,128)(2,1)S(1)}, bf16[2048,128]{1,0:T(8,128)(2,1)S(1)}, u32[]{:S(2)}, u32[]{:S(2)}) collective-permute-start(bf16[2048,128]{1,0:T(8,128)(2,1)S(1)} %get-tuple-element.313), channel_id=1, source_target_pairs={{0,16},{1,17},{2,18},{3,19},{4,20},{5,21},{6,22},{7,23},{8,24},{9,... | collective-permute-start | bytes 1572872 | tf_op jit(solution)/shard_map/ppermute | solution.py:37
  30.8 67.5 %collective-permute-start = (bf16[512,512]{1,0:T(8,128)(2,1)}, bf16[512,512]{1,0:T(8,128)(2,1)S(1)}, u32[]{:S(2)}, u32[]{:S(2)}) collective-permute-start(bf16[512,512]{1,0:T(8,128)(2,1)} %get-tuple-element.158), channel_id=1, source_target_pairs={{0,16},{1,17},{2,18},{3,19},{4,20},{5,21},{6,22},{7,23},{8,24},{9,... | collective-permute-start | bytes 1572872 | tf_op jit(solution)/shard_map/ppermute | solution.py:37
  44.1 55.3 %collective-permute-start.4 = (bf16[1024,128]{1,0:T(8,128)(2,1)S(1)}, bf16[1024,128]{1,0:T(8,128)(2,1)S(1)}, u32[]{:S(2)}, u32[]{:S(2)}) collective-permute-start(bf16[1024,128]{1,0:T(8,128)(2,1)S(1)} %get-tuple-element.308), channel_id=1, source_target_pairs={{0,6},{1,7},{2,4},{3,5},{4,2},{5,3},{6,0},{7,1},{8,14},{9,15},{10,... | collective-permute-start | bytes 786440 | tf_op jit(solution)/shard_map/ppermute | solution.py:37
  48.0 51.5 %collective-permute-start.2 = (bf16[1024,128]{1,0:T(8,128)(2,1)S(1)}, bf16[1024,128]{1,0:T(8,128)(2,1)S(1)}, u32[]{:S(2)}, u32[]{:S(2)}) collective-permute-start(bf16[1024,128]{1,0:T(8,128)(2,1)S(1)} %get-tuple-element.310), channel_id=1, source_target_pairs={{0,2},{1,3},{2,0},{3,1},{4,6},{5,7},{6,4},{7,5},{8,10},{9,11},{10,... | collective-permute-start | bytes 786440 | tf_op jit(solution)/shard_map/ppermute | solution.py:37
  48.0 51.5 %collective-permute-start.3 = (bf16[1024,128]{1,0:T(8,128)(2,1)S(1)}, bf16[1024,128]{1,0:T(8,128)(2,1)S(1)}, u32[]{:S(2)}, u32[]{:S(2)}) collective-permute-start(bf16[1024,128]{1,0:T(8,128)(2,1)S(1)} %get-tuple-element.311), channel_id=1, source_target_pairs={{0,4},{1,5},{2,6},{3,7},{4,0},{5,1},{6,2},{7,3},{8,12},{9,13},{10,... | collective-permute-start | bytes 786440 | tf_op jit(solution)/shard_map/ppermute | solution.py:37
  49.2 49.2 %all-to-all-start = ((f32[4,1,1536]{2,1,0:T(1,128)}), f32[4,1,1536]{2,1,0:T(1,128)S(1)}, u32[]{:S(2)}, u32[]{:S(2)}) async-start(f32[4,1,1536]{2,1,0:T(1,128)} %broadcast_in_dim.4), calls=%async_computation | async-start | bytes 49152 | tf_op jit(solution)/shard_map/all_to_all | solution.py:728
  54.3 215.2 %all-gather.9.cloned.1.call-start = ((), (), s32[]{:S(2)}) async-start(), calls=%async_computation.11 | async-start | bytes 9437184 | tf_op jit(solution)/shard_map/all_gather | solution.py:686
  104.5 202.7 %all-gather.11.cloned.1.call-start = ((), (), s32[]{:S(2)}) async-start(), calls=%async_computation.12 | async-start | bytes 9437184 | tf_op jit(solution)/shard_map/all_gather | solution.py:686
  104.8 15.1 %collective-permute-start.8 = (bf16[512,512]{1,0:T(8,128)(2,1)}, bf16[512,512]{1,0:T(8,128)(2,1)S(1)}, u32[]{:S(2)}, u32[]{:S(2)}) collective-permute-start(bf16[512,512]{1,0:T(8,128)(2,1)} %get-tuple-element.162.refs_1_.refs_7_), channel_id=1, source_target_pairs={{0,16},{1,17},{2,18},{3,19},{4,20},{5,21},{6,22},{7,23},{8,24},{9,... | collective-permute-start | bytes 1572872 | tf_op jit(solution)/shard_map/ppermute | solution.py:37
  106.3 15.1 %collective-permute-start.5 = (bf16[512,512]{1,0:T(8,128)(2,1)}, bf16[512,512]{1,0:T(8,128)(2,1)S(1)}, u32[]{:S(2)}, u32[]{:S(2)}) collective-permute-start(bf16[512,512]{1,0:T(8,128)(2,1)} %get-tuple-element.160.refs_0_.refs_6_), channel_id=1, source_target_pairs={{0,1},{1,0},{2,3},{3,2},{4,5},{5,4},{6,7},{7,6},{8,9},{9,8},{10,11... | collective-permute-start | bytes 1572872 | tf_op jit(solution)/shard_map/ppermute | solution.py:37
  107.8 24.2 %collective-permute-start.6 = (bf16[512,512]{1,0:T(8,128)(2,1)}, bf16[512,512]{1,0:T(8,128)(2,1)S(1)}, u32[]{:S(2)}, u32[]{:S(2)}) collective-permute-start(bf16[512,512]{1,0:T(8,128)(2,1)} %get-tuple-element.162.refs_1_.refs_7_), channel_id=1, source_target_pairs={{0,1},{1,0},{2,3},{3,2},{4,5},{5,4},{6,7},{7,6},{8,9},{9,8},{10,11... | collective-permute-start | bytes 1572872 | tf_op jit(solution)/shard_map/ppermute | solution.py:37
  108.3 23.7 %collective-permute-start.7 = (bf16[512,512]{1,0:T(8,128)(2,1)}, bf16[512,512]{1,0:T(8,128)(2,1)S(1)}, u32[]{:S(2)}, u32[]{:S(2)}) collective-permute-start(bf16[512,512]{1,0:T(8,128)(2,1)} %get-tuple-element.160.refs_0_.refs_6_), channel_id=1, source_target_pairs={{0,16},{1,17},{2,18},{3,19},{4,20},{5,21},{6,22},{7,23},{8,24},{9,... | collective-permute-start | bytes 1572872 | tf_op jit(solution)/shard_map/ppermute | solution.py:37
  119.9 17.7 %collective-permute-start.10 = (bf16[512,512]{1,0:T(8,128)(2,1)S(1)}, bf16[512,512]{1,0:T(8,128)(2,1)S(1)}, u32[]{:S(2)}, u32[]{:S(2)}) collective-permute-start(bf16[512,512]{1,0:T(8,128)(2,1)S(1)} %collective-permute-done.8.refs_5_), channel_id=1, source_target_pairs={{0,1},{1,0},{2,3},{3,2},{4,5},{5,4},{6,7},{7,6},{8,9},{9,8},{10,11... | collective-permute-start | bytes 1572872 | tf_op jit(solution)/shard_map/ppermute | solution.py:37
  121.4 16.2 %collective-permute-start.9 = (bf16[512,512]{1,0:T(8,128)(2,1)S(1)}, bf16[512,512]{1,0:T(8,128)(2,1)S(1)}, u32[]{:S(2)}, u32[]{:S(2)}) collective-permute-start(bf16[512,512]{1,0:T(8,128)(2,1)S(1)} %collective-permute-done.5.refs_2_), channel_id=1, source_target_pairs={{0,16},{1,17},{2,18},{3,19},{4,20},{5,21},{6,22},{7,23},{8,24},{9,... | collective-permute-start | bytes 1572872 | tf_op jit(solution)/shard_map/ppermute | solution.py:37
  188.6 13.3 %collective-permute-start.15 = (bf16[512,512]{1,0:T(8,128)(2,1)}, bf16[512,512]{1,0:T(8,128)(2,1)S(1)}, u32[]{:S(2)}, u32[]{:S(2)}) collective-permute-start(bf16[512,512]{1,0:T(8,128)(2,1)} %get-tuple-element.175), channel_id=1, source_target_pairs={{0,16},{1,17},{2,18},{3,19},{4,20},{5,21},{6,22},{7,23},{8,24},{9,... | collective-permute-start | bytes 1572872 | tf_op jit(solution)/shard_map/ppermute | solution.py:37
  190.0 14.9 %collective-permute-start.14 = (bf16[512,512]{1,0:T(8,128)(2,1)}, bf16[512,512]{1,0:T(8,128)(2,1)S(1)}, u32[]{:S(2)}, u32[]{:S(2)}) collective-permute-start(bf16[512,512]{1,0:T(8,128)(2,1)} %get-tuple-element.168), channel_id=1, source_target_pairs={{0,1},{1,0},{2,3},{3,2},{4,5},{5,4},{6,7},{7,6},{8,9},{9,8},{10,11... | collective-permute-start | bytes 1572872 | tf_op jit(solution)/shard_map/ppermute | solution.py:37
  196.1 20.1 %collective-permute-start.16 = (bf16[512,512]{1,0:T(8,128)(2,1)}, bf16[512,512]{1,0:T(8,128)(2,1)S(1)}, u32[]{:S(2)}, u32[]{:S(2)}) collective-permute-start(bf16[512,512]{1,0:T(8,128)(2,1)} %get-tuple-element.170), channel_id=1, source_target_pairs={{0,1},{1,0},{2,3},{3,2},{4,5},{5,4},{6,7},{7,6},{8,9},{9,8},{10,11... | collective-permute-start | bytes 1572872 | tf_op jit(solution)/shard_map/ppermute | solution.py:37
  201.3 14.9 %collective-permute-start.17 = (bf16[512,512]{1,0:T(8,128)(2,1)}, bf16[512,512]{1,0:T(8,128)(2,1)S(1)}, u32[]{:S(2)}, u32[]{:S(2)}) collective-permute-start(bf16[512,512]{1,0:T(8,128)(2,1)} %get-tuple-element.178), channel_id=1, source_target_pairs={{0,16},{1,17},{2,18},{3,19},{4,20},{5,21},{6,22},{7,23},{8,24},{9,... | collective-permute-start | bytes 1572872 | tf_op jit(solution)/shard_map/ppermute | solution.py:37
  209.3 12.6 %collective-permute-start.19 = (bf16[512,512]{1,0:T(8,128)(2,1)}, bf16[512,512]{1,0:T(8,128)(2,1)S(1)}, u32[]{:S(2)}, u32[]{:S(2)}) collective-permute-start(bf16[512,512]{1,0:T(8,128)(2,1)} %get-tuple-element.183), channel_id=1, source_target_pairs={{0,1},{1,0},{2,3},{3,2},{4,5},{5,4},{6,7},{7,6},{8,9},{9,8},{10,11... | collective-permute-start | bytes 1572872 | tf_op jit(solution)/shard_map/ppermute | solution.py:37
  241.9 15.1 %collective-permute-start.26 = (bf16[512,512]{1,0:T(8,128)(2,1)}, bf16[512,512]{1,0:T(8,128)(2,1)S(1)}, u32[]{:S(2)}, u32[]{:S(2)}) collective-permute-start(bf16[512,512]{1,0:T(8,128)(2,1)} %get-tuple-element.189.refs_1_), channel_id=1, source_target_pairs={{0,16},{1,17},{2,18},{3,19},{4,20},{5,21},{6,22},{7,23},{8,24},{9,... | collective-permute-start | bytes 1572872 | tf_op jit(solution)/shard_map/ppermute | solution.py:37
  242.3 15.4 %collective-permute-start.23 = (bf16[512,512]{1,0:T(8,128)(2,1)}, bf16[512,512]{1,0:T(8,128)(2,1)S(1)}, u32[]{:S(2)}, u32[]{:S(2)}) collective-permute-start(bf16[512,512]{1,0:T(8,128)(2,1)} %get-tuple-element.187.refs_0_), channel_id=1, source_target_pairs={{0,1},{1,0},{2,3},{3,2},{4,5},{5,4},{6,7},{7,6},{8,9},{9,8},{10,11... | collective-permute-start | bytes 1572872 | tf_op jit(solution)/shard_map/ppermute | solution.py:37
  243.3 25.0 %collective-permute-start.35 = (bf16[2048,128]{1,0:T(8,128)(2,1)S(1)}, bf16[2048,128]{1,0:T(8,128)(2,1)S(1)}, u32[]{:S(2)}, u32[]{:S(2)}) collective-permute-start(bf16[2048,128]{1,0:T(8,128)(2,1)S(1)} %get-tuple-element.305), channel_id=1, source_target_pairs={{0,16},{1,17},{2,18},{3,19},{4,20},{5,21},{6,22},{7,23},{8,24},{9,... | collective-permute-start | bytes 1572872 | tf_op jit(solution)/shard_map/ppermute | solution.py:37
  244.8 24.7 %collective-permute-start.24 = (bf16[512,512]{1,0:T(8,128)(2,1)S(1)}, bf16[512,512]{1,0:T(8,128)(2,1)S(1)}, u32[]{:S(2)}, u32[]{:S(2)}) collective-permute-start(bf16[512,512]{1,0:T(8,128)(2,1)S(1)} %copy-done.8), channel_id=1, source_target_pairs={{0,1},{1,0},{2,3},{3,2},{4,5},{5,4},{6,7},{7,6},{8,9},{9,8},{10,11... | collective-permute-start | bytes 1572872 | tf_op jit(solution)/shard_map/ppermute | solution.py:37
  246.2 30.6 %collective-permute-start.25 = (bf16[512,512]{1,0:T(8,128)(2,1)S(1)}, bf16[512,512]{1,0:T(8,128)(2,1)S(1)}, u32[]{:S(2)}, u32[]{:S(2)}) collective-permute-start(bf16[512,512]{1,0:T(8,128)(2,1)S(1)} %copy-done.7), channel_id=1, source_target_pairs={{0,16},{1,17},{2,18},{3,19},{4,20},{5,21},{6,22},{7,23},{8,24},{9,... | collective-permute-start | bytes 1572872 | tf_op jit(solution)/shard_map/ppermute | solution.py:37
  257.1 19.8 %collective-permute-start.28 = (bf16[512,512]{1,0:T(8,128)(2,1)S(1)}, bf16[512,512]{1,0:T(8,128)(2,1)}, u32[]{:S(2)}, u32[]{:S(2)}) collective-permute-start(bf16[512,512]{1,0:T(8,128)(2,1)S(1)} %collective-permute-done.26.refs_5_), channel_id=1, source_target_pairs={{0,1},{1,0},{2,3},{3,2},{4,5},{5,4},{6,7},{7,6},{8,9},{9,8},{10,11... | collective-permute-start | bytes 1572872 | tf_op jit(solution)/shard_map/ppermute | solution.py:37
  257.7 24.9 %collective-permute-start.27 = (bf16[512,512]{1,0:T(8,128)(2,1)S(1)}, bf16[512,512]{1,0:T(8,128)(2,1)}, u32[]{:S(2)}, u32[]{:S(2)}) collective-permute-start(bf16[512,512]{1,0:T(8,128)(2,1)S(1)} %collective-permute-done.23.refs_2_), channel_id=1, source_target_pairs={{0,16},{1,17},{2,18},{3,19},{4,20},{5,21},{6,22},{7,23},{8,24},{9,... | collective-permute-start | bytes 1572872 | tf_op jit(solution)/shard_map/ppermute | solution.py:37
  302.7 45.8 %all-to-all-start.1 = ((bf16[4,1024,128]{2,1,0:T(8,128)(2,1)}), bf16[4,1024,128]{2,1,0:T(8,128)(2,1)S(1)}, u32[]{:S(2)}, u32[]{:S(2)}) async-start(bf16[4,1024,128]{2,1,0:T(8,128)(2,1)} %maximum_select_fusion.2), calls=%async_computation.1 | async-start | bytes 2097152 | tf_op jit(solution)/shard_map/all_to_all | solution.py:770
  306.9 223.7 %reduce-scatter.4.cloned.1.call-start = ((), (), s32[]{:S(2)}) async-start(), calls=%async_computation.7 | async-start | bytes 9437184 | tf_op jit(solution)/shard_map/reduce_scatter | solution.py:690
  313.7 17.3 %collective-permute-start.30 = (bf16[512,512]{1,0:T(8,128)(2,1)}, bf16[512,512]{1,0:T(8,128)(2,1)S(1)}, u32[]{:S(2)}, u32[]{:S(2)}) collective-permute-start(bf16[512,512]{1,0:T(8,128)(2,1)} %get-tuple-element.200), channel_id=1, source_target_pairs={{0,16},{1,17},{2,18},{3,19},{4,20},{5,21},{6,22},{7,23},{8,24},{9,... | collective-permute-start | bytes 1572872 | tf_op jit(solution)/shard_map/ppermute | solution.py:37
  314.8 16.2 %collective-permute-start.29 = (bf16[512,512]{1,0:T(8,128)(2,1)}, bf16[512,512]{1,0:T(8,128)(2,1)S(1)}, u32[]{:S(2)}, u32[]{:S(2)}) collective-permute-start(bf16[512,512]{1,0:T(8,128)(2,1)} %get-tuple-element.193), channel_id=1, source_target_pairs={{0,1},{1,0},{2,3},{3,2},{4,5},{5,4},{6,7},{7,6},{8,9},{9,8},{10,11... | collective-permute-start | bytes 1572872 | tf_op jit(solution)/shard_map/ppermute | solution.py:37
  322.8 16.6 %collective-permute-start.31 = (bf16[512,512]{1,0:T(8,128)(2,1)}, bf16[512,512]{1,0:T(8,128)(2,1)S(1)}, u32[]{:S(2)}, u32[]{:S(2)}) collective-permute-start(bf16[512,512]{1,0:T(8,128)(2,1)} %get-tuple-element.195), channel_id=1, source_target_pairs={{0,1},{1,0},{2,3},{3,2},{4,5},{5,4},{6,7},{7,6},{8,9},{9,8},{10,11... | collective-permute-start | bytes 1572872 | tf_op jit(solution)/shard_map/ppermute | solution.py:37
  330.2 11.5 %collective-permute-start.32 = (bf16[512,512]{1,0:T(8,128)(2,1)}, bf16[512,512]{1,0:T(8,128)(2,1)S(1)}, u32[]{:S(2)}, u32[]{:S(2)}) collective-permute-start(bf16[512,512]{1,0:T(8,128)(2,1)} %get-tuple-element.203), channel_id=1, source_target_pairs={{0,16},{1,17},{2,18},{3,19},{4,20},{5,21},{6,22},{7,23},{8,24},{9,... | collective-permute-start | bytes 1572872 | tf_op jit(solution)/shard_map/ppermute | solution.py:37
  335.6 12.9 %collective-permute-start.34 = (bf16[512,512]{1,0:T(8,128)(2,1)}, bf16[512,512]{1,0:T(8,128)(2,1)S(1)}, u32[]{:S(2)}, u32[]{:S(2)}) collective-permute-start(bf16[512,512]{1,0:T(8,128)(2,1)} %get-tuple-element.208), channel_id=1, source_target_pairs={{0,1},{1,0},{2,3},{3,2},{4,5},{5,4},{6,7},{7,6},{8,9},{9,8},{10,11... | collective-permute-start | bytes 1572872 | tf_op jit(solution)/shard_map/ppermute | solution.py:37
  337.1 11.5 %collective-permute-start.33 = (bf16[512,512]{1,0:T(8,128)(2,1)}, bf16[512,512]{1,0:T(8,128)(2,1)S(1)}, u32[]{:S(2)}, u32[]{:S(2)}) collective-permute-start(bf16[512,512]{1,0:T(8,128)(2,1)} %get-tuple-element.201), channel_id=1, source_target_pairs={{0,16},{1,17},{2,18},{3,19},{4,20},{5,21},{6,22},{7,23},{8,24},{9,... | collective-permute-start | bytes 1572872 | tf_op jit(solution)/shard_map/ppermute | solution.py:37
  370.6 14.7 %collective-permute-start.39 = (bf16[512,512]{1,0:T(8,128)(2,1)}, bf16[512,512]{1,0:T(8,128)(2,1)S(1)}, u32[]{:S(2)}, u32[]{:S(2)}) collective-permute-start(bf16[512,512]{1,0:T(8,128)(2,1)} %get-tuple-element.217.refs_0_), channel_id=1, source_target_pairs={{0,1},{1,0},{2,3},{3,2},{4,5},{5,4},{6,7},{7,6},{8,9},{9,8},{10,11... | collective-permute-start | bytes 1572872 | tf_op jit(solution)/shard_map/ppermute | solution.py:37
  371.3 15.1 %collective-permute-start.42 = (bf16[512,512]{1,0:T(8,128)(2,1)}, bf16[512,512]{1,0:T(8,128)(2,1)S(1)}, u32[]{:S(2)}, u32[]{:S(2)}) collective-permute-start(bf16[512,512]{1,0:T(8,128)(2,1)} %get-tuple-element.218.refs_1_), channel_id=1, source_target_pairs={{0,16},{1,17},{2,18},{3,19},{4,20},{5,21},{6,22},{7,23},{8,24},{9,... | collective-permute-start | bytes 1572872 | tf_op jit(solution)/shard_map/ppermute | solution.py:37
  373.1 18.9 %collective-permute-start.41 = (bf16[512,512]{1,0:T(8,128)(2,1)}, bf16[512,512]{1,0:T(8,128)(2,1)S(1)}, u32[]{:S(2)}, u32[]{:S(2)}) collective-permute-start(bf16[512,512]{1,0:T(8,128)(2,1)} %get-tuple-element.217.refs_0_), channel_id=1, source_target_pairs={{0,16},{1,17},{2,18},{3,19},{4,20},{5,21},{6,22},{7,23},{8,24},{9,... | collective-permute-start | bytes 1572872 | tf_op jit(solution)/shard_map/ppermute | solution.py:37
  373.3 18.6 %collective-permute-start.40 = (bf16[512,512]{1,0:T(8,128)(2,1)}, bf16[512,512]{1,0:T(8,128)(2,1)S(1)}, u32[]{:S(2)}, u32[]{:S(2)}) collective-permute-start(bf16[512,512]{1,0:T(8,128)(2,1)} %get-tuple-element.218.refs_1_), channel_id=1, source_target_pairs={{0,1},{1,0},{2,3},{3,2},{4,5},{5,4},{6,7},{7,6},{8,9},{9,8},{10,11... | collective-permute-start | bytes 1572872 | tf_op jit(solution)/shard_map/ppermute | solution.py:37
  385.3 12.3 %collective-permute-start.43 = (bf16[512,512]{1,0:T(8,128)(2,1)S(1)}, bf16[512,512]{1,0:T(8,128)(2,1)S(1)}, u32[]{:S(2)}, u32[]{:S(2)}) collective-permute-start(bf16[512,512]{1,0:T(8,128)(2,1)S(1)} %collective-permute-done.39.refs_2_), channel_id=1, source_target_pairs={{0,16},{1,17},{2,18},{3,19},{4,20},{5,21},{6,22},{7,23},{8,24},{9,... | collective-permute-start | bytes 1572872 | tf_op jit(solution)/shard_map/ppermute | solution.py:37
  415.2 63.6 %all-to-all-start.2 = ((bf16[4,1024,128]{2,1,0:T(8,128)(2,1)}), bf16[4,1024,128]{2,1,0:T(8,128)(2,1)S(1)}, u32[]{:S(2)}, u32[]{:S(2)}) async-start(bf16[4,1024,128]{2,1,0:T(8,128)(2,1)} %get-tuple-element.219), calls=%async_computation.2 | async-start | bytes 2097152 | tf_op jit(solution)/shard_map/all_to_all | solution.py:620
  418.7 234.6 %reduce-scatter.8.cloned.1.call-start = ((), (), s32[]{:S(2)}) async-start(), calls=%async_computation.9 | async-start | bytes 9437184 | tf_op jit(solution)/shard_map/reduce_scatter | solution.py:690
  445.4 17.6 %collective-permute-start.46 = (bf16[512,512]{1,0:T(8,128)(2,1)}, bf16[512,512]{1,0:T(8,128)(2,1)S(1)}, u32[]{:S(2)}, u32[]{:S(2)}) collective-permute-start(bf16[512,512]{1,0:T(8,128)(2,1)} %get-tuple-element.231), channel_id=1, source_target_pairs={{0,16},{1,17},{2,18},{3,19},{4,20},{5,21},{6,22},{7,23},{8,24},{9,... | collective-permute-start | bytes 1572872 | tf_op jit(solution)/shard_map/ppermute | solution.py:37
  446.8 16.2 %collective-permute-start.45 = (bf16[512,512]{1,0:T(8,128)(2,1)}, bf16[512,512]{1,0:T(8,128)(2,1)S(1)}, u32[]{:S(2)}, u32[]{:S(2)}) collective-permute-start(bf16[512,512]{1,0:T(8,128)(2,1)} %get-tuple-element.224), channel_id=1, source_target_pairs={{0,1},{1,0},{2,3},{3,2},{4,5},{5,4},{6,7},{7,6},{8,9},{9,8},{10,11... | collective-permute-start | bytes 1572872 | tf_op jit(solution)/shard_map/ppermute | solution.py:37
  454.2 15.4 %collective-permute-start.47 = (bf16[512,512]{1,0:T(8,128)(2,1)}, bf16[512,512]{1,0:T(8,128)(2,1)S(1)}, u32[]{:S(2)}, u32[]{:S(2)}) collective-permute-start(bf16[512,512]{1,0:T(8,128)(2,1)} %get-tuple-element.226), channel_id=1, source_target_pairs={{0,1},{1,0},{2,3},{3,2},{4,5},{5,4},{6,7},{7,6},{8,9},{9,8},{10,11... | collective-permute-start | bytes 1572872 | tf_op jit(solution)/shard_map/ppermute | solution.py:37
  467.7 25.2 %collective-permute-start.50 = (bf16[512,512]{1,0:T(8,128)(2,1)}, bf16[512,512]{1,0:T(8,128)(2,1)S(1)}, u32[]{:S(2)}, u32[]{:S(2)}) collective-permute-start(bf16[512,512]{1,0:T(8,128)(2,1)} %get-tuple-element.241), channel_id=1, source_target_pairs={{0,1},{1,0},{2,3},{3,2},{4,5},{5,4},{6,7},{7,6},{8,9},{9,8},{10,11... | collective-permute-start | bytes 1572872 | tf_op jit(solution)/shard_map/ppermute | solution.py:37
  468.4 24.5 %collective-permute-start.49 = (bf16[512,512]{1,0:T(8,128)(2,1)}, bf16[512,512]{1,0:T(8,128)(2,1)S(1)}, u32[]{:S(2)}, u32[]{:S(2)}) collective-permute-start(bf16[512,512]{1,0:T(8,128)(2,1)} %get-tuple-element.232), channel_id=1, source_target_pairs={{0,16},{1,17},{2,18},{3,19},{4,20},{5,21},{6,22},{7,23},{8,24},{9,... | collective-permute-start | bytes 1572872 | tf_op jit(solution)/shard_map/ppermute | solution.py:37
  514.5 198.4 %reduce-scatter.6.cloned.1.call-start = ((), (), s32[]{:S(2)}) async-start(), calls=%async_computation.8 | async-start | bytes 9437184 | tf_op jit(solution)/shard_map/reduce_scatter | solution.py:690
  515.5 13.0 %collective-permute-start.54 = (bf16[512,512]{1,0:T(8,128)(2,1)S(1)}, bf16[512,512]{1,0:T(8,128)(2,1)S(1)}, u32[]{:S(2)}, u32[]{:S(2)}) collective-permute-start(bf16[512,512]{1,0:T(8,128)(2,1)S(1)} %copy-done.20), channel_id=1, source_target_pairs={{0,1},{1,0},{2,3},{3,2},{4,5},{5,4},{6,7},{7,6},{8,9},{9,8},{10,11... | collective-permute-start | bytes 1572872 | tf_op jit(solution)/shard_map/ppermute | solution.py:37
  516.8 12.5 %collective-permute-start.57 = (bf16[512,512]{1,0:T(8,128)(2,1)S(1)}, bf16[512,512]{1,0:T(8,128)(2,1)S(1)}, u32[]{:S(2)}, u32[]{:S(2)}) collective-permute-start(bf16[512,512]{1,0:T(8,128)(2,1)S(1)} %copy-done.21), channel_id=1, source_target_pairs={{0,16},{1,17},{2,18},{3,19},{4,20},{5,21},{6,22},{7,23},{8,24},{9,... | collective-permute-start | bytes 1572872 | tf_op jit(solution)/shard_map/ppermute | solution.py:37
  518.2 16.4 %collective-permute-start.56 = (bf16[512,512]{1,0:T(8,128)(2,1)S(1)}, bf16[512,512]{1,0:T(8,128)(2,1)}, u32[]{:S(2)}, u32[]{:S(2)}) collective-permute-start(bf16[512,512]{1,0:T(8,128)(2,1)S(1)} %copy-done.20), channel_id=1, source_target_pairs={{0,16},{1,17},{2,18},{3,19},{4,20},{5,21},{6,22},{7,23},{8,24},{9,... | collective-permute-start | bytes 1572872 | tf_op jit(solution)/shard_map/ppermute | solution.py:37
  518.8 15.7 %collective-permute-start.55 = (bf16[512,512]{1,0:T(8,128)(2,1)S(1)}, bf16[512,512]{1,0:T(8,128)(2,1)}, u32[]{:S(2)}, u32[]{:S(2)}) collective-permute-start(bf16[512,512]{1,0:T(8,128)(2,1)S(1)} %copy-done.21), channel_id=1, source_target_pairs={{0,1},{1,0},{2,3},{3,2},{4,5},{5,4},{6,7},{7,6},{8,9},{9,8},{10,11... | collective-permute-start | bytes 1572872 | tf_op jit(solution)/shard_map/ppermute | solution.py:37
  528.5 13.8 %collective-permute-start.58 = (bf16[512,512]{1,0:T(8,128)(2,1)S(1)}, bf16[512,512]{1,0:T(8,128)(2,1)}, u32[]{:S(2)}, u32[]{:S(2)}) collective-permute-start(bf16[512,512]{1,0:T(8,128)(2,1)S(1)} %collective-permute-done.54.refs_2_.refs_11_), channel_id=1, source_target_pairs={{0,16},{1,17},{2,18},{3,19},{4,20},{5,21},{6,22},{7,23},{8,24},{9,... | collective-permute-start | bytes 1572872 | tf_op jit(solution)/shard_map/ppermute | solution.py:37
  529.3 13.0 %collective-permute-start.59 = (bf16[512,512]{1,0:T(8,128)(2,1)S(1)}, bf16[512,512]{1,0:T(8,128)(2,1)}, u32[]{:S(2)}, u32[]{:S(2)}) collective-permute-start(bf16[512,512]{1,0:T(8,128)(2,1)S(1)} %collective-permute-done.57.refs_5_.refs_14_), channel_id=1, source_target_pairs={{0,1},{1,0},{2,3},{3,2},{4,5},{5,4},{6,7},{7,6},{8,9},{9,8},{10,11... | collective-permute-start | bytes 1572872 | tf_op jit(solution)/shard_map/ppermute | solution.py:37
  550.7 25.8 %collective-permute-start.60 = (bf16[2048,128]{1,0:T(8,128)(2,1)S(1)}, bf16[2048,128]{1,0:T(8,128)(2,1)S(1)}, u32[]{:S(2)}, u32[]{:S(2)}) collective-permute-start(bf16[2048,128]{1,0:T(8,128)(2,1)S(1)} %get-tuple-element.303), channel_id=1, source_target_pairs={{0,16},{1,17},{2,18},{3,19},{4,20},{5,21},{6,22},{7,23},{8,24},{9,... | collective-permute-start | bytes 1572872 | tf_op jit(solution)/shard_map/ppermute | solution.py:37
  552.9 23.7 %collective-permute-start.61 = (bf16[512,512]{1,0:T(8,128)(2,1)S(1)}, bf16[512,512]{1,0:T(8,128)(2,1)S(1)}, u32[]{:S(2)}, u32[]{:S(2)}) collective-permute-start(bf16[512,512]{1,0:T(8,128)(2,1)S(1)} %get-tuple-element.297), channel_id=1, source_target_pairs={{0,16},{1,17},{2,18},{3,19},{4,20},{5,21},{6,22},{7,23},{8,24},{9,... | collective-permute-start | bytes 1572872 | tf_op jit(solution)/shard_map/ppermute | solution.py:37
  602.9 19.5 %collective-permute-start.63 = (bf16[512,512]{1,0:T(8,128)(2,1)}, bf16[512,512]{1,0:T(8,128)(2,1)S(1)}, u32[]{:S(2)}, u32[]{:S(2)}) collective-permute-start(bf16[512,512]{1,0:T(8,128)(2,1)} %get-tuple-element.266), channel_id=1, source_target_pairs={{0,16},{1,17},{2,18},{3,19},{4,20},{5,21},{6,22},{7,23},{8,24},{9,... | collective-permute-start | bytes 1572872 | tf_op jit(solution)/shard_map/ppermute | solution.py:37
  604.4 18.0 %collective-permute-start.62 = (bf16[512,512]{1,0:T(8,128)(2,1)}, bf16[512,512]{1,0:T(8,128)(2,1)S(1)}, u32[]{:S(2)}, u32[]{:S(2)}) collective-permute-start(bf16[512,512]{1,0:T(8,128)(2,1)} %get-tuple-element.259), channel_id=1, source_target_pairs={{0,1},{1,0},{2,3},{3,2},{4,5},{5,4},{6,7},{7,6},{8,9},{9,8},{10,11... | collective-permute-start | bytes 1572872 | tf_op jit(solution)/shard_map/ppermute | solution.py:37
  612.3 19.1 %collective-permute-start.64 = (bf16[512,512]{1,0:T(8,128)(2,1)}, bf16[512,512]{1,0:T(8,128)(2,1)S(1)}, u32[]{:S(2)}, u32[]{:S(2)}) collective-permute-start(bf16[512,512]{1,0:T(8,128)(2,1)} %get-tuple-element.261), channel_id=1, source_target_pairs={{0,1},{1,0},{2,3},{3,2},{4,5},{5,4},{6,7},{7,6},{8,9},{9,8},{10,11... | collective-permute-start | bytes 1572872 | tf_op jit(solution)/shard_map/ppermute | solution.py:37
  644.9 40.7 %all-to-all-start.3 = ((bf16[4,1024,128]{2,1,0:T(8,128)(2,1)}), bf16[4,1024,128]{2,1,0:T(8,128)(2,1)}, u32[]{:S(2)}, u32[]{:S(2)}) async-start(bf16[4,1024,128]{2,1,0:T(8,128)(2,1)} %shard_map.350), calls=%async_computation.4 | async-start | bytes 2097152 | tf_op jit(solution)/shard_map/all_to_all | solution.py:620
  651.0 39.9 %collective-permute-start.71 = (f32[4,1664]{1,0:T(4,128)S(1)}, f32[4,1664]{1,0:T(4,128)S(1)}, u32[]{:S(2)}, u32[]{:S(2)}) collective-permute-start(f32[4,1664]{1,0:T(4,128)S(1)} %add.91), channel_id=1, source_target_pairs={{0,2},{1,3},{2,0},{3,1},{4,6},{5,7},{6,4},{7,5},{8,10},{9,11},{10,... | collective-permute-start | bytes 79880 | tf_op jit(solution)/shard_map/ppermute | solution.py:37
  655.4 35.5 %collective-permute-start.72 = (bf16[512,512]{1,0:T(8,128)(2,1)}, bf16[512,512]{1,0:T(8,128)(2,1)}, u32[]{:S(2)}, u32[]{:S(2)}) collective-permute-start(bf16[512,512]{1,0:T(8,128)(2,1)} %get-tuple-element.299), channel_id=1, source_target_pairs={{0,16},{1,17},{2,18},{3,19},{4,20},{5,21},{6,22},{7,23},{8,24},{9,... | collective-permute-start | bytes 1572872 | tf_op jit(solution)/shard_map/ppermute | solution.py:37
  714.0 11.6 %collective-permute-start.69 = (bf16[512,512]{1,0:T(8,128)(2,1)S(1)}, bf16[512,512]{1,0:T(8,128)(2,1)S(1)}, u32[]{:S(2)}, u32[]{:S(2)}) collective-permute-start(bf16[512,512]{1,0:T(8,128)(2,1)S(1)} %slice_bitcast_fusion), channel_id=1, source_target_pairs={{0,16},{1,17},{2,18},{3,19},{4,20},{5,21},{6,22},{7,23},{8,24},{9,... | collective-permute-start | bytes 1572872 | tf_op jit(solution)/shard_map/ppermute | solution.py:37
  (106 other events, 568.9 us)
Sparse Core Ops, SparseCore 0:
  28.3 106.2 all-gather.6
  136.2 80.4 all-gather.8
  218.2 80.5 all-gather.10
  415.3 96.7 reduce-scatter.3
  514.6 90.0 reduce-scatter.7
  606.9 105.9 reduce-scatter.5

commit v7 on v6

--- a/solution.py
+++ b/solution.py
@@ -779,14 +779,14 @@
         [shape_of(4, LEN, 128, dtype=BF), full, low_half, low_half, sums_shape], [BLOCKS, TILE, LOW, HIGH, SUMS],
     )
     ffn_wide = square_gather(ffn_low, ffn_high)
+    layer_parts = from_share(layer_share)
+    spot.after(layer_parts)
     down = grad_whole(ffn_wide, act, spot, True)
     grad_down = scatter_zc(down)
-    layer_parts = from_share(tie(layer_share, down))
     grad_pre, sums_up = wide(ffn_wide, full_down, spot, True, finish_slope, (slope,), 1, 1)
     up = []
 
     def after():
-        spot.after(layer_parts)
         up.append(grad_whole(hidden_wide, grad_pre, spot, False))
 
     parts = square_scatter(grad_pre, full_up, spot, False, after=after)

time: 743 us -> 741 us (level)
    unnamed x188 -> x186, local copies, waits for them, and re-layouts: 16.5 us -> 14.8 us
where the time goes in v7:
time: 741 us; the launch traced here: 734 us
  Pallas kernels  315 us (43%)
  waiting for transfers between devices  257 us (35%)
  starting transfers between devices  101 us (14%)
  local copies, waits for them, and re-layouts  29.1 us (4%)
  other arithmetic  17.6 us (2%)
  between operations  15.4 us (2%)
    pallas_call x39, Pallas kernels, call(): pl.pallas_call(body, grid_spec=pltpu.PrefetchScalarGridSpec(num_scalar_pr...  315 us
    ppermute x77, waiting for transfers between devices, swap(): return lax.ppermute(piece, AXES, [(i, i ^ mask) for i in range(32)])  175 us
    ppermute x77, starting transfers between devices, swap(): return lax.ppermute(piece, AXES, [(i, i ^ mask) for i in range(32)])  81.9 us
    all_to_all x1, waiting for transfers between devices, square_device(): lax.all_to_all(jnp.broadcast_to(vectors, (4, vectors.shape[1])), 'z', 0,...  44.1 us
    all_to_all x2, waiting for transfers between devices, from_share(): return lax.all_to_all(share, 'z', 0, 0, tiled=True).reshape(2, 2 * LEN, 128)  30.1 us
    unnamed x186, local copies, waits for them, and re-layouts  14.8 us
  transfers between devices with their start and end apart: 87, of which 41 were waited for; matrix products, arithmetic and copies ran while one was open for 4% of the time, Pallas kernels for 38%

profile of v7, /device:TPU:0, one launch (start us, length us, event | category | flops | bytes accessed | tf_op | source)
XLA Modules:
  0.0 734.3 jit_solution(18339937502678639044)
XLA Ops:
  15.1 11.9 %collective-permute-done.11 = bf16[512,512]{1,0:T(8,128)(2,1)S(1)} collective-permute-done((bf16[512,512]{1,0:T(8,128)(2,1)S(1)}, bf16[512,512]{1,0:T(8,128)(2,1)S(1)}, u32[]{:S(2)}, u32[]{:S(2)}) %collective-permute-start.11) | collective-permute-done | bytes 524320 | tf_op jit(solution)/shard_map/ppermute | solution.py:37
  31.3 11.7 %collective-permute-done.1 = bf16[2048,128]{1,0:T(8,128)(2,1)S(1)} collective-permute-done((bf16[2048,128]{1,0:T(8,128)(2,1)S(1)}, bf16[2048,128]{1,0:T(8,128)(2,1)S(1)}, u32[]{:S(2)}, u32[]{:S(2)}) %collective-permute-start.1) | collective-permute-done | bytes 524320 | tf_op jit(solution)/shard_map/ppermute | solution.py:37
  44.1 3.8 collective-permute-start.4
  49.2 5.1 all-to-all-start
  54.3 44.1 %all-to-all-done = f32[4,1,1536]{2,1,0:T(1,128)S(1)} async-done(((f32[4,1,1536]{2,1,0:T(1,128)}), f32[4,1,1536]{2,1,0:T(1,128)S(1)}, u32[]{:S(2)}, u32[]{:S(2)}) %all-to-all-start) | async-done | bytes 24608 | tf_op jit(solution)/shard_map/all_to_all | solution.py:728
  100.3 4.2 shard_map.314
  108.9 11.0 %collective-permute-done.8.refs_5_ = bf16[512,512]{1,0:T(8,128)(2,1)S(1)} collective-permute-done((bf16[512,512]{1,0:T(8,128)(2,1)}, bf16[512,512]{1,0:T(8,128)(2,1)S(1)}, u32[]{:S(2)}, u32[]{:S(2)}) %collective-permute-start.8) | collective-permute-done | bytes 524320 | tf_op jit(solution)/shard_map/ppermute | solution.py:37
  124.2 7.7 %collective-permute-done.6.refs_3_ = bf16[512,512]{1,0:T(8,128)(2,1)S(1)} collective-permute-done((bf16[512,512]{1,0:T(8,128)(2,1)}, bf16[512,512]{1,0:T(8,128)(2,1)S(1)}, u32[]{:S(2)}, u32[]{:S(2)}) %collective-permute-start.6) | collective-permute-done | bytes 524320 | tf_op jit(solution)/shard_map/ppermute | solution.py:37
  132.0 5.6 collective-permute-done.10.refs_7_
  138.6 16.4 %shard_map.315.queries.whole = bf16[1024,1536]{1,0:T(8,128)(2,1)} custom-call(s32[4]{0:T(128)} %pad_add_fusion.spot, bf16[512,512]{1,0:T(8,128)(2,1)} %get-tuple-element.159.refs_0_.refs_6_, bf16[512,512]{1,0:T(8,128)(2,1)} %get-tuple-element.161.refs_1_.refs_7_, bf16[512,512]{1,0:T(8,128)(2,1)} %copy-done.2, bf16[512,512]{1,0:T(8,128)(2,1)} %copy-done.3, ...), custom_call_target="tpu_custom_call" | custom-call | flops 1610612736 | bytes 3407872 | tf_op jit(solution)/shard_map/pallas_call | solution.py:60
  155.3 9.6 %collective-permute-done.13 = bf16[512,512]{1,0:T(8,128)(2,1)S(1)} collective-permute-done((bf16[512,512]{1,0:T(8,128)(2,1)S(1)}, bf16[512,512]{1,0:T(8,128)(2,1)S(1)}, u32[]{:S(2)}, u32[]{:S(2)}) %collective-permute-start.13) | collective-permute-done | bytes 524320 | tf_op jit(solution)/shard_map/ppermute | solution.py:37
  171.1 12.9 %shard_map.316 = (bf16[1024,512]{1,0:T(8,128)(2,1)}, f32[4,1,1024]{2,1,0:T(1,128)}) custom-call(s32[4]{0:T(128)} %pad_add_fusion.spot, bf16[1024,1536]{1,0:T(8,128)(2,1)} %shard_map.315.queries.whole, bf16[1024,1536]{1,0:T(8,128)(2,1)} %shard_map.315.queries.whole, s32[1,1024]{1,0:T(1,128)} %bitcast.148, s32[1024,1]{1,0:T(8,128)} %copy.44.ids_column), custom_call_target="tpu_custom_call" | custom-call | flops 2147483648 | bytes 1048576 | tf_op jit(solution)/shard_map/pallas_call | solution.py:60
  184.1 4.4 shard_map.317
  191.4 4.6 shard_map.318
  196.6 4.6 shard_map.319
  205.7 3.6 shard_map.320
  211.2 4.9 collective-permute-done.16.refs_2_
  216.1 4.8 shard_map.321
  222.9 6.2 shard_map.322
  236.8 5.1 shard_map.323
  246.3 10.7 %collective-permute-done.26.refs_5_ = bf16[512,512]{1,0:T(8,128)(2,1)S(1)} collective-permute-done((bf16[512,512]{1,0:T(8,128)(2,1)}, bf16[512,512]{1,0:T(8,128)(2,1)S(1)}, u32[]{:S(2)}, u32[]{:S(2)}) %collective-permute-start.26) | collective-permute-done | bytes 524320 | tf_op jit(solution)/shard_map/ppermute | solution.py:37
  259.7 8.6 %collective-permute-done.35 = bf16[2048,128]{1,0:T(8,128)(2,1)S(1)} collective-permute-done((bf16[2048,128]{1,0:T(8,128)(2,1)S(1)}, bf16[2048,128]{1,0:T(8,128)(2,1)S(1)}, u32[]{:S(2)}, u32[]{:S(2)}) %collective-permute-start.35) | collective-permute-done | bytes 524320 | tf_op jit(solution)/shard_map/ppermute | solution.py:37
  269.4 7.3 collective-permute-done.25.refs_4_
  276.8 5.7 collective-permute-done.27.refs_6_
  282.5 20.1 %shard_map.324 = (bf16[1024,2048]{1,0:T(8,128)(2,1)}, bf16[1024,2048]{1,0:T(8,128)(2,1)}) custom-call(s32[4]{0:T(128)} %pad_add_fusion.spot, bf16[512,512]{1,0:T(8,128)(2,1)} %get-tuple-element.186.refs_0_, bf16[512,512]{1,0:T(8,128)(2,1)} %get-tuple-element.188.refs_1_, bf16[512,512]{1,0:T(8,128)(2,1)} %copy-done.10, bf16[512,512]{1,0:T(8,128)(2,1)} %copy-done.11, ...), custom_call_target="tpu_custom_call" | custom-call | flops 2147483648 | bytes 4194304 | tf_op jit(solution)/shard_map/pallas_call | solution.py:60
  302.6 4.4 all-to-all-start.1
  307.1 6.5 shard_map.325
  316.0 6.7 shard_map.326
  323.4 6.6 shard_map.327
  331.9 3.6 shard_map.328
  341.7 6.9 shard_map.329
  349.9 6.6 shard_map.330
  363.8 6.6 shard_map.331
  370.4 3.9 all-to-all-start.2
  378.3 10.1 %collective-permute-done.39.refs_2_ = bf16[512,512]{1,0:T(8,128)(2,1)S(1)} collective-permute-done((bf16[512,512]{1,0:T(8,128)(2,1)S(1)}, bf16[512,512]{1,0:T(8,128)(2,1)S(1)}, u32[]{:S(2)}, u32[]{:S(2)}) %collective-permute-start.39) | collective-permute-done | bytes 524320 | tf_op jit(solution)/shard_map/ppermute | solution.py:37
  390.8 4.8 collective-permute-done.41.refs_4_
  395.6 5.6 collective-permute-done.43.refs_6_
  401.2 15.9 %shard_map.332 = bf16[4,2,512,1024]{3,2,1,0:T(8,128)(2,1)} custom-call(s32[4]{0:T(128)} %pad_add_fusion.spot, bf16[512,512]{1,0:T(8,128)(2,1)} %get-tuple-element.217.refs_0_, bf16[512,512]{1,0:T(8,128)(2,1)} %get-tuple-element.218.refs_1_, bf16[512,512]{1,0:T(8,128)(2,1)} %copy-done.15, bf16[512,512]{1,0:T(8,128)(2,1)} %collective-permute-done.40.refs_3_, ...), custom_call_target="tpu_custom_call" | custom-call | flops 2147483648 | bytes 4194304 | tf_op jit(solution)/shard_map/pallas_call | solution.py:60
  417.6 19.3 %shard_map.333 = (bf16[1024,2048]{1,0:T(8,128)(2,1)}, f32[8,2048]{1,0:T(8,128)}) custom-call(s32[4]{0:T(128)} %pad_add_fusion.spot, bf16[512,512]{1,0:T(8,128)(2,1)} %get-tuple-element.217.refs_0_, bf16[512,512]{1,0:T(8,128)(2,1)} %get-tuple-element.218.refs_1_, bf16[512,512]{1,0:T(8,128)(2,1)} %copy-done.15, ...), custom_call_target="tpu_custom_call" | custom-call | flops 2147483648 | bytes 4194304 | tf_op jit(solution)/shard_map/pallas_call | solution.py:60
  436.9 6.7 shard_map.334
  444.8 6.8 shard_map.335
  453.2 6.8 shard_map.336
  462.3 3.7 shard_map.337
  469.9 7.0 shard_map.338
  476.9 14.1 %shard_map.339 = bf16[4,2,2,512,512]{4,3,2,1,0:T(8,128)(2,1)} custom-call(s32[4]{0:T(128)} %pad_add_fusion.spot, bf16[512,512]{1,0:T(8,128)(2,1)} %get-tuple-element.186.refs_0_, bf16[512,512]{1,0:T(8,128)(2,1)} %get-tuple-element.188.refs_1_, bf16[512,512]{1,0:T(8,128)(2,1)} %copy-done.10, bf16[512,512]{1,0:T(8,128)(2,1)} %copy-done.11, ...), custom_call_target="tpu_custom_call" | custom-call | flops 2147483648 | bytes 4194304 | tf_op jit(solution)/shard_map/pallas_call | solution.py:60
  492.0 6.8 shard_map.340
  506.3 6.2 shard_map.341
  517.6 8.9 %collective-permute-done.54.refs_2_.refs_11_ = bf16[512,512]{1,0:T(8,128)(2,1)S(1)} collective-permute-done((bf16[512,512]{1,0:T(8,128)(2,1)S(1)}, bf16[512,512]{1,0:T(8,128)(2,1)S(1)}, u32[]{:S(2)}, u32[]{:S(2)}) %collective-permute-start.54) | collective-permute-done | bytes 524320 | tf_op jit(solution)/shard_map/ppermute | solution.py:37
  528.4 4.2 collective-permute-done.56.refs_4_.refs_13_
  532.6 7.8 %collective-permute-done.58.refs_6_.refs_15_ = bf16[512,512]{1,0:T(8,128)(2,1)} collective-permute-done((bf16[512,512]{1,0:T(8,128)(2,1)S(1)}, bf16[512,512]{1,0:T(8,128)(2,1)}, u32[]{:S(2)}, u32[]{:S(2)}) %collective-permute-start.58) | collective-permute-done | bytes 524320 | tf_op jit(solution)/shard_map/ppermute | solution.py:37
  540.4 7.5 %shard_map.342.grad_out = bf16[1024,512]{1,0:T(8,128)(2,1)} custom-call(s32[4]{0:T(128)} %pad_add_fusion.spot, bf16[512,512]{1,0:T(8,128)(2,1)} %get-tuple-element.247.refs_0_.refs_9_, bf16[512,512]{1,0:T(8,128)(2,1)} %get-tuple-element.248.refs_1_.refs_10_, bf16[512,512]{1,0:T(8,128)(2,1)} %copy-done.20, ...), custom_call_target="tpu_custom_call" | custom-call | flops 536870912 | bytes 1835008 | tf_op jit(solution)/shard_map/pallas_call | solution.py:60
  551.0 23.1 %shard_map.343 = (bf16[1024,1536]{1,0:T(8,128)(2,1)}, f32[8,1536]{1,0:T(8,128)}) custom-call(s32[4]{0:T(128)} %pad_add_fusion.spot, bf16[1024,1536]{1,0:T(8,128)(2,1)} %shard_map.315.queries.whole, bf16[1024,1536]{1,0:T(8,128)(2,1)} %shard_map.315.queries.whole, s32[1,1024]{1,0:T(1,128)} %bitcast.149, s32[1024,1]{1,0:T(8,128)} %copy.44.ids_column, ...), custom_call_target="tpu_custom_call" | custom-call | flops 4026531840 | bytes 2097152 | tf_op jit(solution)/shard_map/pallas_call | solution.py:60
  574.2 19.9 %shard_map.344 = bf16[4,2,2,512,512]{4,3,2,1,0:T(8,128)(2,1)} custom-call(s32[4]{0:T(128)} %pad_add_fusion.spot, bf16[512,512]{1,0:T(8,128)(2,1)} %get-tuple-element.159.refs_0_.refs_6_, bf16[512,512]{1,0:T(8,128)(2,1)} %get-tuple-element.161.refs_1_.refs_7_, bf16[512,512]{1,0:T(8,128)(2,1)} %copy-done.2, bf16[512,512]{1,0:T(8,128)(2,1)} %copy-done.3, ...), custom_call_target="tpu_custom_call" | custom-call | flops 2147483648 | bytes 5242880 | tf_op jit(solution)/shard_map/pallas_call | solution.py:60
  594.1 6.4 shard_map.345
  603.5 6.4 shard_map.346
  611.0 6.4 shard_map.347
  621.0 3.6 shard_map.348
  629.1 6.7 shard_map.349
  636.9 5.6 shard_map.350
  642.5 4.8 all-to-all-start.3
  653.0 30.1 %all-to-all-done.3 = bf16[4,1024,128]{2,1,0:T(8,128)(2,1)} async-done(((bf16[4,1024,128]{2,1,0:T(8,128)(2,1)}), bf16[4,1024,128]{2,1,0:T(8,128)(2,1)}, u32[]{:S(2)}, u32[]{:S(2)}) %all-to-all-start.3) | async-done | bytes 1048608 | tf_op jit(solution)/shard_map/all_to_all | solution.py:620
  703.5 6.9 reduce-scatter.6.cloned.1.call-done
  714.3 8.8 %collective-permute-done.69.other = bf16[512,512]{1,0:T(8,128)(2,1)S(1)} collective-permute-done((bf16[512,512]{1,0:T(8,128)(2,1)S(1)}, bf16[512,512]{1,0:T(8,128)(2,1)S(1)}, u32[]{:S(2)}, u32[]{:S(2)}) %collective-permute-start.69) | collective-permute-done | bytes 524320 | tf_op jit(solution)/shard_map/ppermute | solution.py:37
  724.0 3.3 shard_map.351
  (405 shorter events, 158.2 us)
Async XLA Ops:
  7.2 130.4 %all-gather.7.cloned.1.call-start = ((), (), s32[]{:S(2)}) async-start(), calls=%async_computation.10 | async-start | bytes 9437184 | tf_op jit(solution)/shard_map/all_gather | solution.py:686
  12.0 15.0 %collective-permute-start.11 = (bf16[512,512]{1,0:T(8,128)(2,1)S(1)}, bf16[512,512]{1,0:T(8,128)(2,1)S(1)}, u32[]{:S(2)}, u32[]{:S(2)}) collective-permute-start(bf16[512,512]{1,0:T(8,128)(2,1)S(1)} %pad_maximum_fusion.3), channel_id=1, source_target_pairs={{0,16},{1,17},{2,18},{3,19},{4,20},{5,21},{6,22},{7,23},{8,24},{9,... | collective-permute-start | bytes 1572872 | tf_op jit(solution)/shard_map/ppermute | solution.py:37
  28.1 14.9 %collective-permute-start.1 = (bf16[2048,128]{1,0:T(8,128)(2,1)S(1)}, bf16[2048,128]{1,0:T(8,128)(2,1)S(1)}, u32[]{:S(2)}, u32[]{:S(2)}) collective-permute-start(bf16[2048,128]{1,0:T(8,128)(2,1)S(1)} %get-tuple-element.311), channel_id=1, source_target_pairs={{0,16},{1,17},{2,18},{3,19},{4,20},{5,21},{6,22},{7,23},{8,24},{9,... | collective-permute-start | bytes 1572872 | tf_op jit(solution)/shard_map/ppermute | solution.py:37
  30.8 67.5 %collective-permute-start = (bf16[512,512]{1,0:T(8,128)(2,1)}, bf16[512,512]{1,0:T(8,128)(2,1)S(1)}, u32[]{:S(2)}, u32[]{:S(2)}) collective-permute-start(bf16[512,512]{1,0:T(8,128)(2,1)} %get-tuple-element.157), channel_id=1, source_target_pairs={{0,16},{1,17},{2,18},{3,19},{4,20},{5,21},{6,22},{7,23},{8,24},{9,... | collective-permute-start | bytes 1572872 | tf_op jit(solution)/shard_map/ppermute | solution.py:37
  44.1 55.3 %collective-permute-start.4 = (bf16[1024,128]{1,0:T(8,128)(2,1)S(1)}, bf16[1024,128]{1,0:T(8,128)(2,1)S(1)}, u32[]{:S(2)}, u32[]{:S(2)}) collective-permute-start(bf16[1024,128]{1,0:T(8,128)(2,1)S(1)} %get-tuple-element.306), channel_id=1, source_target_pairs={{0,6},{1,7},{2,4},{3,5},{4,2},{5,3},{6,0},{7,1},{8,14},{9,15},{10,... | collective-permute-start | bytes 786440 | tf_op jit(solution)/shard_map/ppermute | solution.py:37
  48.0 51.5 %collective-permute-start.2 = (bf16[1024,128]{1,0:T(8,128)(2,1)S(1)}, bf16[1024,128]{1,0:T(8,128)(2,1)S(1)}, u32[]{:S(2)}, u32[]{:S(2)}) collective-permute-start(bf16[1024,128]{1,0:T(8,128)(2,1)S(1)} %get-tuple-element.308), channel_id=1, source_target_pairs={{0,2},{1,3},{2,0},{3,1},{4,6},{5,7},{6,4},{7,5},{8,10},{9,11},{10,... | collective-permute-start | bytes 786440 | tf_op jit(solution)/shard_map/ppermute | solution.py:37
  48.0 51.5 %collective-permute-start.3 = (bf16[1024,128]{1,0:T(8,128)(2,1)S(1)}, bf16[1024,128]{1,0:T(8,128)(2,1)S(1)}, u32[]{:S(2)}, u32[]{:S(2)}) collective-permute-start(bf16[1024,128]{1,0:T(8,128)(2,1)S(1)} %get-tuple-element.309), channel_id=1, source_target_pairs={{0,4},{1,5},{2,6},{3,7},{4,0},{5,1},{6,2},{7,3},{8,12},{9,13},{10,... | collective-permute-start | bytes 786440 | tf_op jit(solution)/shard_map/ppermute | solution.py:37
  49.2 49.2 %all-to-all-start = ((f32[4,1,1536]{2,1,0:T(1,128)}), f32[4,1,1536]{2,1,0:T(1,128)S(1)}, u32[]{:S(2)}, u32[]{:S(2)}) async-start(f32[4,1,1536]{2,1,0:T(1,128)} %broadcast_in_dim.4), calls=%async_computation | async-start | bytes 49152 | tf_op jit(solution)/shard_map/all_to_all | solution.py:728
  54.3 215.1 %all-gather.9.cloned.1.call-start = ((), (), s32[]{:S(2)}) async-start(), calls=%async_computation.11 | async-start | bytes 9437184 | tf_op jit(solution)/shard_map/all_gather | solution.py:686
  104.5 202.5 %all-gather.11.cloned.1.call-start = ((), (), s32[]{:S(2)}) async-start(), calls=%async_computation.12 | async-start | bytes 9437184 | tf_op jit(solution)/shard_map/all_gather | solution.py:686
  104.8 15.1 %collective-permute-start.8 = (bf16[512,512]{1,0:T(8,128)(2,1)}, bf16[512,512]{1,0:T(8,128)(2,1)S(1)}, u32[]{:S(2)}, u32[]{:S(2)}) collective-permute-start(bf16[512,512]{1,0:T(8,128)(2,1)} %get-tuple-element.161.refs_1_.refs_7_), channel_id=1, source_target_pairs={{0,16},{1,17},{2,18},{3,19},{4,20},{5,21},{6,22},{7,23},{8,24},{9,... | collective-permute-start | bytes 1572872 | tf_op jit(solution)/shard_map/ppermute | solution.py:37
  106.3 15.1 %collective-permute-start.5 = (bf16[512,512]{1,0:T(8,128)(2,1)}, bf16[512,512]{1,0:T(8,128)(2,1)S(1)}, u32[]{:S(2)}, u32[]{:S(2)}) collective-permute-start(bf16[512,512]{1,0:T(8,128)(2,1)} %get-tuple-element.159.refs_0_.refs_6_), channel_id=1, source_target_pairs={{0,1},{1,0},{2,3},{3,2},{4,5},{5,4},{6,7},{7,6},{8,9},{9,8},{10,11... | collective-permute-start | bytes 1572872 | tf_op jit(solution)/shard_map/ppermute | solution.py:37
  107.8 24.2 %collective-permute-start.6 = (bf16[512,512]{1,0:T(8,128)(2,1)}, bf16[512,512]{1,0:T(8,128)(2,1)S(1)}, u32[]{:S(2)}, u32[]{:S(2)}) collective-permute-start(bf16[512,512]{1,0:T(8,128)(2,1)} %get-tuple-element.161.refs_1_.refs_7_), channel_id=1, source_target_pairs={{0,1},{1,0},{2,3},{3,2},{4,5},{5,4},{6,7},{7,6},{8,9},{9,8},{10,11... | collective-permute-start | bytes 1572872 | tf_op jit(solution)/shard_map/ppermute | solution.py:37
  108.3 23.7 %collective-permute-start.7 = (bf16[512,512]{1,0:T(8,128)(2,1)}, bf16[512,512]{1,0:T(8,128)(2,1)S(1)}, u32[]{:S(2)}, u32[]{:S(2)}) collective-permute-start(bf16[512,512]{1,0:T(8,128)(2,1)} %get-tuple-element.159.refs_0_.refs_6_), channel_id=1, source_target_pairs={{0,16},{1,17},{2,18},{3,19},{4,20},{5,21},{6,22},{7,23},{8,24},{9,... | collective-permute-start | bytes 1572872 | tf_op jit(solution)/shard_map/ppermute | solution.py:37
  119.9 17.7 %collective-permute-start.10 = (bf16[512,512]{1,0:T(8,128)(2,1)S(1)}, bf16[512,512]{1,0:T(8,128)(2,1)S(1)}, u32[]{:S(2)}, u32[]{:S(2)}) collective-permute-start(bf16[512,512]{1,0:T(8,128)(2,1)S(1)} %collective-permute-done.8.refs_5_), channel_id=1, source_target_pairs={{0,1},{1,0},{2,3},{3,2},{4,5},{5,4},{6,7},{7,6},{8,9},{9,8},{10,11... | collective-permute-start | bytes 1572872 | tf_op jit(solution)/shard_map/ppermute | solution.py:37
  121.4 16.2 %collective-permute-start.9 = (bf16[512,512]{1,0:T(8,128)(2,1)S(1)}, bf16[512,512]{1,0:T(8,128)(2,1)S(1)}, u32[]{:S(2)}, u32[]{:S(2)}) collective-permute-start(bf16[512,512]{1,0:T(8,128)(2,1)S(1)} %collective-permute-done.5.refs_2_), channel_id=1, source_target_pairs={{0,16},{1,17},{2,18},{3,19},{4,20},{5,21},{6,22},{7,23},{8,24},{9,... | collective-permute-start | bytes 1572872 | tf_op jit(solution)/shard_map/ppermute | solution.py:37
  188.5 13.3 %collective-permute-start.15 = (bf16[512,512]{1,0:T(8,128)(2,1)}, bf16[512,512]{1,0:T(8,128)(2,1)S(1)}, u32[]{:S(2)}, u32[]{:S(2)}) collective-permute-start(bf16[512,512]{1,0:T(8,128)(2,1)} %get-tuple-element.174), channel_id=1, source_target_pairs={{0,16},{1,17},{2,18},{3,19},{4,20},{5,21},{6,22},{7,23},{8,24},{9,... | collective-permute-start | bytes 1572872 | tf_op jit(solution)/shard_map/ppermute | solution.py:37
  190.0 14.9 %collective-permute-start.14 = (bf16[512,512]{1,0:T(8,128)(2,1)}, bf16[512,512]{1,0:T(8,128)(2,1)S(1)}, u32[]{:S(2)}, u32[]{:S(2)}) collective-permute-start(bf16[512,512]{1,0:T(8,128)(2,1)} %get-tuple-element.167), channel_id=1, source_target_pairs={{0,1},{1,0},{2,3},{3,2},{4,5},{5,4},{6,7},{7,6},{8,9},{9,8},{10,11... | collective-permute-start | bytes 1572872 | tf_op jit(solution)/shard_map/ppermute | solution.py:37
  196.1 20.1 %collective-permute-start.16 = (bf16[512,512]{1,0:T(8,128)(2,1)}, bf16[512,512]{1,0:T(8,128)(2,1)S(1)}, u32[]{:S(2)}, u32[]{:S(2)}) collective-permute-start(bf16[512,512]{1,0:T(8,128)(2,1)} %get-tuple-element.169), channel_id=1, source_target_pairs={{0,1},{1,0},{2,3},{3,2},{4,5},{5,4},{6,7},{7,6},{8,9},{9,8},{10,11... | collective-permute-start | bytes 1572872 | tf_op jit(solution)/shard_map/ppermute | solution.py:37
  201.2 14.9 %collective-permute-start.17 = (bf16[512,512]{1,0:T(8,128)(2,1)}, bf16[512,512]{1,0:T(8,128)(2,1)S(1)}, u32[]{:S(2)}, u32[]{:S(2)}) collective-permute-start(bf16[512,512]{1,0:T(8,128)(2,1)} %get-tuple-element.177), channel_id=1, source_target_pairs={{0,16},{1,17},{2,18},{3,19},{4,20},{5,21},{6,22},{7,23},{8,24},{9,... | collective-permute-start | bytes 1572872 | tf_op jit(solution)/shard_map/ppermute | solution.py:37
  209.2 12.6 %collective-permute-start.19 = (bf16[512,512]{1,0:T(8,128)(2,1)}, bf16[512,512]{1,0:T(8,128)(2,1)S(1)}, u32[]{:S(2)}, u32[]{:S(2)}) collective-permute-start(bf16[512,512]{1,0:T(8,128)(2,1)} %get-tuple-element.182), channel_id=1, source_target_pairs={{0,1},{1,0},{2,3},{3,2},{4,5},{5,4},{6,7},{7,6},{8,9},{9,8},{10,11... | collective-permute-start | bytes 1572872 | tf_op jit(solution)/shard_map/ppermute | solution.py:37
  241.9 15.1 %collective-permute-start.26 = (bf16[512,512]{1,0:T(8,128)(2,1)}, bf16[512,512]{1,0:T(8,128)(2,1)S(1)}, u32[]{:S(2)}, u32[]{:S(2)}) collective-permute-start(bf16[512,512]{1,0:T(8,128)(2,1)} %get-tuple-element.188.refs_1_), channel_id=1, source_target_pairs={{0,16},{1,17},{2,18},{3,19},{4,20},{5,21},{6,22},{7,23},{8,24},{9,... | collective-permute-start | bytes 1572872 | tf_op jit(solution)/shard_map/ppermute | solution.py:37
  242.1 15.5 %collective-permute-start.23 = (bf16[512,512]{1,0:T(8,128)(2,1)}, bf16[512,512]{1,0:T(8,128)(2,1)S(1)}, u32[]{:S(2)}, u32[]{:S(2)}) collective-permute-start(bf16[512,512]{1,0:T(8,128)(2,1)} %get-tuple-element.186.refs_0_), channel_id=1, source_target_pairs={{0,1},{1,0},{2,3},{3,2},{4,5},{5,4},{6,7},{7,6},{8,9},{9,8},{10,11... | collective-permute-start | bytes 1572872 | tf_op jit(solution)/shard_map/ppermute | solution.py:37
  243.1 25.1 %collective-permute-start.35 = (bf16[2048,128]{1,0:T(8,128)(2,1)S(1)}, bf16[2048,128]{1,0:T(8,128)(2,1)S(1)}, u32[]{:S(2)}, u32[]{:S(2)}) collective-permute-start(bf16[2048,128]{1,0:T(8,128)(2,1)S(1)} %get-tuple-element.303), channel_id=1, source_target_pairs={{0,16},{1,17},{2,18},{3,19},{4,20},{5,21},{6,22},{7,23},{8,24},{9,... | collective-permute-start | bytes 1572872 | tf_op jit(solution)/shard_map/ppermute | solution.py:37
  244.7 24.7 %collective-permute-start.24 = (bf16[512,512]{1,0:T(8,128)(2,1)S(1)}, bf16[512,512]{1,0:T(8,128)(2,1)S(1)}, u32[]{:S(2)}, u32[]{:S(2)}) collective-permute-start(bf16[512,512]{1,0:T(8,128)(2,1)S(1)} %copy-done.8), channel_id=1, source_target_pairs={{0,1},{1,0},{2,3},{3,2},{4,5},{5,4},{6,7},{7,6},{8,9},{9,8},{10,11... | collective-permute-start | bytes 1572872 | tf_op jit(solution)/shard_map/ppermute | solution.py:37
  246.2 30.6 %collective-permute-start.25 = (bf16[512,512]{1,0:T(8,128)(2,1)S(1)}, bf16[512,512]{1,0:T(8,128)(2,1)S(1)}, u32[]{:S(2)}, u32[]{:S(2)}) collective-permute-start(bf16[512,512]{1,0:T(8,128)(2,1)S(1)} %copy-done.7), channel_id=1, source_target_pairs={{0,16},{1,17},{2,18},{3,19},{4,20},{5,21},{6,22},{7,23},{8,24},{9,... | collective-permute-start | bytes 1572872 | tf_op jit(solution)/shard_map/ppermute | solution.py:37
  257.0 19.7 %collective-permute-start.28 = (bf16[512,512]{1,0:T(8,128)(2,1)S(1)}, bf16[512,512]{1,0:T(8,128)(2,1)}, u32[]{:S(2)}, u32[]{:S(2)}) collective-permute-start(bf16[512,512]{1,0:T(8,128)(2,1)S(1)} %collective-permute-done.26.refs_5_), channel_id=1, source_target_pairs={{0,1},{1,0},{2,3},{3,2},{4,5},{5,4},{6,7},{7,6},{8,9},{9,8},{10,11... | collective-permute-start | bytes 1572872 | tf_op jit(solution)/shard_map/ppermute | solution.py:37
  257.6 24.9 %collective-permute-start.27 = (bf16[512,512]{1,0:T(8,128)(2,1)S(1)}, bf16[512,512]{1,0:T(8,128)(2,1)}, u32[]{:S(2)}, u32[]{:S(2)}) collective-permute-start(bf16[512,512]{1,0:T(8,128)(2,1)S(1)} %collective-permute-done.23.refs_2_), channel_id=1, source_target_pairs={{0,16},{1,17},{2,18},{3,19},{4,20},{5,21},{6,22},{7,23},{8,24},{9,... | collective-permute-start | bytes 1572872 | tf_op jit(solution)/shard_map/ppermute | solution.py:37
  302.6 45.9 %all-to-all-start.1 = ((bf16[4,1024,128]{2,1,0:T(8,128)(2,1)}), bf16[4,1024,128]{2,1,0:T(8,128)(2,1)S(1)}, u32[]{:S(2)}, u32[]{:S(2)}) async-start(bf16[4,1024,128]{2,1,0:T(8,128)(2,1)} %maximum_select_fusion.2), calls=%async_computation.1 | async-start | bytes 2097152 | tf_op jit(solution)/shard_map/all_to_all | solution.py:770
  313.6 17.3 %collective-permute-start.30 = (bf16[512,512]{1,0:T(8,128)(2,1)}, bf16[512,512]{1,0:T(8,128)(2,1)S(1)}, u32[]{:S(2)}, u32[]{:S(2)}) collective-permute-start(bf16[512,512]{1,0:T(8,128)(2,1)} %get-tuple-element.199), channel_id=1, source_target_pairs={{0,16},{1,17},{2,18},{3,19},{4,20},{5,21},{6,22},{7,23},{8,24},{9,... | collective-permute-start | bytes 1572872 | tf_op jit(solution)/shard_map/ppermute | solution.py:37
  314.7 16.2 %collective-permute-start.29 = (bf16[512,512]{1,0:T(8,128)(2,1)}, bf16[512,512]{1,0:T(8,128)(2,1)S(1)}, u32[]{:S(2)}, u32[]{:S(2)}) collective-permute-start(bf16[512,512]{1,0:T(8,128)(2,1)} %get-tuple-element.192), channel_id=1, source_target_pairs={{0,1},{1,0},{2,3},{3,2},{4,5},{5,4},{6,7},{7,6},{8,9},{9,8},{10,11... | collective-permute-start | bytes 1572872 | tf_op jit(solution)/shard_map/ppermute | solution.py:37
  322.6 16.8 %collective-permute-start.31 = (bf16[512,512]{1,0:T(8,128)(2,1)}, bf16[512,512]{1,0:T(8,128)(2,1)S(1)}, u32[]{:S(2)}, u32[]{:S(2)}) collective-permute-start(bf16[512,512]{1,0:T(8,128)(2,1)} %get-tuple-element.194), channel_id=1, source_target_pairs={{0,1},{1,0},{2,3},{3,2},{4,5},{5,4},{6,7},{7,6},{8,9},{9,8},{10,11... | collective-permute-start | bytes 1572872 | tf_op jit(solution)/shard_map/ppermute | solution.py:37
  330.0 11.6 %collective-permute-start.32 = (bf16[512,512]{1,0:T(8,128)(2,1)}, bf16[512,512]{1,0:T(8,128)(2,1)S(1)}, u32[]{:S(2)}, u32[]{:S(2)}) collective-permute-start(bf16[512,512]{1,0:T(8,128)(2,1)} %get-tuple-element.202), channel_id=1, source_target_pairs={{0,16},{1,17},{2,18},{3,19},{4,20},{5,21},{6,22},{7,23},{8,24},{9,... | collective-permute-start | bytes 1572872 | tf_op jit(solution)/shard_map/ppermute | solution.py:37
  335.5 13.1 %collective-permute-start.34 = (bf16[512,512]{1,0:T(8,128)(2,1)}, bf16[512,512]{1,0:T(8,128)(2,1)S(1)}, u32[]{:S(2)}, u32[]{:S(2)}) collective-permute-start(bf16[512,512]{1,0:T(8,128)(2,1)} %get-tuple-element.207), channel_id=1, source_target_pairs={{0,1},{1,0},{2,3},{3,2},{4,5},{5,4},{6,7},{7,6},{8,9},{9,8},{10,11... | collective-permute-start | bytes 1572872 | tf_op jit(solution)/shard_map/ppermute | solution.py:37
  336.9 11.7 %collective-permute-start.33 = (bf16[512,512]{1,0:T(8,128)(2,1)}, bf16[512,512]{1,0:T(8,128)(2,1)S(1)}, u32[]{:S(2)}, u32[]{:S(2)}) collective-permute-start(bf16[512,512]{1,0:T(8,128)(2,1)} %get-tuple-element.200), channel_id=1, source_target_pairs={{0,16},{1,17},{2,18},{3,19},{4,20},{5,21},{6,22},{7,23},{8,24},{9,... | collective-permute-start | bytes 1572872 | tf_op jit(solution)/shard_map/ppermute | solution.py:37
  370.4 20.4 %all-to-all-start.2 = ((bf16[4,1024,128]{2,1,0:T(8,128)(2,1)}), bf16[4,1024,128]{2,1,0:T(8,128)(2,1)S(1)}, u32[]{:S(2)}, u32[]{:S(2)}) async-start(bf16[4,1024,128]{2,1,0:T(8,128)(2,1)} %get-tuple-element.214), calls=%async_computation.2 | async-start | bytes 2097152 | tf_op jit(solution)/shard_map/all_to_all | solution.py:620
  374.2 154.2 %reduce-scatter.4.cloned.1.call-start = ((), (), s32[]{:S(2)}) async-start(), calls=%async_computation.7 | async-start | bytes 9437184 | tf_op jit(solution)/shard_map/reduce_scatter | solution.py:690
  374.2 14.2 %collective-permute-start.39 = (bf16[512,512]{1,0:T(8,128)(2,1)S(1)}, bf16[512,512]{1,0:T(8,128)(2,1)S(1)}, u32[]{:S(2)}, u32[]{:S(2)}) collective-permute-start(bf16[512,512]{1,0:T(8,128)(2,1)S(1)} %copy-done.13), channel_id=1, source_target_pairs={{0,1},{1,0},{2,3},{3,2},{4,5},{5,4},{6,7},{7,6},{8,9},{9,8},{10,11... | collective-permute-start | bytes 1572872 | tf_op jit(solution)/shard_map/ppermute | solution.py:37
  376.0 13.8 %collective-permute-start.42 = (bf16[512,512]{1,0:T(8,128)(2,1)S(1)}, bf16[512,512]{1,0:T(8,128)(2,1)S(1)}, u32[]{:S(2)}, u32[]{:S(2)}) collective-permute-start(bf16[512,512]{1,0:T(8,128)(2,1)S(1)} %copy-done.14), channel_id=1, source_target_pairs={{0,16},{1,17},{2,18},{3,19},{4,20},{5,21},{6,22},{7,23},{8,24},{9,... | collective-permute-start | bytes 1572872 | tf_op jit(solution)/shard_map/ppermute | solution.py:37
  376.6 19.0 %collective-permute-start.41 = (bf16[512,512]{1,0:T(8,128)(2,1)S(1)}, bf16[512,512]{1,0:T(8,128)(2,1)}, u32[]{:S(2)}, u32[]{:S(2)}) collective-permute-start(bf16[512,512]{1,0:T(8,128)(2,1)S(1)} %copy-done.13), channel_id=1, source_target_pairs={{0,16},{1,17},{2,18},{3,19},{4,20},{5,21},{6,22},{7,23},{8,24},{9,... | collective-permute-start | bytes 1572872 | tf_op jit(solution)/shard_map/ppermute | solution.py:37
  378.1 17.5 %collective-permute-start.40 = (bf16[512,512]{1,0:T(8,128)(2,1)S(1)}, bf16[512,512]{1,0:T(8,128)(2,1)}, u32[]{:S(2)}, u32[]{:S(2)}) collective-permute-start(bf16[512,512]{1,0:T(8,128)(2,1)S(1)} %copy-done.14), channel_id=1, source_target_pairs={{0,1},{1,0},{2,3},{3,2},{4,5},{5,4},{6,7},{7,6},{8,9},{9,8},{10,11... | collective-permute-start | bytes 1572872 | tf_op jit(solution)/shard_map/ppermute | solution.py:37
  388.4 12.8 %collective-permute-start.43 = (bf16[512,512]{1,0:T(8,128)(2,1)S(1)}, bf16[512,512]{1,0:T(8,128)(2,1)}, u32[]{:S(2)}, u32[]{:S(2)}) collective-permute-start(bf16[512,512]{1,0:T(8,128)(2,1)S(1)} %collective-permute-done.39.refs_2_), channel_id=1, source_target_pairs={{0,16},{1,17},{2,18},{3,19},{4,20},{5,21},{6,22},{7,23},{8,24},{9,... | collective-permute-start | bytes 1572872 | tf_op jit(solution)/shard_map/ppermute | solution.py:37
  417.1 230.5 %reduce-scatter.8.cloned.1.call-start = ((), (), s32[]{:S(2)}) async-start(), calls=%async_computation.9 | async-start | bytes 9437184 | tf_op jit(solution)/shard_map/reduce_scatter | solution.py:690
  443.6 17.6 %collective-permute-start.46 = (bf16[512,512]{1,0:T(8,128)(2,1)}, bf16[512,512]{1,0:T(8,128)(2,1)S(1)}, u32[]{:S(2)}, u32[]{:S(2)}) collective-permute-start(bf16[512,512]{1,0:T(8,128)(2,1)} %get-tuple-element.230), channel_id=1, source_target_pairs={{0,16},{1,17},{2,18},{3,19},{4,20},{5,21},{6,22},{7,23},{8,24},{9,... | collective-permute-start | bytes 1572872 | tf_op jit(solution)/shard_map/ppermute | solution.py:37
  444.4 16.9 %collective-permute-start.45 = (bf16[512,512]{1,0:T(8,128)(2,1)}, bf16[512,512]{1,0:T(8,128)(2,1)S(1)}, u32[]{:S(2)}, u32[]{:S(2)}) collective-permute-start(bf16[512,512]{1,0:T(8,128)(2,1)} %get-tuple-element.223), channel_id=1, source_target_pairs={{0,1},{1,0},{2,3},{3,2},{4,5},{5,4},{6,7},{7,6},{8,9},{9,8},{10,11... | collective-permute-start | bytes 1572872 | tf_op jit(solution)/shard_map/ppermute | solution.py:37
  451.6 15.5 %collective-permute-start.47 = (bf16[512,512]{1,0:T(8,128)(2,1)}, bf16[512,512]{1,0:T(8,128)(2,1)S(1)}, u32[]{:S(2)}, u32[]{:S(2)}) collective-permute-start(bf16[512,512]{1,0:T(8,128)(2,1)} %get-tuple-element.225), channel_id=1, source_target_pairs={{0,1},{1,0},{2,3},{3,2},{4,5},{5,4},{6,7},{7,6},{8,9},{9,8},{10,11... | collective-permute-start | bytes 1572872 | tf_op jit(solution)/shard_map/ppermute | solution.py:37
  466.0 25.0 %collective-permute-start.50 = (bf16[512,512]{1,0:T(8,128)(2,1)}, bf16[512,512]{1,0:T(8,128)(2,1)S(1)}, u32[]{:S(2)}, u32[]{:S(2)}) collective-permute-start(bf16[512,512]{1,0:T(8,128)(2,1)} %get-tuple-element.239), channel_id=1, source_target_pairs={{0,1},{1,0},{2,3},{3,2},{4,5},{5,4},{6,7},{7,6},{8,9},{9,8},{10,11... | collective-permute-start | bytes 1572872 | tf_op jit(solution)/shard_map/ppermute | solution.py:37
  466.8 24.1 %collective-permute-start.49 = (bf16[512,512]{1,0:T(8,128)(2,1)}, bf16[512,512]{1,0:T(8,128)(2,1)S(1)}, u32[]{:S(2)}, u32[]{:S(2)}) collective-permute-start(bf16[512,512]{1,0:T(8,128)(2,1)} %get-tuple-element.231), channel_id=1, source_target_pairs={{0,16},{1,17},{2,18},{3,19},{4,20},{5,21},{6,22},{7,23},{8,24},{9,... | collective-permute-start | bytes 1572872 | tf_op jit(solution)/shard_map/ppermute | solution.py:37
  512.5 198.0 %reduce-scatter.6.cloned.1.call-start = ((), (), s32[]{:S(2)}) async-start(), calls=%async_computation.8 | async-start | bytes 9437184 | tf_op jit(solution)/shard_map/reduce_scatter | solution.py:690
  513.5 12.9 %collective-permute-start.54 = (bf16[512,512]{1,0:T(8,128)(2,1)S(1)}, bf16[512,512]{1,0:T(8,128)(2,1)S(1)}, u32[]{:S(2)}, u32[]{:S(2)}) collective-permute-start(bf16[512,512]{1,0:T(8,128)(2,1)S(1)} %copy-done.18), channel_id=1, source_target_pairs={{0,1},{1,0},{2,3},{3,2},{4,5},{5,4},{6,7},{7,6},{8,9},{9,8},{10,11... | collective-permute-start | bytes 1572872 | tf_op jit(solution)/shard_map/ppermute | solution.py:37
  514.7 12.6 %collective-permute-start.57 = (bf16[512,512]{1,0:T(8,128)(2,1)S(1)}, bf16[512,512]{1,0:T(8,128)(2,1)S(1)}, u32[]{:S(2)}, u32[]{:S(2)}) collective-permute-start(bf16[512,512]{1,0:T(8,128)(2,1)S(1)} %copy-done.19), channel_id=1, source_target_pairs={{0,16},{1,17},{2,18},{3,19},{4,20},{5,21},{6,22},{7,23},{8,24},{9,... | collective-permute-start | bytes 1572872 | tf_op jit(solution)/shard_map/ppermute | solution.py:37
  515.5 17.1 %collective-permute-start.56 = (bf16[512,512]{1,0:T(8,128)(2,1)S(1)}, bf16[512,512]{1,0:T(8,128)(2,1)}, u32[]{:S(2)}, u32[]{:S(2)}) collective-permute-start(bf16[512,512]{1,0:T(8,128)(2,1)S(1)} %copy-done.18), channel_id=1, source_target_pairs={{0,16},{1,17},{2,18},{3,19},{4,20},{5,21},{6,22},{7,23},{8,24},{9,... | collective-permute-start | bytes 1572872 | tf_op jit(solution)/shard_map/ppermute | solution.py:37
  516.7 15.9 %collective-permute-start.55 = (bf16[512,512]{1,0:T(8,128)(2,1)S(1)}, bf16[512,512]{1,0:T(8,128)(2,1)}, u32[]{:S(2)}, u32[]{:S(2)}) collective-permute-start(bf16[512,512]{1,0:T(8,128)(2,1)S(1)} %copy-done.19), channel_id=1, source_target_pairs={{0,1},{1,0},{2,3},{3,2},{4,5},{5,4},{6,7},{7,6},{8,9},{9,8},{10,11... | collective-permute-start | bytes 1572872 | tf_op jit(solution)/shard_map/ppermute | solution.py:37
  526.5 14.0 %collective-permute-start.58 = (bf16[512,512]{1,0:T(8,128)(2,1)S(1)}, bf16[512,512]{1,0:T(8,128)(2,1)}, u32[]{:S(2)}, u32[]{:S(2)}) collective-permute-start(bf16[512,512]{1,0:T(8,128)(2,1)S(1)} %collective-permute-done.54.refs_2_.refs_11_), channel_id=1, source_target_pairs={{0,16},{1,17},{2,18},{3,19},{4,20},{5,21},{6,22},{7,23},{8,24},{9,... | collective-permute-start | bytes 1572872 | tf_op jit(solution)/shard_map/ppermute | solution.py:37
  527.2 13.2 %collective-permute-start.59 = (bf16[512,512]{1,0:T(8,128)(2,1)S(1)}, bf16[512,512]{1,0:T(8,128)(2,1)}, u32[]{:S(2)}, u32[]{:S(2)}) collective-permute-start(bf16[512,512]{1,0:T(8,128)(2,1)S(1)} %collective-permute-done.57.refs_5_.refs_14_), channel_id=1, source_target_pairs={{0,1},{1,0},{2,3},{3,2},{4,5},{5,4},{6,7},{7,6},{8,9},{9,8},{10,11... | collective-permute-start | bytes 1572872 | tf_op jit(solution)/shard_map/ppermute | solution.py:37
  548.9 25.3 %collective-permute-start.60 = (bf16[2048,128]{1,0:T(8,128)(2,1)S(1)}, bf16[2048,128]{1,0:T(8,128)(2,1)S(1)}, u32[]{:S(2)}, u32[]{:S(2)}) collective-permute-start(bf16[2048,128]{1,0:T(8,128)(2,1)S(1)} %get-tuple-element.301), channel_id=1, source_target_pairs={{0,16},{1,17},{2,18},{3,19},{4,20},{5,21},{6,22},{7,23},{8,24},{9,... | collective-permute-start | bytes 1572872 | tf_op jit(solution)/shard_map/ppermute | solution.py:37
  550.1 24.1 %collective-permute-start.61 = (bf16[512,512]{1,0:T(8,128)(2,1)S(1)}, bf16[512,512]{1,0:T(8,128)(2,1)S(1)}, u32[]{:S(2)}, u32[]{:S(2)}) collective-permute-start(bf16[512,512]{1,0:T(8,128)(2,1)S(1)} %get-tuple-element.295), channel_id=1, source_target_pairs={{0,16},{1,17},{2,18},{3,19},{4,20},{5,21},{6,22},{7,23},{8,24},{9,... | collective-permute-start | bytes 1572872 | tf_op jit(solution)/shard_map/ppermute | solution.py:37
  600.5 19.5 %collective-permute-start.63 = (bf16[512,512]{1,0:T(8,128)(2,1)}, bf16[512,512]{1,0:T(8,128)(2,1)S(1)}, u32[]{:S(2)}, u32[]{:S(2)}) collective-permute-start(bf16[512,512]{1,0:T(8,128)(2,1)} %get-tuple-element.264), channel_id=1, source_target_pairs={{0,16},{1,17},{2,18},{3,19},{4,20},{5,21},{6,22},{7,23},{8,24},{9,... | collective-permute-start | bytes 1572872 | tf_op jit(solution)/shard_map/ppermute | solution.py:37
  601.6 18.4 %collective-permute-start.62 = (bf16[512,512]{1,0:T(8,128)(2,1)}, bf16[512,512]{1,0:T(8,128)(2,1)S(1)}, u32[]{:S(2)}, u32[]{:S(2)}) collective-permute-start(bf16[512,512]{1,0:T(8,128)(2,1)} %get-tuple-element.257), channel_id=1, source_target_pairs={{0,1},{1,0},{2,3},{3,2},{4,5},{5,4},{6,7},{7,6},{8,9},{9,8},{10,11... | collective-permute-start | bytes 1572872 | tf_op jit(solution)/shard_map/ppermute | solution.py:37
  609.9 19.1 %collective-permute-start.64 = (bf16[512,512]{1,0:T(8,128)(2,1)}, bf16[512,512]{1,0:T(8,128)(2,1)S(1)}, u32[]{:S(2)}, u32[]{:S(2)}) collective-permute-start(bf16[512,512]{1,0:T(8,128)(2,1)} %get-tuple-element.259), channel_id=1, source_target_pairs={{0,1},{1,0},{2,3},{3,2},{4,5},{5,4},{6,7},{7,6},{8,9},{9,8},{10,11... | collective-permute-start | bytes 1572872 | tf_op jit(solution)/shard_map/ppermute | solution.py:37
  617.4 11.7 %collective-permute-start.65 = (bf16[512,512]{1,0:T(8,128)(2,1)}, bf16[512,512]{1,0:T(8,128)(2,1)S(1)}, u32[]{:S(2)}, u32[]{:S(2)}) collective-permute-start(bf16[512,512]{1,0:T(8,128)(2,1)} %get-tuple-element.267), channel_id=1, source_target_pairs={{0,16},{1,17},{2,18},{3,19},{4,20},{5,21},{6,22},{7,23},{8,24},{9,... | collective-permute-start | bytes 1572872 | tf_op jit(solution)/shard_map/ppermute | solution.py:37
  642.5 40.6 %all-to-all-start.3 = ((bf16[4,1024,128]{2,1,0:T(8,128)(2,1)}), bf16[4,1024,128]{2,1,0:T(8,128)(2,1)}, u32[]{:S(2)}, u32[]{:S(2)}) async-start(bf16[4,1024,128]{2,1,0:T(8,128)(2,1)} %shard_map.350), calls=%async_computation.4 | async-start | bytes 2097152 | tf_op jit(solution)/shard_map/all_to_all | solution.py:620
  648.7 40.1 %collective-permute-start.71 = (f32[4,1664]{1,0:T(4,128)S(1)}, f32[4,1664]{1,0:T(4,128)S(1)}, u32[]{:S(2)}, u32[]{:S(2)}) collective-permute-start(f32[4,1664]{1,0:T(4,128)S(1)} %add.91), channel_id=1, source_target_pairs={{0,2},{1,3},{2,0},{3,1},{4,6},{5,7},{6,4},{7,5},{8,10},{9,11},{10,... | collective-permute-start | bytes 79880 | tf_op jit(solution)/shard_map/ppermute | solution.py:37
  651.9 36.9 %collective-permute-start.72 = (bf16[512,512]{1,0:T(8,128)(2,1)}, bf16[512,512]{1,0:T(8,128)(2,1)}, u32[]{:S(2)}, u32[]{:S(2)}) collective-permute-start(bf16[512,512]{1,0:T(8,128)(2,1)} %get-tuple-element.297), channel_id=1, source_target_pairs={{0,16},{1,17},{2,18},{3,19},{4,20},{5,21},{6,22},{7,23},{8,24},{9,... | collective-permute-start | bytes 1572872 | tf_op jit(solution)/shard_map/ppermute | solution.py:37
  (105 other events, 570.9 us)
Sparse Core Ops, SparseCore 0:
  28.3 106.2 all-gather.6
  136.2 80.4 all-gather.8
  218.2 80.5 all-gather.10
  417.2 88.9 reduce-scatter.3
  512.6 89.6 reduce-scatter.7
  604.5 105.9 reduce-scatter.5
